TPU v7x, 32 devices: a whole 2x2x4 slice. The times are simulated.
32 devices in a mesh: dp: 4 (over z), ctx: 4 (over y, x), exp: 2 (over core).
Axes of the slice: x: 2, y: 2, z: 4, core: 2. Of those that a mesh axis runs over, the one named last changes fastest.
Arguments:
- tokens: bfloat16 [8, 1024, 2048], P(('dp', 'exp'), 'ctx'), may hold values from -6 to 6
- attention_gain: float32 [2048], P(('dp', 'ctx', 'exp')), may hold values from 0.5 to 1.5
- query_weight: float32 [2048, 4096], P(('dp', 'ctx', 'exp')), may hold values from -0.125 to 0.125
- key_weight: float32 [2048, 512], P(('dp', 'ctx', 'exp')), may hold values from -0.125 to 0.125
- value_weight: float32 [2048, 512], P(('dp', 'ctx', 'exp')), may hold values from -0.125 to 0.125
- query_gain: float32 [128], P(('dp', 'ctx', 'exp')), may hold values from 0.5 to 1.5
- key_gain: float32 [128], P(('dp', 'ctx', 'exp')), may hold values from 0.5 to 1.5
- output_weight: float32 [4096, 2048], P(('dp', 'ctx', 'exp')), may hold values from -0.5 to 0.5
- mixture_gain: float32 [2048], P(('dp', 'ctx', 'exp')), may hold values from 0.5 to 1.5
- router_weight: float32 [2048, 32], P(('dp', 'ctx', 'exp')), may hold values from -0.0625 to 0.0625
- gate_weight: bfloat16 [32, 2048, 768], P(('dp', 'ctx', 'exp')), may hold values from -0.125 to 0.125
- up_weight: bfloat16 [32, 2048, 768], P(('dp', 'ctx', 'exp')), may hold values from -0.125 to 0.125
- down_weight: bfloat16 [32, 768, 2048], P(('dp', 'ctx', 'exp')), may hold values from -0.625 to 0.625
- routes: int32 [8, 1024, 8], P(('dp', 'exp'), 'ctx'), may hold values from 0 to 31, all different within a row; in each aligned block of 256 rows (0 to 255, 256 to 511, ..., all dimensions but the last counted through in order) at most 72 rows name the same one
- bounds: int32 [8, 2], P(('dp', 'exp')), may hold values from 1 to 1023, as said below
- cotangent: bfloat16 [8, 1024, 2048], P(('dp', 'exp'), 'ctx'), may hold values from -6 to 6
Outputs:
- output: bfloat16 [8, 1024, 2048], P(('dp', 'exp'), 'ctx')
- tokens_grad: bfloat16 [8, 1024, 2048], P(('dp', 'exp'), 'ctx')
- attention_gain_grad: float32 [2048], P(('dp', 'ctx', 'exp'))
- query_weight_grad: float32 [2048, 4096], P(('dp', 'ctx', 'exp'))
- key_weight_grad: float32 [2048, 512], P(('dp', 'ctx', 'exp'))
- value_weight_grad: float32 [2048, 512], P(('dp', 'ctx', 'exp'))
- query_gain_grad: float32 [128], P(('dp', 'ctx', 'exp'))
- key_gain_grad: float32 [128], P(('dp', 'ctx', 'exp'))
- output_weight_grad: float32 [4096, 2048], P(('dp', 'ctx', 'exp'))
- mixture_gain_grad: float32 [2048], P(('dp', 'ctx', 'exp'))
- router_weight_grad: float32 [2048, 32], P(('dp', 'ctx', 'exp'))
- gate_weight_grad: float32 [32, 2048, 768], P(('dp', 'ctx', 'exp'))
- up_weight_grad: float32 [32, 2048, 768], P(('dp', 'ctx', 'exp'))
- down_weight_grad: float32 [32, 768, 2048], P(('dp', 'ctx', 'exp'))
Inputs may be any that keep to these rules, and one draw needn't show every extreme that they name: `routes`: each row names 8 different experts. Among the 256 tokens of one device no expert is named more than 72 times, and in some devices' tokens some expert exactly 72 times. A sequence's documents are [0, bounds[s, 0]), [bounds[s, 0], bounds[s, 1]) and [bounds[s, 1], 1024); bounds[s, 0] is at most 128 and bounds[s, 1] at least 896.
All inputs are finite; a program needn't handle non-finite values.
Results may differ from a plain program's by a relative error of at most 0.02.
Values may be sent and summed in bfloat16 or wider, within the bound.
A program may use at most 448 MiB of HBM per device.

v0:
```python
import jax
import jax.numpy as jnp
from jax import lax
from jax.sharding import PartitionSpec as P

eps_norm = 1e-06
rope_base = 1000000.0
masked_score = -1e30


def rope_tables(positions, width):
    exponents = jnp.arange(width // 2, dtype=jnp.float32) * (2.0 / width)
    frequency = rope_base ** (-exponents)
    angles = positions.astype(jnp.float32)[:, None] * frequency[None, :]
    angles = jnp.concatenate([angles, angles], axis=-1)
    return (jnp.cos(angles), jnp.sin(angles))


def turn_ahead(values):
    half = values.shape[-1] // 2
    return jnp.concatenate([-values[..., half:], values[..., :half]], axis=-1)


def turn_behind(values):
    half = values.shape[-1] // 2
    return jnp.concatenate([values[..., half:], -values[..., :half]], axis=-1)


def norm_rope(raw, gain, cosine, sine):
    inverse = lax.rsqrt(jnp.mean(raw * raw, axis=-1, keepdims=True) + eps_norm)
    normed = raw * inverse
    scaled = normed * gain
    return (scaled * cosine + turn_ahead(scaled) * sine, normed, inverse)


def norm_rope_back(grad, normed, inverse, gain, cosine, sine):
    scaled_grad = grad * cosine + turn_behind(grad * sine)
    gain_grad = jnp.sum(scaled_grad * normed, axis=(0, 1))
    inner = scaled_grad * gain
    return (
        inverse * (inner - normed * jnp.mean(inner * normed, axis=-1, keepdims=True)),
        gain_grad,
    )


def norm_back(grad, normed, inverse, gain):
    gain_grad = jnp.sum(grad * normed, axis=0)
    scaled = grad * gain
    return (
        inverse * (scaled - normed * jnp.mean(scaled * normed, axis=-1, keepdims=True)),
        gain_grad,
    )


def expert_front(expert_in, gate_weight, up_weight):
    gate_pre = jnp.einsum(
        "necd,edf->necf", expert_in, gate_weight, preferred_element_type=jnp.float32
    )
    up_pre = jnp.einsum("necd,edf->necf", expert_in, up_weight, preferred_element_type=jnp.float32)
    activated = (jax.nn.silu(gate_pre) * up_pre).astype(jnp.bfloat16)
    return (gate_pre, up_pre, activated)


def shards(
    tokens,
    attention_gain,
    query_weight,
    key_weight,
    value_weight,
    query_gain,
    key_gain,
    output_weight,
    mixture_gain,
    router_weight,
    gate_weight,
    up_weight,
    down_weight,
    routes,
    bounds,
    cotangent,
):
    (
        first_gain,
        query_full,
        key_full,
        value_full,
        query_scale,
        key_scale,
        output_full,
        second_gain,
        router_full,
    ) = (
        lax.all_gather(
            attention_gain.astype(jnp.bfloat16), ("dp", "ctx", "exp"), axis=0, tiled=True
        ),
        lax.all_gather(query_weight.astype(jnp.bfloat16), ("dp", "ctx", "exp"), axis=0, tiled=True),
        lax.all_gather(key_weight.astype(jnp.bfloat16), ("dp", "ctx", "exp"), axis=0, tiled=True),
        lax.all_gather(value_weight.astype(jnp.bfloat16), ("dp", "ctx", "exp"), axis=0, tiled=True),
        lax.all_gather(query_gain.astype(jnp.bfloat16), ("dp", "ctx", "exp"), axis=0, tiled=True),
        lax.all_gather(key_gain.astype(jnp.bfloat16), ("dp", "ctx", "exp"), axis=0, tiled=True),
        lax.all_gather(
            output_weight.astype(jnp.bfloat16), ("dp", "ctx", "exp"), axis=0, tiled=True
        ),
        lax.all_gather(mixture_gain.astype(jnp.bfloat16), ("dp", "ctx", "exp"), axis=0, tiled=True),
        lax.all_gather(
            router_weight.astype(jnp.bfloat16), ("dp", "ctx", "exp"), axis=0, tiled=True
        ),
    )
    first_gain = first_gain.astype(jnp.float32)
    second_gain = second_gain.astype(jnp.float32)
    query_scale = query_scale.astype(jnp.float32)
    key_scale = key_scale.astype(jnp.float32)
    tok_count = tokens.shape[1]
    width = tokens.shape[2]
    head_dim = query_scale.shape[0]
    heads = query_full.shape[1] // head_dim
    kv_heads = key_full.shape[1] // head_dim
    group_size = heads // kv_heads
    score_scale = head_dim ** (-0.5)
    inputs = tokens[0].astype(jnp.float32)
    first_inverse = lax.rsqrt(jnp.mean(inputs * inputs, axis=-1, keepdims=True) + eps_norm)
    first_normed = inputs * first_inverse
    hidden = (first_normed * first_gain).astype(jnp.bfloat16)
    positions = lax.axis_index("ctx") * tok_count + jnp.arange(tok_count, dtype=jnp.int32)
    cosine, sine = rope_tables(positions, head_dim)
    cosine = cosine[:, None, :]
    sine = sine[:, None, :]
    query_raw = jnp.dot(hidden, query_full, preferred_element_type=jnp.float32).reshape(
        tok_count, heads, head_dim
    )
    key_raw = jnp.dot(hidden, key_full, preferred_element_type=jnp.float32).reshape(
        tok_count, kv_heads, head_dim
    )
    value_raw = jnp.dot(hidden, value_full, preferred_element_type=jnp.float32).reshape(
        tok_count, kv_heads, head_dim
    )
    query_rot, query_normed, query_inverse = norm_rope(query_raw, query_scale, cosine, sine)
    key_rot, key_normed, key_inverse = norm_rope(key_raw, key_scale, cosine, sine)
    query_low = query_rot.astype(jnp.bfloat16)
    key_low = key_rot.astype(jnp.bfloat16)
    value_low = value_raw.astype(jnp.bfloat16)
    keys_all, values_all = (
        lax.all_gather(key_low, "ctx", axis=0, tiled=True),
        lax.all_gather(value_low, "ctx", axis=0, tiled=True),
    )
    seq_len = keys_all.shape[0]
    key_pos = jnp.arange(seq_len, dtype=jnp.int32)
    first_end = bounds[0, 0]
    second_end = bounds[0, 1]
    doc_query = (positions >= first_end).astype(jnp.int32) + (positions >= second_end).astype(
        jnp.int32
    )
    doc_key = (key_pos >= first_end).astype(jnp.int32) + (key_pos >= second_end).astype(jnp.int32)
    allowed = (key_pos[None, :] <= positions[:, None]) & (doc_key[None, :] == doc_query[:, None])
    attended_parts = []
    lse_parts = []
    for group_index in range(kv_heads):
        query_group = query_low[:, group_index * group_size : (group_index + 1) * group_size, :]
        scores = (
            jnp.einsum(
                "tgd,sd->gts",
                query_group,
                keys_all[:, group_index, :],
                preferred_element_type=jnp.float32,
            )
            * score_scale
        )
        scores = jnp.where(allowed[None], scores, masked_score)
        highest = jnp.max(scores, axis=-1, keepdims=True)
        weights = jnp.exp(scores - highest)
        totals = jnp.sum(weights, axis=-1, keepdims=True)
        shares_low = (weights / totals).astype(jnp.bfloat16)
        attended_parts.append(
            jnp.einsum(
                "gts,sd->tgd",
                shares_low,
                values_all[:, group_index, :],
                preferred_element_type=jnp.float32,
            )
        )
        lse_parts.append(highest + jnp.log(totals))
    attended = jnp.concatenate(attended_parts, axis=1)
    attended_low = attended.astype(jnp.bfloat16).reshape(tok_count, heads * head_dim)
    branch = jnp.dot(attended_low, output_full, preferred_element_type=jnp.float32)
    middle = inputs + branch
    second_inverse = lax.rsqrt(jnp.mean(middle * middle, axis=-1, keepdims=True) + eps_norm)
    second_normed = middle * second_inverse
    mixed_low = (second_normed * second_gain).astype(jnp.bfloat16)
    logits = jnp.dot(mixed_low, router_full, preferred_element_type=jnp.float32)
    selected = routes[0]
    gates = jax.nn.softmax(jnp.take_along_axis(logits, selected, axis=1), axis=-1)
    experts = router_full.shape[1]
    topk = selected.shape[1]
    base_rows = tok_count * topk // experts
    capacity = base_rows + max(1, base_rows // 8)
    local_experts = gate_weight.shape[0]
    devices_all = experts // local_experts
    assignments = tok_count * topk
    flat_choice = selected.reshape(-1)
    route_table = (
        selected[:, :, None] == jnp.arange(experts, dtype=jnp.int32)[None, None, :]
    ).astype(jnp.float32)
    token_hot = jnp.sum(route_table, axis=1).astype(jnp.bfloat16)
    row_ids = jnp.arange(tok_count, dtype=jnp.int32)
    earlier = (row_ids[None, :] < row_ids[:, None]).astype(jnp.bfloat16)
    before = jnp.dot(earlier, token_hot, preferred_element_type=jnp.float32)
    rank = jnp.einsum("tke,te->tk", route_table, before).reshape(-1).astype(jnp.int32)
    slot_of = flat_choice * capacity + rank
    slot_assign = (
        jnp.full((experts * capacity,), assignments, jnp.int32)
        .at[slot_of]
        .set(jnp.arange(assignments, dtype=jnp.int32))
    )
    slot_token = slot_assign // topk
    padded_rows = jnp.concatenate([mixed_low, jnp.zeros((1, width), jnp.bfloat16)], axis=0)
    send_rows = padded_rows[slot_token].reshape(devices_all, local_experts * capacity, width)
    received = lax.all_to_all(
        send_rows, ("dp", "ctx", "exp"), split_axis=0, concat_axis=0, tiled=True
    )
    expert_in = received.reshape(devices_all, local_experts, capacity, width)
    gate_pre, up_pre, activated = expert_front(expert_in, gate_weight, up_weight)
    expert_out = jnp.einsum(
        "necf,efd->necd", activated, down_weight, preferred_element_type=jnp.float32
    ).astype(jnp.bfloat16)
    expert_out = expert_out.reshape(devices_all, local_experts * capacity, width)
    returned = lax.all_to_all(
        expert_out, ("dp", "ctx", "exp"), split_axis=0, concat_axis=0, tiled=True
    )
    picked_rows = returned.reshape(experts * capacity, width)[slot_of].reshape(
        tok_count, topk, width
    )
    mixture = jnp.einsum("tk,tkd->td", gates, picked_rows.astype(jnp.float32))
    result = middle + mixture
    output = result.astype(jnp.bfloat16)[None]
    grad_out = cotangent[0].astype(jnp.float32)
    gate_grads = jnp.einsum("td,tkd->tk", grad_out, picked_rows.astype(jnp.float32))
    picked_grads = gates * (gate_grads - jnp.sum(gates * gate_grads, axis=-1, keepdims=True))
    logit_grads = jnp.sum(picked_grads[:, :, None] * route_table, axis=1).astype(jnp.bfloat16)
    gate_flat = jnp.concatenate([gates.reshape(-1), jnp.zeros((1,), jnp.float32)])
    grad_rows = jnp.concatenate([cotangent[0], jnp.zeros((1, width), jnp.bfloat16)], axis=0)
    slot_grads = (
        gate_flat[slot_assign][:, None] * grad_rows[slot_token].astype(jnp.float32)
    ).astype(jnp.bfloat16)
    slot_grads = slot_grads.reshape(devices_all, local_experts * capacity, width)
    grads_in = lax.all_to_all(
        slot_grads, ("dp", "ctx", "exp"), split_axis=0, concat_axis=0, tiled=True
    )
    grads_in = grads_in.reshape(devices_all, local_experts, capacity, width)
    act_grad = jnp.einsum(
        "necd,efd->necf", grads_in, down_weight, preferred_element_type=jnp.float32
    )
    down_grad = jnp.einsum(
        "necf,necd->efd", activated, grads_in, preferred_element_type=jnp.float32
    )
    sigma = jax.nn.sigmoid(gate_pre)
    up_grad_pre = (act_grad * (gate_pre * sigma)).astype(jnp.bfloat16)
    gate_grad_pre = (act_grad * up_pre * sigma * (1.0 + gate_pre * (1.0 - sigma))).astype(
        jnp.bfloat16
    )
    gate_w_grad = jnp.einsum(
        "necd,necf->edf", expert_in, gate_grad_pre, preferred_element_type=jnp.float32
    )
    up_w_grad = jnp.einsum(
        "necd,necf->edf", expert_in, up_grad_pre, preferred_element_type=jnp.float32
    )
    rows_grad = jnp.einsum(
        "necf,edf->necd", gate_grad_pre, gate_weight, preferred_element_type=jnp.float32
    ) + jnp.einsum("necf,edf->necd", up_grad_pre, up_weight, preferred_element_type=jnp.float32)
    rows_grad = rows_grad.astype(jnp.bfloat16).reshape(devices_all, local_experts * capacity, width)
    back_rows = lax.all_to_all(
        rows_grad, ("dp", "ctx", "exp"), split_axis=0, concat_axis=0, tiled=True
    )
    assign_grads = back_rows.reshape(experts * capacity, width)[slot_of].reshape(
        tok_count, topk, width
    )
    mixed_grad = jnp.sum(assign_grads.astype(jnp.float32), axis=1)
    mixed_grad = mixed_grad + jnp.einsum(
        "te,de->td", logit_grads, router_full, preferred_element_type=jnp.float32
    )
    router_grad = jnp.einsum(
        "td,te->de", mixed_low, logit_grads, preferred_element_type=jnp.float32
    )
    middle_back, second_gain_grad = norm_back(
        mixed_grad, second_normed, second_inverse, second_gain
    )
    middle_grad = grad_out + middle_back
    branch_low = middle_grad.astype(jnp.bfloat16)
    output_w_grad = jnp.einsum(
        "ti,td->id", attended_low, branch_low, preferred_element_type=jnp.float32
    )
    attended_grad = jnp.einsum(
        "td,id->ti", branch_low, output_full, preferred_element_type=jnp.float32
    )
    attended_grad = attended_grad.astype(jnp.bfloat16).reshape(tok_count, heads, head_dim)
    query_grad_parts = []
    key_grad_parts = []
    value_grad_parts = []
    for group_index in range(kv_heads):
        query_group = query_low[:, group_index * group_size : (group_index + 1) * group_size, :]
        grad_group = attended_grad[:, group_index * group_size : (group_index + 1) * group_size, :]
        scores = (
            jnp.einsum(
                "tgd,sd->gts",
                query_group,
                keys_all[:, group_index, :],
                preferred_element_type=jnp.float32,
            )
            * score_scale
        )
        scores = jnp.where(allowed[None], scores, masked_score)
        shares = jnp.exp(scores - lse_parts[group_index])
        shares_low = shares.astype(jnp.bfloat16)
        share_grads = jnp.einsum(
            "tgd,sd->gts",
            grad_group,
            values_all[:, group_index, :],
            preferred_element_type=jnp.float32,
        )
        centre = jnp.sum(shares * share_grads, axis=-1, keepdims=True)
        score_grads = (shares * (share_grads - centre)).astype(jnp.bfloat16)
        query_grad_parts.append(
            jnp.einsum(
                "gts,sd->tgd",
                score_grads,
                keys_all[:, group_index, :],
                preferred_element_type=jnp.float32,
            )
            * score_scale
        )
        key_grad_parts.append(
            jnp.einsum("gts,tgd->sd", score_grads, query_group, preferred_element_type=jnp.float32)
            * score_scale
        )
        value_grad_parts.append(
            jnp.einsum("gts,tgd->sd", shares_low, grad_group, preferred_element_type=jnp.float32)
        )
    query_grad = jnp.concatenate(query_grad_parts, axis=1)
    key_grads = jnp.stack(key_grad_parts, axis=1)
    value_grads = jnp.stack(value_grad_parts, axis=1)
    key_grad_local, value_grad_local = (
        lax.psum_scatter(
            key_grads.astype(jnp.bfloat16), "ctx", scatter_dimension=0, tiled=True
        ).astype(jnp.float32),
        lax.psum_scatter(
            value_grads.astype(jnp.bfloat16), "ctx", scatter_dimension=0, tiled=True
        ).astype(jnp.float32),
    )
    query_raw_grad, query_gain_grad = norm_rope_back(
        query_grad, query_normed, query_inverse, query_scale, cosine, sine
    )
    key_raw_grad, key_gain_grad = norm_rope_back(
        key_grad_local, key_normed, key_inverse, key_scale, cosine, sine
    )
    query_grad_low = query_raw_grad.astype(jnp.bfloat16).reshape(tok_count, heads * head_dim)
    key_grad_low = key_raw_grad.astype(jnp.bfloat16).reshape(tok_count, kv_heads * head_dim)
    value_grad_low = value_grad_local.astype(jnp.bfloat16).reshape(tok_count, kv_heads * head_dim)
    query_w_grad = jnp.einsum(
        "td,ti->di", hidden, query_grad_low, preferred_element_type=jnp.float32
    )
    key_w_grad = jnp.einsum("td,ti->di", hidden, key_grad_low, preferred_element_type=jnp.float32)
    value_w_grad = jnp.einsum(
        "td,ti->di", hidden, value_grad_low, preferred_element_type=jnp.float32
    )
    hidden_grad = (
        jnp.einsum("ti,di->td", query_grad_low, query_full, preferred_element_type=jnp.float32)
        + jnp.einsum("ti,di->td", key_grad_low, key_full, preferred_element_type=jnp.float32)
        + jnp.einsum("ti,di->td", value_grad_low, value_full, preferred_element_type=jnp.float32)
    )
    input_back, first_gain_grad = norm_back(hidden_grad, first_normed, first_inverse, first_gain)
    tokens_grad = (middle_grad + input_back).astype(jnp.bfloat16)[None]
    (
        first_share,
        query_share,
        key_share,
        value_share,
        query_gain_share,
        key_gain_share,
        output_share,
        second_share,
        router_share,
    ) = (
        lax.psum_scatter(first_gain_grad, ("dp", "ctx", "exp"), scatter_dimension=0, tiled=True),
        lax.psum_scatter(query_w_grad, ("dp", "ctx", "exp"), scatter_dimension=0, tiled=True),
        lax.psum_scatter(key_w_grad, ("dp", "ctx", "exp"), scatter_dimension=0, tiled=True),
        lax.psum_scatter(value_w_grad, ("dp", "ctx", "exp"), scatter_dimension=0, tiled=True),
        lax.psum_scatter(query_gain_grad, ("dp", "ctx", "exp"), scatter_dimension=0, tiled=True),
        lax.psum_scatter(key_gain_grad, ("dp", "ctx", "exp"), scatter_dimension=0, tiled=True),
        lax.psum_scatter(output_w_grad, ("dp", "ctx", "exp"), scatter_dimension=0, tiled=True),
        lax.psum_scatter(second_gain_grad, ("dp", "ctx", "exp"), scatter_dimension=0, tiled=True),
        lax.psum_scatter(router_grad, ("dp", "ctx", "exp"), scatter_dimension=0, tiled=True),
    )
    return (
        output,
        tokens_grad,
        first_share,
        query_share,
        key_share,
        value_share,
        query_gain_share,
        key_gain_share,
        output_share,
        second_share,
        router_share,
        gate_w_grad,
        up_w_grad,
        down_grad,
    )


def solution(mesh):
    in_specs = (
        P(("dp", "exp"), "ctx", None),
        P(("dp", "ctx", "exp")),
        P(("dp", "ctx", "exp"), None),
        P(("dp", "ctx", "exp"), None),
        P(("dp", "ctx", "exp"), None),
        P(("dp", "ctx", "exp")),
        P(("dp", "ctx", "exp")),
        P(("dp", "ctx", "exp"), None),
        P(("dp", "ctx", "exp")),
        P(("dp", "ctx", "exp"), None),
        P(("dp", "ctx", "exp"), None, None),
        P(("dp", "ctx", "exp"), None, None),
        P(("dp", "ctx", "exp"), None, None),
        P(("dp", "exp"), "ctx", None),
        P(("dp", "exp"), None),
        P(("dp", "exp"), "ctx", None),
    )
    out_specs = (
        P(("dp", "exp"), "ctx", None),
        P(("dp", "exp"), "ctx", None),
        P(("dp", "ctx", "exp")),
        P(("dp", "ctx", "exp"), None),
        P(("dp", "ctx", "exp"), None),
        P(("dp", "ctx", "exp"), None),
        P(("dp", "ctx", "exp")),
        P(("dp", "ctx", "exp")),
        P(("dp", "ctx", "exp"), None),
        P(("dp", "ctx", "exp")),
        P(("dp", "ctx", "exp"), None),
        P(("dp", "ctx", "exp"), None, None),
        P(("dp", "ctx", "exp"), None, None),
        P(("dp", "ctx", "exp"), None, None),
    )
    return jax.shard_map(shards, mesh=mesh, in_specs=in_specs, out_specs=out_specs, check_vma=False)
```

profile of v0, /device:TPU:14, one launch (start us, length us, event | category | flops | bytes accessed | tf_op | source)
XLA Modules:
  0.0 2647.3 jit_solution(226074249389378029)
XLA Ops:
  16.3 40.6 %all-reduce.11 = (bf16[2048]{0:T(1024)(128)(2,1)S(1)}, bf16[128]{0:T(256)(128)(2,1)S(1)}, bf16[128]{0:T(256)(128)(2,1)S(1)}, bf16[2048]{0:T(1024)(128)(2,1)S(1)}) all-reduce(bf16[2048]{0:T(1024)(128)(2,1)S(1)} %dynamic-update-slice, bf16[128]{0:T(256)(128)(2,1)S(1)} %dynamic-update-slice.2, ...), channel_id=1, replica_groups=mesh['dp'=4,'ctx'=4,'exp'=2] {'dp','ctx','exp'}, use_global_device_ids=true, to_apply=%add.2 | all-reduce | flops 4352 | bytes 17408
  75.9 50.4 %all-gather.8.cloned.1.call-done = bf16[2048,512]{1,0:T(8,128)(2,1)} async-done(((bf16[64,512]{1,0:T(8,128)(2,1)}), bf16[2048,512]{1,0:T(8,128)(2,1)}) %all-gather.8.cloned.1.call-update) | async-done | bytes 2097168 | tf_op jit(solution)/shard_map/all_gather | solution.py:98
  139.3 31.1 %all-gather = bf16[32,64,32]{1,2,0:T(8,128)(2,1)S(1)} all-gather(bf16[1,64,32]{1,2,0:T(8,128)(2,1)S(1)} %convert_bitcast_fusion.1), channel_id=1, replica_groups=mesh['dp'=4,'ctx'=4,'exp'=2] {'dp','ctx','exp'}, dimensions={0}, use_global_device_ids=true | all-gather | bytes 135168 | tf_op jit(solution)/shard_map/all_gather | solution.py:105
  184.4 19.7 gather_fusion.3
  207.6 37.0 %all-gather.16.cloned.1.call-done = bf16[2048,4096]{1,0:T(8,128)(2,1)} async-done(((bf16[64,4096]{1,0:T(8,128)(2,1)}), bf16[2048,4096]{1,0:T(8,128)(2,1)}) %all-gather.16.cloned.1.call-update) | async-done | bytes 16777232 | tf_op jit(solution)/shard_map/all_gather | solution.py:96
  244.5 22.0 copy.151
  329.2 89.3 %all-gather.18.cloned.1.call-done = bf16[4096,2048]{1,0:T(8,128)(2,1)} async-done(((bf16[128,2048]{1,0:T(8,128)(2,1)}), bf16[4096,2048]{1,0:T(8,128)(2,1)}) %all-gather.18.cloned.1.call-update) | async-done | bytes 16777232 | tf_op jit(solution)/shard_map/all_gather | solution.py:101
  432.8 16.8 gather_fusion.5
  481.1 19.7 gather_fusion
  500.8 181.3 %all-to-all-done.2 = bf16[32,72,2048]{2,1,0:T(8,128)(2,1)} async-done(((bf16[32,72,2048]{2,1,0:T(8,128)(2,1)}), bf16[32,72,2048]{2,1,0:T(8,128)(2,1)}, u32[]{:S(2)}, u32[]{:S(2)}) %all-to-all-start.2) | async-done | bytes 9437216 | tf_op jit(solution)/shard_map/all_to_all | solution.py:245
  704.6 190.4 %all-to-all-done = bf16[32,72,2048]{2,1,0:T(8,128)(2,1)} async-done(((bf16[32,72,2048]{2,1,0:T(8,128)(2,1)}), bf16[32,72,2048]{2,1,0:T(8,128)(2,1)}, u32[]{:S(2)}, u32[]{:S(2)}) %all-to-all-start) | async-done | bytes 9437216 | tf_op jit(solution)/shard_map/all_to_all | solution.py:217
  908.0 17.9 fusion.53
  960.7 14.7 add_convert_fusion
  975.5 175.0 %all-to-all-done.1 = bf16[32,72,2048]{2,1,0:T(8,128)(2,1)} async-done(((bf16[32,72,2048]{2,1,0:T(8,128)(2,1)}), bf16[32,72,2048]{2,1,0:T(8,128)(2,1)}, u32[]{:S(2)}, u32[]{:S(2)}) %all-to-all-start.1) | async-done | bytes 9437216 | tf_op jit(solution)/shard_map/all_to_all | solution.py:226
  1160.3 21.5 gather_fusion.1
  1198.1 165.4 %all-to-all-done.3 = bf16[32,72,2048]{2,1,0:T(8,128)(2,1)} async-done(((bf16[32,72,2048]{2,1,0:T(8,128)(2,1)}), bf16[32,72,2048]{2,1,0:T(8,128)(2,1)}, u32[]{:S(2)}, u32[]{:S(2)}) %all-to-all-start.3) | async-done | bytes 9437216 | tf_op jit(solution)/shard_map/all_to_all | solution.py:270
  1363.5 21.6 gather_fusion.4
  1475.8 22.3 reduce-scatter.10.cloned.1.call-done
  1506.6 14.8 fusion.162
  1611.4 71.3 %all-reduce.10 = (f32[2048]{0:T(1024)S(1)}, f32[128]{0:T(128)S(1)}, f32[128]{0:T(128)S(1)}, f32[2048]{0:T(1024)S(1)}) all-reduce(f32[2048]{0:T(1024)S(1)} %get-tuple-element.18, f32[128]{0:T(128)S(1)} %get-tuple-element.14, f32[128]{0:T(128)S(1)} %get-tuple-element.20, ...), channel_id=4, replica_groups=mesh['dp'=4,'ctx'=4,'exp'=2] {'dp','ctx','exp'}, use_global_device_ids=true, to_apply=%region_30.31.clone | all-reduce | flops 4352 | bytes 34816
  1689.2 54.0 %reduce-scatter.18.cloned.1.call-done = f32[64,512]{1,0:T(8,128)} async-done(((f32[2048,512]{1,0:T(8,128)}), f32[64,512]{1,0:T(8,128)}) %reduce-scatter.18.cloned.1.call-update) | async-done | bytes 131088 | tf_op jit(solution)/shard_map/reduce_scatter | solution.py:385
  1743.2 139.8 %reduce-scatter.16.cloned.1.call-done = f32[64,512]{1,0:T(8,128)} async-done(((f32[2048,512]{1,0:T(8,128)}), f32[64,512]{1,0:T(8,128)}) %reduce-scatter.16.cloned.1.call-update) | async-done | bytes 131088 | tf_op jit(solution)/shard_map/reduce_scatter | solution.py:384
  1882.9 392.4 %reduce-scatter.20.cloned.1.call-done = f32[128,2048]{1,0:T(8,128)} async-done(((f32[4096,2048]{1,0:T(8,128)}), f32[128,2048]{1,0:T(8,128)}) %reduce-scatter.20.cloned.1.call-update) | async-done | bytes 1048592 | tf_op jit(solution)/shard_map/reduce_scatter | solution.py:388
  2275.4 364.9 %reduce-scatter.14.cloned.1.call-done = f32[64,4096]{1,0:T(8,128)} async-done(((f32[2048,4096]{1,0:T(8,128)}), f32[64,4096]{1,0:T(8,128)}) %reduce-scatter.14.cloned.1.call-update) | async-done | bytes 1048592 | tf_op jit(solution)/shard_map/reduce_scatter | solution.py:383
  (445 shorter events, 457.0 us)
Async XLA Ops:
  7.2 900.8 %copy-start = (bf16[1,2048,768]{2,1,0:T(8,128)(2,1)S(1)}, bf16[1,2048,768]{2,1,0:T(8,128)(2,1)}, u32[]{:S(2)}) copy-start(bf16[1,2048,768]{2,1,0:T(8,128)(2,1)} %param.26) | copy-start | bytes 9437188
  7.2 60.3 %all-gather.12.cloned.1.call-start = ((), (), s32[]{:S(2)}) async-start(), calls=%async_computation.13 | async-start | bytes 2162688 | tf_op jit(solution)/shard_map/all_gather | solution.py:97
  9.0 117.3 %all-gather.8.cloned.1.call-start = ((), (), s32[]{:S(2)}) async-start(), calls=%async_computation.11 | async-start | bytes 2162688 | tf_op jit(solution)/shard_map/all_gather | solution.py:98
  10.6 233.9 %all-gather.16.cloned.1.call-start = ((), (), s32[]{:S(2)}) async-start(), calls=%async_computation.15 | async-start | bytes 17301504 | tf_op jit(solution)/shard_map/all_gather | solution.py:96
  12.7 267.3 %all-gather.14.cloned.1.call-start = ((), (), s32[]{:S(2)}) async-start(), calls=%async_computation.14 | async-start | bytes 1310720 | tf_op jit(solution)/shard_map/all_gather | solution.py:143
  56.9 209.7 %copy-start.49 = (f32[2048]{0:T(1024)}, f32[2048]{0:T(1024)S(1)}, u32[]{:S(2)}) copy-start(f32[2048]{0:T(1024)S(1)} %convert_element_type.247) | copy-start | bytes 24580
  59.1 207.4 %copy-start.59 = (f32[256]{0:T(256)}, f32[256]{0:T(256)S(1)}, u32[]{:S(2)}) copy-start(f32[256]{0:T(256)S(1)} %add_rsqrt_fusion.3) | copy-start | bytes 3076
  75.8 236.6 %all-gather.10.cloned.1.call-start = ((), (), s32[]{:S(2)}) async-start(), calls=%async_computation.12 | async-start | bytes 1310720 | tf_op jit(solution)/shard_map/all_gather | solution.py:144
  133.6 285.0 %all-gather.18.cloned.1.call-start = ((), (), s32[]{:S(2)}) async-start(), calls=%async_computation.16 | async-start | bytes 17301504 | tf_op jit(solution)/shard_map/all_gather | solution.py:101
  135.8 294.1 %copy-start.57 = (f32[2048]{0:T(1024)}, f32[2048]{0:T(1024)S(1)}, u32[]{:S(2)}) copy-start(f32[2048]{0:T(1024)S(1)} %convert_element_type.272) | copy-start | bytes 24580
  472.9 209.2 %all-to-all-start.2 = ((bf16[32,72,2048]{2,1,0:T(8,128)(2,1)}), bf16[32,72,2048]{2,1,0:T(8,128)(2,1)}, u32[]{:S(2)}, u32[]{:S(2)}) async-start(bf16[32,72,2048]{2,1,0:T(8,128)(2,1)} %fusion), calls=%async_computation.2 | async-start | bytes 18874368 | tf_op jit(solution)/shard_map/all_to_all | solution.py:245
  682.1 213.0 %all-to-all-start = ((bf16[32,72,2048]{2,1,0:T(8,128)(2,1)}), bf16[32,72,2048]{2,1,0:T(8,128)(2,1)}, u32[]{:S(2)}, u32[]{:S(2)}) async-start(bf16[32,72,2048]{2,1,0:T(8,128)(2,1)} %bitcast.475), calls=%async_computation | async-start | bytes 18874368 | tf_op jit(solution)/shard_map/all_to_all | solution.py:217
  937.5 213.0 %all-to-all-start.1 = ((bf16[32,72,2048]{2,1,0:T(8,128)(2,1)}), bf16[32,72,2048]{2,1,0:T(8,128)(2,1)}, u32[]{:S(2)}, u32[]{:S(2)}) async-start(bf16[32,72,2048]{2,1,0:T(8,128)(2,1)} %convolution_convert_fusion), calls=%async_computation.1 | async-start | bytes 18874368 | tf_op jit(solution)/shard_map/all_to_all | solution.py:226
  975.5 184.8 %copy-start.70 = (f32[8,256]{1,0:T(8,128)S(1)}, f32[8,256]{1,0:T(8,128)}, u32[]{:S(2)}) copy-start(f32[8,256]{1,0:T(8,128)} %copy-done.69) | copy-start | bytes 24580
  975.5 184.8 %copy-start.77 = (f32[8,256]{1,0:T(8,128)S(1)}, f32[8,256]{1,0:T(8,128)}, u32[]{:S(2)}) copy-start(f32[8,256]{1,0:T(8,128)} %copy-done.76) | copy-start | bytes 24580
  1150.5 213.0 %all-to-all-start.3 = ((bf16[32,72,2048]{2,1,0:T(8,128)(2,1)}), bf16[32,72,2048]{2,1,0:T(8,128)(2,1)}, u32[]{:S(2)}, u32[]{:S(2)}) async-start(bf16[32,72,2048]{2,1,0:T(8,128)(2,1)} %add_convert_fusion), calls=%async_computation.3 | async-start | bytes 18874368 | tf_op jit(solution)/shard_map/all_to_all | solution.py:270
  1160.1 311.0 %reduce-scatter.12.cloned.1.call-start = ((), (), s32[]{:S(2)}) async-start(), calls=%async_computation.18 | async-start | bytes 1310720 | tf_op jit(solution)/shard_map/reduce_scatter | solution.py:344
  1430.0 68.2 %reduce-scatter.10.cloned.1.call-start = ((), (), s32[]{:S(2)}) async-start(), calls=%async_computation.17 | async-start | bytes 1310720 | tf_op jit(solution)/shard_map/reduce_scatter | solution.py:341
  1469.2 134.3 %reduce-scatter.22.cloned.1.call-start = ((), (), s32[]{:S(2)}) async-start(), calls=%async_computation.23 | async-start | bytes 1081344
  1470.9 272.3 %reduce-scatter.18.cloned.1.call-start = ((), (), s32[]{:S(2)}) async-start(), calls=%async_computation.21 | async-start | bytes 4325376 | tf_op jit(solution)/shard_map/reduce_scatter | solution.py:385
  1475.8 407.2 %reduce-scatter.16.cloned.1.call-start = ((), (), s32[]{:S(2)}) async-start(), calls=%async_computation.20 | async-start | bytes 4325376 | tf_op jit(solution)/shard_map/reduce_scatter | solution.py:384
  1505.0 770.3 %reduce-scatter.20.cloned.1.call-start = ((), (), s32[]{:S(2)}) async-start(), calls=%async_computation.22 | async-start | bytes 34603008 | tf_op jit(solution)/shard_map/reduce_scatter | solution.py:388
  1521.5 1118.8 %reduce-scatter.14.cloned.1.call-start = ((), (), s32[]{:S(2)}) async-start(), calls=%async_computation.19 | async-start | bytes 34603008 | tf_op jit(solution)/shard_map/reduce_scatter | solution.py:383
  1607.5 1032.8 %copy-start.1 = (bf16[1,2048,768]{2,1,0:T(8,128)(2,1)S(1)}, bf16[1,2048,768]{2,1,0:T(8,128)(2,1)}, u32[]{:S(2)}) copy-start(bf16[1,2048,768]{2,1,0:T(8,128)(2,1)} %param.26) | copy-start | bytes 9437188
  (110 other events, 2572.9 us)
Sparse Core Ops, SparseCore 0:
  11.5 55.9 all-gather.11
  70.9 55.2 all-gather.7
  129.7 114.7 all-gather.15
  246.8 25.7 all-gather.13
  274.8 26.6 all-gather.9
  304.8 113.7 all-gather.17
  1430.1 28.6 reduce-scatter.11
  1469.3 28.7 reduce-scatter.9
  1500.4 103.0 reduce-scatter.21
  1606.3 136.8 reduce-scatter.17
  1746.2 136.7 reduce-scatter.15
  1885.8 389.5 reduce-scatter.19
  2278.3 361.9 reduce-scatter.13
where the time goes:
time: 2660 us; the launch traced here: 2650 us
  waiting for transfers between devices  1870 us (70%)
  matrix products  294 us (11%)
  local copies, waits for them, and re-layouts  187 us (7%)
  blocking collectives  143 us (5%)
  other arithmetic  96.8 us (4%)
  starting transfers between devices  35.4 us (1%)
    reduce_scatter x1, waiting for transfers between devices, shards(): lax.psum_scatter(output_w_grad, ('dp', 'ctx', 'exp'), scatter_dimension=0...  392 us
    reduce_scatter x1, waiting for transfers between devices, shards(): lax.psum_scatter(query_w_grad, ('dp', 'ctx', 'exp'), scatter_dimension=0,...  365 us
    all_to_all x1, waiting for transfers between devices, shards(): lax.all_to_all(send_rows, ('dp', 'ctx', 'exp'), split_axis=0, concat_axis...  190 us
    all_to_all x1, waiting for transfers between devices, shards(): lax.all_to_all(slot_grads, ('dp', 'ctx', 'exp'), split_axis=0, concat_axi...  181 us
    all_to_all x1, waiting for transfers between devices, shards(): lax.all_to_all(expert_out, ('dp', 'ctx', 'exp'), split_axis=0, concat_axi...  175 us
    all_to_all x1, waiting for transfers between devices, shards(): lax.all_to_all(rows_grad, ('dp', 'ctx', 'exp'), split_axis=0, concat_axis...  165 us
    reduce_scatter x1, waiting for transfers between devices, shards(): lax.psum_scatter(key_w_grad, ('dp', 'ctx', 'exp'), scatter_dimension=0, t...  140 us
    unnamed x2, blocking collectives  112 us
  transfers between devices with their start and end apart: 17, of which 14 were waited for; matrix products, arithmetic and copies ran while one was open for 15% of the time, Pallas kernels for 0%

commit v1 on v0

v1 whole, which is shorter than its diff:
```python
import jax
import jax.numpy as jnp
from jax import lax
from jax.sharding import PartitionSpec as P

eps_norm = 1e-06
rope_base = 1000000.0
masked_score = -1e30
ALL = ("dp", "ctx", "exp")
PLANE = ("ctx", "exp")


def rope_tables(positions, width):
    exponents = jnp.arange(width // 2, dtype=jnp.float32) * (2.0 / width)
    frequency = rope_base ** (-exponents)
    angles = positions.astype(jnp.float32)[:, None] * frequency[None, :]
    angles = jnp.concatenate([angles, angles], axis=-1)
    return (jnp.cos(angles), jnp.sin(angles))


def turn_ahead(values):
    half = values.shape[-1] // 2
    return jnp.concatenate([-values[..., half:], values[..., :half]], axis=-1)


def turn_behind(values):
    half = values.shape[-1] // 2
    return jnp.concatenate([values[..., half:], -values[..., :half]], axis=-1)


def norm_rope(raw, gain, cosine, sine):
    inverse = lax.rsqrt(jnp.mean(raw * raw, axis=-1, keepdims=True) + eps_norm)
    normed = raw * inverse
    scaled = normed * gain
    return (scaled * cosine + turn_ahead(scaled) * sine, normed, inverse)


def norm_rope_back(grad, normed, inverse, gain, cosine, sine):
    scaled_grad = grad * cosine + turn_behind(grad * sine)
    gain_grad = jnp.sum(scaled_grad * normed, axis=(0, 1))
    inner = scaled_grad * gain
    return (
        inverse * (inner - normed * jnp.mean(inner * normed, axis=-1, keepdims=True)),
        gain_grad,
    )


def norm_back(grad, normed, inverse, gain):
    gain_grad = jnp.sum(grad * normed, axis=0)
    scaled = grad * gain
    return (
        inverse * (scaled - normed * jnp.mean(scaled * normed, axis=-1, keepdims=True)),
        gain_grad,
    )


def line_gather(block, axis):
    n = lax.axis_size(axis)
    me = lax.axis_index(axis)
    before, after = [], []
    up = down = block
    for step in range(1, n):
        up = lax.ppermute(up, axis, [(i, i + 1) for i in range(step - 1, n - 1)])
        down = lax.ppermute(down, axis, [(i, i - 1) for i in range(1, n - step + 1)])
        before.insert(0, up)
        after.append(down)
    return lax.dynamic_slice_in_dim(jnp.stack(before + [block] + after), n - 1 - me, n, 0)


def line_scatter(parts, axis):
    n = lax.axis_size(axis)
    me = lax.axis_index(axis)

    def part(i):
        return lax.dynamic_index_in_dim(parts, jnp.clip(i, 0, n - 1), 0, keepdims=False)

    up = down = None
    for step in range(1, n):
        send_up, send_down = part(me + n - step), part(me - n + step)
        if up is not None:
            send_up, send_down = add_low(send_up, up), add_low(send_down, down)
        up = lax.ppermute(send_up, axis, [(i, i + 1) for i in range(step)])
        down = lax.ppermute(send_down, axis, [(i, i - 1) for i in range(n - step, n)])
    return part(me).astype(jnp.float32) + up.astype(jnp.float32) + down.astype(jnp.float32)


def add_low(left, right):
    return (left.astype(jnp.float32) + right.astype(jnp.float32)).astype(left.dtype)


def flip(block, axis, bit):
    return lax.ppermute(block, axis, [(i, i ^ bit) for i in range(lax.axis_size(axis))])


def square_gather(block, axis):
    if lax.axis_size(axis) != 4:
        return lax.all_gather(block, axis, axis=0, tiled=False)
    half = block.shape[-1] // 2
    me = lax.axis_index(axis)
    by_x, by_y = flip(block, axis, 1), flip(block, axis, 2)
    far = jnp.concatenate(
        [flip(by_x[..., :half], axis, 2), flip(by_y[..., half:], axis, 1)], axis=-1
    )
    whole = jnp.zeros((4,) + block.shape, block.dtype)
    for bits, piece in enumerate((block, by_x, by_y, far)):
        whole = lax.dynamic_update_index_in_dim(whole, piece, me ^ bits, 0)
    return whole


def square_scatter(parts, axis):
    if lax.axis_size(axis) != 4:
        return lax.psum_scatter(parts, axis, scatter_dimension=0, tiled=False).astype(jnp.float32)
    half = parts.shape[-1] // 2
    me = lax.axis_index(axis)
    own, to_x, to_y, far = [
        lax.dynamic_index_in_dim(parts, me ^ bits, 0, keepdims=False) for bits in range(4)
    ]
    first = flip(jnp.stack([to_x[..., :half], far[..., :half]]), axis, 1)
    second = flip(jnp.stack([to_y[..., half:], far[..., half:]]), axis, 2)
    later_first = flip(add_low(to_y[..., :half], first[1]), axis, 2)
    later_second = flip(add_low(to_x[..., half:], second[1]), axis, 1)
    own = own.astype(jnp.float32)
    first = own[..., :half] + first[0].astype(jnp.float32) + later_first.astype(jnp.float32)
    second = own[..., half:] + second[0].astype(jnp.float32) + later_second.astype(jnp.float32)
    return jnp.concatenate([first, second], axis=-1)


def pair_gather(block, axis):
    if lax.axis_size(axis) != 2:
        return lax.all_gather(block, axis, axis=0, tiled=False)
    other = flip(block, axis, 1)
    first = lax.axis_index(axis) == 0
    return jnp.stack([jnp.where(first, block, other), jnp.where(first, other, block)])


def pair_scatter(parts, axis):
    if lax.axis_size(axis) != 2:
        return lax.psum_scatter(parts, axis, scatter_dimension=0, tiled=False)
    first = lax.axis_index(axis) == 0
    other = flip(jnp.where(first, parts[1], parts[0]), axis, 1)
    return add_low(jnp.where(first, parts[0], parts[1]), other)


def swap(parts, axis):
    return lax.all_to_all(parts, axis, split_axis=0, concat_axis=0, tiled=True)


def shards(
    tokens,
    attention_gain,
    query_weight,
    key_weight,
    value_weight,
    query_gain,
    key_gain,
    output_weight,
    mixture_gain,
    router_weight,
    gate_weight,
    up_weight,
    down_weight,
    routes,
    bounds,
    cotangent,
):
    low, full = jnp.bfloat16, jnp.float32
    n_dp, n_ctx, n_exp = (lax.axis_size(a) for a in ALL)
    devices = n_dp * n_ctx * n_exp
    tok_count, width = tokens.shape[1], tokens.shape[2]
    seq_len = tok_count * n_ctx
    head_dim = query_gain.shape[0] * devices
    rows = query_weight.shape[0]
    heads = query_weight.shape[1] // head_dim
    kv_heads = key_weight.shape[1] // head_dim
    kv_here = kv_heads // n_ctx
    group_size = heads // kv_heads
    q_cols, kv_cols = heads * head_dim // n_ctx, kv_here * head_dim
    experts = router_weight.shape[1]
    topk = routes.shape[2]
    base_rows = tok_count * topk // experts
    capacity = base_rows + max(1, base_rows // 8)
    plane = experts // n_dp
    local_experts = gate_weight.shape[0]
    score_scale = head_dim ** (-0.5)
    dp_index = lax.axis_index("dp")

    gain_len = query_gain.shape[0]
    small = jnp.concatenate(
        [
            attention_gain[:, None],
            mixture_gain[:, None],
            jnp.pad(jnp.concatenate([query_gain, key_gain]), (0, rows - 2 * gain_len))[:, None],
            router_weight,
        ],
        axis=1,
    ).astype(low)
    small = jnp.pad(small, ((0, 0), (0, -small.shape[1] % 128)))
    extra = small.shape[1]

    def by_ctx(weight):
        return weight.astype(low).reshape(rows, n_ctx, -1).transpose(1, 0, 2)

    front = jnp.concatenate(
        [
            by_ctx(query_weight),
            by_ctx(key_weight),
            by_ctx(value_weight),
            jnp.broadcast_to(small[None], (n_ctx, rows, extra)),
        ],
        axis=2,
    )
    front = pair_gather(line_gather(swap(front, "ctx"), "dp"), "exp")
    front = front.transpose(1, 2, 0, 3, 4).reshape(width, -1)
    front_weight = front[:, : q_cols + 2 * kv_cols]
    small = front[:, q_cols + 2 * kv_cols :]
    first_gain = small[:, 0].astype(full)
    second_gain = small[:, 1].astype(full)
    head_gains = small[:, 2].reshape(devices, rows)
    query_scale = head_gains[:, :gain_len].reshape(-1).astype(full)
    key_scale = head_gains[:, gain_len : 2 * gain_len].reshape(-1).astype(full)
    router_full = small[:, 3 : 3 + experts]

    whole_tokens = square_gather(tokens[0], "ctx").reshape(seq_len, width)
    back = line_gather(output_weight.astype(low), "dp")
    back = pair_gather(swap(back, "ctx"), "exp")
    output_part = back.transpose(1, 0, 2, 3).reshape(q_cols, width)

    column_grads = line_gather(cotangent[0], "dp")
    column_routes = line_gather(routes[0], "dp")
    chosen = jnp.any(
        column_routes[:, :, :, None] == jnp.arange(experts, dtype=jnp.int32), axis=2
    )
    hot = lax.dynamic_slice_in_dim(chosen.astype(low), dp_index * plane, plane, 2)
    row_ids = jnp.arange(tok_count, dtype=jnp.int32)
    earlier = (row_ids[None, :] < row_ids[:, None]).astype(low)
    before = jnp.einsum("st,btj->bsj", earlier, hot, preferred_element_type=full)
    slots = jnp.arange(capacity, dtype=full)
    pick = (
        (before.transpose(0, 2, 1)[:, :, None, :] == slots[None, None, :, None])
        & (hot.transpose(0, 2, 1)[:, :, None, :] > 0)
    ).astype(low)

    def send_out(blocks):
        return jnp.einsum("bjrt,btd->jbrd", pick, blocks, preferred_element_type=low)

    def bring_back(sent):
        return jnp.einsum("bjrt,jbrd->btd", pick, sent, preferred_element_type=full)

    grad_rows = swap(send_out(column_grads), PLANE)

    inputs = whole_tokens.astype(full)
    first_inverse = lax.rsqrt(jnp.mean(inputs * inputs, axis=-1, keepdims=True) + eps_norm)
    hidden = ((inputs * first_inverse) * first_gain).astype(low)
    positions = jnp.arange(seq_len, dtype=jnp.int32)
    cosine, sine = rope_tables(positions, head_dim)
    cosine = cosine[:, None, :]
    sine = sine[:, None, :]
    raw = jnp.dot(hidden, front_weight, preferred_element_type=full)
    query_raw = raw[:, :q_cols].reshape(seq_len, -1, head_dim)
    key_raw = raw[:, q_cols : q_cols + kv_cols].reshape(seq_len, -1, head_dim)
    value_raw = raw[:, q_cols + kv_cols :].reshape(seq_len, -1, head_dim)
    query_rot, query_normed, query_inverse = norm_rope(query_raw, query_scale, cosine, sine)
    key_rot, key_normed, key_inverse = norm_rope(key_raw, key_scale, cosine, sine)
    query_low = query_rot.astype(low)
    key_low = key_rot.astype(low)
    value_low = value_raw.astype(low)
    first_end, second_end = bounds[0, 0], bounds[0, 1]
    document = (positions >= first_end).astype(jnp.int32) + (positions >= second_end).astype(
        jnp.int32
    )
    allowed = (positions[None, :] <= positions[:, None]) & (document[None, :] == document[:, None])
    attended_parts, lse_parts = [], []
    for g in range(kv_here):
        query_group = query_low[:, g * group_size : (g + 1) * group_size]
        scores = (
            jnp.einsum("tgd,sd->gts", query_group, key_low[:, g], preferred_element_type=full)
            * score_scale
        )
        scores = jnp.where(allowed[None], scores, masked_score)
        highest = jnp.max(scores, axis=-1, keepdims=True)
        weights = jnp.exp(scores - highest)
        totals = jnp.sum(weights, axis=-1, keepdims=True)
        shares_low = (weights / totals).astype(low)
        attended_parts.append(
            jnp.einsum("gts,sd->tgd", shares_low, value_low[:, g], preferred_element_type=full)
        )
        lse_parts.append(highest + jnp.log(totals))
    attended_low = jnp.concatenate(attended_parts, axis=1).astype(low).reshape(seq_len, q_cols)
    branch = jnp.dot(attended_low, output_part, preferred_element_type=full).astype(low)
    branch = square_scatter(branch.reshape(n_ctx, tok_count, width), "ctx")

    own = tokens[0].astype(full)
    middle = own + branch
    second_inverse = lax.rsqrt(jnp.mean(middle * middle, axis=-1, keepdims=True) + eps_norm)
    second_normed = middle * second_inverse
    mixed_low = (second_normed * second_gain).astype(low)

    column_mixed = line_gather(mixed_low, "dp")
    logits = jnp.einsum("btd,de->bte", column_mixed, router_full, preferred_element_type=full)
    logits = jnp.where(chosen, logits, masked_score)
    gates = jnp.exp(logits - jnp.max(logits, axis=-1, keepdims=True))
    gates = gates / jnp.sum(gates, axis=-1, keepdims=True)
    plane_gates = lax.dynamic_slice_in_dim(gates, dp_index * plane, plane, 2)
    own_gates = lax.dynamic_index_in_dim(gates, dp_index, 0, keepdims=False)
    slot_gates = jnp.sum(
        pick.astype(full) * plane_gates.transpose(0, 2, 1)[:, :, None, :], axis=-1
    ).transpose(1, 0, 2)
    slot_gates = swap(slot_gates, PLANE)[..., None]
    expert_in = swap(send_out(column_mixed), PLANE)

    sources = n_ctx * n_exp

    def by_expert(v):
        v = v.reshape((sources, local_experts, n_dp * capacity) + v.shape[3:])
        return v.transpose(1, 0, 2, 3).reshape(local_experts, -1, v.shape[-1])

    def by_source(v):
        v = v.reshape(local_experts, sources, n_dp * capacity, -1).transpose(1, 0, 2, 3)
        return v.reshape(sources * local_experts, n_dp, capacity, -1)

    grad_rows, expert_in, slot_gates = by_expert(grad_rows), by_expert(expert_in), by_expert(slot_gates)
    act_grad = (
        jnp.einsum("ecd,efd->ecf", grad_rows, down_weight, preferred_element_type=full)
        * slot_gates
    )
    gate_pre = jnp.einsum("ecd,edf->ecf", expert_in, gate_weight, preferred_element_type=full)
    up_pre = jnp.einsum("ecd,edf->ecf", expert_in, up_weight, preferred_element_type=full)
    sigma = jax.nn.sigmoid(gate_pre)
    silu = gate_pre * sigma
    activated = (silu * up_pre).astype(low)
    up_grad = (act_grad * silu).astype(low)
    gate_grad = (act_grad * up_pre * sigma * (1.0 + gate_pre * (1.0 - sigma))).astype(low)
    row_grads = (
        jnp.einsum("ecf,edf->ecd", gate_grad, gate_weight, preferred_element_type=full)
        + jnp.einsum("ecf,edf->ecd", up_grad, up_weight, preferred_element_type=full)
    ).astype(low)
    row_grads = swap(by_source(row_grads), PLANE)
    expert_out = jnp.einsum(
        "ecf,efd->ecd", activated, down_weight, preferred_element_type=full
    ).astype(low)
    slot_dots = jnp.sum(expert_out.astype(full) * grad_rows.astype(full), axis=-1, keepdims=True)
    slot_dots = swap(by_source(slot_dots), PLANE)[..., 0]
    scaled_out = (expert_out.astype(full) * slot_gates).astype(low)
    scaled_out = swap(by_source(scaled_out), PLANE)
    out_grads = (grad_rows.astype(full) * slot_gates).astype(low)
    down_grad = jnp.einsum("ecf,ecd->efd", activated, out_grads, preferred_element_type=full)
    gate_w_grad = jnp.einsum("ecd,ecf->edf", expert_in, gate_grad, preferred_element_type=full)
    up_w_grad = jnp.einsum("ecd,ecf->edf", expert_in, up_grad, preferred_element_type=full)

    dots = jnp.sum(
        pick.astype(full) * slot_dots.transpose(1, 0, 2)[..., None], axis=2
    ).transpose(0, 2, 1)
    dots = swap(dots, "dp").transpose(1, 0, 2).reshape(tok_count, experts)
    picked_grads = own_gates * (dots - jnp.sum(own_gates * dots, axis=-1, keepdims=True))
    logit_grads = picked_grads.astype(low)
    mixed_grad = line_scatter(bring_back(row_grads).astype(low), "dp")
    mixed_grad = mixed_grad + jnp.einsum(
        "te,de->td", logit_grads, router_full, preferred_element_type=full
    )
    mixture = line_scatter(bring_back(scaled_out).astype(low), "dp")
    output = (middle + mixture).astype(low)[None]
    router_grad = jnp.einsum("td,te->de", mixed_low, logit_grads, preferred_element_type=full)
    grad_out = cotangent[0].astype(full)
    middle_back, second_gain_grad = norm_back(
        mixed_grad, second_normed, second_inverse, second_gain
    )
    middle_grad = grad_out + middle_back

    branch_low = square_gather(middle_grad.astype(low), "ctx").reshape(seq_len, width)
    output_w_grad = jnp.einsum("ti,td->id", attended_low, branch_low, preferred_element_type=full)
    attended_grad = jnp.einsum("td,id->ti", branch_low, output_part, preferred_element_type=full)
    attended_grad = attended_grad.astype(low).reshape(seq_len, -1, head_dim)
    query_grad_parts, key_grad_parts, value_grad_parts = [], [], []
    for g in range(kv_here):
        query_group = query_low[:, g * group_size : (g + 1) * group_size]
        grad_group = attended_grad[:, g * group_size : (g + 1) * group_size]
        scores = (
            jnp.einsum("tgd,sd->gts", query_group, key_low[:, g], preferred_element_type=full)
            * score_scale
        )
        scores = jnp.where(allowed[None], scores, masked_score)
        shares = jnp.exp(scores - lse_parts[g])
        shares_low = shares.astype(low)
        share_grads = jnp.einsum(
            "tgd,sd->gts", grad_group, value_low[:, g], preferred_element_type=full
        )
        centre = jnp.sum(shares * share_grads, axis=-1, keepdims=True)
        score_grads = (shares * (share_grads - centre)).astype(low)
        query_grad_parts.append(
            jnp.einsum("gts,sd->tgd", score_grads, key_low[:, g], preferred_element_type=full)
            * score_scale
        )
        key_grad_parts.append(
            jnp.einsum("gts,tgd->sd", score_grads, query_group, preferred_element_type=full)
            * score_scale
        )
        value_grad_parts.append(
            jnp.einsum("gts,tgd->sd", shares_low, grad_group, preferred_element_type=full)
        )
    query_grad = jnp.concatenate(query_grad_parts, axis=1)
    key_grad = jnp.stack(key_grad_parts, axis=1)
    value_grad = jnp.stack(value_grad_parts, axis=1)
    query_raw_grad, query_gain_grad = norm_rope_back(
        query_grad, query_normed, query_inverse, query_scale, cosine, sine
    )
    key_raw_grad, key_gain_grad = norm_rope_back(
        key_grad, key_normed, key_inverse, key_scale, cosine, sine
    )
    raw_grad = jnp.concatenate(
        [
            query_raw_grad.reshape(seq_len, -1),
            key_raw_grad.reshape(seq_len, -1),
            value_grad.reshape(seq_len, -1),
        ],
        axis=1,
    ).astype(low)
    hidden_grad = jnp.einsum("ti,di->td", raw_grad, front_weight, preferred_element_type=full)
    hidden_grad = square_scatter(hidden_grad.astype(low).reshape(n_ctx, tok_count, width), "ctx")
    own_inverse = lax.rsqrt(jnp.mean(own * own, axis=-1, keepdims=True) + eps_norm)
    input_back, first_gain_grad = norm_back(hidden_grad, own * own_inverse, own_inverse, first_gain)
    tokens_grad = (middle_grad + input_back).astype(low)[None]

    front_grad = jnp.einsum("td,ti->di", hidden, raw_grad, preferred_element_type=full).astype(low)
    front_grad = front_grad.reshape(n_dp, n_ctx, n_exp, rows, -1).transpose(2, 0, 1, 3, 4)
    front_grad = line_scatter(pair_scatter(front_grad, "exp"), "dp").astype(low)
    front_grad = swap(front_grad, "ctx").astype(full)
    query_share = front_grad[:, :, :q_cols].transpose(1, 0, 2).reshape(rows, -1)
    key_share = front_grad[:, :, q_cols : q_cols + kv_cols].transpose(1, 0, 2).reshape(rows, -1)
    value_share = front_grad[:, :, q_cols + kv_cols :].transpose(1, 0, 2).reshape(rows, -1)
    back_grad = output_w_grad.astype(low).reshape(n_ctx, n_exp, -1, width).transpose(1, 0, 2, 3)
    back_grad = swap(pair_scatter(back_grad, "exp"), "ctx")
    output_share = line_scatter(back_grad, "dp")
    packed = jnp.concatenate(
        [
            first_gain_grad.reshape(devices, -1),
            second_gain_grad.reshape(devices, -1),
            query_gain_grad.reshape(devices, -1),
            key_gain_grad.reshape(devices, -1),
            router_grad.reshape(devices, -1),
        ],
        axis=1,
    )
    packed = jnp.pad(packed, ((0, 0), (0, -packed.shape[1] % 1024)))
    packed = lax.psum_scatter(packed, ALL, scatter_dimension=0, tiled=False)
    ends = [rows, 2 * rows, 2 * rows + gain_len, 2 * rows + 2 * gain_len]
    first_share = packed[: ends[0]]
    second_share = packed[ends[0] : ends[1]]
    query_gain_share = packed[ends[1] : ends[2]]
    key_gain_share = packed[ends[2] : ends[3]]
    router_share = packed[ends[3] : ends[3] + rows * experts].reshape(rows, experts)
    return (
        output,
        tokens_grad,
        first_share,
        query_share,
        key_share,
        value_share,
        query_gain_share,
        key_gain_share,
        output_share,
        second_share,
        router_share,
        gate_w_grad,
        up_w_grad,
        down_grad,
    )


def solution(mesh):
    rows = P(ALL)
    sequences = P(("dp", "exp"), "ctx")
    in_specs = (sequences,) + (rows,) * 12 + (sequences, P(("dp", "exp")), sequences)
    out_specs = (sequences,) * 2 + (rows,) * 12
    return jax.shard_map(shards, mesh=mesh, in_specs=in_specs, out_specs=out_specs, check_vma=False)
```

time: 2660 us -> 1440 us (0.54)
  waiting for transfers between devices: 1870 us -> 585 us
  starting transfers between devices: 35.4 us -> 231 us
  blocking collectives: 143 us -> 7.11 us
  other arithmetic: 96.8 us -> 181 us
  local copies, waits for them, and re-layouts: 187 us -> 136 us
    reduce_scatter x6 -> x0, waiting for transfers between devices: 973 us -> none  [the longest x1 392 us: shards(): lax.psum_scatter(output_w_grad, ('dp', 'ctx', 'exp'), scatter_dimension=0...]
    all_to_all x4 -> x10, waiting for transfers between devices: 712 us -> 191 us  [swap(): return lax.all_to_all(parts, axis, split_axis=0, concat_axis=0, tiled=True)]
    ppermute x0 -> x74, waiting for transfers between devices: none -> 293 us  [the longest x15 79.1 us: line_gather(): up = lax.ppermute(up, axis, [(i, i + 1) for i in range(step - 1, n - 1)])]
    all_gather x6 -> x0, waiting for transfers between devices: 185 us -> none  [the longest x1 89.3 us: shards(): lax.all_gather(output_weight.astype(jnp.bfloat16), ('dp', 'ctx', 'exp'),...]
    ppermute x0 -> x74, starting transfers between devices: none -> 169 us  [the longest x12 49 us: line_scatter(): up = lax.ppermute(send_up, axis, [(i, i + 1) for i in range(step)])]
    gather x9 -> x0, local copies, waits for them, and re-layouts: 112 us -> none  [the longest x1 21.6 us: shards(): back_rows.reshape(experts * capacity, width)[slot_of]]
    unnamed x2 -> x0, blocking collectives: 112 us -> none
    unnamed x14 -> x2, waiting for transfers between devices: 4.4 us -> 101 us
  transfers between devices with their start and end apart: 17 -> 85, of which waited for: 14 -> 38; matrix products, arithmetic and copies ran while one was open for 15% -> 29% of each run, Pallas kernels for 0% -> 0%
where the time goes in v1:
time: 1440 us; the launch traced here: 1430 us
  waiting for transfers between devices  585 us (41%)
  matrix products  277 us (19%)
  starting transfers between devices  231 us (16%)
  other arithmetic  181 us (13%)
  local copies, waits for them, and re-layouts  136 us (9%)
  between operations  16.6 us (1%)
    all_to_all x10, waiting for transfers between devices, swap(): return lax.all_to_all(parts, axis, split_axis=0, concat_axis=0, tiled=True)  191 us
    unnamed x2, waiting for transfers between devices  101 us
    ppermute x15, waiting for transfers between devices, line_gather(): up = lax.ppermute(up, axis, [(i, i + 1) for i in range(step - 1, n - 1)])  79.1 us
    ppermute x15, waiting for transfers between devices, line_gather(): lax.ppermute(down, axis, [(i, i - 1) for i in range(1, n - step + 1)])  70.7 us
    ppermute x20, waiting for transfers between devices, flip(): lax.ppermute(block, axis, [(i, i ^ bit) for i in range(lax.axis_size(axis...  62.3 us
    all_to_all x10, starting transfers between devices, swap(): return lax.all_to_all(parts, axis, split_axis=0, concat_axis=0, tiled=True)  61.9 us
    ppermute x12, starting transfers between devices, line_scatter(): up = lax.ppermute(send_up, axis, [(i, i + 1) for i in range(step)])  49 us
    ppermute x15, starting transfers between devices, line_gather(): lax.ppermute(down, axis, [(i, i - 1) for i in range(1, n - step + 1)])  44.1 us
  transfers between devices with their start and end apart: 85, of which 38 were waited for; matrix products, arithmetic and copies ran while one was open for 29% of the time, Pallas kernels for 0%

profile of v1, /device:TPU:14, one launch (start us, length us, event | category | flops | bytes accessed | tf_op | source)
XLA Modules:
  0.0 1434.6 jit_solution(16909134040381056770)
XLA Ops:
  54.8 16.2 %collective-permute-done.15 = bf16[128,2048]{1,0:T(8,128)(2,1)S(1)} collective-permute-done((bf16[128,2048]{1,0:T(8,128)(2,1)}, bf16[128,2048]{1,0:T(8,128)(2,1)S(1)}, u32[]{:S(2)}, u32[]{:S(2)}) %collective-permute-start.15) | collective-permute-done | bytes 524320 | tf_op jit(solution)/shard_map/ppermute | solution.py:64
  228.4 21.5 %fusion.193 = (f32[8,1024]{1,0:T(8,128)S(1)}, f32[8,1024,1024]{1,2,0:T(8,128)}) fusion(bf16[1024,128]{1,0:T(8,128)(2,1)S(1)} %get-tuple-element.170, pred[1024,1024]{0,1:T(8,128)(4,1)} %fusion.36, f32[1024,1024]{1,0:T(8,128)} %copy.333, f32[1024,1024]{1,0:T(8,128)} %copy.332, f32[1024,1024]{1,0:T(8,128)} %copy.331, f32[1024,1280]{1,0:T(8,128)} %copy-done.9, ...), kind=kOutput, calls=%fused_computation.406 | convolution fusion | flops 2177884160 | bytes 51679232 | tf_op jit(solution)/shard_map/tgd,sd->gts/dot_general | solution.py:276
  249.9 13.1 fusion.4
  263.0 14.4 %fusion.97 = bf16[128,8,1024]{2,0,1:T(8,128)(2,1)S(1)} fusion(f32[8,1024,1024]{1,2,0:T(8,128)} %get-tuple-element.184, f32[8,1024]{1,0:T(8,128)S(1)} %fusion.4, f32[8,1024]{1,0:T(8,128)S(1)} %get-tuple-element.183, f32[1024,1280]{1,0:T(8,128)} %copy-done.9), kind=kOutput, calls=%fused_computation.160 | convolution fusion | flops 2173698048 | bytes 35979264 | tf_op jit(solution)/shard_map/gts,sd->tgd/dot_general | solution.py:285
  285.8 21.6 %collective-permute-done.20 = bf16[2,256,1024]{2,1,0:T(8,128)(2,1)S(1)} collective-permute-done((bf16[2,256,1024]{2,1,0:T(8,128)(2,1)S(1)}, bf16[2,256,1024]{2,1,0:T(8,128)(2,1)S(1)}, u32[]{:S(2)}, u32[]{:S(2)}) %collective-permute-start.20) | collective-permute-done | bytes 1048608 | tf_op jit(solution)/shard_map/ppermute | solution.py:92
  334.0 17.7 %collective-permute-done.28 = bf16[256,2048]{1,0:T(8,128)(2,1)} collective-permute-done((bf16[256,2048]{1,0:T(8,128)(2,1)}, bf16[256,2048]{1,0:T(8,128)(2,1)}, u32[]{:S(2)}, u32[]{:S(2)}) %collective-permute-start.28) | collective-permute-done | bytes 1048608 | tf_op jit(solution)/shard_map/ppermute | solution.py:63
  389.9 18.0 %collective-permute-done.32 = bf16[256,2048]{1,0:T(8,128)(2,1)S(1)} collective-permute-done((bf16[256,2048]{1,0:T(8,128)(2,1)}, bf16[256,2048]{1,0:T(8,128)(2,1)S(1)}, u32[]{:S(2)}, u32[]{:S(2)}) %collective-permute-start.32) | collective-permute-done | bytes 1048608 | tf_op jit(solution)/shard_map/ppermute | solution.py:64
  457.9 21.5 %collective-permute-done.40 = bf16[256,2048]{1,0:T(8,128)(2,1)S(1)} collective-permute-done((bf16[256,2048]{1,0:T(8,128)(2,1)}, bf16[256,2048]{1,0:T(8,128)(2,1)S(1)}, u32[]{:S(2)}, u32[]{:S(2)}) %collective-permute-start.40) | collective-permute-done | bytes 1048608 | tf_op jit(solution)/shard_map/ppermute | solution.py:63
  485.0 18.7 %collective-permute-done.41 = bf16[256,2048]{1,0:T(8,128)(2,1)S(1)} collective-permute-done((bf16[256,2048]{1,0:T(8,128)(2,1)S(1)}, bf16[256,2048]{1,0:T(8,128)(2,1)S(1)}, u32[]{:S(2)}, u32[]{:S(2)}) %collective-permute-start.41) | collective-permute-done | bytes 1048608 | tf_op jit(solution)/shard_map/ppermute | solution.py:63
  511.8 20.4 %collective-permute-done.45 = bf16[256,2048]{1,0:T(8,128)(2,1)S(1)} collective-permute-done((bf16[256,2048]{1,0:T(8,128)(2,1)S(1)}, bf16[256,2048]{1,0:T(8,128)(2,1)S(1)}, u32[]{:S(2)}, u32[]{:S(2)}) %collective-permute-start.45) | collective-permute-done | bytes 1048608 | tf_op jit(solution)/shard_map/ppermute | solution.py:64
  580.5 13.3 multiply_convert_fusion.2
  593.9 71.8 %all-to-all-done.5 = bf16[8,4,72,2048]{3,2,1,0:T(8,128)(2,1)} async-done(((bf16[8,4,72,2048]{3,2,1,0:T(8,128)(2,1)}), bf16[8,4,72,2048]{3,2,1,0:T(8,128)(2,1)}, u32[]{:S(2)}, u32[]{:S(2)}) %all-to-all-start.5) | async-done | bytes 9437216 | tf_op jit(solution)/shard_map/all_to_all | solution.py:145
  665.7 13.7 fusion.7
  702.8 15.7 %multiply_convert_fusion = (bf16[2304,768]{1,0:T(8,128)(2,1)}, bf16[2304,768]{1,0:T(8,128)(2,1)S(1)}) fusion(f32[2304]{0:T(1024)S(1)} %mul.495, f32[2304,768]{1,0:T(8,128)} %copy-done.84, f32[2304,768]{1,0:T(8,128)} %get-tuple-element.186, bf16[2304,2048]{1,0:T(8,128)(2,1)} %bitcast.110, bf16[1,768,2048]{2,1,0:T(8,128)(2,1)S(1)} %copy-done), kind=kOutput, calls=%fused_computation.36 | convolution fusion | flops 7272529920 | bytes 33825792 | tf_op jit(solution)/shard_map/ecd,efd->ecf/dot_general | solution.py:323
  729.1 14.7 %add_convert_fusion = bf16[2304,2048]{1,0:T(8,128)(2,1)} fusion(f32[2304,2048]{1,0:T(8,128)} %fusion.52, bf16[2304,768]{1,0:T(8,128)(2,1)} %get-tuple-element.118, bf16[1,2048,768]{2,1,0:T(8,128)(2,1)S(1)} %copy-done.78), kind=kOutput, calls=%fused_computation.18 | convolution fusion | flops 7257194496 | bytes 34996224 | tf_op jit(solution)/shard_map/ecf,edf->ecd/dot_general | solution.py:335
  760.2 94.2 %all-to-all-done.6 = bf16[8,4,72,2048]{3,2,1,0:T(8,128)(2,1)} async-done(((bf16[8,4,72,2048]{3,2,1,0:T(8,128)(2,1)}), bf16[8,4,72,2048]{3,2,1,0:T(8,128)(2,1)}, u32[]{:S(2)}, u32[]{:S(2)}) %all-to-all-start.6) | async-done | bytes 9437216 | tf_op jit(solution)/shard_map/all_to_all | solution.py:145
  874.0 24.4 %collective-permute-done.46 = bf16[256,2048]{1,0:T(8,128)(2,1)S(1)} collective-permute-done((bf16[256,2048]{1,0:T(8,128)(2,1)S(1)}, bf16[256,2048]{1,0:T(8,128)(2,1)S(1)}, u32[]{:S(2)}, u32[]{:S(2)}) %collective-permute-start.46) | collective-permute-done | bytes 1048608 | tf_op jit(solution)/shard_map/ppermute | solution.py:82
  902.3 13.1 convolution_bitcast_fusion.2
  1035.0 13.6 fusion.109
  1048.7 21.8 %fusion.1 = (f32[8,1024]{1,0:T(8,128)S(1)}, f32[1024,1024,8]{1,0,2:T(8,128)}) fusion(f32[8,1024,1024]{1,2,0:T(8,128)} %get-tuple-element.184, f32[8,1024]{1,0:T(8,128)S(1)} %log_add_fusion, bf16[1024,8,128]{0,2,1:T(8,128)(2,1)S(1)} %bitcast.572, f32[1024,1280]{1,0:T(8,128)} %copy-done.9), kind=kOutput, calls=%fused_computation.3 | convolution fusion | flops 2172641280 | bytes 69533696 | tf_op jit(solution)/shard_map/tgd,sd->gts/dot_general | solution.py:384
  1070.5 28.2 %fusion.3 = bf16[8,1024,1024]{1,2,0:T(8,128)(2,1)} fusion(f32[1024,1024,8]{1,0,2:T(8,128)} %get-tuple-element.193, f32[8,1024,1024]{1,2,0:T(8,128)} %get-tuple-element.184, f32[8,1024]{1,0:T(8,128)S(1)} %get-tuple-element.192, f32[8,1024]{1,0:T(8,128)S(1)} %log_add_fusion), kind=kLoop, calls=%fused_computation.5 | loop fusion | flops 33554432 | bytes 83951616 | tf_op jit(solution)/shard_map/convert_element_type | solution.py:388
  1165.9 15.6 %collective-permute-done.58 = bf16[2,256,1024]{2,1,0:T(8,128)(2,1)S(1)} collective-permute-done((bf16[2,256,1024]{2,1,0:T(8,128)(2,1)S(1)}, bf16[2,256,1024]{2,1,0:T(8,128)(2,1)S(1)}, u32[]{:S(2)}, u32[]{:S(2)}) %collective-permute-start.58) | collective-permute-done | bytes 1048608 | tf_op jit(solution)/shard_map/ppermute | solution.py:92
  1246.4 17.1 %collective-permute-start.63 = (bf16[4,64,1280]{2,1,0:T(8,128)(2,1)}, bf16[4,64,1280]{2,1,0:T(8,128)(2,1)}, u32[]{:S(2)}, u32[]{:S(2)}) collective-permute-start(bf16[4,64,1280]{2,1,0:T(8,128)(2,1)} %get-tuple-element.144), channel_id=1, source_target_pairs={{0,8},{8,16},{16,24},{1,9},{9,17},{17,25},{2,10},{10,18},{18,26},{... | collective-permute-start | bytes 1966088 | tf_op jit(solution)/shard_map/ppermute | solution.py:82
  1287.1 101.3 %all-reduce.6.cloned.1.call-done = f32[32,3072]{1,0:T(8,128)} async-done(((f32[32,3072]{1,0:T(8,128)}), f32[32,3072]{1,0:T(8,128)}) %all-reduce.6.cloned.1.call-update) | async-done | bytes 393232
  (555 shorter events, 776.1 us)
Async XLA Ops:
  35.8 93.7 %collective-permute-start = (bf16[256,2048]{1,0:T(8,128)(2,1)}, bf16[256,2048]{1,0:T(8,128)(2,1)}, u32[]{:S(2)}, u32[]{:S(2)}) collective-permute-start(bf16[256,2048]{1,0:T(8,128)(2,1)} %bitcast), channel_id=1, source_target_pairs={{0,2},{2,0},{4,6},{6,4},{1,3},{3,1},{5,7},{7,5},{8,10},{10,8},{12,... | collective-permute-start | bytes 3145736 | tf_op jit(solution)/shard_map/ppermute | solution.py:92
  38.2 33.4 %collective-permute-start.7 = (bf16[4,64,1408]{2,1,0:T(8,128)(2,1)}, bf16[4,64,1408]{2,1,0:T(8,128)(2,1)}, u32[]{:S(2)}, u32[]{:S(2)}) collective-permute-start(bf16[4,64,1408]{2,1,0:T(8,128)(2,1)} %all-to-all-done), channel_id=1, source_target_pairs={{8,0},{16,8},{24,16},{9,1},{17,9},{25,17},{10,2},{18,10},{26,18},{... | collective-permute-start | bytes 2162696 | tf_op jit(solution)/shard_map/ppermute | solution.py:64
  71.0 61.1 %collective-permute-start.1 = (bf16[256,2048]{1,0:T(8,128)(2,1)}, bf16[256,2048]{1,0:T(8,128)(2,1)}, u32[]{:S(2)}, u32[]{:S(2)}) collective-permute-start(bf16[256,2048]{1,0:T(8,128)(2,1)} %bitcast), channel_id=1, source_target_pairs={{0,4},{2,6},{4,0},{6,2},{1,5},{3,7},{5,1},{7,3},{8,12},{10,14},{12... | collective-permute-start | bytes 3145736 | tf_op jit(solution)/shard_map/ppermute | solution.py:92
  332.1 54.7 %collective-permute-start.31 = (bf16[256,2048]{1,0:T(8,128)(2,1)}, bf16[256,2048]{1,0:T(8,128)(2,1)}, u32[]{:S(2)}, u32[]{:S(2)}) collective-permute-start(bf16[256,2048]{1,0:T(8,128)(2,1)} %multiply_convert_fusion.4), channel_id=1, source_target_pairs={{8,0},{16,8},{24,16},{9,1},{17,9},{25,17},{10,2},{18,10},{26,18},{... | collective-permute-start | bytes 3145736 | tf_op jit(solution)/shard_map/ppermute | solution.py:64
  351.6 37.1 %collective-permute-start.29 = (bf16[256,2048]{1,0:T(8,128)(2,1)}, bf16[256,2048]{1,0:T(8,128)(2,1)}, u32[]{:S(2)}, u32[]{:S(2)}) collective-permute-start(bf16[256,2048]{1,0:T(8,128)(2,1)} %collective-permute-done.28), channel_id=1, source_target_pairs={{8,16},{16,24},{9,17},{17,25},{10,18},{18,26},{11,19},{19,27},{12,... | collective-permute-start | bytes 3145736 | tf_op jit(solution)/shard_map/ppermute | solution.py:63
  445.4 109.5 %all-to-all-start.2 = ((bf16[8,4,72,2048]{3,2,1,0:T(8,128)(2,1)}), bf16[8,4,72,2048]{3,2,1,0:T(8,128)(2,1)}, u32[]{:S(2)}, u32[]{:S(2)}) async-start(bf16[8,4,72,2048]{3,2,1,0:T(8,128)(2,1)} %copy.290), calls=%async_computation.2 | async-start | bytes 18874368 | tf_op jit(solution)/shard_map/all_to_all | solution.py:145
  554.9 110.8 %all-to-all-start.5 = ((bf16[8,4,72,2048]{3,2,1,0:T(8,128)(2,1)}), bf16[8,4,72,2048]{3,2,1,0:T(8,128)(2,1)}, u32[]{:S(2)}, u32[]{:S(2)}) async-start(bf16[8,4,72,2048]{3,2,1,0:T(8,128)(2,1)} %copy.294), calls=%async_computation.5 | async-start | bytes 18874368 | tf_op jit(solution)/shard_map/all_to_all | solution.py:145
  696.9 46.8 %all-to-all-start.8 = ((f32[4,256,8]{1,2,0:T(8,128)}), f32[4,256,8]{1,2,0:T(8,128)S(1)}, u32[]{:S(2)}, u32[]{:S(2)}) async-start(f32[4,256,8]{1,2,0:T(8,128)} %bitcast.125), calls=%async_computation.8 | async-start | bytes 65536 | tf_op jit(solution)/shard_map/all_to_all | solution.py:145
  743.8 110.6 %all-to-all-start.6 = ((bf16[8,4,72,2048]{3,2,1,0:T(8,128)(2,1)}), bf16[8,4,72,2048]{3,2,1,0:T(8,128)(2,1)}, u32[]{:S(2)}, u32[]{:S(2)}) async-start(bf16[8,4,72,2048]{3,2,1,0:T(8,128)(2,1)} %bitcast.575), calls=%async_computation.6 | async-start | bytes 18874368 | tf_op jit(solution)/shard_map/all_to_all | solution.py:145
  854.4 110.3 %all-to-all-start.4 = ((bf16[8,4,72,2048]{3,2,1,0:T(8,128)(2,1)}), bf16[8,4,72,2048]{3,2,1,0:T(8,128)(2,1)}, u32[]{:S(2)}, u32[]{:S(2)}) async-start(bf16[8,4,72,2048]{3,2,1,0:T(8,128)(2,1)} %bitcast.556), calls=%async_computation.4 | async-start | bytes 18874368 | tf_op jit(solution)/shard_map/all_to_all | solution.py:145
  873.3 42.1 %collective-permute-start.49 = (bf16[256,2048]{1,0:T(8,128)(2,1)S(1)}, bf16[256,2048]{1,0:T(8,128)(2,1)S(1)}, u32[]{:S(2)}, u32[]{:S(2)}) collective-permute-start(bf16[256,2048]{1,0:T(8,128)(2,1)S(1)} %get-tuple-element.131), channel_id=1, source_target_pairs={{24,16},{25,17},{26,18},{27,19},{28,20},{29,21},{30,22},{31,23}} | collective-permute-start | bytes 3145736 | tf_op jit(solution)/shard_map/ppermute | solution.py:83
  942.3 33.1 %collective-permute-start.48 = (bf16[256,2048]{1,0:T(8,128)(2,1)}, bf16[256,2048]{1,0:T(8,128)(2,1)}, u32[]{:S(2)}, u32[]{:S(2)}) collective-permute-start(bf16[256,2048]{1,0:T(8,128)(2,1)} %get-tuple-element.128), channel_id=1, source_target_pairs={{0,8},{8,16},{16,24},{1,9},{9,17},{17,25},{2,10},{10,18},{18,26},{... | collective-permute-start | bytes 3145736 | tf_op jit(solution)/shard_map/ppermute | solution.py:82
  1004.2 154.2 %collective-permute-start.37 = (bf16[256,2048]{1,0:T(8,128)(2,1)}, bf16[256,2048]{1,0:T(8,128)(2,1)}, u32[]{:S(2)}, u32[]{:S(2)}) collective-permute-start(bf16[256,2048]{1,0:T(8,128)(2,1)} %get-tuple-element.135), channel_id=1, source_target_pairs={{24,16},{25,17},{26,18},{27,19},{28,20},{29,21},{30,22},{31,23}} | collective-permute-start | bytes 3145736 | tf_op jit(solution)/shard_map/ppermute | solution.py:83
  1008.9 149.6 %collective-permute-start.35 = (bf16[256,2048]{1,0:T(8,128)(2,1)}, bf16[256,2048]{1,0:T(8,128)(2,1)}, u32[]{:S(2)}, u32[]{:S(2)}) collective-permute-start(bf16[256,2048]{1,0:T(8,128)(2,1)} %fusion.91), channel_id=1, source_target_pairs={{0,8},{8,16},{1,9},{9,17},{2,10},{10,18},{3,11},{11,19},{4,12},{12... | collective-permute-start | bytes 3145736 | tf_op jit(solution)/shard_map/ppermute | solution.py:82
  1163.1 117.7 %collective-permute-start.36 = (bf16[256,2048]{1,0:T(8,128)(2,1)}, bf16[256,2048]{1,0:T(8,128)(2,1)}, u32[]{:S(2)}, u32[]{:S(2)}) collective-permute-start(bf16[256,2048]{1,0:T(8,128)(2,1)} %get-tuple-element.132), channel_id=1, source_target_pairs={{0,8},{8,16},{16,24},{1,9},{9,17},{17,25},{2,10},{10,18},{18,26},{... | collective-permute-start | bytes 3145736 | tf_op jit(solution)/shard_map/ppermute | solution.py:82
  1183.8 33.6 %collective-permute-start.59 = (bf16[256,1024]{1,0:T(8,128)(2,1)}, bf16[256,1024]{1,0:T(8,128)(2,1)}, u32[]{:S(2)}, u32[]{:S(2)}) collective-permute-start(bf16[256,1024]{1,0:T(8,128)(2,1)} %fusion.137), channel_id=1, source_target_pairs={{0,2},{2,0},{4,6},{6,4},{1,3},{3,1},{5,7},{7,5},{8,10},{10,8},{12,... | collective-permute-start | bytes 1572872 | tf_op jit(solution)/shard_map/ppermute | solution.py:92
  1186.2 34.9 %collective-permute-start.57 = (bf16[256,1024]{1,0:T(8,128)(2,1)}, bf16[256,1024]{1,0:T(8,128)(2,1)}, u32[]{:S(2)}, u32[]{:S(2)}) collective-permute-start(bf16[256,1024]{1,0:T(8,128)(2,1)} %fusion.138), channel_id=1, source_target_pairs={{0,4},{2,6},{4,0},{6,2},{1,5},{3,7},{5,1},{7,3},{8,12},{10,14},{12... | collective-permute-start | bytes 1572872 | tf_op jit(solution)/shard_map/ppermute | solution.py:92
  1193.4 33.2 %all-to-all-start.10 = ((bf16[4,128,2048]{2,1,0:T(8,128)(2,1)}), bf16[4,128,2048]{2,1,0:T(8,128)(2,1)}, u32[]{:S(2)}, u32[]{:S(2)}) async-start(bf16[4,128,2048]{2,1,0:T(8,128)(2,1)} %fusion.32), calls=%async_computation.10 | async-start | bytes 4194304 | tf_op jit(solution)/shard_map/all_to_all | solution.py:145
  1199.4 189.0 %all-reduce.6.cloned.1.call-start = ((), (), s32[]{:S(2)}) async-start(), calls=%async_computation.11 | async-start | bytes 786432
  1211.5 71.3 %collective-permute-start.39 = (bf16[256,2048]{1,0:T(8,128)(2,1)}, bf16[256,2048]{1,0:T(8,128)(2,1)}, u32[]{:S(2)}, u32[]{:S(2)}) collective-permute-start(bf16[256,2048]{1,0:T(8,128)(2,1)} %fusion.90), channel_id=1, source_target_pairs={{8,0},{16,8},{24,16},{9,1},{17,9},{25,17},{10,2},{18,10},{26,18},{... | collective-permute-start | bytes 3145736 | tf_op jit(solution)/shard_map/ppermute | solution.py:83
  1243.7 146.1 %collective-permute-start.71 = (bf16[128,2048]{1,0:T(8,128)(2,1)}, bf16[128,2048]{1,0:T(8,128)(2,1)}, u32[]{:S(2)}, u32[]{:S(2)}) collective-permute-start(bf16[128,2048]{1,0:T(8,128)(2,1)} %get-tuple-element.151), channel_id=1, source_target_pairs={{24,16},{25,17},{26,18},{27,19},{28,20},{29,21},{30,22},{31,23}} | collective-permute-start | bytes 1572872 | tf_op jit(solution)/shard_map/ppermute | solution.py:83
  1246.4 150.7 %collective-permute-start.63 = (bf16[4,64,1280]{2,1,0:T(8,128)(2,1)}, bf16[4,64,1280]{2,1,0:T(8,128)(2,1)}, u32[]{:S(2)}, u32[]{:S(2)}) collective-permute-start(bf16[4,64,1280]{2,1,0:T(8,128)(2,1)} %get-tuple-element.144), channel_id=1, source_target_pairs={{0,8},{8,16},{16,24},{1,9},{9,17},{17,25},{2,10},{10,18},{18,26},{... | collective-permute-start | bytes 1966088 | tf_op jit(solution)/shard_map/ppermute | solution.py:82
  1271.8 118.0 %collective-permute-start.69 = (bf16[128,2048]{1,0:T(8,128)(2,1)}, bf16[128,2048]{1,0:T(8,128)(2,1)}, u32[]{:S(2)}, u32[]{:S(2)}) collective-permute-start(bf16[128,2048]{1,0:T(8,128)(2,1)} %fusion.134), channel_id=1, source_target_pairs={{0,8},{8,16},{1,9},{9,17},{2,10},{10,18},{3,11},{11,19},{4,12},{12... | collective-permute-start | bytes 1572872 | tf_op jit(solution)/shard_map/ppermute | solution.py:82
  1280.8 116.3 %collective-permute-start.66 = (bf16[4,64,1280]{2,1,0:T(8,128)(2,1)}, bf16[4,64,1280]{2,1,0:T(8,128)(2,1)}, u32[]{:S(2)}, u32[]{:S(2)}) collective-permute-start(bf16[4,64,1280]{2,1,0:T(8,128)(2,1)} %fusion.99), channel_id=1, source_target_pairs={{8,0},{16,8},{24,16},{9,1},{17,9},{25,17},{10,2},{18,10},{26,18},{... | collective-permute-start | bytes 1966088 | tf_op jit(solution)/shard_map/ppermute | solution.py:83
  (146 other events, 3443.1 us)
Sparse Core Ops, SparseCore 0:
  1243.8 144.5 all-reduce.5

commit v2 on v1

v2 whole, which is shorter than its diff:
```python
import functools

import jax
import jax.numpy as jnp
from jax import lax
from jax.experimental import pallas as pl
from jax.experimental.pallas import tpu as pltpu
from jax.sharding import PartitionSpec as P

eps_norm = 1e-06
rope_base = 1000000.0
masked_score = -1e30
ALL = ("dp", "ctx", "exp")
PLANE = ("ctx", "exp")
VMEM = 56 << 20
MESH = pl.DeviceIdType.MESH


def rope_tables(positions, width):
    exponents = jnp.arange(width // 2, dtype=jnp.float32) * (2.0 / width)
    frequency = rope_base ** (-exponents)
    angles = positions.astype(jnp.float32)[:, None] * frequency[None, :]
    angles = jnp.concatenate([angles, angles], axis=-1)
    return (jnp.cos(angles), jnp.sin(angles))


def norm_back(grad, normed, inverse, gain):
    gain_grad = jnp.sum(grad * normed, axis=0)
    scaled = grad * gain
    return (
        inverse * (scaled - normed * jnp.mean(scaled * normed, axis=-1, keepdims=True)),
        gain_grad,
    )


def line_gather(block, axis):
    n = lax.axis_size(axis)
    me = lax.axis_index(axis)
    before, after = [], []
    up = down = block
    for step in range(1, n):
        up = lax.ppermute(up, axis, [(i, i + 1) for i in range(step - 1, n - 1)])
        down = lax.ppermute(down, axis, [(i, i - 1) for i in range(1, n - step + 1)])
        before.insert(0, up)
        after.append(down)
    return lax.dynamic_slice_in_dim(jnp.stack(before + [block] + after), n - 1 - me, n, 0)


def line_scatter(parts, axis):
    n = lax.axis_size(axis)
    me = lax.axis_index(axis)

    def part(i):
        return lax.dynamic_index_in_dim(parts, jnp.clip(i, 0, n - 1), 0, keepdims=False)

    up = down = None
    for step in range(1, n):
        send_up, send_down = part(me + n - step), part(me - n + step)
        if up is not None:
            send_up, send_down = add_low(send_up, up), add_low(send_down, down)
        up = lax.ppermute(send_up, axis, [(i, i + 1) for i in range(step)])
        down = lax.ppermute(send_down, axis, [(i, i - 1) for i in range(n - step, n)])
    return part(me).astype(jnp.float32) + up.astype(jnp.float32) + down.astype(jnp.float32)


def add_low(left, right):
    return (left.astype(jnp.float32) + right.astype(jnp.float32)).astype(left.dtype)


def flip(block, axis, bit):
    return lax.ppermute(block, axis, [(i, i ^ bit) for i in range(lax.axis_size(axis))])


def square_gather(block, axis):
    if lax.axis_size(axis) != 4:
        return lax.all_gather(block, axis, axis=0, tiled=False)
    half = block.shape[-1] // 2
    me = lax.axis_index(axis)
    by_x, by_y = flip(block, axis, 1), flip(block, axis, 2)
    far = jnp.concatenate(
        [flip(by_x[..., :half], axis, 2), flip(by_y[..., half:], axis, 1)], axis=-1
    )
    whole = jnp.zeros((4,) + block.shape, block.dtype)
    for bits, piece in enumerate((block, by_x, by_y, far)):
        whole = lax.dynamic_update_index_in_dim(whole, piece, me ^ bits, 0)
    return whole


def square_scatter(parts, axis):
    if lax.axis_size(axis) != 4:
        return lax.psum_scatter(parts, axis, scatter_dimension=0, tiled=False).astype(jnp.float32)
    half = parts.shape[-1] // 2
    me = lax.axis_index(axis)
    own, to_x, to_y, far = [
        lax.dynamic_index_in_dim(parts, me ^ bits, 0, keepdims=False) for bits in range(4)
    ]
    first = flip(jnp.stack([to_x[..., :half], far[..., :half]]), axis, 1)
    second = flip(jnp.stack([to_y[..., half:], far[..., half:]]), axis, 2)
    later_first = flip(add_low(to_y[..., :half], first[1]), axis, 2)
    later_second = flip(add_low(to_x[..., half:], second[1]), axis, 1)
    own = own.astype(jnp.float32)
    first = own[..., :half] + first[0].astype(jnp.float32) + later_first.astype(jnp.float32)
    second = own[..., half:] + second[0].astype(jnp.float32) + later_second.astype(jnp.float32)
    return jnp.concatenate([first, second], axis=-1)


def pair_gather(block, axis):
    if lax.axis_size(axis) != 2:
        return lax.all_gather(block, axis, axis=0, tiled=False)
    other = flip(block, axis, 1)
    first = lax.axis_index(axis) == 0
    return jnp.stack([jnp.where(first, block, other), jnp.where(first, other, block)])


def pair_scatter(parts, axis):
    if lax.axis_size(axis) != 2:
        return lax.psum_scatter(parts, axis, scatter_dimension=0, tiled=False)
    first = lax.axis_index(axis) == 0
    other = flip(jnp.where(first, parts[1], parts[0]), axis, 1)
    return add_low(jnp.where(first, parts[0], parts[1]), other)


def swap(parts, axis):
    return lax.all_to_all(parts, axis, split_axis=0, concat_axis=0, tiled=True)


def project_kernel(x_ref, gain_ref, weight_ref, scale_ref, cos_ref, sin_ref, hidden_ref, raw_ref, out_ref, *, q_heads, kv_heads):
    x = x_ref[...].astype(jnp.float32)
    inverse = lax.rsqrt(jnp.mean(x * x, axis=-1, keepdims=True) + eps_norm)
    hidden = ((x * inverse) * gain_ref[...]).astype(jnp.bfloat16)
    hidden_ref[...] = hidden
    raw = jnp.dot(hidden, weight_ref[...], preferred_element_type=jnp.float32)
    raw_ref[...] = raw
    width = cos_ref.shape[1]
    cosine, sine = cos_ref[...], sin_ref[...]
    for h in range(q_heads + kv_heads):
        here = slice(h * width, (h + 1) * width)
        part = raw[:, here]
        scale = scale_ref[0:1, :] if h < q_heads else scale_ref[1:2, :]
        factor = lax.rsqrt(jnp.mean(part * part, axis=-1, keepdims=True) + eps_norm)
        scaled = part * factor * scale
        turned = pltpu.roll(scaled, width // 2, 1)
        out_ref[:, here] = (scaled * cosine + turned * sine).astype(jnp.bfloat16)
    rest = slice((q_heads + kv_heads) * width, raw.shape[1])
    out_ref[:, rest] = raw[:, rest].astype(jnp.bfloat16)


def project(x, gain, weight, scales, cosine, sine, q_heads, kv_heads, block):
    rows, width = x.shape
    columns = weight.shape[1]
    head = cosine.shape[1]
    whole = lambda shape: pl.BlockSpec(shape, lambda i: (0, 0))
    return pl.pallas_call(
        functools.partial(project_kernel, q_heads=q_heads, kv_heads=kv_heads),
        grid=(rows // block,),
        in_specs=[
            pl.BlockSpec((block, width), lambda i: (i, 0)),
            whole((1, width)),
            whole((width, columns)),
            whole((2, head)),
            pl.BlockSpec((block, head), lambda i: (i, 0)),
            pl.BlockSpec((block, head), lambda i: (i, 0)),
        ],
        out_specs=[
            pl.BlockSpec((block, width), lambda i: (i, 0)),
            pl.BlockSpec((block, columns), lambda i: (i, 0)),
            pl.BlockSpec((block, columns), lambda i: (i, 0)),
        ],
        out_shape=[
            jax.ShapeDtypeStruct((rows, width), jnp.bfloat16),
            jax.ShapeDtypeStruct((rows, columns), jnp.float32),
            jax.ShapeDtypeStruct((rows, columns), jnp.bfloat16),
        ],
        compiler_params=pltpu.CompilerParams(vmem_limit_bytes=VMEM),
        cost_estimate=pl.CostEstimate(
            flops=2 * rows * width * columns, bytes_accessed=30 << 20, transcendentals=0
        ),
    )(x, gain, weight, scales, cosine, sine)


def seen(bounds_ref, first, rows, keys):
    query = first + lax.broadcasted_iota(jnp.int32, (rows, 1), 0)
    low_end, high_end = bounds_ref[0, 0], bounds_ref[0, 1]
    start = jnp.where(query >= high_end, high_end, jnp.where(query >= low_end, low_end, 0))
    key = lax.broadcasted_iota(jnp.int32, (rows, keys), 1)
    return (key <= query) & (key >= start)


def shares_of(query, keys, allowed, score_scale):
    scores = lax.dot_general(
        query, keys, (((1,), (1,)), ((), ())), preferred_element_type=jnp.float32
    )
    scores = jnp.where(allowed, scores * score_scale, masked_score)
    weights = jnp.exp(scores - jnp.max(scores, axis=-1, keepdims=True))
    return weights / jnp.sum(weights, axis=-1, keepdims=True)


def attend_kernel(bounds_ref, query_ref, key_ref, value_ref, out_ref, *, block, score_scale):
    rows = query_ref.shape[0]
    for first in range(0, rows, block):
        last = first + block
        allowed = seen(bounds_ref, first, block, last)
        shares = shares_of(query_ref[first:last, :], key_ref[:last, :], allowed, score_scale)
        out_ref[first:last, :] = jnp.dot(
            shares.astype(jnp.bfloat16), value_ref[:last, :], preferred_element_type=jnp.float32
        ).astype(jnp.bfloat16)


def attend(bounds, turned, heads, kv_heads, head, block):
    rows = turned.shape[0]
    group = heads // kv_heads
    return pl.pallas_call(
        functools.partial(attend_kernel, block=block, score_scale=head ** (-0.5)),
        grid=(heads,),
        in_specs=[
            pl.BlockSpec(memory_space=pltpu.SMEM),
            pl.BlockSpec((rows, head), lambda h: (0, h)),
            pl.BlockSpec((rows, head), lambda h: (0, heads + h // group)),
            pl.BlockSpec((rows, head), lambda h: (0, heads + kv_heads + h // group)),
        ],
        out_specs=pl.BlockSpec((rows, head), lambda h: (0, h)),
        out_shape=jax.ShapeDtypeStruct((rows, heads * head), jnp.bfloat16),
        compiler_params=pltpu.CompilerParams(vmem_limit_bytes=VMEM),
        cost_estimate=pl.CostEstimate(
            flops=2 * heads * rows * rows * head,
            bytes_accessed=6 << 20,
            transcendentals=heads * rows * rows // 2,
        ),
    )(bounds, turned, turned, turned)


def attend_back_kernel(
    bounds_ref, query_ref, key_ref, value_ref, grad_ref, raw_ref, scale_ref, cos_ref, sin_ref,
    out_ref, gain_ref, key_sum, value_sum, *, block, heads, group, score_scale,
):
    step = pl.program_id(0)
    rows = query_ref.shape[0]
    low, full = jnp.bfloat16, jnp.float32
    kv_heads = heads // group

    def norm_rope_back(grad, raw, scale, cosine, sine):
        inverse = lax.rsqrt(jnp.mean(raw * raw, axis=-1, keepdims=True) + eps_norm)
        normed = raw * inverse
        turned = grad * cosine + pltpu.roll(grad * sine, grad.shape[-1] // 2, 1)
        inner = turned * scale
        back = inverse * (inner - normed * jnp.mean(inner * normed, axis=-1, keepdims=True))
        return back, jnp.sum(turned * normed, axis=0, keepdims=True)

    @pl.when(step == 0)
    def _():
        gain_ref[...] = jnp.zeros_like(gain_ref)

    @pl.when(lax.rem(step, group) == 0)
    def _():
        @pl.when(step < heads)
        def _():
            for kv in range(kv_heads):
                @pl.when(step == kv * group)
                def _():
                    key_sum[kv] = jnp.zeros((rows, key_ref.shape[1]), full)
                    value_sum[kv] = jnp.zeros((rows, key_ref.shape[1]), full)

    @pl.when(step < heads)
    def _():
        kv = jnp.minimum(step // group, kv_heads - 1)
        gains = jnp.zeros((1, query_ref.shape[1]), full)
        for first in range(0, rows, block):
            last = first + block
            query, keys, values = query_ref[first:last, :], key_ref[:last, :], value_ref[:last, :]
            grad = grad_ref[first:last, :]
            allowed = seen(bounds_ref, first, block, last)
            shares = shares_of(query, keys, allowed, score_scale)
            share_grads = lax.dot_general(
                grad, values, (((1,), (1,)), ((), ())), preferred_element_type=full
            )
            centre = jnp.sum(shares * share_grads, axis=-1, keepdims=True)
            score_grads = (shares * (share_grads - centre)).astype(low)
            key_sum[kv, :last, :] += lax.dot_general(
                score_grads, query, (((0,), (0,)), ((), ())), preferred_element_type=full
            )
            value_sum[kv, :last, :] += lax.dot_general(
                shares.astype(low), grad, (((0,), (0,)), ((), ())), preferred_element_type=full
            )
            query_grad = jnp.dot(score_grads, keys, preferred_element_type=full) * score_scale
            back, gain = norm_rope_back(
                query_grad, raw_ref[first:last, :], scale_ref[0:1, :], cos_ref[first:last, :],
                sin_ref[first:last, :],
            )
            out_ref[first:last, :] = back.astype(low)
            gains += gain
        gain_ref[0:1, :] += gains

    @pl.when((step >= heads) & (step < heads + kv_heads))
    def _():
        back, gain = norm_rope_back(
            key_sum[step - heads] * score_scale, raw_ref[...], scale_ref[1:2, :], cos_ref[...],
            sin_ref[...],
        )
        out_ref[...] = back.astype(low)
        gain_ref[1:2, :] += gain

    @pl.when(step >= heads + kv_heads)
    def _():
        out_ref[...] = value_sum[step - heads - kv_heads].astype(low)


def attend_back(bounds, turned, grad, raw, scales, cosine, sine, heads, kv_heads, head, block):
    rows = turned.shape[0]
    group = heads // kv_heads
    columns = turned.shape[1]
    within = lambda h: jnp.minimum(h, heads - 1)
    tables = pl.BlockSpec((rows, head), lambda h: (0, 0))
    return pl.pallas_call(
        functools.partial(
            attend_back_kernel, block=block, heads=heads, group=group, score_scale=head ** (-0.5)
        ),
        grid=(heads + 2 * kv_heads,),
        in_specs=[
            pl.BlockSpec(memory_space=pltpu.SMEM),
            pl.BlockSpec((rows, head), lambda h: (0, within(h))),
            pl.BlockSpec((rows, head), lambda h: (0, heads + within(h) // group)),
            pl.BlockSpec((rows, head), lambda h: (0, heads + kv_heads + within(h) // group)),
            pl.BlockSpec((rows, head), lambda h: (0, within(h))),
            pl.BlockSpec((rows, head), lambda h: (0, jnp.minimum(h, heads + kv_heads - 1))),
            pl.BlockSpec((2, head), lambda h: (0, 0)),
            tables,
            tables,
        ],
        out_specs=[
            pl.BlockSpec((rows, head), lambda h: (0, h)),
            pl.BlockSpec((2, head), lambda h: (0, 0)),
        ],
        out_shape=[
            jax.ShapeDtypeStruct((rows, columns), jnp.bfloat16),
            jax.ShapeDtypeStruct((2, head), jnp.float32),
        ],
        scratch_shapes=[pltpu.VMEM((kv_heads, rows, head), jnp.float32)] * 2,
        compiler_params=pltpu.CompilerParams(vmem_limit_bytes=VMEM),
        cost_estimate=pl.CostEstimate(
            flops=5 * heads * rows * rows * head,
            bytes_accessed=12 << 20,
            transcendentals=heads * rows * rows // 2,
        ),
    )(bounds, turned, turned, turned, grad, raw, scales, cosine, sine)


def greet(sizes):
    n = sizes["dp"]
    barrier = pltpu.get_barrier_semaphore()
    me = lax.axis_index("dp")
    for step in (-1, 1):
        @pl.when((me + step >= 0) & (me + step < n))
        def _():
            pl.semaphore_signal(
                barrier, inc=1, device_id={"dp": me + step}, device_id_type=MESH
            )
    number = sizes["ctx"] * sizes["exp"]
    for ahead in range(number - 1, 0, -1):
        pl.semaphore_signal(
            barrier, inc=1, device_id=place(sizes, peer(sizes, ahead)), device_id_type=MESH
        )
    neighbours = (me + n - 1) // n + (2 * n - 2 - me) // n
    pl.semaphore_wait(barrier, number - 1 + neighbours)


def plane_index(sizes):
    return lax.axis_index("ctx") * sizes["exp"] + lax.axis_index("exp")


def peer(sizes, ahead):
    number = sizes["ctx"] * sizes["exp"]
    return lax.rem(plane_index(sizes) + ahead, number)


def place(sizes, index):
    return {"ctx": index // sizes["exp"], "exp": lax.rem(index, sizes["exp"])}


def cut(widths, part):
    pieces = []
    for number, width in enumerate(widths):
        step = min(width, part)
        pieces += [(number, first, step) for first in range(0, width, step)]
    return pieces


def dispatch_kernel(*refs, sizes, pieces, arrays):
    blocks, pick_ref, outs = refs[:arrays], refs[arrays], refs[arrays + 1 : 2 * arrays + 1]
    columns, packed = refs[2 * arrays + 1 : 3 * arrays + 1], refs[3 * arrays + 1 : 4 * arrays + 1]
    line_send, line_recv, plane_send, plane_recv, own_sem = refs[4 * arrays + 1 :]
    n, number = sizes["dp"], sizes["ctx"] * sizes["exp"]
    me, here = lax.axis_index("dp"), plane_index(sizes)
    tokens = blocks[0].shape[0]
    groups, dests, rows, span = pick_ref.shape
    greet(sizes)

    def line_copy(f, origin, step):
        a, first, part = pieces[f]
        return pltpu.make_async_remote_copy(
            src_ref=columns[a].at[origin, :, pl.ds(first, part)],
            dst_ref=columns[a].at[origin, :, pl.ds(first, part)],
            send_sem=line_send.at[f, origin, (step + 1) // 2],
            recv_sem=line_recv.at[f, origin],
            device_id={"dp": me + step},
            device_id_type=MESH,
        )

    def send_own(f):
        a, first, part = pieces[f]
        columns[a][me, :, pl.ds(first, part)] = blocks[a][:, pl.ds(first, part)]
        for step in (-1, 1):
            @pl.when((me + step >= 0) & (me + step < n))
            def _():
                line_copy(f, me, step).start()

    def plane_copy(f, ahead):
        a, first, part = pieces[f]
        target = peer(sizes, ahead)
        return pltpu.make_async_remote_copy(
            src_ref=packed[a].at[target, :, pl.ds(first, part)],
            dst_ref=outs[a].at[here, :, pl.ds(first, part)],
            send_sem=plane_send.at[f, ahead],
            recv_sem=plane_recv.at[f, ahead],
            device_id=place(sizes, target),
            device_id_type=MESH,
        )

    def own_copy(f):
        a, first, part = pieces[f]
        return pltpu.make_async_copy(
            packed[a].at[here, :, pl.ds(first, part)],
            outs[a].at[here, :, pl.ds(first, part)],
            own_sem.at[f],
        )

    send_own(0)
    for f, (a, first, part) in enumerate(pieces):
        for distance in range(1, n):
            for step in (-1, 1):
                origin = me - step * distance
                beyond = me + step

                @pl.when((origin >= 0) & (origin < n))
                def _():
                    line_copy(f, origin, step).wait_recv()

                    @pl.when((beyond >= 0) & (beyond < n))
                    def _():
                        line_copy(f, origin, step).start()

            if distance == max(1, n - 2) and f + 1 < len(pieces):
                send_own(f + 1)
        for g in range(groups):
            given = columns[a][pl.ds(g * span // tokens, span // tokens), :, pl.ds(first, part)]
            given = given.reshape(span, part)

            @pl.loop(0, dests)
            def _(j):
                packed[a][j, pl.ds(g * rows, rows), pl.ds(first, part)] = jnp.dot(
                    pick_ref[g, j], given, preferred_element_type=jnp.float32
                ).astype(jnp.bfloat16)

        for ahead in range(number - 1, 0, -1):
            plane_copy(f, ahead).start()
        own_copy(f).start()

    for f in range(len(pieces)):
        for distance in range(n):
            for step in (-1, 1):
                origin = me - step * distance
                beyond = me + step

                @pl.when((origin >= 0) & (origin < n) & (beyond >= 0) & (beyond < n))
                def _():
                    line_copy(f, origin, step).wait_send()

        for ahead in range(1, number):
            plane_copy(f, ahead).wait()
        own_copy(f).wait()


def dispatch(blocks, pick, sizes, collective, part=512):
    tokens = blocks[0].shape[0]
    widths = [block.shape[1] for block in blocks]
    n, number = sizes["dp"], sizes["ctx"] * sizes["exp"]
    groups, dests, rows, _ = pick.shape
    pieces = cut(widths, part)
    count = len(pieces)
    return pl.pallas_call(
        functools.partial(dispatch_kernel, sizes=sizes, pieces=pieces, arrays=len(blocks)),
        in_specs=[pl.BlockSpec(memory_space=pltpu.VMEM)] * (len(blocks) + 1),
        out_specs=[pl.BlockSpec(memory_space=pl.ANY)] * len(blocks),
        out_shape=[
            jax.ShapeDtypeStruct((number, groups * rows, width), jnp.bfloat16) for width in widths
        ],
        scratch_shapes=[pltpu.VMEM((n, tokens, width), jnp.bfloat16) for width in widths]
        + [pltpu.VMEM((dests, groups * rows, width), jnp.bfloat16) for width in widths]
        + [
            pltpu.SemaphoreType.DMA((count, n, 2)),
            pltpu.SemaphoreType.DMA((count, n)),
            pltpu.SemaphoreType.DMA((count, number)),
            pltpu.SemaphoreType.DMA((count, number)),
            pltpu.SemaphoreType.DMA((count,)),
        ],
        compiler_params=pltpu.CompilerParams(
            collective_id=collective, has_side_effects=True, vmem_limit_bytes=VMEM
        ),
        cost_estimate=pl.CostEstimate(
            flops=10 << 30, bytes_accessed=600 << 20, transcendentals=0
        ),
    )(*blocks, pick)


def combine_kernel(*refs, sizes, pieces, arrays):
    sent, pick_ref, outs = refs[:arrays], refs[arrays], refs[arrays + 1 : 2 * arrays + 1]
    back, leaving, landing = [refs[k * arrays + 1 : (k + 1) * arrays + 1] for k in (2, 3, 4)]
    sums, line_send, line_recv, plane_send, plane_recv, own_sem = refs[5 * arrays + 1 :]
    n, number = sizes["dp"], sizes["ctx"] * sizes["exp"]
    me, here = lax.axis_index("dp"), plane_index(sizes)
    tokens = outs[0].shape[0]
    groups, span, _ = pick_ref.shape
    rows = sent[0].shape[1] // groups
    full, low = jnp.float32, jnp.bfloat16
    greet(sizes)

    def plane_copy(f, ahead):
        a, first, part = pieces[f]
        target = peer(sizes, ahead)
        return pltpu.make_async_remote_copy(
            src_ref=sent[a].at[target, :, pl.ds(first, part)],
            dst_ref=back[a].at[here, :, pl.ds(first, part)],
            send_sem=plane_send.at[f, ahead],
            recv_sem=plane_recv.at[f, ahead],
            device_id=place(sizes, target),
            device_id_type=MESH,
        )

    def own_copy(f):
        a, first, part = pieces[f]
        return pltpu.make_async_copy(
            sent[a].at[here, :, pl.ds(first, part)],
            back[a].at[here, :, pl.ds(first, part)],
            own_sem.at[f],
        )

    for f in range(len(pieces)):
        for ahead in range(number - 1, 0, -1):
            plane_copy(f, ahead).start()
        own_copy(f).start()

    def line_copy(f, target, step):
        a, first, part = pieces[f]
        return pltpu.make_async_remote_copy(
            src_ref=leaving[a].at[target, :, pl.ds(first, part)],
            dst_ref=landing[a].at[target + (step + 1) // 2, :, pl.ds(first, part)],
            send_sem=line_send.at[f, target],
            recv_sem=line_recv.at[f, target + (step + 1) // 2],
            device_id={"dp": me + step},
            device_id_type=MESH,
        )

    for f, (a, first, part) in enumerate(pieces):
        here_columns = pl.ds(first, part)
        for ahead in range(1, number):
            plane_copy(f, ahead).wait_recv()
        own_copy(f).wait()
        for g in range(groups):
            gathered = back[a][:, pl.ds(g * rows, rows), here_columns].reshape(number * rows, part)
            sums[pl.ds(g * span // tokens, span // tokens), :, pl.ds(0, part)] = jnp.dot(
                pick_ref[g], gathered, preferred_element_type=full
            ).reshape(span // tokens, tokens, part)

        for distance in range(n - 1, 0, -1):
            for step in (-1, 1):
                target = me + step * distance
                behind = me - step

                @pl.when((target >= 0) & (target < n))
                def _():
                    own = sums[target, :, pl.ds(0, part)]

                    @pl.when((behind >= 0) & (behind < n))
                    def _():
                        line_copy(f, target, step).wait_recv()
                        coming = landing[a][target + (step + 1) // 2, :, here_columns]
                        leaving[a][target, :, here_columns] = (own + coming.astype(full)).astype(low)

                    @pl.when((behind < 0) | (behind >= n))
                    def _():
                        leaving[a][target, :, here_columns] = own.astype(low)

                    line_copy(f, target, step).start()

        outs[a][:, here_columns] = sums[me, :, pl.ds(0, part)]
        for step in (-1, 1):
            @pl.when((me - step >= 0) & (me - step < n))
            def _():
                line_copy(f, me, step).wait_recv()
                outs[a][:, here_columns] += landing[a][me + (step + 1) // 2, :, here_columns].astype(full)

    for f in range(len(pieces)):
        for ahead in range(1, number):
            plane_copy(f, ahead).wait_send()
        for distance in range(1, n):
            for step in (-1, 1):
                target = me + step * distance

                @pl.when((target >= 0) & (target < n))
                def _():
                    line_copy(f, target, step).wait_send()


def combine(sent, pick, tokens, sizes, collective, part=512):
    number, back_rows = sent[0].shape[:2]
    widths = [v.shape[2] for v in sent]
    n = sizes["dp"]
    pieces = cut(widths, part)
    count = len(pieces)
    return pl.pallas_call(
        functools.partial(combine_kernel, sizes=sizes, pieces=pieces, arrays=len(sent)),
        in_specs=[pl.BlockSpec(memory_space=pl.ANY)] * len(sent)
        + [pl.BlockSpec(memory_space=pltpu.VMEM)],
        out_specs=[pl.BlockSpec(memory_space=pltpu.VMEM)] * len(sent),
        out_shape=[jax.ShapeDtypeStruct((tokens, width), jnp.float32) for width in widths],
        scratch_shapes=[pltpu.VMEM((number, back_rows, width), jnp.bfloat16) for width in widths]
        + [pltpu.VMEM((n, tokens, width), jnp.bfloat16) for width in widths]
        + [pltpu.VMEM((n + 1, tokens, width), jnp.bfloat16) for width in widths]
        + [
            pltpu.VMEM((n, tokens, max(p[2] for p in pieces)), jnp.float32),
            pltpu.SemaphoreType.DMA((count, n)),
            pltpu.SemaphoreType.DMA((count, n + 1)),
            pltpu.SemaphoreType.DMA((count, number)),
            pltpu.SemaphoreType.DMA((count, number)),
            pltpu.SemaphoreType.DMA((count,)),
        ],
        compiler_params=pltpu.CompilerParams(
            collective_id=collective, has_side_effects=True, vmem_limit_bytes=VMEM
        ),
        cost_estimate=pl.CostEstimate(
            flops=5 << 30, bytes_accessed=300 << 20, transcendentals=0
        ),
    )(*sent, pick)


def expert_kernel(
    here_ref, in_ref, parts_ref, grad_ref, gate_w_ref, up_w_ref, down_w_ref, active_ref, gate_ref,
    up_ref, rows_ref, scaled_ref, dots_ref, *, experts,
):
    full, low = jnp.float32, jnp.bfloat16
    across = (((1,), (1,)), ((), ()))
    grads = grad_ref[0]
    column = lax.broadcasted_iota(jnp.int32, (1, parts_ref.shape[2]), 1)
    mine = lax.rem(column, experts) == here_ref[0]
    parts = parts_ref[0].astype(full)
    gates = jnp.sum(jnp.where(mine & (column < 3 * experts), parts, 0.0), axis=-1, keepdims=True)
    gate_pre = jnp.dot(in_ref[0], gate_w_ref[0], preferred_element_type=full)
    up_pre = jnp.dot(in_ref[0], up_w_ref[0], preferred_element_type=full)
    act_grad = gates * lax.dot_general(grads, down_w_ref[0], across, preferred_element_type=full)
    sigma = 1.0 / (1.0 + jnp.exp(-gate_pre))
    silu = gate_pre * sigma
    activated = silu * up_pre
    active = activated.astype(low)
    active_ref[0] = (gates * activated).astype(low)
    up_grad = (act_grad * silu).astype(low)
    gate_grad = (act_grad * up_pre * sigma * (1.0 + gate_pre * (1.0 - sigma))).astype(low)
    up_ref[0] = up_grad
    gate_ref[0] = gate_grad
    rows_ref[0] = (
        lax.dot_general(gate_grad, gate_w_ref[0], across, preferred_element_type=full)
        + lax.dot_general(up_grad, up_w_ref[0], across, preferred_element_type=full)
    ).astype(low)
    given = jnp.dot(active, down_w_ref[0], preferred_element_type=full).astype(low).astype(full)
    scaled_ref[0] = (gates * given).astype(low)
    dots = jnp.sum(given * grads.astype(full), axis=-1, keepdims=True)
    first = dots.astype(low).astype(full)
    second = (dots - first).astype(low).astype(full)
    third = dots - first - second
    spread = jnp.where(column < experts, first, jnp.where(column < 2 * experts, second, third))
    dots_ref[0] = jnp.where(mine & (column < 3 * experts), spread, 0.0).astype(low)


def expert(here, rows_in, parts, grads, gate_weight, up_weight, down_weight, experts):
    sources, rows, width = rows_in.shape
    inner = gate_weight.shape[2]
    extra = parts.shape[2]
    by_source = lambda columns: pl.BlockSpec((1, rows, columns), lambda i: (i, 0, 0))
    fixed = lambda shape: pl.BlockSpec(
        shape, lambda i: (0, 0, 0), pipeline_mode=pl.Buffered(buffer_count=1)
    )
    out = lambda columns: jax.ShapeDtypeStruct((sources, rows, columns), jnp.bfloat16)
    return pl.pallas_call(
        functools.partial(expert_kernel, experts=experts),
        grid=(sources,),
        in_specs=[
            pl.BlockSpec(memory_space=pltpu.SMEM),
            by_source(width),
            by_source(extra),
            by_source(width),
            fixed((1, width, inner)),
            fixed((1, width, inner)),
            fixed((1, inner, width)),
        ],
        out_specs=[by_source(c) for c in (inner, inner, inner, width, width, extra)],
        out_shape=[out(c) for c in (inner, inner, inner, width, width, extra)],
        compiler_params=pltpu.CompilerParams(vmem_limit_bytes=VMEM),
        cost_estimate=pl.CostEstimate(
            flops=12 * sources * rows * width * inner, bytes_accessed=60 << 20, transcendentals=0
        ),
    )(here, rows_in, parts, grads, gate_weight, up_weight, down_weight)


def shards(
    tokens,
    attention_gain,
    query_weight,
    key_weight,
    value_weight,
    query_gain,
    key_gain,
    output_weight,
    mixture_gain,
    router_weight,
    gate_weight,
    up_weight,
    down_weight,
    routes,
    bounds,
    cotangent,
):
    low, full = jnp.bfloat16, jnp.float32
    n_dp, n_ctx, n_exp = (lax.axis_size(a) for a in ALL)
    devices = n_dp * n_ctx * n_exp
    tok_count, width = tokens.shape[1], tokens.shape[2]
    seq_len = tok_count * n_ctx
    head_dim = query_gain.shape[0] * devices
    rows = query_weight.shape[0]
    heads = query_weight.shape[1] // head_dim
    kv_heads = key_weight.shape[1] // head_dim
    kv_here = kv_heads // n_ctx
    group_size = heads // kv_heads
    q_cols, kv_cols = heads * head_dim // n_ctx, kv_here * head_dim
    experts = router_weight.shape[1]
    topk = routes.shape[2]
    base_rows = tok_count * topk // experts
    capacity = base_rows + max(1, base_rows // 8)
    plane = experts // n_dp
    local_experts = gate_weight.shape[0]
    score_scale = head_dim ** (-0.5)
    dp_index = lax.axis_index("dp")

    gain_len = query_gain.shape[0]
    small = jnp.concatenate(
        [
            attention_gain[:, None],
            mixture_gain[:, None],
            jnp.pad(jnp.concatenate([query_gain, key_gain]), (0, rows - 2 * gain_len))[:, None],
            router_weight,
        ],
        axis=1,
    ).astype(low)
    small = jnp.pad(small, ((0, 0), (0, -small.shape[1] % 128)))
    extra = small.shape[1]

    def by_ctx(weight):
        return weight.astype(low).reshape(rows, n_ctx, -1).transpose(1, 0, 2)

    front = jnp.concatenate(
        [
            by_ctx(query_weight),
            by_ctx(key_weight),
            by_ctx(value_weight),
            jnp.broadcast_to(small[None], (n_ctx, rows, extra)),
        ],
        axis=2,
    )
    front = pair_gather(line_gather(swap(front, "ctx"), "dp"), "exp")
    front = front.transpose(1, 2, 0, 3, 4).reshape(width, -1)
    front_weight = front[:, : q_cols + 2 * kv_cols]
    small = front[:, q_cols + 2 * kv_cols :]
    first_gain = small[:, 0].astype(full)
    second_gain = small[:, 1].astype(full)
    head_gains = small[:, 2].reshape(devices, rows)
    query_scale = head_gains[:, :gain_len].reshape(-1).astype(full)
    key_scale = head_gains[:, gain_len : 2 * gain_len].reshape(-1).astype(full)
    router_full = small[:, 3 : 3 + experts]

    whole_tokens = square_gather(tokens[0], "ctx").reshape(seq_len, width)
    back = line_gather(output_weight.astype(low), "dp")
    back = pair_gather(swap(back, "ctx"), "exp")
    output_part = back.transpose(1, 0, 2, 3).reshape(q_cols, width)

    column_routes = line_gather(routes[0], "dp")
    chosen = jnp.any(
        column_routes[:, :, :, None] == jnp.arange(experts, dtype=jnp.int32), axis=2
    )
    hot = lax.dynamic_slice_in_dim(chosen.astype(low), dp_index * plane, plane, 2)
    row_ids = jnp.arange(tok_count, dtype=jnp.int32)
    earlier = (row_ids[None, :] < row_ids[:, None]).astype(low)
    before = jnp.einsum("st,btj->bsj", earlier, hot, preferred_element_type=full)
    together = 2 if 2 * capacity % 16 == 0 and n_dp % 2 == 0 else n_dp
    groups = n_dp // together
    slot_rows = -(-together * capacity // 16) * 16
    sizes = {"dp": n_dp, "ctx": n_ctx, "exp": n_exp}

    def grouped(v):
        return v.reshape(groups, together * tok_count, -1)

    block_first = jnp.tile(jnp.arange(together, dtype=full) * capacity, groups)[:, None, None]
    slot_at = grouped(jnp.where(hot > 0, before + block_first, -1.0))
    slots = jnp.arange(slot_rows, dtype=full)
    pick = (slot_at.transpose(0, 2, 1)[:, :, None, :] == slots[:, None]).astype(low)
    pick_back = (slot_at[:, :, :, None] == slots).astype(low).reshape(groups, -1, plane * slot_rows)

    def bring_back(sent):
        sent = sent.reshape(plane, groups, slot_rows, -1).transpose(1, 0, 2, 3)
        sent = sent.reshape(groups, plane * slot_rows, -1)
        sums = jnp.einsum("gts,gsd->gtd", pick_back, sent, preferred_element_type=full)
        return sums.reshape(n_dp, tok_count, -1)

    positions = jnp.arange(seq_len, dtype=jnp.int32)
    cosine, sine = rope_tables(positions, head_dim)
    half = head_dim // 2
    sine = jnp.concatenate([-sine[:, :half], sine[:, half:]], axis=1)
    scales = jnp.stack([query_scale, key_scale])
    heads_here = heads // n_ctx
    hidden, raw, turned = project(
        whole_tokens, first_gain[None], front_weight, scales, cosine, sine, heads_here, kv_here,
        tok_count,
    )
    attended_low = attend(bounds, turned, heads_here, kv_here, head_dim, tok_count)
    branch = jnp.dot(attended_low, output_part, preferred_element_type=full).astype(low)
    branch = square_scatter(branch.reshape(n_ctx, tok_count, width), "ctx")

    own = tokens[0].astype(full)
    middle = own + branch
    second_inverse = lax.rsqrt(jnp.mean(middle * middle, axis=-1, keepdims=True) + eps_norm)
    second_normed = middle * second_inverse
    mixed_low = (second_normed * second_gain).astype(low)

    logits = jnp.dot(mixed_low, router_full, preferred_element_type=full)
    own_chosen = jnp.any(routes[0][:, :, None] == jnp.arange(experts, dtype=jnp.int32), axis=1)
    logits = jnp.where(own_chosen, logits, masked_score)
    own_gates = jnp.exp(logits - jnp.max(logits, axis=-1, keepdims=True))
    own_gates = own_gates / jnp.sum(own_gates, axis=-1, keepdims=True)
    first_part = lax.reduce_precision(own_gates, 8, 7)
    second_part = lax.reduce_precision(own_gates - first_part, 8, 7)
    third_part = lax.reduce_precision(own_gates - first_part - second_part, 8, 7)
    gate_parts = jnp.concatenate([first_part, second_part, third_part], axis=1).astype(low)
    gate_parts = jnp.pad(gate_parts, ((0, 0), (0, -gate_parts.shape[1] % 128)))
    expert_in, part_rows, grad_rows = dispatch(
        (mixed_low, gate_parts, cotangent[0]), pick, sizes, 1
    )
    here = (dp_index * n_ctx + lax.axis_index("ctx")) * n_exp + lax.axis_index("exp")
    active, gate_grad, up_grad, row_grads, scaled_out, dot_rows = expert(
        here[None], expert_in, part_rows, grad_rows, gate_weight, up_weight, down_weight, experts
    )
    mixed_grad, dots = combine((row_grads, dot_rows), pick_back, tok_count, sizes, 2)
    weight_sum = lambda left, right: jnp.einsum(
        "scd,scf->df", left, right, preferred_element_type=full
    )[None]
    down_grad = weight_sum(active, grad_rows)
    gate_w_grad = weight_sum(expert_in, gate_grad)
    up_w_grad = weight_sum(expert_in, up_grad)
    scaled_out = swap(scaled_out, PLANE)

    dots = dots[:, :experts] + dots[:, experts : 2 * experts] + dots[:, 2 * experts : 3 * experts]
    picked_grads = own_gates * (dots - jnp.sum(own_gates * dots, axis=-1, keepdims=True))
    logit_grads = picked_grads.astype(low)
    mixed_grad = mixed_grad + jnp.einsum(
        "te,de->td", logit_grads, router_full, preferred_element_type=full
    )
    mixture = line_scatter(bring_back(scaled_out).astype(low), "dp")
    output = (middle + mixture).astype(low)[None]
    router_grad = jnp.einsum("td,te->de", mixed_low, logit_grads, preferred_element_type=full)
    grad_out = cotangent[0].astype(full)
    middle_back, second_gain_grad = norm_back(
        mixed_grad, second_normed, second_inverse, second_gain
    )
    middle_grad = grad_out + middle_back

    branch_low = square_gather(middle_grad.astype(low), "ctx").reshape(seq_len, width)
    output_w_grad = jnp.einsum("ti,td->id", attended_low, branch_low, preferred_element_type=full)
    attended_grad = jnp.einsum("td,id->ti", branch_low, output_part, preferred_element_type=full)
    raw_grad, head_gain_grads = attend_back(
        bounds, turned, attended_grad.astype(low), raw, scales, cosine, sine, heads_here, kv_here,
        head_dim, tok_count,
    )
    query_gain_grad, key_gain_grad = head_gain_grads[0], head_gain_grads[1]
    hidden_grad = jnp.einsum("ti,di->td", raw_grad, front_weight, preferred_element_type=full)
    hidden_grad = square_scatter(hidden_grad.astype(low).reshape(n_ctx, tok_count, width), "ctx")
    own_inverse = lax.rsqrt(jnp.mean(own * own, axis=-1, keepdims=True) + eps_norm)
    input_back, first_gain_grad = norm_back(hidden_grad, own * own_inverse, own_inverse, first_gain)
    tokens_grad = (middle_grad + input_back).astype(low)[None]

    front_grad = jnp.einsum("td,ti->di", hidden, raw_grad, preferred_element_type=full).astype(low)
    front_grad = front_grad.reshape(n_dp, n_ctx, n_exp, rows, -1).transpose(2, 0, 1, 3, 4)
    front_grad = line_scatter(pair_scatter(front_grad, "exp"), "dp").astype(low)
    front_grad = swap(front_grad, "ctx").astype(full)
    query_share = front_grad[:, :, :q_cols].transpose(1, 0, 2).reshape(rows, -1)
    key_share = front_grad[:, :, q_cols : q_cols + kv_cols].transpose(1, 0, 2).reshape(rows, -1)
    value_share = front_grad[:, :, q_cols + kv_cols :].transpose(1, 0, 2).reshape(rows, -1)
    back_grad = output_w_grad.astype(low).reshape(n_ctx, n_exp, -1, width).transpose(1, 0, 2, 3)
    back_grad = swap(pair_scatter(back_grad, "exp"), "ctx")
    output_share = line_scatter(back_grad, "dp")
    packed = jnp.concatenate(
        [
            first_gain_grad.reshape(devices, -1),
            second_gain_grad.reshape(devices, -1),
            query_gain_grad.reshape(devices, -1),
            key_gain_grad.reshape(devices, -1),
            router_grad.reshape(devices, -1),
        ],
        axis=1,
    )
    packed = jnp.pad(packed, ((0, 0), (0, -packed.shape[1] % 1024)))
    packed = packed.reshape(n_dp, n_ctx, n_exp, -1).transpose(2, 1, 0, 3)
    packed = square_scatter(pair_scatter(packed, "exp"), "ctx")
    packed = line_scatter(packed, "dp")
    ends = [rows, 2 * rows, 2 * rows + gain_len, 2 * rows + 2 * gain_len]
    first_share = packed[: ends[0]]
    second_share = packed[ends[0] : ends[1]]
    query_gain_share = packed[ends[1] : ends[2]]
    key_gain_share = packed[ends[2] : ends[3]]
    router_share = packed[ends[3] : ends[3] + rows * experts].reshape(rows, experts)
    return (
        output,
        tokens_grad,
        first_share,
        query_share,
        key_share,
        value_share,
        query_gain_share,
        key_gain_share,
        output_share,
        second_share,
        router_share,
        gate_w_grad,
        up_w_grad,
        down_grad,
    )


def solution(mesh):
    rows = P(ALL)
    sequences = P(("dp", "exp"), "ctx")
    in_specs = (sequences,) + (rows,) * 12 + (sequences, P(("dp", "exp")), sequences)
    out_specs = (sequences,) * 2 + (rows,) * 12
    return jax.shard_map(shards, mesh=mesh, in_specs=in_specs, out_specs=out_specs, check_vma=False)
```

time: 1440 us -> 1160 us (0.81); the launches traced: 1430 us -> 1140 us
  Pallas kernels: 0 us -> 505 us
  waiting for transfers between devices: 585 us -> 214 us
  matrix products: 277 us -> 86.9 us
  other arithmetic: 181 us -> 80.3 us
  local copies, waits for them, and re-layouts: 136 us -> 74.9 us
  starting transfers between devices: 231 us -> 174 us
    pallas_call x0 -> x6, Pallas kernels: none -> 505 us  [the longest x1 234 us: dispatch(): pl.pallas_call(functools.partial(dispatch_kernel, sizes=sizes, pieces=pie...]
    dot_general x20 -> x5, matrix products: 238 us -> 48.1 us  [the longest x3 36.3 us: shards(): jnp.einsum('scd,scf->df', left, right, preferred_element_type=full)[None]]
    all_to_all x10 -> x5, waiting for transfers between devices: 191 us -> 7.95 us  [swap(): return lax.all_to_all(parts, axis, split_axis=0, concat_axis=0, tiled=True)]
    unnamed x2 -> x0, waiting for transfers between devices: 101 us -> none
    ppermute x15 -> x9, waiting for transfers between devices: 79.1 us -> 2.81 us  [line_gather(): up = lax.ppermute(up, axis, [(i, i + 1) for i in range(step - 1, n - 1)])]
    ppermute x20 -> x25, waiting for transfers between devices: 62.3 us -> 128 us  [flip(): lax.ppermute(block, axis, [(i, i ^ bit) for i in range(lax.axis_size(axis...]
    ppermute x15 -> x9, waiting for transfers between devices: 70.7 us -> 9.73 us  [line_gather(): lax.ppermute(down, axis, [(i, i - 1) for i in range(1, n - step + 1)])]
    all_to_all x10 -> x5, starting transfers between devices: 61.9 us -> 25.9 us  [swap(): return lax.all_to_all(parts, axis, split_axis=0, concat_axis=0, tiled=True)]
  transfers between devices with their start and end apart: 85 -> 72, of which waited for: 38 -> 23; matrix products, arithmetic and copies ran while one was open for 29% -> 18% of each run, Pallas kernels for 0% -> 3%
where the time goes in v2:
time: 1160 us; the launch traced here: 1140 us
  Pallas kernels  505 us (44%)
  waiting for transfers between devices  214 us (18%)
  starting transfers between devices  174 us (15%)
  matrix products  86.9 us (7%)
  other arithmetic  80.3 us (7%)
  local copies, waits for them, and re-layouts  74.9 us (6%)
    pallas_call x1, Pallas kernels, dispatch(): pl.pallas_call(functools.partial(dispatch_kernel, sizes=sizes, pieces=pie...  234 us
    pallas_call x1, Pallas kernels, combine(): pl.pallas_call(functools.partial(combine_kernel, sizes=sizes, pieces=piec...  146 us
    ppermute x25, waiting for transfers between devices, flip(): lax.ppermute(block, axis, [(i, i ^ bit) for i in range(lax.axis_size(axis...  128 us
    pallas_call x1, Pallas kernels, expert(): pl.pallas_call(functools.partial(expert_kernel, experts=experts), grid=(s...  56.3 us
    ppermute x12, waiting for transfers between devices, line_scatter(): up = lax.ppermute(send_up, axis, [(i, i + 1) for i in range(step)])  46.8 us
    ppermute x12, starting transfers between devices, line_scatter(): up = lax.ppermute(send_up, axis, [(i, i + 1) for i in range(step)])  43.1 us
    ppermute x9, starting transfers between devices, line_gather(): up = lax.ppermute(up, axis, [(i, i + 1) for i in range(step - 1, n - 1)])  40.5 us
    dot_general x3, matrix products, shards(): jnp.einsum('scd,scf->df', left, right, preferred_element_type=full)[None]  36.3 us
  transfers between devices with their start and end apart: 72, of which 23 were waited for; matrix products, arithmetic and copies ran while one was open for 18% of the time, Pallas kernels for 3%

profile of v2, /device:TPU:14, one launch (start us, length us, event | category | flops | bytes accessed | tf_op | source)
XLA Modules:
  0.0 1138.6 jit_solution(17968454444079170983)
XLA Ops:
  60.5 18.6 %collective-permute-start.5 = (bf16[4,64,1408]{2,1,0:T(8,128)(2,1)}, bf16[4,64,1408]{2,1,0:T(8,128)(2,1)}, u32[]{:S(2)}, u32[]{:S(2)}) collective-permute-start(bf16[4,64,1408]{2,1,0:T(8,128)(2,1)} %collective-permute-done.4), channel_id=1, source_target_pairs={{8,16},{16,24},{9,17},{17,25},{10,18},{18,26},{11,19},{19,27},{12,... | collective-permute-start | bytes 2162696 | tf_op jit(solution)/shard_map/ppermute | solution.py:42
  99.8 6.2 collective-permute-done.8
  120.5 7.9 all-to-all-done.1
  160.5 12.4 %shard_map.263 = (bf16[1024,2048]{1,0:T(8,128)(2,1)}, f32[1024,1280]{1,0:T(8,128)}, bf16[1024,1280]{1,0:T(8,128)(2,1)}) custom-call(bf16[1024,2048]{1,0:T(8,128)(2,1)} %bitcast.4.x_ref, f32[1,2048]{1,0:T(1,128)} %bitcast.450, bf16[2048,1280]{1,0:T(8,128)(2,1)} %slice.286.weight_ref, f32[2,128]{1,0:T(2,128)} %maximum_convert_fusion.scale_ref, ...), custom_call_target="tpu_custom_call" | custom-call | flops 5368709120 | bytes 31457280 | tf_op jit(solution)/shard_map/pallas_call | solution.py:153
  173.0 20.8 %shard_map.264 = bf16[1024,1024]{1,0:T(8,128)(2,1)} custom-call(s32[1,2]{1,0:T(1,128)} %bounds_ref.3, bf16[1024,1280]{1,0:T(8,128)(2,1)} %get-tuple-element.30.query_ref.key_ref.value_ref, bf16[1024,1280]{1,0:T(8,128)(2,1)} %get-tuple-element.30.query_ref.key_ref.value_ref, bf16[1024,1280]{1,0:T(8,128)(2,1)} %get-tuple-element.30.query_ref.key_ref.value_ref), custom_call_target="tpu_custom_call" | custom-call | flops 2147483648 | bytes 6291456 | tf_op jit(solution)/shard_map/pallas_call | solution.py:212
  193.7 6.3 convolution_convert_fusion.4
  215.6 11.0 collective-permute-done.20
  248.0 234.2 %shard_map.265 = (bf16[8,288,2048]{2,1,0:T(8,128)(2,1)}, bf16[8,288,128]{2,1,0:T(8,128)(2,1)}, bf16[8,288,2048]{2,1,0:T(8,128)(2,1)}) custom-call(bf16[256,2048]{1,0:T(8,128)(2,1)} %copy-done.20, bf16[256,128]{1,0:T(8,128)(2,1)} %fusion.65.refs_1_, bf16[256,2048]{1,0:T(8,128)(2,1)} %bitcast.428, bf16[2,8,144,512]{3,2,1,0:T(8,128)(2,1)} %fusion.1.refs_3_), custom_call_target="tpu_custom_call" | custom-call | flops 10737418240 | bytes 629145600 | tf_op jit(solution)/shard_map/pallas_call | solution.py:489
  482.2 56.3 %shard_map.266 = (bf16[8,288,768]{2,1,0:T(8,128)(2,1)}, bf16[8,288,768]{2,1,0:T(8,128)(2,1)}, bf16[8,288,768]{2,1,0:T(8,128)(2,1)}, bf16[8,288,2048]{2,1,0:T(8,1...) custom-call(s32[1]{0:T(128)} %bitcast.61.here_ref, ...), custom_call_target="tpu_custom_call" | custom-call | flops 43486543872 | bytes 62914560 | tf_op jit(solution)/shard_map/pallas_call | solution.py:691
  538.5 145.9 %shard_map.267 = (f32[256,2048]{1,0:T(8,128)}, f32[256,128]{1,0:T(8,128)}) custom-call(bf16[8,288,2048]{2,1,0:T(8,128)(2,1)} %get-tuple-element.35.refs_0_, bf16[8,288,128]{2,1,0:T(8,128)(2,1)} %get-tuple-element.36.refs_1_, bf16[2,512,1152]{2,1,0:T(8,128)(2,1)} %get-tuple-element.84.refs_2_), custom_call_target="tpu_custom_call" | custom-call | flops 5368709120 | bytes 314572800 | tf_op jit(solution)/shard_map/pallas_call | solution.py:619
  695.1 12.2 %convolution_bitcast_fusion.1 = f32[1,2048,768]{2,1,0:T(8,128)} fusion(bf16[8,288,2048]{2,1,0:T(8,128)(2,1)} %get-tuple-element.31.in_ref, bf16[8,288,768]{2,1,0:T(8,128)(2,1)S(1)} %copy-done.45), kind=kOutput, calls=%fused_computation.13 | convolution fusion | flops 7247757312 | bytes 19267584 | tf_op jit(solution)/shard_map/scd,scf->df/dot_general | solution.py:858
  729.5 35.8 %shard_map.268 = (bf16[1024,1280]{1,0:T(8,128)(2,1)}, f32[2,128]{1,0:T(2,128)}) custom-call(s32[1,2]{1,0:T(1,128)} %bounds_ref.3, bf16[1024,1280]{1,0:T(8,128)(2,1)} %get-tuple-element.30.query_ref.key_ref.value_ref, bf16[1024,1280]{1,0:T(8,128)(2,1)} %get-tuple-element.30.query_ref.key_ref.value_ref, ...), custom_call_target="tpu_custom_call" | custom-call | flops 5368709120 | bytes 12582912 | tf_op jit(solution)/shard_map/pallas_call | solution.py:313
  765.3 9.1 convolution_convert_fusion.2
  778.9 11.9 %convolution_bitcast_fusion.2 = f32[1,2048,768]{2,1,0:T(8,128)} fusion(bf16[8,288,2048]{2,1,0:T(8,128)(2,1)} %get-tuple-element.31.in_ref, bf16[8,288,768]{2,1,0:T(8,128)(2,1)S(1)} %copy-done.44), kind=kOutput, calls=%fused_computation.14 | convolution fusion | flops 7247757312 | bytes 19267584 | tf_op jit(solution)/shard_map/scd,scf->df/dot_general | solution.py:858
  805.3 6.7 all-to-all-start.2
  821.1 7.4 convolution_convert_fusion.3
  830.4 85.2 %collective-permute-done.45 = f32[2,4,1536]{2,1,0:T(4,128)S(1)} collective-permute-done((f32[2,4,1536]{2,1,0:T(4,128)S(1)}, f32[2,4,1536]{2,1,0:T(4,128)S(1)}, u32[]{:S(2)}, u32[]{:S(2)}) %collective-permute-start.45) | collective-permute-done | bytes 49184 | tf_op jit(solution)/shard_map/ppermute | solution.py:71
  929.9 12.1 %convolution_bitcast_fusion = f32[1,768,2048]{2,1,0:T(8,128)} fusion(bf16[8,288,768]{2,1,0:T(8,128)(2,1)S(1)} %copy-done.43, bf16[8,288,2048]{2,1,0:T(8,128)(2,1)} %get-tuple-element.33.grad_ref), kind=kOutput, calls=%fused_computation.12 | convolution fusion | flops 7247757312 | bytes 19267584 | tf_op jit(solution)/shard_map/scd,scf->df/dot_general | solution.py:858
  974.0 9.3 copy.82
  983.4 9.7 convolution_convert_fusion.1
  1003.7 28.2 %collective-permute-done.61 = bf16[128,2048]{1,0:T(8,128)(2,1)S(1)} collective-permute-done((bf16[128,2048]{1,0:T(8,128)(2,1)S(1)}, bf16[128,2048]{1,0:T(8,128)(2,1)S(1)}, u32[]{:S(2)}, u32[]{:S(2)}) %collective-permute-start.61) | collective-permute-done | bytes 524320 | tf_op jit(solution)/shard_map/ppermute | solution.py:61
  1056.3 17.5 %collective-permute-done.29 = bf16[256,2048]{1,0:T(8,128)(2,1)S(1)} collective-permute-done((bf16[256,2048]{1,0:T(8,128)(2,1)S(1)}, bf16[256,2048]{1,0:T(8,128)(2,1)S(1)}, u32[]{:S(2)}, u32[]{:S(2)}) %collective-permute-start.29) | collective-permute-done | bytes 1048608 | tf_op jit(solution)/shard_map/ppermute | solution.py:61
  1093.4 11.5 %collective-permute-start.30 = (bf16[256,2048]{1,0:T(8,128)(2,1)}, bf16[256,2048]{1,0:T(8,128)(2,1)}, u32[]{:S(2)}, u32[]{:S(2)}) collective-permute-start(bf16[256,2048]{1,0:T(8,128)(2,1)} %get-tuple-element.96), channel_id=1, source_target_pairs={{0,8},{8,16},{16,24},{1,9},{9,17},{17,25},{2,10},{10,18},{18,26},{... | collective-permute-start | bytes 3145736 | tf_op jit(solution)/shard_map/ppermute | solution.py:61
  1117.6 16.4 %collective-permute-done.33 = bf16[256,2048]{1,0:T(8,128)(2,1)} collective-permute-done((bf16[256,2048]{1,0:T(8,128)(2,1)}, bf16[256,2048]{1,0:T(8,128)(2,1)}, u32[]{:S(2)}, u32[]{:S(2)}) %collective-permute-start.33) | collective-permute-done | bytes 1048608 | tf_op jit(solution)/shard_map/ppermute | solution.py:62
  (407 shorter events, 342.8 us)
Async XLA Ops:
  6.3 33.4 %collective-permute-start.14 = (bf16[128,2048]{1,0:T(8,128)(2,1)}, bf16[128,2048]{1,0:T(8,128)(2,1)}, u32[]{:S(2)}, u32[]{:S(2)}) collective-permute-start(bf16[128,2048]{1,0:T(8,128)(2,1)} %convert_element_type.450), channel_id=1, source_target_pairs={{8,0},{16,8},{24,16},{9,1},{17,9},{25,17},{10,2},{18,10},{26,18},{... | collective-permute-start | bytes 1572872 | tf_op jit(solution)/shard_map/ppermute | solution.py:43
  9.4 36.5 %collective-permute-start.22 = (s32[256,8]{0,1:T(8,128)}, s32[256,8]{0,1:T(8,128)S(1)}, u32[]{:S(2)}, u32[]{:S(2)}) collective-permute-start(s32[256,8]{0,1:T(8,128)} %bitcast.456), channel_id=1, source_target_pairs={{0,8},{8,16},{16,24},{1,9},{9,17},{17,25},{2,10},{10,18},{18,26},{... | collective-permute-start | bytes 24584 | tf_op jit(solution)/shard_map/ppermute | solution.py:42
  12.1 42.5 %collective-permute-start.25 = (s32[256,8]{0,1:T(8,128)}, s32[256,8]{0,1:T(8,128)S(1)}, u32[]{:S(2)}, u32[]{:S(2)}) collective-permute-start(s32[256,8]{0,1:T(8,128)} %bitcast.457), channel_id=1, source_target_pairs={{8,0},{16,8},{24,16},{9,1},{17,9},{25,17},{10,2},{18,10},{26,18},{... | collective-permute-start | bytes 24584 | tf_op jit(solution)/shard_map/ppermute | solution.py:43
  54.7 76.4 %collective-permute-start = (bf16[256,2048]{1,0:T(8,128)(2,1)S(1)}, bf16[256,2048]{1,0:T(8,128)(2,1)}, u32[]{:S(2)}, u32[]{:S(2)}) collective-permute-start(bf16[256,2048]{1,0:T(8,128)(2,1)S(1)} %bitcast.420), channel_id=1, source_target_pairs={{0,2},{2,0},{4,6},{6,4},{1,3},{3,1},{5,7},{7,5},{8,10},{10,8},{12,... | collective-permute-start | bytes 3145736 | tf_op jit(solution)/shard_map/ppermute | solution.py:71
  57.3 31.3 %collective-permute-start.7 = (bf16[4,64,1408]{2,1,0:T(8,128)(2,1)S(1)}, bf16[4,64,1408]{2,1,0:T(8,128)(2,1)}, u32[]{:S(2)}, u32[]{:S(2)}) collective-permute-start(bf16[4,64,1408]{2,1,0:T(8,128)(2,1)S(1)} %all-to-all-done), channel_id=1, source_target_pairs={{8,0},{16,8},{24,16},{9,1},{17,9},{25,17},{10,2},{18,10},{26,18},{... | collective-permute-start | bytes 2162696 | tf_op jit(solution)/shard_map/ppermute | solution.py:43
  59.2 30.6 %collective-permute-start.16 = (bf16[128,2048]{1,0:T(8,128)(2,1)}, bf16[128,2048]{1,0:T(8,128)(2,1)S(1)}, u32[]{:S(2)}, u32[]{:S(2)}) collective-permute-start(bf16[128,2048]{1,0:T(8,128)(2,1)} %collective-permute-done.15), channel_id=1, source_target_pairs={{8,0},{9,1},{10,2},{11,3},{12,4},{13,5},{14,6},{15,7}} | collective-permute-start | bytes 1572872 | tf_op jit(solution)/shard_map/ppermute | solution.py:43
  60.5 31.2 %collective-permute-start.5 = (bf16[4,64,1408]{2,1,0:T(8,128)(2,1)}, bf16[4,64,1408]{2,1,0:T(8,128)(2,1)}, u32[]{:S(2)}, u32[]{:S(2)}) collective-permute-start(bf16[4,64,1408]{2,1,0:T(8,128)(2,1)} %collective-permute-done.4), channel_id=1, source_target_pairs={{8,16},{16,24},{9,17},{17,25},{10,18},{18,26},{11,19},{19,27},{12,... | collective-permute-start | bytes 2162696 | tf_op jit(solution)/shard_map/ppermute | solution.py:42
  84.6 48.2 %collective-permute-start.1 = (bf16[256,2048]{1,0:T(8,128)(2,1)S(1)}, bf16[256,2048]{1,0:T(8,128)(2,1)}, u32[]{:S(2)}, u32[]{:S(2)}) collective-permute-start(bf16[256,2048]{1,0:T(8,128)(2,1)S(1)} %bitcast.421), channel_id=1, source_target_pairs={{0,4},{2,6},{4,0},{6,2},{1,5},{3,7},{5,1},{7,3},{8,12},{10,14},{12... | collective-permute-start | bytes 3145736 | tf_op jit(solution)/shard_map/ppermute | solution.py:71
  88.5 117.7 %collective-permute-start.27 = (s32[256,8]{0,1:T(8,128)S(1)}, s32[256,8]{0,1:T(8,128)S(1)}, u32[]{:S(2)}, u32[]{:S(2)}) collective-permute-start(s32[256,8]{0,1:T(8,128)S(1)} %collective-permute-done.26), channel_id=1, source_target_pairs={{8,0},{9,1},{10,2},{11,3},{12,4},{13,5},{14,6},{15,7}} | collective-permute-start | bytes 24584 | tf_op jit(solution)/shard_map/ppermute | solution.py:43
  94.8 33.6 %all-to-all-start.1 = ((bf16[4,128,2048]{2,1,0:T(8,128)(2,1)}), bf16[4,128,2048]{2,1,0:T(8,128)(2,1)S(1)}, u32[]{:S(2)}, u32[]{:S(2)}) async-start(bf16[4,128,2048]{2,1,0:T(8,128)(2,1)} %constant_dynamic-slice_fusion.5), calls=%async_computation.1 | async-start | bytes 4194304 | tf_op jit(solution)/shard_map/all_to_all | solution.py:124
  805.3 157.1 %all-to-all-start.2 = ((bf16[8,288,2048]{2,1,0:T(8,128)(2,1)}), bf16[8,288,2048]{2,1,0:T(8,128)(2,1)}, u32[]{:S(2)}, u32[]{:S(2)}) async-start(bf16[8,288,2048]{2,1,0:T(8,128)(2,1)} %get-tuple-element.34), calls=%async_computation.2 | async-start | bytes 18874368 | tf_op jit(solution)/shard_map/all_to_all | solution.py:124
  829.5 86.2 %collective-permute-start.45 = (f32[2,4,1536]{2,1,0:T(4,128)S(1)}, f32[2,4,1536]{2,1,0:T(4,128)S(1)}, u32[]{:S(2)}, u32[]{:S(2)}) collective-permute-start(f32[2,4,1536]{2,1,0:T(4,128)S(1)} %pad_maximum_fusion.11), channel_id=1, source_target_pairs={{0,4},{2,6},{4,0},{6,2},{1,5},{3,7},{5,1},{7,3},{8,12},{10,14},{12... | collective-permute-start | bytes 147464 | tf_op jit(solution)/shard_map/ppermute | solution.py:71
  830.3 128.1 %collective-permute-start.60 = (bf16[4,128,2048]{2,1,0:T(8,128)(2,1)S(1)}, bf16[4,128,2048]{2,1,0:T(8,128)(2,1)S(1)}, u32[]{:S(2)}, u32[]{:S(2)}) collective-permute-start(bf16[4,128,2048]{2,1,0:T(8,128)(2,1)S(1)} %select_bitcast_fusion.2), channel_id=1, source_target_pairs={{0,1},{1,0},{2,3},{3,2},{4,5},{5,4},{6,7},{7,6},{8,9},{9,8},{10,11... | collective-permute-start | bytes 6291464 | tf_op jit(solution)/shard_map/ppermute | solution.py:71
  951.6 89.2 %collective-permute-start.49 = (f32[3072]{0:T(1024)S(1)}, f32[3072]{0:T(1024)S(1)}, u32[]{:S(2)}, u32[]{:S(2)}) collective-permute-start(f32[3072]{0:T(1024)S(1)} %add.366), channel_id=1, source_target_pairs={{0,8},{8,16},{16,24},{1,9},{9,17},{17,25},{2,10},{10,18},{18,26},{... | collective-permute-start | bytes 36872 | tf_op jit(solution)/shard_map/ppermute | solution.py:61
  956.4 85.2 %collective-permute-start.52 = (f32[3072]{0:T(1024)S(1)}, f32[3072]{0:T(1024)S(1)}, u32[]{:S(2)}, u32[]{:S(2)}) collective-permute-start(f32[3072]{0:T(1024)S(1)} %add.369), channel_id=1, source_target_pairs={{8,0},{16,8},{24,16},{9,1},{17,9},{25,17},{10,2},{18,10},{26,18},{... | collective-permute-start | bytes 36872 | tf_op jit(solution)/shard_map/ppermute | solution.py:62
  960.9 38.2 %collective-permute-start.57 = (bf16[4,64,1280]{2,1,0:T(8,128)(2,1)}, bf16[4,64,1280]{2,1,0:T(8,128)(2,1)}, u32[]{:S(2)}, u32[]{:S(2)}) collective-permute-start(bf16[4,64,1280]{2,1,0:T(8,128)(2,1)} %get-tuple-element.109), channel_id=1, source_target_pairs={{24,16},{25,17},{26,18},{27,19},{28,20},{29,21},{30,22},{31,23}} | collective-permute-start | bytes 1966088 | tf_op jit(solution)/shard_map/ppermute | solution.py:62
  962.5 35.4 %all-to-all-start.4 = ((bf16[4,128,2048]{2,1,0:T(8,128)(2,1)}), bf16[4,128,2048]{2,1,0:T(8,128)(2,1)}, u32[]{:S(2)}, u32[]{:S(2)}) async-start(bf16[4,128,2048]{2,1,0:T(8,128)(2,1)} %fusion.2), calls=%async_computation.4 | async-start | bytes 4194304 | tf_op jit(solution)/shard_map/all_to_all | solution.py:124
  996.6 37.8 %collective-permute-start.28 = (bf16[256,2048]{1,0:T(8,128)(2,1)}, bf16[256,2048]{1,0:T(8,128)(2,1)}, u32[]{:S(2)}, u32[]{:S(2)}) collective-permute-start(bf16[256,2048]{1,0:T(8,128)(2,1)} %get-tuple-element.98), channel_id=1, source_target_pairs={{0,8},{1,9},{2,10},{3,11},{4,12},{5,13},{6,14},{7,15}} | collective-permute-start | bytes 3145736 | tf_op jit(solution)/shard_map/ppermute | solution.py:61
  999.2 32.8 %collective-permute-start.61 = (bf16[128,2048]{1,0:T(8,128)(2,1)S(1)}, bf16[128,2048]{1,0:T(8,128)(2,1)S(1)}, u32[]{:S(2)}, u32[]{:S(2)}) collective-permute-start(bf16[128,2048]{1,0:T(8,128)(2,1)S(1)} %get-tuple-element.112), channel_id=1, source_target_pairs={{0,8},{1,9},{2,10},{3,11},{4,12},{5,13},{6,14},{7,15}} | collective-permute-start | bytes 1572872 | tf_op jit(solution)/shard_map/ppermute | solution.py:61
  1000.5 48.1 %collective-permute-start.64 = (bf16[128,2048]{1,0:T(8,128)(2,1)S(1)}, bf16[128,2048]{1,0:T(8,128)(2,1)S(1)}, u32[]{:S(2)}, u32[]{:S(2)}) collective-permute-start(bf16[128,2048]{1,0:T(8,128)(2,1)S(1)} %get-tuple-element.113), channel_id=1, source_target_pairs={{24,16},{25,17},{26,18},{27,19},{28,20},{29,21},{30,22},{31,23}} | collective-permute-start | bytes 1572872 | tf_op jit(solution)/shard_map/ppermute | solution.py:62
  1041.6 32.2 %collective-permute-start.29 = (bf16[256,2048]{1,0:T(8,128)(2,1)S(1)}, bf16[256,2048]{1,0:T(8,128)(2,1)S(1)}, u32[]{:S(2)}, u32[]{:S(2)}) collective-permute-start(bf16[256,2048]{1,0:T(8,128)(2,1)S(1)} %fusion.17), channel_id=1, source_target_pairs={{0,8},{8,16},{1,9},{9,17},{2,10},{10,18},{3,11},{11,19},{4,12},{12... | collective-permute-start | bytes 3145736 | tf_op jit(solution)/shard_map/ppermute | solution.py:61
  1046.5 41.4 %collective-permute-start.56 = (bf16[4,64,1280]{2,1,0:T(8,128)(2,1)S(1)}, bf16[4,64,1280]{2,1,0:T(8,128)(2,1)S(1)}, u32[]{:S(2)}, u32[]{:S(2)}) collective-permute-start(bf16[4,64,1280]{2,1,0:T(8,128)(2,1)S(1)} %get-tuple-element.106), channel_id=1, source_target_pairs={{0,8},{8,16},{16,24},{1,9},{9,17},{17,25},{2,10},{10,18},{18,26},{... | collective-permute-start | bytes 1966088 | tf_op jit(solution)/shard_map/ppermute | solution.py:61
  1048.6 39.2 %collective-permute-start.59 = (bf16[4,64,1280]{2,1,0:T(8,128)(2,1)S(1)}, bf16[4,64,1280]{2,1,0:T(8,128)(2,1)S(1)}, u32[]{:S(2)}, u32[]{:S(2)}) collective-permute-start(bf16[4,64,1280]{2,1,0:T(8,128)(2,1)S(1)} %fusion.23), channel_id=1, source_target_pairs={{8,0},{16,8},{24,16},{9,1},{17,9},{25,17},{10,2},{18,10},{26,18},{... | collective-permute-start | bytes 1966088 | tf_op jit(solution)/shard_map/ppermute | solution.py:62
  1077.8 37.3 %collective-permute-start.63 = (bf16[128,2048]{1,0:T(8,128)(2,1)}, bf16[128,2048]{1,0:T(8,128)(2,1)}, u32[]{:S(2)}, u32[]{:S(2)}) collective-permute-start(bf16[128,2048]{1,0:T(8,128)(2,1)} %get-tuple-element.110), channel_id=1, source_target_pairs={{0,8},{8,16},{16,24},{1,9},{9,17},{17,25},{2,10},{10,18},{18,26},{... | collective-permute-start | bytes 1572872 | tf_op jit(solution)/shard_map/ppermute | solution.py:61
  (94 other events, 1982.2 us)

commit v3 on v2

--- a/solution.py
+++ b/solution.py
@@ -12,7 +12,7 @@
 masked_score = -1e30
 ALL = ("dp", "ctx", "exp")
 PLANE = ("ctx", "exp")
-VMEM = 56 << 20
+VMEM = 60 << 20
 MESH = pl.DeviceIdType.MESH
 
 
@@ -24,102 +24,6 @@
     return (jnp.cos(angles), jnp.sin(angles))
 
 
-def norm_back(grad, normed, inverse, gain):
-    gain_grad = jnp.sum(grad * normed, axis=0)
-    scaled = grad * gain
-    return (
-        inverse * (scaled - normed * jnp.mean(scaled * normed, axis=-1, keepdims=True)),
-        gain_grad,
-    )
-
-
-def line_gather(block, axis):
-    n = lax.axis_size(axis)
-    me = lax.axis_index(axis)
-    before, after = [], []
-    up = down = block
-    for step in range(1, n):
-        up = lax.ppermute(up, axis, [(i, i + 1) for i in range(step - 1, n - 1)])
-        down = lax.ppermute(down, axis, [(i, i - 1) for i in range(1, n - step + 1)])
-        before.insert(0, up)
-        after.append(down)
-    return lax.dynamic_slice_in_dim(jnp.stack(before + [block] + after), n - 1 - me, n, 0)
-
-
-def line_scatter(parts, axis):
-    n = lax.axis_size(axis)
-    me = lax.axis_index(axis)
-
-    def part(i):
-        return lax.dynamic_index_in_dim(parts, jnp.clip(i, 0, n - 1), 0, keepdims=False)
-
-    up = down = None
-    for step in range(1, n):
-        send_up, send_down = part(me + n - step), part(me - n + step)
-        if up is not None:
-            send_up, send_down = add_low(send_up, up), add_low(send_down, down)
-        up = lax.ppermute(send_up, axis, [(i, i + 1) for i in range(step)])
-        down = lax.ppermute(send_down, axis, [(i, i - 1) for i in range(n - step, n)])
-    return part(me).astype(jnp.float32) + up.astype(jnp.float32) + down.astype(jnp.float32)
-
-
-def add_low(left, right):
-    return (left.astype(jnp.float32) + right.astype(jnp.float32)).astype(left.dtype)
-
-
-def flip(block, axis, bit):
-    return lax.ppermute(block, axis, [(i, i ^ bit) for i in range(lax.axis_size(axis))])
-
-
-def square_gather(block, axis):
-    if lax.axis_size(axis) != 4:
-        return lax.all_gather(block, axis, axis=0, tiled=False)
-    half = block.shape[-1] // 2
-    me = lax.axis_index(axis)
-    by_x, by_y = flip(block, axis, 1), flip(block, axis, 2)
-    far = jnp.concatenate(
-        [flip(by_x[..., :half], axis, 2), flip(by_y[..., half:], axis, 1)], axis=-1
-    )
-    whole = jnp.zeros((4,) + block.shape, block.dtype)
-    for bits, piece in enumerate((block, by_x, by_y, far)):
-        whole = lax.dynamic_update_index_in_dim(whole, piece, me ^ bits, 0)
-    return whole
-
-
-def square_scatter(parts, axis):
-    if lax.axis_size(axis) != 4:
-        return lax.psum_scatter(parts, axis, scatter_dimension=0, tiled=False).astype(jnp.float32)
-    half = parts.shape[-1] // 2
-    me = lax.axis_index(axis)
-    own, to_x, to_y, far = [
-        lax.dynamic_index_in_dim(parts, me ^ bits, 0, keepdims=False) for bits in range(4)
-    ]
-    first = flip(jnp.stack([to_x[..., :half], far[..., :half]]), axis, 1)
-    second = flip(jnp.stack([to_y[..., half:], far[..., half:]]), axis, 2)
-    later_first = flip(add_low(to_y[..., :half], first[1]), axis, 2)
-    later_second = flip(add_low(to_x[..., half:], second[1]), axis, 1)
-    own = own.astype(jnp.float32)
-    first = own[..., :half] + first[0].astype(jnp.float32) + later_first.astype(jnp.float32)
-    second = own[..., half:] + second[0].astype(jnp.float32) + later_second.astype(jnp.float32)
-    return jnp.concatenate([first, second], axis=-1)
-
-
-def pair_gather(block, axis):
-    if lax.axis_size(axis) != 2:
-        return lax.all_gather(block, axis, axis=0, tiled=False)
-    other = flip(block, axis, 1)
-    first = lax.axis_index(axis) == 0
-    return jnp.stack([jnp.where(first, block, other), jnp.where(first, other, block)])
-
-
-def pair_scatter(parts, axis):
-    if lax.axis_size(axis) != 2:
-        return lax.psum_scatter(parts, axis, scatter_dimension=0, tiled=False)
-    first = lax.axis_index(axis) == 0
-    other = flip(jnp.where(first, parts[1], parts[0]), axis, 1)
-    return add_low(jnp.where(first, parts[0], parts[1]), other)
-
-
 def swap(parts, axis):
     return lax.all_to_all(parts, axis, split_axis=0, concat_axis=0, tiled=True)
 
@@ -129,7 +33,9 @@
     inverse = lax.rsqrt(jnp.mean(x * x, axis=-1, keepdims=True) + eps_norm)
     hidden = ((x * inverse) * gain_ref[...]).astype(jnp.bfloat16)
     hidden_ref[...] = hidden
-    raw = jnp.dot(hidden, weight_ref[...], preferred_element_type=jnp.float32)
+    raw = jnp.dot(
+        hidden, weight_ref[:, : raw_ref.shape[1]], preferred_element_type=jnp.float32
+    )
     raw_ref[...] = raw
     width = cos_ref.shape[1]
     cosine, sine = cos_ref[...], sin_ref[...]
@@ -145,9 +51,8 @@
     out_ref[:, rest] = raw[:, rest].astype(jnp.bfloat16)
 
 
-def project(x, gain, weight, scales, cosine, sine, q_heads, kv_heads, block):
+def project(x, gain, weight, columns, scales, cosine, sine, q_heads, kv_heads, block):
     rows, width = x.shape
-    columns = weight.shape[1]
     head = cosine.shape[1]
     whole = lambda shape: pl.BlockSpec(shape, lambda i: (0, 0))
     return pl.pallas_call(
@@ -156,7 +61,7 @@
         in_specs=[
             pl.BlockSpec((block, width), lambda i: (i, 0)),
             whole((1, width)),
-            whole((width, columns)),
+            whole(weight.shape),
             whole((2, head)),
             pl.BlockSpec((block, head), lambda i: (i, 0)),
             pl.BlockSpec((block, head), lambda i: (i, 0)),
@@ -231,10 +136,12 @@
 
 def attend_back_kernel(
     bounds_ref, query_ref, key_ref, value_ref, grad_ref, raw_ref, scale_ref, cos_ref, sin_ref,
-    out_ref, gain_ref, key_sum, value_sum, *, block, heads, group, score_scale,
+    back_ref, out_ref, gain_ref, back_out, key_sum, value_sum, *back_scratch, block, heads, group,
+    score_scale, sizes,
 ):
     step = pl.program_id(0)
     rows = query_ref.shape[0]
+    scatter_back(step, heads + 2 * heads // group, back_ref, back_out, back_scratch, sizes)
     low, full = jnp.bfloat16, jnp.float32
     kv_heads = heads // group
 
@@ -304,7 +211,122 @@
         out_ref[...] = value_sum[step - heads - kv_heads].astype(low)
 
 
-def attend_back(bounds, turned, grad, raw, scales, cosine, sine, heads, kv_heads, head, block):
+def scatter_back(step, steps, back_ref, back_out, scratch, sizes):
+    (
+        pairs, total, arrived, leaving, landing, own_sem, pair_send, pair_recv, across_send,
+        across_recv, line_send, line_recv,
+    ) = scratch
+    n, n_ctx, n_exp = sizes["dp"], sizes["ctx"], sizes["exp"]
+    z, c, k = (lax.axis_index(a) for a in ALL)
+    full, low = jnp.float32, jnp.bfloat16
+
+    def remote(source, target, send, recv, device):
+        return pltpu.make_async_remote_copy(
+            src_ref=source, dst_ref=target, send_sem=send, recv_sem=recv, device_id=device,
+            device_id_type=MESH,
+        )
+
+    def pair(ahead):
+        target = lax.rem(k + ahead, n_exp)
+        return remote(
+            back_ref.at[:, target], pairs.at[ahead], pair_send.at[ahead], pair_recv.at[ahead],
+            {"exp": target},
+        )
+
+    def across(ahead):
+        target = lax.rem(c + ahead, n_ctx)
+        return remote(
+            total.at[target], arrived.at[c], across_send.at[ahead], across_recv.at[ahead],
+            {"ctx": target},
+        )
+
+    def line(target, way):
+        return remote(
+            leaving.at[target], landing.at[target + (way + 1) // 2], line_send.at[target],
+            line_recv.at[target + (way + 1) // 2], {"dp": z + way},
+        )
+
+    def in_line(index):
+        return (index >= 0) & (index < n)
+
+    own = pltpu.make_async_copy(back_ref.at[:, k], pairs.at[0], own_sem.at[0])
+
+    @pl.when(step == 0)
+    def _():
+        greet(sizes)
+        own.start()
+        for ahead in range(1, n_exp):
+            pair(ahead).start()
+
+    @pl.when(step == 1)
+    def _():
+        own.wait()
+        for ahead in range(1, n_exp):
+            pair(ahead).wait_recv()
+        for group in range(n_ctx):
+            summed = pairs[0, group].astype(full)
+            for ahead in range(1, n_exp):
+                summed = summed + pairs[ahead, group].astype(full)
+            total[group] = summed.astype(low)
+        for ahead in range(1, n_ctx):
+            across(ahead).start()
+        arrived[c] = total[c]
+
+    for distance in range(n - 1, 0, -1):
+        @pl.when(step == min(2 + 3 * (n - 1 - distance), steps - 2))
+        def _():
+            if distance == n - 1:
+                for ahead in range(1, n_ctx):
+                    across(ahead).wait_recv()
+            for way in (-1, 1):
+                target = z + way * distance
+
+                @pl.when(in_line(target))
+                def _():
+                    @pl.when(in_line(z - way))
+                    def _():
+                        line(target, way).wait_recv()
+                        leaving[target] = (
+                            arrived[target].astype(full)
+                            + landing[target + (way + 1) // 2].astype(full)
+                        ).astype(low)
+
+                    @pl.when(jnp.logical_not(in_line(z - way)))
+                    def _():
+                        leaving[target] = arrived[target]
+
+                    line(target, way).start()
+
+    @pl.when(step == steps - 1)
+    def _():
+        back_out[...] = arrived[z].astype(full)
+        for way in (-1, 1):
+            @pl.when(in_line(z - way))
+            def _():
+                line(z, way).wait_recv()
+                back_out[...] += landing[z + (way + 1) // 2].astype(full)
+
+        for ahead in range(1, n_exp):
+            pair(ahead).wait_send()
+        for ahead in range(1, n_ctx):
+            across(ahead).wait_send()
+        for distance in range(1, n):
+            for way in (-1, 1):
+                target = z + way * distance
+
+                @pl.when(in_line(target))
+                def _():
+                    line(target, way).wait_send()
+
+
+def attend_back(
+    bounds, turned, grad, raw, scales, cosine, sine, back, heads, kv_heads, head, block, sizes,
+    collective,
+):
+    n, n_ctx, n_exp = sizes["dp"], sizes["ctx"], sizes["exp"]
+    b_rows, b_width = back.shape[2:]
+    piece = lambda *lead: pltpu.VMEM(lead + (b_rows, b_width), jnp.bfloat16)
+    dma = lambda *shape: pltpu.SemaphoreType.DMA(shape)
     rows = turned.shape[0]
     group = heads // kv_heads
     columns = turned.shape[1]
@@ -312,7 +334,8 @@
     tables = pl.BlockSpec((rows, head), lambda h: (0, 0))
     return pl.pallas_call(
         functools.partial(
-            attend_back_kernel, block=block, heads=heads, group=group, score_scale=head ** (-0.5)
+            attend_back_kernel, block=block, heads=heads, group=group, score_scale=head ** (-0.5),
+            sizes=sizes,
         ),
         grid=(heads + 2 * kv_heads,),
         in_specs=[
@@ -325,23 +348,149 @@
             pl.BlockSpec((2, head), lambda h: (0, 0)),
             tables,
             tables,
+            pl.BlockSpec(memory_space=pl.ANY),
         ],
         out_specs=[
             pl.BlockSpec((rows, head), lambda h: (0, h)),
             pl.BlockSpec((2, head), lambda h: (0, 0)),
+            pl.BlockSpec((b_rows, b_width), lambda h: (0, 0)),
         ],
         out_shape=[
             jax.ShapeDtypeStruct((rows, columns), jnp.bfloat16),
             jax.ShapeDtypeStruct((2, head), jnp.float32),
-        ],
-        scratch_shapes=[pltpu.VMEM((kv_heads, rows, head), jnp.float32)] * 2,
-        compiler_params=pltpu.CompilerParams(vmem_limit_bytes=VMEM),
+            jax.ShapeDtypeStruct((b_rows, b_width), jnp.float32),
+        ],
+        scratch_shapes=[pltpu.VMEM((kv_heads, rows, head), jnp.float32)] * 2
+        + [piece(n_exp, n_ctx), piece(n_ctx), piece(n_ctx), piece(n), piece(n + 1)]
+        + [dma(1), dma(n_exp), dma(n_exp), dma(n_ctx), dma(n_ctx), dma(n), dma(n + 1)],
+        compiler_params=pltpu.CompilerParams(
+            collective_id=collective, has_side_effects=True, vmem_limit_bytes=VMEM
+        ),
         cost_estimate=pl.CostEstimate(
             flops=5 * heads * rows * rows * head,
             bytes_accessed=12 << 20,
             transcendentals=heads * rows * rows // 2,
         ),
-    )(bounds, turned, turned, turned, grad, raw, scales, cosine, sine)
+    )(bounds, turned, turned, turned, grad, raw, scales, cosine, sine, back)
+
+
+def square(sizes):
+    me = lax.axis_index("ctx")
+    return me + 1 - 2 * lax.rem(me, 2), lax.rem(me + 2, 4)
+
+
+def remote(source, target, send, recv, device):
+    return pltpu.make_async_remote_copy(
+        src_ref=source, dst_ref=target, send_sem=send, recv_sem=recv, device_id=device,
+        device_id_type=MESH,
+    )
+
+
+class SquareGather:
+    def __init__(self, sizes, block, whole, send, recv, own_sem):
+        self.block, self.whole, self.send, self.recv = block, whole, send, recv
+        self.me = lax.axis_index("ctx")
+        self.by = square(sizes)
+        self.half = block.shape[1] // 2
+        self.own = pltpu.make_async_copy(block, whole.at[self.me], own_sem)
+
+    def copy(self, place, part, side, number):
+        columns = pl.ds(part * self.half, self.half)
+        target = self.whole.at[place, :, columns]
+        source = self.block.at[:, columns] if number < 4 else target
+        return remote(
+            source, target, self.send.at[number], self.recv.at[number], {"ctx": self.by[side]}
+        )
+
+    def first(self, number):
+        part, side = ((0, 0), (1, 1), (1, 0), (0, 1))[number]
+        return self.copy(self.me, part, side, number)
+
+    def start(self):
+        self.own.start()
+        for number in range(4):
+            self.first(number).start()
+
+    def pass_on(self):
+        for part in (0, 1):
+            self.first(part).wait_recv()
+            self.copy(self.by[part], part, 1 - part, 4 + part).start()
+
+    def finish(self):
+        for number in (2, 3):
+            self.first(number).wait_recv()
+        for part in (0, 1):
+            last = self.copy(self.by[part], part, 1 - part, 4 + part)
+            last.wait_recv()
+            last.wait_send()
+        for number in range(4):
+            self.first(number).wait_send()
+        self.own.wait()
+
+
+class SquareScatter:
+    def __init__(self, sizes, parts, far_in, turn_out, turn_in, send, recv):
+        self.parts, self.far_in, self.turn_out, self.turn_in = parts, far_in, turn_out, turn_in
+        self.send, self.recv = send, recv
+        self.me = lax.axis_index("ctx")
+        self.by = square(sizes)
+        self.far = sizes["ctx"] - 1 - self.me
+        half = parts.shape[2] // 2
+        self.columns = (pl.ds(0, half), pl.ds(half, half))
+
+    def first(self, side, number):
+        place = self.by[side] if number == 0 else self.far
+        index = 2 * side + number
+        return remote(
+            self.parts.at[place, :, self.columns[side]], self.far_in.at[side, number],
+            self.send.at[index], self.recv.at[index], {"ctx": self.by[side]},
+        )
+
+    def second(self, side):
+        return remote(
+            self.turn_out.at[side], self.turn_in.at[side], self.send.at[4 + side],
+            self.recv.at[4 + side], {"ctx": self.by[1 - side]},
+        )
+
+    def start(self, number):
+        for side in (0, 1):
+            self.first(side, number).start()
+
+    def turn(self):
+        for side in (0, 1):
+            self.first(side, 1).wait_recv()
+            own = self.parts[self.by[1 - side], :, self.columns[side]].astype(jnp.float32)
+            self.turn_out[side] = (own + self.far_in[side, 1].astype(jnp.float32)).astype(
+                jnp.bfloat16
+            )
+            self.second(side).start()
+
+    def finish(self, total):
+        for side in (0, 1):
+            self.first(side, 0).wait_recv()
+            self.second(side).wait_recv()
+            total[:, self.columns[side]] = (
+                self.parts[self.me, :, self.columns[side]].astype(jnp.float32)
+                + self.far_in[side, 0].astype(jnp.float32)
+                + self.turn_in[side].astype(jnp.float32)
+            )
+
+    def close(self):
+        for side in (0, 1):
+            for number in (0, 1):
+                self.first(side, number).wait_send()
+            self.second(side).wait_send()
+
+
+def square_scratch(rows, width):
+    half = width // 2
+    return [
+        pltpu.VMEM((2, 2, rows, half), jnp.bfloat16),
+        pltpu.VMEM((2, rows, half), jnp.bfloat16),
+        pltpu.VMEM((2, rows, half), jnp.bfloat16),
+        pltpu.SemaphoreType.DMA((6,)),
+        pltpu.SemaphoreType.DMA((6,)),
+    ]
 
 
 def greet(sizes):
@@ -384,30 +533,32 @@
     return pieces
 
 
-def dispatch_kernel(*refs, sizes, pieces, arrays):
-    blocks, pick_ref, outs = refs[:arrays], refs[arrays], refs[arrays + 1 : 2 * arrays + 1]
-    columns, packed = refs[2 * arrays + 1 : 3 * arrays + 1], refs[3 * arrays + 1 : 4 * arrays + 1]
-    line_send, line_recv, plane_send, plane_recv, own_sem = refs[4 * arrays + 1 :]
-    n, number = sizes["dp"], sizes["ctx"] * sizes["exp"]
+def dispatch_kernel(
+    attended_ref, back_ref, token_ref, gain_ref, router_ref, chosen_ref, cot_ref, pick_ref,
+    grads_out, mixed_out, parts_out, middle_ref, gates_ref,
+    branch, far_in, turn_out, turn_in, sq_send, sq_recv, mixed, *refs, sizes, pieces, experts,
+):
+    outs, refs = (grads_out, mixed_out, parts_out), refs
+    columns, packed = refs[:3], refs[3:6]
+    line_send, line_recv, plane_send, plane_recv, own_sem = refs[6:]
+    n, n_ctx, number = sizes["dp"], sizes["ctx"], sizes["ctx"] * sizes["exp"]
     me, here = lax.axis_index("dp"), plane_index(sizes)
-    tokens = blocks[0].shape[0]
+    tokens, width = token_ref.shape
     groups, dests, rows, span = pick_ref.shape
+    full, low = jnp.float32, jnp.bfloat16
     greet(sizes)
 
     def line_copy(f, origin, step):
         a, first, part = pieces[f]
-        return pltpu.make_async_remote_copy(
-            src_ref=columns[a].at[origin, :, pl.ds(first, part)],
-            dst_ref=columns[a].at[origin, :, pl.ds(first, part)],
-            send_sem=line_send.at[f, origin, (step + 1) // 2],
-            recv_sem=line_recv.at[f, origin],
-            device_id={"dp": me + step},
-            device_id_type=MESH,
+        return remote(
+            columns[a].at[origin, :, pl.ds(first, part)],
+            columns[a].at[origin, :, pl.ds(first, part)],
+            line_send.at[f, origin, (step + 1) // 2],
+            line_recv.at[f, origin],
+            {"dp": me + step},
         )
 
     def send_own(f):
-        a, first, part = pieces[f]
-        columns[a][me, :, pl.ds(first, part)] = blocks[a][:, pl.ds(first, part)]
         for step in (-1, 1):
             @pl.when((me + step >= 0) & (me + step < n))
             def _():
@@ -416,13 +567,12 @@
     def plane_copy(f, ahead):
         a, first, part = pieces[f]
         target = peer(sizes, ahead)
-        return pltpu.make_async_remote_copy(
-            src_ref=packed[a].at[target, :, pl.ds(first, part)],
-            dst_ref=outs[a].at[here, :, pl.ds(first, part)],
-            send_sem=plane_send.at[f, ahead],
-            recv_sem=plane_recv.at[f, ahead],
-            device_id=place(sizes, target),
-            device_id_type=MESH,
+        return remote(
+            packed[a].at[target, :, pl.ds(first, part)],
+            outs[a].at[here, :, pl.ds(first, part)],
+            plane_send.at[f, ahead],
+            plane_recv.at[f, ahead],
+            place(sizes, target),
         )
 
     def own_copy(f):
@@ -433,8 +583,8 @@
             own_sem.at[f],
         )
 
-    send_own(0)
-    for f, (a, first, part) in enumerate(pieces):
+    def spread(f):
+        a, first, part = pieces[f]
         for distance in range(1, n):
             for step in (-1, 1):
                 origin = me - step * distance
@@ -457,13 +607,66 @@
             @pl.loop(0, dests)
             def _(j):
                 packed[a][j, pl.ds(g * rows, rows), pl.ds(first, part)] = jnp.dot(
-                    pick_ref[g, j], given, preferred_element_type=jnp.float32
-                ).astype(jnp.bfloat16)
-
+                    pick_ref[g, j], given, preferred_element_type=full
+                ).astype(low)
+
+    def push(f):
         for ahead in range(number - 1, 0, -1):
             plane_copy(f, ahead).start()
         own_copy(f).start()
 
+    columns[0][me] = cot_ref[...]
+    send_own(0)
+
+    scatter = SquareScatter(sizes, branch, far_in, turn_out, turn_in, sq_send, sq_recv)
+
+    def project_block(place):
+        branch[place] = jnp.dot(
+            attended_ref[pl.ds(place * tokens, tokens), :], back_ref[...],
+            preferred_element_type=full,
+        ).astype(low)
+
+    project_block(scatter.far)
+    scatter.start(1)
+    for near in scatter.by:
+        project_block(near)
+    scatter.start(0)
+    project_block(scatter.me)
+    spread(0)
+    scatter.turn()
+    push(0)
+    scatter.finish(middle_ref)
+    middle_ref[...] += token_ref[...].astype(full)
+    middle = middle_ref[...]
+    inverse = lax.rsqrt(jnp.mean(middle * middle, axis=-1, keepdims=True) + eps_norm)
+    mixed[...] = ((middle * inverse) * gain_ref[...]).astype(low)
+    columns[1][me] = mixed[...]
+    logits = jnp.dot(mixed[...], router_ref[...], preferred_element_type=full)
+    chosen = chosen_ref[...] > 0
+    logits = jnp.where(chosen, logits, masked_score)
+    gates = jnp.exp(logits - jnp.max(logits, axis=-1, keepdims=True))
+    gates = jnp.where(chosen, gates, 0.0)
+    gates = gates / jnp.sum(gates, axis=-1, keepdims=True)
+    gates_ref[...] = gates
+    first_part = gates.astype(low).astype(full)
+    second_part = (gates - first_part).astype(low).astype(full)
+    third_part = gates - first_part - second_part
+    lanes = gates.shape[1]
+    if experts == lanes:
+        terms = jnp.concatenate([first_part, second_part, third_part], axis=1)
+    else:
+        terms = (
+            first_part
+            + pltpu.roll(second_part, experts, 1)
+            + pltpu.roll(third_part, 2 * experts, 1)
+        )
+    columns[2][me] = terms.astype(low)
+
+    for f in range(1, len(pieces)):
+        spread(f)
+        push(f)
+
+    scatter.close()
     for f in range(len(pieces)):
         for distance in range(n):
             for step in (-1, 1):
@@ -479,22 +682,32 @@
         own_copy(f).wait()
 
 
-def dispatch(blocks, pick, sizes, collective, part=512):
-    tokens = blocks[0].shape[0]
-    widths = [block.shape[1] for block in blocks]
-    n, number = sizes["dp"], sizes["ctx"] * sizes["exp"]
+def dispatch(attended, back, tokens, gain, router, chosen, cot, pick, experts, sizes, collective, part=512):
+    rows_here, width = tokens.shape
+    lanes = router.shape[1]
+    widths = [width, width, lanes if 3 * experts <= lanes else 3 * lanes]
+    n, n_ctx, number = sizes["dp"], sizes["ctx"], sizes["ctx"] * sizes["exp"]
     groups, dests, rows, _ = pick.shape
     pieces = cut(widths, part)
     count = len(pieces)
+    vmem, anywhere = pl.BlockSpec(memory_space=pltpu.VMEM), pl.BlockSpec(memory_space=pl.ANY)
     return pl.pallas_call(
-        functools.partial(dispatch_kernel, sizes=sizes, pieces=pieces, arrays=len(blocks)),
-        in_specs=[pl.BlockSpec(memory_space=pltpu.VMEM)] * (len(blocks) + 1),
-        out_specs=[pl.BlockSpec(memory_space=pl.ANY)] * len(blocks),
+        functools.partial(dispatch_kernel, sizes=sizes, pieces=pieces, experts=experts),
+        in_specs=[vmem] * 8,
+        out_specs=[anywhere] * 3 + [vmem] * 2,
         out_shape=[
-            jax.ShapeDtypeStruct((number, groups * rows, width), jnp.bfloat16) for width in widths
-        ],
-        scratch_shapes=[pltpu.VMEM((n, tokens, width), jnp.bfloat16) for width in widths]
-        + [pltpu.VMEM((dests, groups * rows, width), jnp.bfloat16) for width in widths]
+            jax.ShapeDtypeStruct((number, groups * rows, columns), jnp.bfloat16)
+            for columns in widths
+        ]
+        + [
+            jax.ShapeDtypeStruct((rows_here, width), jnp.float32),
+            jax.ShapeDtypeStruct((rows_here, lanes), jnp.float32),
+        ],
+        scratch_shapes=[pltpu.VMEM((n_ctx, rows_here, width), jnp.bfloat16)]
+        + square_scratch(rows_here, width)
+        + [pltpu.VMEM((rows_here, width), jnp.bfloat16)]
+        + [pltpu.VMEM((n, rows_here, columns), jnp.bfloat16) for columns in widths]
+        + [pltpu.VMEM((dests, groups * rows, columns), jnp.bfloat16) for columns in widths]
         + [
             pltpu.SemaphoreType.DMA((count, n, 2)),
             pltpu.SemaphoreType.DMA((count, n)),
@@ -505,34 +718,36 @@
         compiler_params=pltpu.CompilerParams(
             collective_id=collective, has_side_effects=True, vmem_limit_bytes=VMEM
         ),
-        cost_estimate=pl.CostEstimate(
-            flops=10 << 30, bytes_accessed=600 << 20, transcendentals=0
-        ),
-    )(*blocks, pick)
-
-
-def combine_kernel(*refs, sizes, pieces, arrays):
-    sent, pick_ref, outs = refs[:arrays], refs[arrays], refs[arrays + 1 : 2 * arrays + 1]
-    back, leaving, landing = [refs[k * arrays + 1 : (k + 1) * arrays + 1] for k in (2, 3, 4)]
-    sums, line_send, line_recv, plane_send, plane_recv, own_sem = refs[5 * arrays + 1 :]
+    )(attended, back, tokens, gain, router, chosen, cot, pick)
+
+
+def combine_kernel(
+    rows_ref, dots_ref, pick_ref, carried_ref, middle_ref, cot_ref, gain_ref, gates_ref, router_ref,
+    carried_out, whole_ref, middle_grad_ref, gain_grad_ref, router_grad_ref,
+    back_rows, back_dots, leave_rows, leave_dots, land_rows, land_dots, total_rows, total_dots,
+    sums, branch, line_send, line_recv, plane_send, plane_recv, own_sem, sq_send, sq_recv, sq_own,
+    *, sizes, pieces, experts,
+):
+    sent, back = (dots_ref, rows_ref), (back_dots, back_rows)
+    leaving, landing = (leave_dots, leave_rows), (land_dots, land_rows)
+    totals = (total_dots, total_rows)
     n, number = sizes["dp"], sizes["ctx"] * sizes["exp"]
     me, here = lax.axis_index("dp"), plane_index(sizes)
-    tokens = outs[0].shape[0]
+    tokens = middle_ref.shape[0]
     groups, span, _ = pick_ref.shape
-    rows = sent[0].shape[1] // groups
+    rows = rows_ref.shape[1] // groups
     full, low = jnp.float32, jnp.bfloat16
     greet(sizes)
 
     def plane_copy(f, ahead):
         a, first, part = pieces[f]
         target = peer(sizes, ahead)
-        return pltpu.make_async_remote_copy(
-            src_ref=sent[a].at[target, :, pl.ds(first, part)],
-            dst_ref=back[a].at[here, :, pl.ds(first, part)],
-            send_sem=plane_send.at[f, ahead],
-            recv_sem=plane_recv.at[f, ahead],
-            device_id=place(sizes, target),
-            device_id_type=MESH,
+        return remote(
+            sent[a].at[target, :, pl.ds(first, part)],
+            back[a].at[here, :, pl.ds(first, part)],
+            plane_send.at[f, ahead],
+            plane_recv.at[f, ahead],
+            place(sizes, target),
         )
 
     def own_copy(f):
@@ -550,22 +765,21 @@
 
     def line_copy(f, target, step):
         a, first, part = pieces[f]
-        return pltpu.make_async_remote_copy(
-            src_ref=leaving[a].at[target, :, pl.ds(first, part)],
-            dst_ref=landing[a].at[target + (step + 1) // 2, :, pl.ds(first, part)],
-            send_sem=line_send.at[f, target],
-            recv_sem=line_recv.at[f, target + (step + 1) // 2],
-            device_id={"dp": me + step},
-            device_id_type=MESH,
+        return remote(
+            leaving[a].at[target, :, pl.ds(first, part)],
+            landing[a].at[target + (step + 1) // 2, :, pl.ds(first, part)],
+            line_send.at[f, target],
+            line_recv.at[f, target + (step + 1) // 2],
+            {"dp": me + step},
         )
 
     for f, (a, first, part) in enumerate(pieces):
-        here_columns = pl.ds(first, part)
+        columns = pl.ds(first, part)
         for ahead in range(1, number):
             plane_copy(f, ahead).wait_recv()
         own_copy(f).wait()
         for g in range(groups):
-            gathered = back[a][:, pl.ds(g * rows, rows), here_columns].reshape(number * rows, part)
+            gathered = back[a][:, pl.ds(g * rows, rows), columns].reshape(number * rows, part)
             sums[pl.ds(g * span // tokens, span // tokens), :, pl.ds(0, part)] = jnp.dot(
                 pick_ref[g], gathered, preferred_element_type=full
             ).reshape(span // tokens, tokens, part)
@@ -582,21 +796,51 @@
                     @pl.when((behind >= 0) & (behind < n))
                     def _():
                         line_copy(f, target, step).wait_recv()
-                        coming = landing[a][target + (step + 1) // 2, :, here_columns]
-                        leaving[a][target, :, here_columns] = (own + coming.astype(full)).astype(low)
+                        coming = landing[a][target + (step + 1) // 2, :, columns]
+                        leaving[a][target, :, columns] = (own + coming.astype(full)).astype(low)
 
                     @pl.when((behind < 0) | (behind >= n))
                     def _():
-                        leaving[a][target, :, here_columns] = own.astype(low)
+                        leaving[a][target, :, columns] = own.astype(low)
 
                     line_copy(f, target, step).start()
 
-        outs[a][:, here_columns] = sums[me, :, pl.ds(0, part)]
+        totals[a][:, columns] = sums[me, :, pl.ds(0, part)]
         for step in (-1, 1):
             @pl.when((me - step >= 0) & (me - step < n))
             def _():
                 line_copy(f, me, step).wait_recv()
-                outs[a][:, here_columns] += landing[a][me + (step + 1) // 2, :, here_columns].astype(full)
+                totals[a][:, columns] += landing[a][me + (step + 1) // 2, :, columns].astype(full)
+
+    gates = gates_ref[...]
+    lanes = gates.shape[1]
+    if experts == lanes:
+        dots = sum(total_dots[:, k * lanes : (k + 1) * lanes] for k in range(3))
+    else:
+        dots = total_dots[...]
+        dots = dots + pltpu.roll(dots, lanes - experts, 1) + pltpu.roll(dots, lanes - 2 * experts, 1)
+    picked = gates * (dots - jnp.sum(gates * dots, axis=-1, keepdims=True))
+    logit_grads = picked.astype(low)
+    mixed_grad = total_rows[...] + lax.dot_general(
+        logit_grads, router_ref[...], (((1,), (1,)), ((), ())), preferred_element_type=full
+    )
+    middle = middle_ref[...]
+    inverse = lax.rsqrt(jnp.mean(middle * middle, axis=-1, keepdims=True) + eps_norm)
+    normed = middle * inverse
+    gain_grad_ref[...] = jnp.sum(mixed_grad * normed, axis=0, keepdims=True)
+    scaled = mixed_grad * gain_ref[...]
+    middle_grad = cot_ref[...].astype(full) + inverse * (
+        scaled - normed * jnp.mean(scaled * normed, axis=-1, keepdims=True)
+    )
+    middle_grad_ref[...] = middle_grad
+    branch[...] = middle_grad.astype(low)
+    collect = SquareGather(sizes, branch, whole_ref, sq_send, sq_recv, sq_own.at[0])
+    collect.start()
+    router_grad_ref[...] = lax.dot_general(
+        logit_grads, (normed * gain_ref[...]).astype(low), (((0,), (0,)), ((), ())),
+        preferred_element_type=full,
+    )
+    collect.pass_on()
 
     for f in range(len(pieces)):
         for ahead in range(1, number):
@@ -608,38 +852,47 @@
                 @pl.when((target >= 0) & (target < n))
                 def _():
                     line_copy(f, target, step).wait_send()
-
-
-def combine(sent, pick, tokens, sizes, collective, part=512):
-    number, back_rows = sent[0].shape[:2]
-    widths = [v.shape[2] for v in sent]
-    n = sizes["dp"]
-    pieces = cut(widths, part)
+    collect.finish()
+
+
+def combine(rows, dots, pick, carried, middle, cot, gain, gates, router, experts, sizes, collective, part=512):
+    number, back_rows, width = rows.shape
+    extra = dots.shape[2]
+    tokens = middle.shape[0]
+    lanes = router.shape[1]
+    n, n_ctx = sizes["dp"], sizes["ctx"]
+    low, full = jnp.bfloat16, jnp.float32
+    pieces = cut([extra, width], part)
     count = len(pieces)
+    both = (width, extra)
+    vmem, anywhere = pl.BlockSpec(memory_space=pltpu.VMEM), pl.BlockSpec(memory_space=pl.ANY)
+    dma = lambda *shape: pltpu.SemaphoreType.DMA(shape)
     return pl.pallas_call(
-        functools.partial(combine_kernel, sizes=sizes, pieces=pieces, arrays=len(sent)),
-        in_specs=[pl.BlockSpec(memory_space=pl.ANY)] * len(sent)
-        + [pl.BlockSpec(memory_space=pltpu.VMEM)],
-        out_specs=[pl.BlockSpec(memory_space=pltpu.VMEM)] * len(sent),
-        out_shape=[jax.ShapeDtypeStruct((tokens, width), jnp.float32) for width in widths],
-        scratch_shapes=[pltpu.VMEM((number, back_rows, width), jnp.bfloat16) for width in widths]
-        + [pltpu.VMEM((n, tokens, width), jnp.bfloat16) for width in widths]
-        + [pltpu.VMEM((n + 1, tokens, width), jnp.bfloat16) for width in widths]
+        functools.partial(combine_kernel, sizes=sizes, pieces=pieces, experts=experts),
+        in_specs=[anywhere, anywhere, vmem, anywhere] + [vmem] * 5,
+        out_specs=[anywhere, anywhere] + [vmem] * 3,
+        out_shape=[
+            jax.ShapeDtypeStruct(carried.shape, carried.dtype),
+            jax.ShapeDtypeStruct((n_ctx, tokens, width), low),
+            jax.ShapeDtypeStruct((tokens, width), full),
+            jax.ShapeDtypeStruct((1, width), full),
+            jax.ShapeDtypeStruct((lanes, width), full),
+        ],
+        input_output_aliases={3: 0},
+        scratch_shapes=[pltpu.VMEM((number, back_rows, w), low) for w in both]
+        + [pltpu.VMEM((n, tokens, w), low) for w in both]
+        + [pltpu.VMEM((n + 1, tokens, w), low) for w in both]
+        + [pltpu.VMEM((tokens, w), full) for w in both]
         + [
-            pltpu.VMEM((n, tokens, max(p[2] for p in pieces)), jnp.float32),
-            pltpu.SemaphoreType.DMA((count, n)),
-            pltpu.SemaphoreType.DMA((count, n + 1)),
-            pltpu.SemaphoreType.DMA((count, number)),
-            pltpu.SemaphoreType.DMA((count, number)),
-            pltpu.SemaphoreType.DMA((count,)),
+            pltpu.VMEM((n, tokens, max(p[2] for p in pieces)), full),
+            pltpu.VMEM((tokens, width), low),
+            dma(count, n), dma(count, n + 1), dma(count, number), dma(count, number), dma(count),
+            dma(6), dma(6), dma(1),
         ],
         compiler_params=pltpu.CompilerParams(
             collective_id=collective, has_side_effects=True, vmem_limit_bytes=VMEM
         ),
-        cost_estimate=pl.CostEstimate(
-            flops=5 << 30, bytes_accessed=300 << 20, transcendentals=0
-        ),
-    )(*sent, pick)
+    )(rows, dots, pick, carried, middle, cot, gain, gates, router)
 
 
 def expert_kernel(
@@ -707,6 +960,452 @@
             flops=12 * sources * rows * width * inner, bytes_accessed=60 << 20, transcendentals=0
         ),
     )(here, rows_in, parts, grads, gate_weight, up_weight, down_weight)
+
+
+def gather_kernel(
+    token_ref, front_ref, back_ref, route_ref, tokens_ref, fronts_ref, backs_ref, routes_ref,
+    held, sq_send, sq_recv, own_sem, fa_send, fa_recv, fl_send, fl_recv, fp_send, fp_recv,
+    bl_send, bl_recv, ba_send, ba_recv, bp_send, bp_recv, rl_send, rl_recv, *, sizes,
+):
+    n, n_ctx, n_exp = sizes["dp"], sizes["ctx"], sizes["exp"]
+    z, c, k = (lax.axis_index(a) for a in ALL)
+    by_x, by_y = square(sizes)
+    far = n_ctx - 1 - c
+    half = token_ref.shape[1] // 2
+    greet(sizes)
+
+    def remote(source, target, send, recv, device):
+        return pltpu.make_async_remote_copy(
+            src_ref=source, dst_ref=target, send_sem=send, recv_sem=recv, device_id=device,
+            device_id_type=MESH,
+        )
+
+    def front_across(ahead):
+        target = lax.rem(c + ahead, n_ctx)
+        return remote(
+            front_ref.at[target], fronts_ref.at[z, c, k], fa_send.at[ahead], fa_recv.at[ahead],
+            {"ctx": target},
+        )
+
+    def front_line(origin, step):
+        here = fronts_ref.at[origin, :, k]
+        return remote(
+            here, here, fl_send.at[origin, (step + 1) // 2], fl_recv.at[origin], {"dp": z + step}
+        )
+
+    def front_pair(origin, ahead):
+        here = fronts_ref.at[origin, :, k]
+        return remote(
+            here, here, fp_send.at[origin, ahead], fp_recv.at[origin, ahead],
+            {"exp": lax.rem(k + ahead, n_exp)},
+        )
+
+    def back_line(origin, step):
+        here = held.at[origin]
+        return remote(
+            here, here, bl_send.at[origin, (step + 1) // 2], bl_recv.at[origin], {"dp": z + step}
+        )
+
+    def back_across(ahead):
+        target = lax.rem(c + ahead, n_ctx)
+        return remote(
+            held.at[target], backs_ref.at[c, k], ba_send.at[ahead], ba_recv.at[ahead],
+            {"ctx": target},
+        )
+
+    def back_pair(source, ahead):
+        here = backs_ref.at[source, k]
+        return remote(
+            here, here, bp_send.at[source, ahead], bp_recv.at[source, ahead],
+            {"exp": lax.rem(k + ahead, n_exp)},
+        )
+
+    def route_line(origin, step):
+        here = routes_ref.at[origin]
+        return remote(
+            here, here, rl_send.at[origin, (step + 1) // 2], rl_recv.at[origin], {"dp": z + step}
+        )
+
+    def columns(part):
+        return pl.ds(part * half, half)
+
+    def token_copy(place, part, to_y, number):
+        here = tokens_ref.at[place, :, columns(part)]
+        source = token_ref.at[:, columns(part)] if number < 4 else here
+        return remote(
+            source, here, sq_send.at[number], sq_recv.at[number], {"ctx": by_y if to_y else by_x}
+        )
+
+    firsts = [(0, False, 0), (1, True, 1), (1, False, 2), (0, True, 3)]
+
+    def in_line(step):
+        return (z + step >= 0) & (z + step < n)
+
+    own_copies = [
+        pltpu.make_async_copy(token_ref, tokens_ref.at[c], own_sem.at[0]),
+        pltpu.make_async_copy(front_ref.at[c], fronts_ref.at[z, c, k], own_sem.at[1]),
+        pltpu.make_async_copy(back_ref, held.at[z], own_sem.at[2]),
+        pltpu.make_async_copy(route_ref, routes_ref.at[z], own_sem.at[3]),
+    ]
+    for copy in own_copies:
+        copy.start()
+    for ahead in range(1, n_ctx):
+        front_across(ahead).start()
+    for part, to_y, number in firsts:
+        token_copy(c, part, to_y, number).start()
+    for copy in own_copies:
+        copy.wait()
+    for step in (-1, 1):
+        @pl.when(in_line(step))
+        def _():
+            back_line(z, step).start()
+            route_line(z, step).start()
+    for ahead in range(1, n_ctx):
+        front_across(ahead).wait_recv()
+    for step in (-1, 1):
+        @pl.when(in_line(step))
+        def _():
+            front_line(z, step).start()
+    for ahead in range(1, n_exp):
+        front_pair(z, ahead).start()
+    token_copy(by_x, 0, False, 0).wait_recv()
+    token_copy(by_x, 0, True, 4).start()
+    token_copy(by_y, 1, True, 1).wait_recv()
+    token_copy(by_y, 1, False, 5).start()
+
+    def pass_on(line, origin, step, after):
+        @pl.when((origin >= 0) & (origin < n))
+        def _():
+            line(origin, step).wait_recv()
+
+            @pl.when(in_line(step))
+            def _():
+                line(origin, step).start()
+
+            after(origin)
+
+    def to_siblings(origin):
+        for ahead in range(1, n_exp):
+            front_pair(origin, ahead).start()
+
+    for distance in range(1, n):
+        for step in (-1, 1):
+            pass_on(front_line, z - step * distance, step, to_siblings)
+            pass_on(route_line, z - step * distance, step, lambda origin: None)
+    for distance in range(1, n):
+        for step in (-1, 1):
+            pass_on(back_line, z - step * distance, step, lambda origin: None)
+    for ahead in range(1, n_ctx):
+        back_across(ahead).start()
+    own_back = pltpu.make_async_copy(held.at[c], backs_ref.at[c, k], own_sem.at[4])
+    own_back.start()
+    own_back.wait()
+    for ahead in range(1, n_exp):
+        back_pair(c, ahead).start()
+    for behind in range(1, n_ctx):
+        back_across(behind).wait_recv()
+        source = lax.rem(c + n_ctx - behind, n_ctx)
+        for ahead in range(1, n_exp):
+            back_pair(source, ahead).start()
+
+    token_copy(by_x, 1, False, 2).wait_recv()
+    token_copy(by_y, 0, True, 3).wait_recv()
+    token_copy(far, 0, True, 4).wait_recv()
+    token_copy(far, 1, False, 5).wait_recv()
+    for part, to_y, number in firsts + [(0, True, 4), (1, False, 5)]:
+        token_copy(c, part, to_y, number).wait_send()
+    for ahead in range(1, n_ctx):
+        front_across(ahead).wait_send()
+        back_across(ahead).wait_send()
+    for origin in range(n):
+        for ahead in range(1, n_exp):
+            front_pair(origin, ahead).wait()
+    for source in range(n_ctx):
+        for ahead in range(1, n_exp):
+            back_pair(source, ahead).wait()
+    for line in (route_line, front_line, back_line):
+        for distance in range(n):
+            for step in (-1, 1):
+                origin = z - step * distance
+
+                @pl.when((origin >= 0) & (origin < n) & in_line(step))
+                def _():
+                    line(origin, step).wait_send()
+
+
+def gather(tokens, front, back, routes, sizes, collective):
+    n, n_ctx, n_exp = sizes["dp"], sizes["ctx"], sizes["exp"]
+    _, rows, columns = front.shape
+    dma = lambda *shape: pltpu.SemaphoreType.DMA(shape)
+    return pl.pallas_call(
+        functools.partial(gather_kernel, sizes=sizes),
+        in_specs=[pl.BlockSpec(memory_space=pltpu.VMEM)] * 4,
+        out_specs=[pl.BlockSpec(memory_space=pl.ANY)] * 4,
+        out_shape=[
+            jax.ShapeDtypeStruct((n_ctx,) + tokens.shape, tokens.dtype),
+            jax.ShapeDtypeStruct((n, n_ctx, n_exp, rows, columns), front.dtype),
+            jax.ShapeDtypeStruct((n_ctx, n_exp) + back.shape, back.dtype),
+            jax.ShapeDtypeStruct((n,) + routes.shape, routes.dtype),
+        ],
+        scratch_shapes=[
+            pltpu.VMEM((n,) + back.shape, back.dtype),
+            dma(6), dma(6), dma(5),
+            dma(n_ctx), dma(n_ctx), dma(n, 2), dma(n), dma(n, n_exp), dma(n, n_exp),
+            dma(n, 2), dma(n), dma(n_ctx), dma(n_ctx), dma(n_ctx, n_exp), dma(n_ctx, n_exp),
+            dma(n, 2), dma(n),
+        ],
+        compiler_params=pltpu.CompilerParams(
+            collective_id=collective, has_side_effects=True, vmem_limit_bytes=VMEM
+        ),
+    )(tokens, front, back, routes)
+
+
+def scatter_kernel(
+    hidden_ref, front_ref, middle_ref, token_ref, gain_ref, small_ref, sent_ref, pick_ref,
+    result_ref, tokens_grad_ref, front_out, output_ref, small_out,
+    far_in, turn_out, turn_in, hidden_sum, front_pairs, front_sum, front_line_in, front_low, front_in,
+    rows_in, mix_out, mix_in, small_all, small_in,
+    h_send, h_recv, fp_send, fp_recv, fl_send, fl_recv, fa_send, fa_recv,
+    m_load, ml_send, ml_recv, s_send, s_recv, *, sizes, part,
+):
+    n, n_ctx, n_exp = sizes["dp"], sizes["ctx"], sizes["exp"]
+    devices = n * n_ctx * n_exp
+    z, c, k = (lax.axis_index(a) for a in ALL)
+    here = (z * n_ctx + c) * n_exp + k
+    tokens, width = token_ref.shape
+    full, low = jnp.float32, jnp.bfloat16
+
+    barrier = pltpu.get_barrier_semaphore()
+
+    def device_of(index):
+        return {
+            "dp": index // (n_ctx * n_exp),
+            "ctx": lax.rem(index // n_exp, n_ctx),
+            "exp": lax.rem(index, n_exp),
+        }
+
+    @pl.loop(1, devices)
+    def _(ahead):
+        pl.semaphore_signal(
+            barrier, inc=1, device_id=device_of(lax.rem(here + ahead, devices)),
+            device_id_type=MESH,
+        )
+
+    pl.semaphore_wait(barrier, devices - 1)
+
+    def in_line(step):
+        return (z + step >= 0) & (z + step < n)
+
+    hidden = SquareScatter(sizes, hidden_ref, far_in, turn_out, turn_in, h_send, h_recv)
+
+    def front_pair(ahead):
+        target = lax.rem(k + ahead, n_exp)
+        return remote(
+            front_ref.at[:, :, target], front_pairs.at[ahead - 1], fp_send.at[ahead],
+            fp_recv.at[ahead], {"exp": target},
+        )
+
+    for ahead in range(1, n_exp):
+        front_pair(ahead).start()
+    hidden.start(1)
+    hidden.start(0)
+
+    def front_line(target, step):
+        return remote(
+            front_low.at[target], front_line_in.at[target + (step + 1) // 2], fl_send.at[target],
+            fl_recv.at[target + (step + 1) // 2], {"dp": z + step},
+        )
+
+    def front_across(ahead):
+        target = lax.rem(c + ahead, n_ctx)
+        return remote(
+            front_sum.at[target], front_in.at[c], fa_send.at[ahead], fa_recv.at[ahead],
+            {"ctx": target},
+        )
+
+    def mix_line(target, step):
+        return remote(
+            mix_out.at[target], mix_in.at[target + (step + 1) // 2], ml_send.at[target],
+            ml_recv.at[target + (step + 1) // 2], {"dp": z + step},
+        )
+
+    def load(piece):
+        return pltpu.make_async_copy(
+            sent_ref.at[:, :, pl.ds(piece * part, part)], rows_in.at[piece % 2],
+            m_load.at[piece % 2],
+        )
+
+    def front_own(target):
+        total = front_ref[target, :, k].astype(full)
+        for ahead in range(1, n_exp):
+            total = total + front_pairs[ahead - 1, target].astype(full)
+        return total
+
+    def line_step(line, leaving, landing, own, distance):
+        for step in (-1, 1):
+            target = z + step * distance
+
+            @pl.when((target >= 0) & (target < n))
+            def _():
+                @pl.when(in_line(-step))
+                def _():
+                    line(target, step).wait_recv()
+                    leaving[target] = (
+                        own(target) + landing[target + (step + 1) // 2].astype(full)
+                    ).astype(low)
+
+                if own is not mix_own:
+                    @pl.when(jnp.logical_not(in_line(-step)))
+                    def _():
+                        leaving[target] = own(target).astype(low)
+
+                line(target, step).start()
+
+    def mix_own(target):
+        return mix_out[target].astype(full)
+
+    load(0).start()
+    for ahead in range(1, n_exp):
+        front_pair(ahead).wait_recv()
+    line_step(front_line, front_low, front_line_in, front_own, n - 1)
+
+    groups, span, _ = pick_ref.shape
+    number, back_rows, _ = sent_ref.shape
+    rows = back_rows // groups
+    pieces = width // part
+    for piece in range(pieces):
+        if piece + 1 < pieces:
+            load(piece + 1).start()
+        load(piece).wait()
+        for g in range(groups):
+            gathered = rows_in[piece % 2, :, pl.ds(g * rows, rows), :].reshape(number * rows, part)
+            mix_out[pl.ds(g * span // tokens, span // tokens), :, pl.ds(piece * part, part)] = (
+                jnp.dot(pick_ref[g], gathered, preferred_element_type=full)
+                .astype(low)
+                .reshape(span // tokens, tokens, part)
+            )
+    line_step(mix_line, mix_out, mix_in, mix_own, n - 1)
+    hidden.turn()
+    for distance in range(n - 2, 0, -1):
+        line_step(front_line, front_low, front_line_in, front_own, distance)
+        line_step(mix_line, mix_out, mix_in, mix_own, distance)
+
+    hidden.finish(hidden_sum)
+    x = token_ref[...].astype(full)
+    inverse = lax.rsqrt(jnp.mean(x * x, axis=-1, keepdims=True) + eps_norm)
+    normed = x * inverse
+    grad = hidden_sum[...]
+    scaled = grad * gain_ref[...]
+    tokens_grad_ref[...] = (
+        middle_ref[...]
+        + inverse * (scaled - normed * jnp.mean(scaled * normed, axis=-1, keepdims=True))
+    ).astype(low)
+    gain_grad = jnp.sum(grad * normed, axis=0, keepdims=True)
+    owned = gain_grad.shape[1] // devices
+    small_all[...] = small_ref[...]
+    for index in range(devices):
+        small_all[index, 0:1, 0:owned] = gain_grad[:, index * owned : (index + 1) * owned]
+
+    def small_copy(ahead):
+        target = lax.rem(here + ahead, devices)
+        return remote(
+            small_all.at[target], small_in.at[ahead], s_send.at[ahead], s_recv.at[ahead],
+            device_of(target),
+        )
+
+    @pl.loop(1, devices)
+    def _(ahead):
+        small_copy(ahead).start()
+
+    front_sum[...] = front_own(z).astype(low)
+    for step in (-1, 1):
+        @pl.when(in_line(-step))
+        def _():
+            front_line(z, step).wait_recv()
+            front_sum[...] = (
+                front_sum[...].astype(full) + front_line_in[z + (step + 1) // 2].astype(full)
+            ).astype(low)
+    for ahead in range(1, n_ctx):
+        front_across(ahead).start()
+    front_in[c] = front_sum[c]
+    hidden_sum[...] = result_ref[...] + mix_own(z)
+    for step in (-1, 1):
+        @pl.when(in_line(-step))
+        def _():
+            mix_line(z, step).wait_recv()
+            hidden_sum[...] += mix_in[z + (step + 1) // 2].astype(full)
+    output_ref[...] = hidden_sum[...].astype(low)
+    small_out[...] = small_all[here]
+
+    @pl.loop(1, devices)
+    def _(ahead):
+        small_copy(ahead).wait_recv()
+        small_out[...] += small_in[ahead]
+
+    for ahead in range(1, n_ctx):
+        front_across(ahead).wait_recv()
+    front_out[...] = front_in[...].astype(full)
+
+    @pl.loop(1, devices)
+    def _(ahead):
+        small_copy(ahead).wait_send()
+
+    hidden.close()
+    for ahead in range(1, n_exp):
+        front_pair(ahead).wait_send()
+    for ahead in range(1, n_ctx):
+        front_across(ahead).wait_send()
+    for distance in range(1, n):
+        for step in (-1, 1):
+            target = z + step * distance
+
+            @pl.when((target >= 0) & (target < n))
+            def _():
+                front_line(target, step).wait_send()
+                mix_line(target, step).wait_send()
+
+
+def scatter(hidden, front, middle, tokens, gain, small, sent, pick, result, sizes, collective, part=512):
+    n, n_ctx, n_exp = sizes["dp"], sizes["ctx"], sizes["exp"]
+    low, full = jnp.bfloat16, jnp.float32
+    _, rows, width = hidden.shape
+    f_rows, f_cols = front.shape[3:]
+    number, back_rows, _ = sent.shape
+    devices, s_rows, s_cols = small.shape
+    dma = lambda *shape: pltpu.SemaphoreType.DMA(shape)
+    vmem = pl.BlockSpec(memory_space=pltpu.VMEM)
+    return pl.pallas_call(
+        functools.partial(scatter_kernel, sizes=sizes, part=part),
+        in_specs=[vmem] * 6 + [pl.BlockSpec(memory_space=pl.ANY), vmem, vmem],
+        out_specs=[vmem] * 4,
+        out_shape=[
+            jax.ShapeDtypeStruct((rows, width), low),
+            jax.ShapeDtypeStruct((n_ctx, f_rows, f_cols), full),
+            jax.ShapeDtypeStruct((rows, width), low),
+            jax.ShapeDtypeStruct((s_rows, s_cols), full),
+        ],
+        scratch_shapes=[
+            pltpu.VMEM((2, 2, rows, width // 2), low),
+            pltpu.VMEM((2, rows, width // 2), low),
+            pltpu.VMEM((2, rows, width // 2), low),
+            pltpu.VMEM((rows, width), full),
+            pltpu.VMEM((n_exp - 1, n, n_ctx, f_rows, f_cols), low),
+            pltpu.VMEM((n_ctx, f_rows, f_cols), low),
+            pltpu.VMEM((n + 1, n_ctx, f_rows, f_cols), low),
+            pltpu.VMEM((n, n_ctx, f_rows, f_cols), low),
+            pltpu.VMEM((n_ctx, f_rows, f_cols), low),
+            pltpu.VMEM((2, number, back_rows, part), low),
+            pltpu.VMEM((n, rows, width), low),
+            pltpu.VMEM((n + 1, rows, width), low),
+            pltpu.VMEM((devices, s_rows, s_cols), full),
+            pltpu.VMEM((devices, s_rows, s_cols), full),
+            dma(6), dma(6), dma(n_exp), dma(n_exp), dma(n), dma(n + 1), dma(n_ctx), dma(n_ctx),
+            dma(2), dma(n), dma(n + 1), dma(devices), dma(devices),
+        ],
+        compiler_params=pltpu.CompilerParams(
+            collective_id=collective, has_side_effects=True, vmem_limit_bytes=VMEM
+        ),
+    )(hidden, front, middle, tokens, gain, small, sent, pick, result)
 
 
 def shards(
@@ -773,8 +1472,13 @@
         ],
         axis=2,
     )
-    front = pair_gather(line_gather(swap(front, "ctx"), "dp"), "exp")
-    front = front.transpose(1, 2, 0, 3, 4).reshape(width, -1)
+    sizes = {"dp": n_dp, "ctx": n_ctx, "exp": n_exp}
+    whole_tokens, front, output_part, column_routes = gather(
+        tokens[0], front, output_weight.astype(low), routes[0], sizes, 3
+    )
+    whole_tokens = whole_tokens.reshape(seq_len, width)
+    front = front.reshape(width, -1)
+    output_part = output_part.reshape(q_cols, width)
     front_weight = front[:, : q_cols + 2 * kv_cols]
     small = front[:, q_cols + 2 * kv_cols :]
     first_gain = small[:, 0].astype(full)
@@ -784,12 +1488,6 @@
     key_scale = head_gains[:, gain_len : 2 * gain_len].reshape(-1).astype(full)
     router_full = small[:, 3 : 3 + experts]
 
-    whole_tokens = square_gather(tokens[0], "ctx").reshape(seq_len, width)
-    back = line_gather(output_weight.astype(low), "dp")
-    back = pair_gather(swap(back, "ctx"), "exp")
-    output_part = back.transpose(1, 0, 2, 3).reshape(q_cols, width)
-
-    column_routes = line_gather(routes[0], "dp")
     chosen = jnp.any(
         column_routes[:, :, :, None] == jnp.arange(experts, dtype=jnp.int32), axis=2
     )
@@ -800,7 +1498,6 @@
     together = 2 if 2 * capacity % 16 == 0 and n_dp % 2 == 0 else n_dp
     groups = n_dp // together
     slot_rows = -(-together * capacity // 16) * 16
-    sizes = {"dp": n_dp, "ctx": n_ctx, "exp": n_exp}
 
     def grouped(v):
         return v.reshape(groups, together * tok_count, -1)
@@ -810,12 +1507,6 @@
     slots = jnp.arange(slot_rows, dtype=full)
     pick = (slot_at.transpose(0, 2, 1)[:, :, None, :] == slots[:, None]).astype(low)
     pick_back = (slot_at[:, :, :, None] == slots).astype(low).reshape(groups, -1, plane * slot_rows)
-
-    def bring_back(sent):
-        sent = sent.reshape(plane, groups, slot_rows, -1).transpose(1, 0, 2, 3)
-        sent = sent.reshape(groups, plane * slot_rows, -1)
-        sums = jnp.einsum("gts,gsd->gtd", pick_back, sent, preferred_element_type=full)
-        return sums.reshape(n_dp, tok_count, -1)
 
     positions = jnp.arange(seq_len, dtype=jnp.int32)
     cosine, sine = rope_tables(positions, head_dim)
@@ -824,37 +1515,30 @@
     scales = jnp.stack([query_scale, key_scale])
     heads_here = heads // n_ctx
     hidden, raw, turned = project(
-        whole_tokens, first_gain[None], front_weight, scales, cosine, sine, heads_here, kv_here,
-        tok_count,
+        whole_tokens, first_gain[None], front, q_cols + 2 * kv_cols, scales, cosine, sine,
+        heads_here, kv_here, tok_count,
     )
     attended_low = attend(bounds, turned, heads_here, kv_here, head_dim, tok_count)
-    branch = jnp.dot(attended_low, output_part, preferred_element_type=full).astype(low)
-    branch = square_scatter(branch.reshape(n_ctx, tok_count, width), "ctx")
-
-    own = tokens[0].astype(full)
-    middle = own + branch
-    second_inverse = lax.rsqrt(jnp.mean(middle * middle, axis=-1, keepdims=True) + eps_norm)
-    second_normed = middle * second_inverse
-    mixed_low = (second_normed * second_gain).astype(low)
-
-    logits = jnp.dot(mixed_low, router_full, preferred_element_type=full)
-    own_chosen = jnp.any(routes[0][:, :, None] == jnp.arange(experts, dtype=jnp.int32), axis=1)
-    logits = jnp.where(own_chosen, logits, masked_score)
-    own_gates = jnp.exp(logits - jnp.max(logits, axis=-1, keepdims=True))
-    own_gates = own_gates / jnp.sum(own_gates, axis=-1, keepdims=True)
-    first_part = lax.reduce_precision(own_gates, 8, 7)
-    second_part = lax.reduce_precision(own_gates - first_part, 8, 7)
-    third_part = lax.reduce_precision(own_gates - first_part - second_part, 8, 7)
-    gate_parts = jnp.concatenate([first_part, second_part, third_part], axis=1).astype(low)
-    gate_parts = jnp.pad(gate_parts, ((0, 0), (0, -gate_parts.shape[1] % 128)))
-    expert_in, part_rows, grad_rows = dispatch(
-        (mixed_low, gate_parts, cotangent[0]), pick, sizes, 1
+
+    lanes = -(-experts // 128) * 128
+    router_wide = jnp.pad(router_full, ((0, 0), (0, lanes - experts)))
+    own_chosen = jnp.any(
+        routes[0][:, :, None] == jnp.arange(lanes, dtype=jnp.int32), axis=1
+    ).astype(full)
+    grad_rows, expert_in, part_rows, middle, own_gates = dispatch(
+        attended_low, output_part, tokens[0], second_gain[None], router_wide, own_chosen,
+        cotangent[0], pick, experts, sizes, 1,
     )
     here = (dp_index * n_ctx + lax.axis_index("ctx")) * n_exp + lax.axis_index("exp")
     active, gate_grad, up_grad, row_grads, scaled_out, dot_rows = expert(
         here[None], expert_in, part_rows, grad_rows, gate_weight, up_weight, down_weight, experts
     )
-    mixed_grad, dots = combine((row_grads, dot_rows), pick_back, tok_count, sizes, 2)
+    scaled_out, branch_low, middle_grad, second_gain_grad, router_grad = combine(
+        row_grads, dot_rows, pick_back, scaled_out, middle, cotangent[0], second_gain[None],
+        own_gates, router_wide, experts, sizes, 2,
+    )
+    router_grad = router_grad[:experts].T
+    branch_low = branch_low.reshape(seq_len, width)
     weight_sum = lambda left, right: jnp.einsum(
         "scd,scf->df", left, right, preferred_element_type=full
     )[None]
@@ -863,48 +1547,19 @@
     up_w_grad = weight_sum(expert_in, up_grad)
     scaled_out = swap(scaled_out, PLANE)
 
-    dots = dots[:, :experts] + dots[:, experts : 2 * experts] + dots[:, 2 * experts : 3 * experts]
-    picked_grads = own_gates * (dots - jnp.sum(own_gates * dots, axis=-1, keepdims=True))
-    logit_grads = picked_grads.astype(low)
-    mixed_grad = mixed_grad + jnp.einsum(
-        "te,de->td", logit_grads, router_full, preferred_element_type=full
-    )
-    mixture = line_scatter(bring_back(scaled_out).astype(low), "dp")
-    output = (middle + mixture).astype(low)[None]
-    router_grad = jnp.einsum("td,te->de", mixed_low, logit_grads, preferred_element_type=full)
-    grad_out = cotangent[0].astype(full)
-    middle_back, second_gain_grad = norm_back(
-        mixed_grad, second_normed, second_inverse, second_gain
-    )
-    middle_grad = grad_out + middle_back
-
-    branch_low = square_gather(middle_grad.astype(low), "ctx").reshape(seq_len, width)
     output_w_grad = jnp.einsum("ti,td->id", attended_low, branch_low, preferred_element_type=full)
     attended_grad = jnp.einsum("td,id->ti", branch_low, output_part, preferred_element_type=full)
-    raw_grad, head_gain_grads = attend_back(
-        bounds, turned, attended_grad.astype(low), raw, scales, cosine, sine, heads_here, kv_here,
-        head_dim, tok_count,
+    raw_grad, head_gain_grads, output_share = attend_back(
+        bounds, turned, attended_grad.astype(low), raw, scales, cosine, sine,
+        output_w_grad.astype(low).reshape(n_ctx, n_exp, -1, width), heads_here, kv_here,
+        head_dim, tok_count, sizes, 5,
     )
     query_gain_grad, key_gain_grad = head_gain_grads[0], head_gain_grads[1]
     hidden_grad = jnp.einsum("ti,di->td", raw_grad, front_weight, preferred_element_type=full)
-    hidden_grad = square_scatter(hidden_grad.astype(low).reshape(n_ctx, tok_count, width), "ctx")
-    own_inverse = lax.rsqrt(jnp.mean(own * own, axis=-1, keepdims=True) + eps_norm)
-    input_back, first_gain_grad = norm_back(hidden_grad, own * own_inverse, own_inverse, first_gain)
-    tokens_grad = (middle_grad + input_back).astype(low)[None]
-
     front_grad = jnp.einsum("td,ti->di", hidden, raw_grad, preferred_element_type=full).astype(low)
-    front_grad = front_grad.reshape(n_dp, n_ctx, n_exp, rows, -1).transpose(2, 0, 1, 3, 4)
-    front_grad = line_scatter(pair_scatter(front_grad, "exp"), "dp").astype(low)
-    front_grad = swap(front_grad, "ctx").astype(full)
-    query_share = front_grad[:, :, :q_cols].transpose(1, 0, 2).reshape(rows, -1)
-    key_share = front_grad[:, :, q_cols : q_cols + kv_cols].transpose(1, 0, 2).reshape(rows, -1)
-    value_share = front_grad[:, :, q_cols + kv_cols :].transpose(1, 0, 2).reshape(rows, -1)
-    back_grad = output_w_grad.astype(low).reshape(n_ctx, n_exp, -1, width).transpose(1, 0, 2, 3)
-    back_grad = swap(pair_scatter(back_grad, "exp"), "ctx")
-    output_share = line_scatter(back_grad, "dp")
     packed = jnp.concatenate(
         [
-            first_gain_grad.reshape(devices, -1),
+            jnp.zeros((devices, rows), full),
             second_gain_grad.reshape(devices, -1),
             query_gain_grad.reshape(devices, -1),
             key_gain_grad.reshape(devices, -1),
@@ -912,10 +1567,26 @@
         ],
         axis=1,
     )
-    packed = jnp.pad(packed, ((0, 0), (0, -packed.shape[1] % 1024)))
-    packed = packed.reshape(n_dp, n_ctx, n_exp, -1).transpose(2, 1, 0, 3)
-    packed = square_scatter(pair_scatter(packed, "exp"), "ctx")
-    packed = line_scatter(packed, "dp")
+    packed = jnp.pad(packed, ((0, 0), (0, -packed.shape[1] % 1024))).reshape(devices, 8, -1)
+    tokens_grad, front_grad, output, packed = scatter(
+        hidden_grad.astype(low).reshape(n_ctx, tok_count, width),
+        front_grad.reshape(n_dp, n_ctx, n_exp, rows, -1),
+        middle_grad,
+        tokens[0],
+        first_gain[None],
+        packed,
+        scaled_out,
+        pick_back,
+        middle,
+        sizes,
+        4,
+    )
+    output = output[None]
+    tokens_grad = tokens_grad[None]
+    query_share = front_grad[:, :, :q_cols].transpose(1, 0, 2).reshape(rows, -1)
+    key_share = front_grad[:, :, q_cols : q_cols + kv_cols].transpose(1, 0, 2).reshape(rows, -1)
+    value_share = front_grad[:, :, q_cols + kv_cols :].transpose(1, 0, 2).reshape(rows, -1)
+    packed = packed.reshape(-1)
     ends = [rows, 2 * rows, 2 * rows + gain_len, 2 * rows + 2 * gain_len]
     first_share = packed[: ends[0]]
     second_share = packed[ends[0] : ends[1]]

time: 1160 us -> 1050 us (0.905); the launches traced: 1140 us -> 1040 us
  Pallas kernels: 505 us -> 919 us
  waiting for transfers between devices: 214 us -> 0.01 us
  starting transfers between devices: 174 us -> 6.8 us
  other arithmetic: 80.3 us -> 22.3 us
  local copies, waits for them, and re-layouts: 74.9 us -> 31 us
  matrix products: 86.9 us -> 62.2 us
    pallas_call x0 -> x2, Pallas kernels: none -> 229 us  [the longest x1 134 us: scatter(): pl.pallas_call(functools.partial(scatter_kernel, sizes=sizes, part=part),...]
    ppermute x67 -> x0, waiting for transfers between devices: 207 us -> none  [the longest x25 128 us: flip(): lax.ppermute(block, axis, [(i, i ^ bit) for i in range(lax.axis_size(axis...]
    ppermute x67 -> x0, starting transfers between devices: 148 us -> none  [the longest x12 43.1 us: line_scatter(): up = lax.ppermute(send_up, axis, [(i, i + 1) for i in range(step)])]
    pallas_call x1, Pallas kernels: 35.8 us -> 152 us  [attend_back(): pl.pallas_call(functools.partial(attend_back_kernel, block=block, heads=h...]
    pallas_call x1, Pallas kernels: 234 us -> 283 us  [dispatch(): pl.pallas_call(functools.partial(dispatch_kernel, sizes=sizes, pieces=pie...]
    convert_element_type x20 -> x2, other arithmetic: 31.9 us -> 2.79 us  [the longest x1 2.12 us: shards(): output_weight.astype(low)]
    dot_general x5 -> x0, matrix products: 22.1 us -> none  [the longest x1 9.73 us: bring_back(): jnp.einsum('gts,gsd->gtd', pick_back, sent, preferred_element_type=full)]
    pallas_call x1, Pallas kernels: 146 us -> 165 us  [combine(): pl.pallas_call(functools.partial(combine_kernel, sizes=sizes, pieces=piec...]
  transfers between devices with their start and end apart: 72 -> 1, of which waited for: 23 -> 0; matrix products, arithmetic and copies ran while one was open for 18% -> 6% of each run, Pallas kernels for 3% -> 15%
where the time goes in v3:
time: 1050 us; the launch traced here: 1040 us
  Pallas kernels  919 us (88%)
  matrix products  62.2 us (6%)
  local copies, waits for them, and re-layouts  31 us (3%)
  other arithmetic  22.3 us (2%)
    pallas_call x1, Pallas kernels, dispatch(): pl.pallas_call(functools.partial(dispatch_kernel, sizes=sizes, pieces=pie...  283 us
    pallas_call x1, Pallas kernels, combine(): pl.pallas_call(functools.partial(combine_kernel, sizes=sizes, pieces=piec...  165 us
    pallas_call x1, Pallas kernels, attend_back(): pl.pallas_call(functools.partial(attend_back_kernel, block=block, heads=h...  152 us
    pallas_call x1, Pallas kernels, scatter(): pl.pallas_call(functools.partial(scatter_kernel, sizes=sizes, part=part),...  134 us
    pallas_call x1, Pallas kernels, gather(): pl.pallas_call(functools.partial(gather_kernel, sizes=sizes), in_specs=[p...  95.3 us
    pallas_call x1, Pallas kernels, expert(): pl.pallas_call(functools.partial(expert_kernel, experts=experts), grid=(s...  56.3 us
    dot_general x3, matrix products, shards(): jnp.einsum('scd,scf->df', left, right, preferred_element_type=full)[None]  29.9 us
  transfers between devices with their start and end apart: 1, of which 0 were waited for; matrix products, arithmetic and copies ran while one was open for 6% of the time, Pallas kernels for 15%

profile of v3, /device:TPU:14, one launch (start us, length us, event | category | flops | bytes accessed | tf_op | source)
XLA Modules:
  0.0 1042.8 jit_solution(12797308080273358670)
XLA Ops:
  6.4 2.1 convert_element_type.107.back_ref
  9.6 95.3 %shard_map.263 = (bf16[4,256,2048]{2,1,0:T(8,128)(2,1)}, bf16[4,4,2,64,1408]{4,3,2,1,0:T(8,128)(2,1)}, bf16[4,2,128,2048]{3,2,1,0:T(8,128)(2,1)}, s32[4,256,8]{2,1,0:T(8,128)}) custom-call(bf16[256,2048]{1,0:T(8,128)(2,1)} %bitcast.96, bf16[4,64,1408]{2,1,0:T(8,128)(2,1)} %pad_maximum_fusion.front_ref, bf16[128,2048]{1,0:T(8,128)(2,1)} %convert_element_type.107.back_ref, ...), custom_call_target="tpu_custom_call" | custom-call | tf_op jit(solution)/shard_map/pallas_call | solution.py:1140
  106.3 2.4 convert_reduce_fusion
  111.0 2.7 fusion.10
  114.6 1.9 fusion.2.pick_ref
  118.1 2.8 eq.68
  120.9 6.0 copy.51
  128.6 12.4 %shard_map.264 = (bf16[1024,2048]{1,0:T(8,128)(2,1)}, f32[1024,1280]{1,0:T(8,128)}, bf16[1024,1280]{1,0:T(8,128)(2,1)}) custom-call(bf16[1024,2048]{1,0:T(8,128)(2,1)} %bitcast.132, f32[1,2048]{1,0:T(1,128)} %bitcast.126, bf16[2048,1408]{1,0:T(8,128)(2,1)} %bitcast.118, f32[2,128]{1,0:T(2,128)} %maximum_convert_fusion.scale_ref, ...), custom_call_target="tpu_custom_call" | custom-call | flops 5368709120 | bytes 31457280 | tf_op jit(solution)/shard_map/pallas_call | solution.py:58
  140.9 20.6 %shard_map.265.attended_ref = bf16[1024,1024]{1,0:T(8,128)(2,1)} custom-call(s32[1,2]{1,0:T(1,128)} %bounds_ref.3, bf16[1024,1280]{1,0:T(8,128)(2,1)} %get-tuple-element.46.query_ref.key_ref.value_ref, bf16[1024,1280]{1,0:T(8,128)(2,1)} %get-tuple-element.46.query_ref.key_ref.value_ref, bf16[1024,1280]{1,0:T(8,128)(2,1)} %get-tuple-element.46.query_ref.key_ref.value_ref), custom_call_target="tpu_custom_call" | custom-call | flops 2147483648 | bytes 6291456 | tf_op jit(solution)/shard_map/pallas_call | solution.py:117
  161.6 4.2 compare_convert_fusion.pick_ref
  165.8 283.1 %shard_map.266 = (bf16[8,288,2048]{2,1,0:T(8,128)(2,1)}, bf16[8,288,2048]{2,1,0:T(8,128)(2,1)}, bf16[8,288,128]{2,1,0:T(8,128)(2,1)}, f32[256,2048]{1,0:T(8,128)}, f32[256,128]{1,0:T(8,128)}) custom-call(bf16[1024,1024]{1,0:T(8,128)(2,1)} %shard_map.265.attended_ref, bf16[1024,2048]{1,0:T(8,128)(2,1)} %bitcast.102, bf16[256,2048]{1,0:T(8,128)(2,1)} %bitcast.97, ...), custom_call_target="tpu_custom_call" | custom-call | tf_op jit(solution)/shard_map/pallas_call | solution.py:694
  448.8 56.3 %shard_map.267 = (bf16[8,288,768]{2,1,0:T(8,128)(2,1)}, bf16[8,288,768]{2,1,0:T(8,128)(2,1)}, bf16[8,288,768]{2,1,0:T(8,128)(2,1)}, bf16[8,288,2048]{2,1,0:T(8,1...) custom-call(s32[1]{0:T(128)} %bitcast.10.here_ref, ...), custom_call_target="tpu_custom_call" | custom-call | flops 43486543872 | bytes 62914560 | tf_op jit(solution)/shard_map/pallas_call | solution.py:944
  505.1 165.1 %shard_map.268 = (bf16[8,288,2048]{2,1,0:T(8,128)(2,1)}, bf16[4,256,2048]{2,1,0:T(8,128)(2,1)}, f32[256,2048]{1,0:T(8,128)}, f32[1,2048]{1,0:T(1,128)}, f32[128,2048]{1,0:T(8,128)}) custom-call(bf16[8,288,2048]{2,1,0:T(8,128)(2,1)} %get-tuple-element.52.rows_ref, bf16[8,288,128]{2,1,0:T(8,128)(2,1)} %get-tuple-element.53.dots_ref, ...), custom_call_target="tpu_custom_call", output_to_operand_aliasing={{0}: (3, {})} | custom-call | tf_op jit(solution)/shard_map/pallas_call | solution.py:870
  670.2 6.8 all-to-all-start
  677.1 8.5 convolution_convert_fusion.1
  685.5 5.8 convolution_convert_fusion.2.grad_ref
  691.3 152.3 %shard_map.269 = (bf16[1024,1280]{1,0:T(8,128)(2,1)}, f32[2,128]{1,0:T(2,128)}, f32[128,2048]{1,0:T(8,128)}) custom-call(s32[1,2]{1,0:T(1,128)} %bounds_ref.3, bf16[1024,1280]{1,0:T(8,128)(2,1)} %get-tuple-element.46.query_ref.key_ref.value_ref, bf16[1024,1280]{1,0:T(8,128)(2,1)} %get-tuple-element.46.query_ref.key_ref.value_ref, ...), custom_call_target="tpu_custom_call" | custom-call | flops 5368709120 | bytes 12582912 | tf_op jit(solution)/shard_map/pallas_call | solution.py:335
  848.7 10.4 fusion.3
  859.2 7.5 convolution_convert_fusion
  866.8 9.7 convolution_bitcast_fusion
  876.5 9.9 convolution_bitcast_fusion.1
  886.4 10.3 convolution_bitcast_fusion.2
  896.7 134.1 %shard_map.270 = (bf16[256,2048]{1,0:T(8,128)(2,1)}, f32[4,64,1280]{2,1,0:T(8,128)}, bf16[256,2048]{1,0:T(8,128)(2,1)}, f32[8,384]{1,0:T(8,128)}) custom-call(bf16[4,256,2048]{2,1,0:T(8,128)(2,1)} %bitcast.104, bf16[4,4,2,64,1280]{4,3,2,1,0:T(8,128)(2,1)} %bitcast.99, f32[256,2048]{1,0:T(8,128)} %get-tuple-element.61.middle_ref, bf16[256,2048]{1,0:T(8,128)(2,1)} %bitcast.98, ...), custom_call_target="tpu_custom_call" | custom-call | tf_op jit(solution)/shard_map/pallas_call | solution.py:1377
  1038.3 2.3 copy.77
  (108 shorter events, 29.1 us)
Async XLA Ops:
  0.6 7.9 copy-start.6
  0.7 7.9 copy-start.7
  6.4 103.6 %copy-start.2 = (s32[1,256,8]{2,1,0:T(8,128)S(1)}, s32[1,256,8]{2,1,0:T(8,128)}, u32[]{:S(2)}) copy-start(s32[1,256,8]{2,1,0:T(8,128)} %copy.49) | copy-start | bytes 24580
  104.8 9.1 copy-start.5
  670.2 6.8 copy-start
  670.2 226.5 %all-to-all-start = ((bf16[8,288,2048]{2,1,0:T(8,128)(2,1)}), bf16[8,288,2048]{2,1,0:T(8,128)(2,1)}, u32[]{:S(2)}, u32[]{:S(2)}) async-start(bf16[8,288,2048]{2,1,0:T(8,128)(2,1)} %get-tuple-element.65), calls=%async_computation | async-start | bytes 18874368 | tf_op jit(solution)/shard_map/all_to_all | solution.py:28
  677.0 8.5 copy-start.1
  677.0 8.5 copy-start.9
  691.3 155.6 %copy-start.8 = (f32[1,2048]{1,0:T(1,128)S(1)}, f32[1,2048]{1,0:T(1,128)}, u32[]{:S(2)}) copy-start(f32[1,2048]{1,0:T(1,128)} %get-tuple-element.62) | copy-start | bytes 24580
  848.7 10.4 %copy-start.10 = (bf16[1024,1280]{1,0:T(8,128)(2,1)S(1)}, bf16[1024,1280]{1,0:T(8,128)(2,1)}, u32[]{:S(2)}) copy-start(bf16[1024,1280]{1,0:T(8,128)(2,1)} %get-tuple-element.59) | copy-start | bytes 7864324
  848.7 10.4 %copy-start.11 = (bf16[1024,2048]{1,0:T(8,128)(2,1)S(1)}, bf16[1024,2048]{1,0:T(8,128)(2,1)}, u32[]{:S(2)}) copy-start(bf16[1024,2048]{1,0:T(8,128)(2,1)} %get-tuple-element.60) | copy-start | bytes 12582916
  848.7 18.0 %slice-start.3 = ((s8[9437184]{0:T(1024)(128)(4,1)}), s8[4194304]{0:T(1024)(128)(4,1)S(1)}, s32[]{:S(2)}) async-start(s8[9437184]{0:T(1024)(128)(4,1)} %bitcast.130), calls=%async_computation.4 | async-start | bytes 8388608
  848.7 18.0 %slice-start.4 = ((s8[9437184]{0:T(1024)(128)(4,1)}), s8[4194304]{0:T(1024)(128)(4,1)S(1)}, s32[]{:S(2)}) async-start(s8[9437184]{0:T(1024)(128)(4,1)} %bitcast.130), calls=%async_computation.5 | async-start | bytes 8388608
  859.2 7.6 slice-start.5
  859.2 7.6 copy-start.12
  859.2 17.3 %slice-start = ((s8[9437184]{0:T(1024)(128)(4,1)}), s8[4194304]{0:T(1024)(128)(4,1)S(1)}, s32[]{:S(2)}) async-start(s8[9437184]{0:T(1024)(128)(4,1)} %bitcast.128), calls=%async_computation.1 | async-start | bytes 8388608
  859.2 17.3 %slice-start.1 = ((s8[9437184]{0:T(1024)(128)(4,1)}), s8[4194304]{0:T(1024)(128)(4,1)S(1)}, s32[]{:S(2)}) async-start(s8[9437184]{0:T(1024)(128)(4,1)} %bitcast.128), calls=%async_computation.2 | async-start | bytes 8388608
  866.8 9.7 slice-start.2
  866.8 9.7 copy-start.14
  876.5 9.9 copy-start.13
  1030.8 9.9 copy-start.4
  1032.2 9.5 copy-start.3

commit v4 on v3

--- a/solution.py
+++ b/solution.py
@@ -11,7 +11,6 @@
 rope_base = 1000000.0
 masked_score = -1e30
 ALL = ("dp", "ctx", "exp")
-PLANE = ("ctx", "exp")
 VMEM = 60 << 20
 MESH = pl.DeviceIdType.MESH
 
@@ -22,10 +21,6 @@
     angles = positions.astype(jnp.float32)[:, None] * frequency[None, :]
     angles = jnp.concatenate([angles, angles], axis=-1)
     return (jnp.cos(angles), jnp.sin(angles))
-
-
-def swap(parts, axis):
-    return lax.all_to_all(parts, axis, split_axis=0, concat_axis=0, tiled=True)
 
 
 def project_kernel(x_ref, gain_ref, weight_ref, scale_ref, cos_ref, sin_ref, hidden_ref, raw_ref, out_ref, *, q_heads, kv_heads):
@@ -134,246 +129,6 @@
     )(bounds, turned, turned, turned)
 
 
-def attend_back_kernel(
-    bounds_ref, query_ref, key_ref, value_ref, grad_ref, raw_ref, scale_ref, cos_ref, sin_ref,
-    back_ref, out_ref, gain_ref, back_out, key_sum, value_sum, *back_scratch, block, heads, group,
-    score_scale, sizes,
-):
-    step = pl.program_id(0)
-    rows = query_ref.shape[0]
-    scatter_back(step, heads + 2 * heads // group, back_ref, back_out, back_scratch, sizes)
-    low, full = jnp.bfloat16, jnp.float32
-    kv_heads = heads // group
-
-    def norm_rope_back(grad, raw, scale, cosine, sine):
-        inverse = lax.rsqrt(jnp.mean(raw * raw, axis=-1, keepdims=True) + eps_norm)
-        normed = raw * inverse
-        turned = grad * cosine + pltpu.roll(grad * sine, grad.shape[-1] // 2, 1)
-        inner = turned * scale
-        back = inverse * (inner - normed * jnp.mean(inner * normed, axis=-1, keepdims=True))
-        return back, jnp.sum(turned * normed, axis=0, keepdims=True)
-
-    @pl.when(step == 0)
-    def _():
-        gain_ref[...] = jnp.zeros_like(gain_ref)
-
-    @pl.when(lax.rem(step, group) == 0)
-    def _():
-        @pl.when(step < heads)
-        def _():
-            for kv in range(kv_heads):
-                @pl.when(step == kv * group)
-                def _():
-                    key_sum[kv] = jnp.zeros((rows, key_ref.shape[1]), full)
-                    value_sum[kv] = jnp.zeros((rows, key_ref.shape[1]), full)
-
-    @pl.when(step < heads)
-    def _():
-        kv = jnp.minimum(step // group, kv_heads - 1)
-        gains = jnp.zeros((1, query_ref.shape[1]), full)
-        for first in range(0, rows, block):
-            last = first + block
-            query, keys, values = query_ref[first:last, :], key_ref[:last, :], value_ref[:last, :]
-            grad = grad_ref[first:last, :]
-            allowed = seen(bounds_ref, first, block, last)
-            shares = shares_of(query, keys, allowed, score_scale)
-            share_grads = lax.dot_general(
-                grad, values, (((1,), (1,)), ((), ())), preferred_element_type=full
-            )
-            centre = jnp.sum(shares * share_grads, axis=-1, keepdims=True)
-            score_grads = (shares * (share_grads - centre)).astype(low)
-            key_sum[kv, :last, :] += lax.dot_general(
-                score_grads, query, (((0,), (0,)), ((), ())), preferred_element_type=full
-            )
-            value_sum[kv, :last, :] += lax.dot_general(
-                shares.astype(low), grad, (((0,), (0,)), ((), ())), preferred_element_type=full
-            )
-            query_grad = jnp.dot(score_grads, keys, preferred_element_type=full) * score_scale
-            back, gain = norm_rope_back(
-                query_grad, raw_ref[first:last, :], scale_ref[0:1, :], cos_ref[first:last, :],
-                sin_ref[first:last, :],
-            )
-            out_ref[first:last, :] = back.astype(low)
-            gains += gain
-        gain_ref[0:1, :] += gains
-
-    @pl.when((step >= heads) & (step < heads + kv_heads))
-    def _():
-        back, gain = norm_rope_back(
-            key_sum[step - heads] * score_scale, raw_ref[...], scale_ref[1:2, :], cos_ref[...],
-            sin_ref[...],
-        )
-        out_ref[...] = back.astype(low)
-        gain_ref[1:2, :] += gain
-
-    @pl.when(step >= heads + kv_heads)
-    def _():
-        out_ref[...] = value_sum[step - heads - kv_heads].astype(low)
-
-
-def scatter_back(step, steps, back_ref, back_out, scratch, sizes):
-    (
-        pairs, total, arrived, leaving, landing, own_sem, pair_send, pair_recv, across_send,
-        across_recv, line_send, line_recv,
-    ) = scratch
-    n, n_ctx, n_exp = sizes["dp"], sizes["ctx"], sizes["exp"]
-    z, c, k = (lax.axis_index(a) for a in ALL)
-    full, low = jnp.float32, jnp.bfloat16
-
-    def remote(source, target, send, recv, device):
-        return pltpu.make_async_remote_copy(
-            src_ref=source, dst_ref=target, send_sem=send, recv_sem=recv, device_id=device,
-            device_id_type=MESH,
-        )
-
-    def pair(ahead):
-        target = lax.rem(k + ahead, n_exp)
-        return remote(
-            back_ref.at[:, target], pairs.at[ahead], pair_send.at[ahead], pair_recv.at[ahead],
-            {"exp": target},
-        )
-
-    def across(ahead):
-        target = lax.rem(c + ahead, n_ctx)
-        return remote(
-            total.at[target], arrived.at[c], across_send.at[ahead], across_recv.at[ahead],
-            {"ctx": target},
-        )
-
-    def line(target, way):
-        return remote(
-            leaving.at[target], landing.at[target + (way + 1) // 2], line_send.at[target],
-            line_recv.at[target + (way + 1) // 2], {"dp": z + way},
-        )
-
-    def in_line(index):
-        return (index >= 0) & (index < n)
-
-    own = pltpu.make_async_copy(back_ref.at[:, k], pairs.at[0], own_sem.at[0])
-
-    @pl.when(step == 0)
-    def _():
-        greet(sizes)
-        own.start()
-        for ahead in range(1, n_exp):
-            pair(ahead).start()
-
-    @pl.when(step == 1)
-    def _():
-        own.wait()
-        for ahead in range(1, n_exp):
-            pair(ahead).wait_recv()
-        for group in range(n_ctx):
-            summed = pairs[0, group].astype(full)
-            for ahead in range(1, n_exp):
-                summed = summed + pairs[ahead, group].astype(full)
-            total[group] = summed.astype(low)
-        for ahead in range(1, n_ctx):
-            across(ahead).start()
-        arrived[c] = total[c]
-
-    for distance in range(n - 1, 0, -1):
-        @pl.when(step == min(2 + 3 * (n - 1 - distance), steps - 2))
-        def _():
-            if distance == n - 1:
-                for ahead in range(1, n_ctx):
-                    across(ahead).wait_recv()
-            for way in (-1, 1):
-                target = z + way * distance
-
-                @pl.when(in_line(target))
-                def _():
-                    @pl.when(in_line(z - way))
-                    def _():
-                        line(target, way).wait_recv()
-                        leaving[target] = (
-                            arrived[target].astype(full)
-                            + landing[target + (way + 1) // 2].astype(full)
-                        ).astype(low)
-
-                    @pl.when(jnp.logical_not(in_line(z - way)))
-                    def _():
-                        leaving[target] = arrived[target]
-
-                    line(target, way).start()
-
-    @pl.when(step == steps - 1)
-    def _():
-        back_out[...] = arrived[z].astype(full)
-        for way in (-1, 1):
-            @pl.when(in_line(z - way))
-            def _():
-                line(z, way).wait_recv()
-                back_out[...] += landing[z + (way + 1) // 2].astype(full)
-
-        for ahead in range(1, n_exp):
-            pair(ahead).wait_send()
-        for ahead in range(1, n_ctx):
-            across(ahead).wait_send()
-        for distance in range(1, n):
-            for way in (-1, 1):
-                target = z + way * distance
-
-                @pl.when(in_line(target))
-                def _():
-                    line(target, way).wait_send()
-
-
-def attend_back(
-    bounds, turned, grad, raw, scales, cosine, sine, back, heads, kv_heads, head, block, sizes,
-    collective,
-):
-    n, n_ctx, n_exp = sizes["dp"], sizes["ctx"], sizes["exp"]
-    b_rows, b_width = back.shape[2:]
-    piece = lambda *lead: pltpu.VMEM(lead + (b_rows, b_width), jnp.bfloat16)
-    dma = lambda *shape: pltpu.SemaphoreType.DMA(shape)
-    rows = turned.shape[0]
-    group = heads // kv_heads
-    columns = turned.shape[1]
-    within = lambda h: jnp.minimum(h, heads - 1)
-    tables = pl.BlockSpec((rows, head), lambda h: (0, 0))
-    return pl.pallas_call(
-        functools.partial(
-            attend_back_kernel, block=block, heads=heads, group=group, score_scale=head ** (-0.5),
-            sizes=sizes,
-        ),
-        grid=(heads + 2 * kv_heads,),
-        in_specs=[
-            pl.BlockSpec(memory_space=pltpu.SMEM),
-            pl.BlockSpec((rows, head), lambda h: (0, within(h))),
-            pl.BlockSpec((rows, head), lambda h: (0, heads + within(h) // group)),
-            pl.BlockSpec((rows, head), lambda h: (0, heads + kv_heads + within(h) // group)),
-            pl.BlockSpec((rows, head), lambda h: (0, within(h))),
-            pl.BlockSpec((rows, head), lambda h: (0, jnp.minimum(h, heads + kv_heads - 1))),
-            pl.BlockSpec((2, head), lambda h: (0, 0)),
-            tables,
-            tables,
-            pl.BlockSpec(memory_space=pl.ANY),
-        ],
-        out_specs=[
-            pl.BlockSpec((rows, head), lambda h: (0, h)),
-            pl.BlockSpec((2, head), lambda h: (0, 0)),
-            pl.BlockSpec((b_rows, b_width), lambda h: (0, 0)),
-        ],
-        out_shape=[
-            jax.ShapeDtypeStruct((rows, columns), jnp.bfloat16),
-            jax.ShapeDtypeStruct((2, head), jnp.float32),
-            jax.ShapeDtypeStruct((b_rows, b_width), jnp.float32),
-        ],
-        scratch_shapes=[pltpu.VMEM((kv_heads, rows, head), jnp.float32)] * 2
-        + [piece(n_exp, n_ctx), piece(n_ctx), piece(n_ctx), piece(n), piece(n + 1)]
-        + [dma(1), dma(n_exp), dma(n_exp), dma(n_ctx), dma(n_ctx), dma(n), dma(n + 1)],
-        compiler_params=pltpu.CompilerParams(
-            collective_id=collective, has_side_effects=True, vmem_limit_bytes=VMEM
-        ),
-        cost_estimate=pl.CostEstimate(
-            flops=5 * heads * rows * rows * head,
-            bytes_accessed=12 << 20,
-            transcendentals=heads * rows * rows // 2,
-        ),
-    )(bounds, turned, turned, turned, grad, raw, scales, cosine, sine, back)
-
-
 def square(sizes):
     me = lax.axis_index("ctx")
     return me + 1 - 2 * lax.rem(me, 2), lax.rem(me + 2, 4)
@@ -429,9 +184,9 @@
 
 
 class SquareScatter:
-    def __init__(self, sizes, parts, far_in, turn_out, turn_in, send, recv):
+    def __init__(self, sizes, parts, far_in, turn_out, turn_in, send, recv, rows):
         self.parts, self.far_in, self.turn_out, self.turn_in = parts, far_in, turn_out, turn_in
-        self.send, self.recv = send, recv
+        self.send, self.recv, self.rows = send, recv, pl.ds(0, rows)
         self.me = lax.axis_index("ctx")
         self.by = square(sizes)
         self.far = sizes["ctx"] - 1 - self.me
@@ -442,7 +197,7 @@
         place = self.by[side] if number == 0 else self.far
         index = 2 * side + number
         return remote(
-            self.parts.at[place, :, self.columns[side]], self.far_in.at[side, number],
+            self.parts.at[place, self.rows, self.columns[side]], self.far_in.at[side, number],
             self.send.at[index], self.recv.at[index], {"ctx": self.by[side]},
         )
 
@@ -459,7 +214,7 @@
     def turn(self):
         for side in (0, 1):
             self.first(side, 1).wait_recv()
-            own = self.parts[self.by[1 - side], :, self.columns[side]].astype(jnp.float32)
+            own = self.parts[self.by[1 - side], self.rows, self.columns[side]].astype(jnp.float32)
             self.turn_out[side] = (own + self.far_in[side, 1].astype(jnp.float32)).astype(
                 jnp.bfloat16
             )
@@ -470,7 +225,7 @@
             self.first(side, 0).wait_recv()
             self.second(side).wait_recv()
             total[:, self.columns[side]] = (
-                self.parts[self.me, :, self.columns[side]].astype(jnp.float32)
+                self.parts[self.me, self.rows, self.columns[side]].astype(jnp.float32)
                 + self.far_in[side, 0].astype(jnp.float32)
                 + self.turn_in[side].astype(jnp.float32)
             )
@@ -618,7 +373,9 @@
     columns[0][me] = cot_ref[...]
     send_own(0)
 
-    scatter = SquareScatter(sizes, branch, far_in, turn_out, turn_in, sq_send, sq_recv)
+    scatter = SquareScatter(
+        sizes, branch, far_in, turn_out, turn_in, sq_send, sq_recv, tokens
+    )
 
     def project_block(place):
         branch[place] = jnp.dot(
@@ -722,8 +479,9 @@
 
 
 def combine_kernel(
-    rows_ref, dots_ref, pick_ref, carried_ref, middle_ref, cot_ref, gain_ref, gates_ref, router_ref,
-    carried_out, whole_ref, middle_grad_ref, gain_grad_ref, router_grad_ref,
+    rows_ref, dots_ref, pick_ref, middle_ref, cot_ref, gain_ref, gates_ref, router_ref,
+    in_ref, grad_ref, active_ref, gate_ref, up_ref,
+    whole_ref, middle_grad_ref, gain_grad_ref, router_grad_ref, gate_out, up_out, down_out,
     back_rows, back_dots, leave_rows, leave_dots, land_rows, land_dots, total_rows, total_dots,
     sums, branch, line_send, line_recv, plane_send, plane_recv, own_sem, sq_send, sq_recv, sq_own,
     *, sizes, pieces, experts,
@@ -734,8 +492,7 @@
     n, number = sizes["dp"], sizes["ctx"] * sizes["exp"]
     me, here = lax.axis_index("dp"), plane_index(sizes)
     tokens = middle_ref.shape[0]
-    groups, span, _ = pick_ref.shape
-    rows = rows_ref.shape[1] // groups
+    groups, _, rows, span = pick_ref.shape
     full, low = jnp.float32, jnp.bfloat16
     greet(sizes)
 
@@ -773,15 +530,49 @@
             {"dp": me + step},
         )
 
+    inner, chunk = active_ref.shape[1], 256
+    slots = in_ref.shape[0]
+
+    def weight_sum(left, right, out, by_left):
+        def body(left_ref, right_ref, out_ref):
+            out_ref[...] = lax.dot_general(
+                left_ref[...], right_ref[...], (((0,), (0,)), ((), ())), preferred_element_type=full
+            )
+
+        if by_left:
+            grid = left.shape[1] // chunk
+            specs = [
+                pl.BlockSpec((slots, chunk), lambda i: (0, i)),
+                pl.BlockSpec((slots, inner), lambda i: (0, 0)),
+            ]
+            out_spec = pl.BlockSpec((chunk, inner), lambda i: (i, 0))
+        else:
+            grid = right.shape[1] // chunk
+            specs = [
+                pl.BlockSpec((slots, inner), lambda i: (0, 0)),
+                pl.BlockSpec((slots, chunk), lambda i: (0, i)),
+            ]
+            out_spec = pl.BlockSpec((inner, chunk), lambda i: (0, i))
+        pltpu.emit_pipeline(body, grid=(grid,), in_specs=specs, out_specs=[out_spec])(
+            left, right, out
+        )
+
     for f, (a, first, part) in enumerate(pieces):
         columns = pl.ds(first, part)
+        if f == 1:
+            weight_sum(in_ref, gate_ref, gate_out, True)
+        elif f == 2:
+            weight_sum(in_ref, up_ref, up_out, True)
+        elif f == 3:
+            weight_sum(active_ref, grad_ref, down_out, False)
         for ahead in range(1, number):
             plane_copy(f, ahead).wait_recv()
         own_copy(f).wait()
         for g in range(groups):
             gathered = back[a][:, pl.ds(g * rows, rows), columns].reshape(number * rows, part)
-            sums[pl.ds(g * span // tokens, span // tokens), :, pl.ds(0, part)] = jnp.dot(
-                pick_ref[g], gathered, preferred_element_type=full
+            sums[pl.ds(g * span // tokens, span // tokens), :, pl.ds(0, part)] = lax.dot_general(
+                pick_ref[g].reshape(number * rows, span), gathered, (((0,), (0,)), ((), ())),
+                preferred_element_type=full,
             ).reshape(span // tokens, tokens, part)
 
         for distance in range(n - 1, 0, -1):
@@ -855,11 +646,16 @@
     collect.finish()
 
 
-def combine(rows, dots, pick, carried, middle, cot, gain, gates, router, experts, sizes, collective, part=512):
+def combine(
+    rows, dots, pick, middle, cot, gain, gates, router, rows_in, grads_in, active, gate_grad,
+    up_grad, experts, sizes, collective, part=512,
+):
     number, back_rows, width = rows.shape
     extra = dots.shape[2]
     tokens = middle.shape[0]
     lanes = router.shape[1]
+    inner = active.shape[2]
+    flat = lambda v: v.reshape(-1, v.shape[2])
     n, n_ctx = sizes["dp"], sizes["ctx"]
     low, full = jnp.bfloat16, jnp.float32
     pieces = cut([extra, width], part)
@@ -869,16 +665,17 @@
     dma = lambda *shape: pltpu.SemaphoreType.DMA(shape)
     return pl.pallas_call(
         functools.partial(combine_kernel, sizes=sizes, pieces=pieces, experts=experts),
-        in_specs=[anywhere, anywhere, vmem, anywhere] + [vmem] * 5,
-        out_specs=[anywhere, anywhere] + [vmem] * 3,
+        in_specs=[anywhere, anywhere] + [vmem] * 6 + [anywhere] * 5,
+        out_specs=[anywhere] + [vmem] * 3 + [anywhere] * 3,
         out_shape=[
-            jax.ShapeDtypeStruct(carried.shape, carried.dtype),
             jax.ShapeDtypeStruct((n_ctx, tokens, width), low),
             jax.ShapeDtypeStruct((tokens, width), full),
             jax.ShapeDtypeStruct((1, width), full),
             jax.ShapeDtypeStruct((lanes, width), full),
+            jax.ShapeDtypeStruct((width, inner), full),
+            jax.ShapeDtypeStruct((width, inner), full),
+            jax.ShapeDtypeStruct((inner, width), full),
         ],
-        input_output_aliases={3: 0},
         scratch_shapes=[pltpu.VMEM((number, back_rows, w), low) for w in both]
         + [pltpu.VMEM((n, tokens, w), low) for w in both]
         + [pltpu.VMEM((n + 1, tokens, w), low) for w in both]
@@ -892,7 +689,10 @@
         compiler_params=pltpu.CompilerParams(
             collective_id=collective, has_side_effects=True, vmem_limit_bytes=VMEM
         ),
-    )(rows, dots, pick, carried, middle, cot, gain, gates, router)
+    )(
+        rows, dots, pick, middle, cot, gain, gates, router, flat(rows_in), flat(grads_in),
+        flat(active), flat(gate_grad), flat(up_grad),
+    )
 
 
 def expert_kernel(
@@ -1055,23 +855,15 @@
         token_copy(c, part, to_y, number).start()
     for copy in own_copies:
         copy.wait()
-    for step in (-1, 1):
-        @pl.when(in_line(step))
-        def _():
-            back_line(z, step).start()
-            route_line(z, step).start()
-    for ahead in range(1, n_ctx):
-        front_across(ahead).wait_recv()
-    for step in (-1, 1):
-        @pl.when(in_line(step))
-        def _():
-            front_line(z, step).start()
-    for ahead in range(1, n_exp):
-        front_pair(z, ahead).start()
-    token_copy(by_x, 0, False, 0).wait_recv()
-    token_copy(by_x, 0, True, 4).start()
-    token_copy(by_y, 1, True, 1).wait_recv()
-    token_copy(by_y, 1, False, 5).start()
+
+    def start_line(line):
+        for step in (-1, 1):
+            @pl.when(in_line(step))
+            def _():
+                line(z, step).start()
+
+    start_line(back_line)
+    start_line(route_line)
 
     def pass_on(line, origin, step, after):
         @pl.when((origin >= 0) & (origin < n))
@@ -1084,17 +876,26 @@
 
             after(origin)
 
+    def nothing(origin):
+        pass
+
     def to_siblings(origin):
         for ahead in range(1, n_exp):
             front_pair(origin, ahead).start()
 
+    for ahead in range(1, n_ctx):
+        front_across(ahead).wait_recv()
+    to_siblings(z)
     for distance in range(1, n):
         for step in (-1, 1):
-            pass_on(front_line, z - step * distance, step, to_siblings)
-            pass_on(route_line, z - step * distance, step, lambda origin: None)
-    for distance in range(1, n):
-        for step in (-1, 1):
-            pass_on(back_line, z - step * distance, step, lambda origin: None)
+            pass_on(back_line, z - step * distance, step, nothing)
+        if distance == 1:
+            token_copy(by_x, 0, False, 0).wait_recv()
+            token_copy(by_x, 0, True, 4).start()
+            token_copy(by_y, 1, True, 1).wait_recv()
+            token_copy(by_y, 1, False, 5).start()
+        if distance == max(1, n - 2):
+            start_line(front_line)
     for ahead in range(1, n_ctx):
         back_across(ahead).start()
     own_back = pltpu.make_async_copy(held.at[c], backs_ref.at[c, k], own_sem.at[4])
@@ -1102,6 +903,10 @@
     own_back.wait()
     for ahead in range(1, n_exp):
         back_pair(c, ahead).start()
+    for distance in range(1, n):
+        for step in (-1, 1):
+            pass_on(front_line, z - step * distance, step, to_siblings)
+            pass_on(route_line, z - step * distance, step, nothing)
     for behind in range(1, n_ctx):
         back_across(behind).wait_recv()
         source = lax.rem(c + n_ctx - behind, n_ctx)
@@ -1160,151 +965,348 @@
     )(tokens, front, back, routes)
 
 
-def scatter_kernel(
-    hidden_ref, front_ref, middle_ref, token_ref, gain_ref, small_ref, sent_ref, pick_ref,
-    result_ref, tokens_grad_ref, front_out, output_ref, small_out,
-    far_in, turn_out, turn_in, hidden_sum, front_pairs, front_sum, front_line_in, front_low, front_in,
-    rows_in, mix_out, mix_in, small_all, small_in,
-    h_send, h_recv, fp_send, fp_recv, fl_send, fl_recv, fa_send, fa_recv,
-    m_load, ml_send, ml_recv, s_send, s_recv, *, sizes, part,
+def finish_kernel(
+    bounds_ref, query_ref, key_ref, value_ref, grad_ref, raw_ref, scale_ref, cos_ref, sin_ref,
+    hidden_ref, weight_ref, back_ref, rows_ref, pick_ref, result_ref, middle_ref, token_ref,
+    gain_ref, small_ref,
+    tokens_grad_ref, front_out, output_ref, back_out, small_out, landed_ref, back_in,
+    key_sum, value_sum, raw_grad, head_gains, shared, arrived, back_one, fronts, front_pairs,
+    front_in, rows_in, leaving, landing, far_in, turn_out, turn_in, hidden_send, hidden_recv,
+    total, loaded, staged, small_all, small_in,
+    own_sem, load_sem, stage_sem, bp_send, bp_recv, ba_send, ba_recv, bl_send, bl_recv,
+    fp_send, fp_recv, fl_send, fl_recv, fa_send, fa_recv, plane_send, plane_recv, plane_own,
+    line_send, line_recv, s_send, s_recv, *, block, heads, group, score_scale, sizes, part, chunk,
 ):
+    step = pl.program_id(0)
+    rows, head = query_ref.shape
+    low, full = jnp.bfloat16, jnp.float32
+    kv_heads = heads // group
+    first_chunk = heads + 2 * kv_heads
     n, n_ctx, n_exp = sizes["dp"], sizes["ctx"], sizes["exp"]
-    devices = n * n_ctx * n_exp
+    devices, number = n * n_ctx * n_exp, n_ctx * n_exp
     z, c, k = (lax.axis_index(a) for a in ALL)
-    here = (z * n_ctx + c) * n_exp + k
+    here, in_plane = (z * n_ctx + c) * n_exp + k, plane_index(sizes)
     tokens, width = token_ref.shape
-    full, low = jnp.float32, jnp.bfloat16
-
-    barrier = pltpu.get_barrier_semaphore()
+    b_rows = back_out.shape[0]
+    pieces = width // part
+    chunks = width // chunk
+
+    def in_line(index):
+        return (index >= 0) & (index < n)
 
     def device_of(index):
         return {
-            "dp": index // (n_ctx * n_exp),
+            "dp": index // number,
             "ctx": lax.rem(index // n_exp, n_ctx),
             "exp": lax.rem(index, n_exp),
         }
 
-    @pl.loop(1, devices)
-    def _(ahead):
-        pl.semaphore_signal(
-            barrier, inc=1, device_id=device_of(lax.rem(here + ahead, devices)),
-            device_id_type=MESH,
-        )
-
-    pl.semaphore_wait(barrier, devices - 1)
-
-    def in_line(step):
-        return (z + step >= 0) & (z + step < n)
-
-    hidden = SquareScatter(sizes, hidden_ref, far_in, turn_out, turn_in, h_send, h_recv)
+    def back_own():
+        return pltpu.make_async_copy(
+            back_ref.at[:, k], shared.at[:, pl.ds(0, b_rows)], own_sem.at[0]
+        )
+
+    def back_pair(ahead):
+        target = lax.rem(k + ahead, n_exp)
+        return remote(
+            back_ref.at[:, target], shared.at[:, pl.ds(ahead * b_rows, b_rows)],
+            bp_send.at[ahead], bp_recv.at[ahead], {"exp": target},
+        )
+
+    def back_across(ahead):
+        target = lax.rem(c + ahead, n_ctx)
+        return remote(
+            shared.at[target, pl.ds(0, b_rows)], arrived.at[c], ba_send.at[ahead],
+            ba_recv.at[ahead], {"ctx": target},
+        )
+
+    def back_line(target, way):
+        return remote(
+            arrived.at[target], back_in.at[target + (way + 1) // 2], bl_send.at[target],
+            bl_recv.at[target + (way + 1) // 2], {"dp": z + way},
+        )
+
+    def along_line(line, add, distance):
+        for way in (-1, 1):
+            target = z + way * distance
+
+            @pl.when(in_line(target))
+            def _():
+                @pl.when(in_line(z - way))
+                def _():
+                    line(target, way).wait_recv()
+                    add(target, target + (way + 1) // 2)
+
+                line(target, way).start()
+
+    def end_line(line, add):
+        for way in (-1, 1):
+            @pl.when(in_line(z - way))
+            def _():
+                line(z, way).wait_recv()
+                add((way + 1) // 2 + z)
+
+    def close_line(line):
+        for distance in range(1, n):
+            for way in (-1, 1):
+                @pl.when(in_line(z + way * distance))
+                def _():
+                    line(z + way * distance, way).wait_send()
+
+    def back_arrived(slot):
+        copy = pltpu.make_async_copy(back_in.at[slot], back_one, stage_sem.at[1])
+        copy.start()
+        copy.wait()
+        return back_one[...].astype(full)
+
+    def add_back(target, slot):
+        arrived[target] = (arrived[target].astype(full) + back_arrived(slot)).astype(low)
+
+    def plane_copy(piece, ahead):
+        target = peer(sizes, ahead)
+        columns = pl.ds(piece * part, part)
+        return remote(
+            rows_ref.at[target, :, columns], landed_ref.at[in_plane, :, columns],
+            plane_send.at[piece, ahead], plane_recv.at[piece, ahead], place(sizes, target),
+        )
+
+    def plane_own_copy(piece):
+        columns = pl.ds(piece * part, part)
+        return pltpu.make_async_copy(
+            rows_ref.at[in_plane, :, columns], landed_ref.at[in_plane, :, columns],
+            plane_own.at[piece],
+        )
+
+    def push(piece):
+        for ahead in range(number - 1, 0, -1):
+            plane_copy(piece, ahead).start()
+        plane_own_copy(piece).start()
+
+    def small_load():
+        return pltpu.make_async_copy(small_ref, small_all, own_sem.at[1])
+
+    @pl.when(step == 0)
+    def _():
+        head_gains[...] = jnp.zeros_like(head_gains)
+        barrier = pltpu.get_barrier_semaphore()
+
+        @pl.loop(1, devices)
+        def _(ahead):
+            pl.semaphore_signal(
+                barrier, inc=1, device_id=device_of(lax.rem(here + ahead, devices)),
+                device_id_type=MESH,
+            )
+
+        pl.semaphore_wait(barrier, devices - 1)
+        back_own().start()
+        for ahead in range(1, n_exp):
+            back_pair(ahead).start()
+        small_load().start()
+
+    @pl.when(step == 1)
+    def _():
+        back_own().wait()
+        for ahead in range(1, n_exp):
+            back_pair(ahead).wait_recv()
+        for index in range(n_ctx):
+            summed = shared[index, 0:b_rows].astype(full)
+            for ahead in range(1, n_exp):
+                summed = summed + shared[index, ahead * b_rows : (ahead + 1) * b_rows].astype(full)
+            shared[index, 0:b_rows] = summed.astype(low)
+        for ahead in range(1, n_ctx):
+            back_across(ahead).start()
+        arrived[c] = shared[c, 0:b_rows]
+        for piece in range(pieces):
+            push(piece)
+        small_load().wait()
+
+    for distance in range(n - 1, 0, -1):
+        @pl.when(step == min(6 + 3 * (n - 1 - distance), first_chunk + chunks - 2))
+        def _():
+            if distance == n - 1:
+                for ahead in range(1, n_ctx):
+                    back_across(ahead).wait_recv()
+                    back_across(ahead).wait_send()
+                for ahead in range(1, n_exp):
+                    back_pair(ahead).wait_send()
+            along_line(back_line, add_back, distance)
+
+    def norm_rope_back(grad, raw, scale, cosine, sine):
+        inverse = lax.rsqrt(jnp.mean(raw * raw, axis=-1, keepdims=True) + eps_norm)
+        normed = raw * inverse
+        turned = grad * cosine + pltpu.roll(grad * sine, grad.shape[-1] // 2, 1)
+        inner = turned * scale
+        back = inverse * (inner - normed * jnp.mean(inner * normed, axis=-1, keepdims=True))
+        return back, jnp.sum(turned * normed, axis=0, keepdims=True)
+
+    for kv in range(kv_heads):
+        @pl.when(step == kv * group)
+        def _():
+            key_sum[kv] = jnp.zeros((rows, head), full)
+            value_sum[kv] = jnp.zeros((rows, head), full)
+
+    here_columns = pl.ds(pl.multiple_of(step * head, head), head)
+
+    @pl.when(step < heads)
+    def _():
+        kv = step // group
+        gains = jnp.zeros((1, head), full)
+        for first in range(0, rows, block):
+            last = first + block
+            query, keys, values = query_ref[first:last, :], key_ref[:last, :], value_ref[:last, :]
+            grad = grad_ref[first:last, :]
+            allowed = seen(bounds_ref, first, block, last)
+            shares = shares_of(query, keys, allowed, score_scale)
+            share_grads = lax.dot_general(
+                grad, values, (((1,), (1,)), ((), ())), preferred_element_type=full
+            )
+            centre = jnp.sum(shares * share_grads, axis=-1, keepdims=True)
+            score_grads = (shares * (share_grads - centre)).astype(low)
+            key_sum[kv, :last, :] += lax.dot_general(
+                score_grads, query, (((0,), (0,)), ((), ())), preferred_element_type=full
+            )
+            value_sum[kv, :last, :] += lax.dot_general(
+                shares.astype(low), grad, (((0,), (0,)), ((), ())), preferred_element_type=full
+            )
+            query_grad = jnp.dot(score_grads, keys, preferred_element_type=full) * score_scale
+            back, gain = norm_rope_back(
+                query_grad, raw_ref[first:last, :], scale_ref[0:1, :], cos_ref[first:last, :],
+                sin_ref[first:last, :],
+            )
+            raw_grad[first:last, here_columns] = back.astype(low)
+            gains += gain
+        head_gains[0:1, :] += gains
+
+    @pl.when((step >= heads) & (step < heads + kv_heads))
+    def _():
+        back, gain = norm_rope_back(
+            key_sum[step - heads] * score_scale, raw_ref[...], scale_ref[1:2, :], cos_ref[...],
+            sin_ref[...],
+        )
+        raw_grad[:, here_columns] = back.astype(low)
+        head_gains[1:2, :] += gain
+
+    @pl.when((step >= heads + kv_heads) & (step < first_chunk))
+    def _():
+        raw_grad[:, here_columns] = value_sum[step - heads - kv_heads].astype(low)
+
+    @pl.when((step >= first_chunk) & (step < first_chunk + chunks))
+    def _():
+        q = step - first_chunk
+        grads = raw_grad[...]
+        shared[:, 0:tokens, pl.ds(pl.multiple_of(q * chunk, chunk), chunk)] = (
+            lax.dot_general(
+                grads, weight_ref[:, : grads.shape[1]], (((1,), (1,)), ((), ())),
+                preferred_element_type=full,
+            )
+            .astype(low)
+            .reshape(n_ctx, tokens, chunk)
+        )
+        fronts[q // 2, lax.rem(q, 2)] = (
+            lax.dot_general(
+                hidden_ref[...], grads, (((0,), (0,)), ((), ())), preferred_element_type=full
+            )
+            .astype(low)
+            .reshape(fronts.shape[2:])
+        )
 
     def front_pair(ahead):
         target = lax.rem(k + ahead, n_exp)
         return remote(
-            front_ref.at[:, :, target], front_pairs.at[ahead - 1], fp_send.at[ahead],
+            fronts.at[:, :, :, target], front_pairs.at[ahead - 1], fp_send.at[ahead],
             fp_recv.at[ahead], {"exp": target},
         )
 
-    for ahead in range(1, n_exp):
-        front_pair(ahead).start()
-    hidden.start(1)
-    hidden.start(0)
-
-    def front_line(target, step):
-        return remote(
-            front_low.at[target], front_line_in.at[target + (step + 1) // 2], fl_send.at[target],
-            fl_recv.at[target + (step + 1) // 2], {"dp": z + step},
+    def front_line(target, way):
+        return remote(
+            fronts.at[target, :, :, k], front_in.at[target + (way + 1) // 2], fl_send.at[target],
+            fl_recv.at[target + (way + 1) // 2], {"dp": z + way},
         )
 
     def front_across(ahead):
         target = lax.rem(c + ahead, n_ctx)
         return remote(
-            front_sum.at[target], front_in.at[c], fa_send.at[ahead], fa_recv.at[ahead],
-            {"ctx": target},
-        )
-
-    def mix_line(target, step):
-        return remote(
-            mix_out.at[target], mix_in.at[target + (step + 1) // 2], ml_send.at[target],
-            ml_recv.at[target + (step + 1) // 2], {"dp": z + step},
-        )
-
-    def load(piece):
+            fronts.at[z, target // (n_ctx // 2), lax.rem(target, n_ctx // 2), k], front_out.at[c],
+            fa_send.at[ahead], fa_recv.at[ahead], {"ctx": target},
+        )
+
+    def add_front(target, slot):
+        fronts[target, :, :, k] = (
+            fronts[target, :, :, k].astype(full) + front_in[slot].astype(full)
+        ).astype(low)
+
+    def line_of(piece):
+        columns = pl.ds(piece * part, part)
+
+        def line(target, way):
+            return remote(
+                leaving.at[target, :, columns],
+                landing.at[target + (way + 1) // 2, :, columns],
+                line_send.at[piece, target], line_recv.at[piece, target + (way + 1) // 2],
+                {"dp": z + way},
+            )
+
+        return line
+
+    def load_rows(piece):
         return pltpu.make_async_copy(
-            sent_ref.at[:, :, pl.ds(piece * part, part)], rows_in.at[piece % 2],
-            m_load.at[piece % 2],
-        )
-
-    def front_own(target):
-        total = front_ref[target, :, k].astype(full)
-        for ahead in range(1, n_exp):
-            total = total + front_pairs[ahead - 1, target].astype(full)
-        return total
-
-    def line_step(line, leaving, landing, own, distance):
-        for step in (-1, 1):
-            target = z + step * distance
-
-            @pl.when((target >= 0) & (target < n))
-            def _():
-                @pl.when(in_line(-step))
-                def _():
-                    line(target, step).wait_recv()
-                    leaving[target] = (
-                        own(target) + landing[target + (step + 1) // 2].astype(full)
-                    ).astype(low)
-
-                if own is not mix_own:
-                    @pl.when(jnp.logical_not(in_line(-step)))
-                    def _():
-                        leaving[target] = own(target).astype(low)
-
-                line(target, step).start()
-
-    def mix_own(target):
-        return mix_out[target].astype(full)
-
-    load(0).start()
-    for ahead in range(1, n_exp):
-        front_pair(ahead).wait_recv()
-    line_step(front_line, front_low, front_line_in, front_own, n - 1)
-
-    groups, span, _ = pick_ref.shape
-    number, back_rows, _ = sent_ref.shape
-    rows = back_rows // groups
-    pieces = width // part
-    for piece in range(pieces):
-        if piece + 1 < pieces:
-            load(piece + 1).start()
-        load(piece).wait()
+            landed_ref.at[:, :, pl.ds(piece * part, part)], rows_in, load_sem.at[0]
+        )
+
+    def load_part(source, piece):
+        return pltpu.make_async_copy(
+            source.at[:, pl.ds(piece * part, part)], loaded.at[piece % 2], load_sem.at[1 + piece % 2]
+        )
+
+    def mix_in(piece):
+        for ahead in range(1, number):
+            plane_copy(piece, ahead).wait_recv()
+        plane_own_copy(piece).wait()
+        load_rows(piece).start()
+        load_part(result_ref, piece).start()
+        load_rows(piece).wait()
+        groups, _, back_rows, span = pick_ref.shape
+        columns = pl.ds(piece * part, part)
         for g in range(groups):
-            gathered = rows_in[piece % 2, :, pl.ds(g * rows, rows), :].reshape(number * rows, part)
-            mix_out[pl.ds(g * span // tokens, span // tokens), :, pl.ds(piece * part, part)] = (
-                jnp.dot(pick_ref[g], gathered, preferred_element_type=full)
+            gathered = rows_in[:, pl.ds(g * back_rows, back_rows), :]
+            leaving[pl.ds(g * span // tokens, span // tokens), :, columns] = (
+                lax.dot_general(
+                    pick_ref[g].reshape(number * back_rows, span),
+                    gathered.reshape(number * back_rows, part),
+                    (((0,), (0,)), ((), ())),
+                    preferred_element_type=full,
+                )
                 .astype(low)
                 .reshape(span // tokens, tokens, part)
             )
-    line_step(mix_line, mix_out, mix_in, mix_own, n - 1)
-    hidden.turn()
-    for distance in range(n - 2, 0, -1):
-        line_step(front_line, front_low, front_line_in, front_own, distance)
-        line_step(mix_line, mix_out, mix_in, mix_own, distance)
-
-    hidden.finish(hidden_sum)
-    x = token_ref[...].astype(full)
-    inverse = lax.rsqrt(jnp.mean(x * x, axis=-1, keepdims=True) + eps_norm)
-    normed = x * inverse
-    grad = hidden_sum[...]
-    scaled = grad * gain_ref[...]
-    tokens_grad_ref[...] = (
-        middle_ref[...]
-        + inverse * (scaled - normed * jnp.mean(scaled * normed, axis=-1, keepdims=True))
-    ).astype(low)
-    gain_grad = jnp.sum(grad * normed, axis=0, keepdims=True)
-    owned = gain_grad.shape[1] // devices
-    small_all[...] = small_ref[...]
-    for index in range(devices):
-        small_all[index, 0:1, 0:owned] = gain_grad[:, index * owned : (index + 1) * owned]
+
+    def start_total(piece):
+        columns = pl.ds(piece * part, part)
+        load_part(result_ref, piece).wait()
+        total[:, columns] = leaving[z, :, columns].astype(full) + loaded[piece % 2]
+
+    def mix_line(piece, distance):
+        columns = pl.ds(piece * part, part)
+
+        def add(target, slot):
+            leaving[target, :, columns] = (
+                leaving[target, :, columns].astype(full) + landing[slot, :, columns].astype(full)
+            ).astype(low)
+
+        along_line(line_of(piece), add, distance)
+
+    def mix_end(piece):
+        columns = pl.ds(piece * part, part)
+
+        def add(slot):
+            total[:, columns] += landing[slot, :, columns].astype(full)
+
+        end_line(line_of(piece), add)
+
+    @pl.when(step == first_chunk + chunks - 1)
+    def _():
+        mix_in(0)
+        mix_line(0, n - 1)
 
     def small_copy(ahead):
         target = lax.rem(here + ahead, devices)
@@ -1313,99 +1315,215 @@
             device_of(target),
         )
 
-    @pl.loop(1, devices)
-    def _(ahead):
-        small_copy(ahead).start()
-
-    front_sum[...] = front_own(z).astype(low)
-    for step in (-1, 1):
-        @pl.when(in_line(-step))
-        def _():
-            front_line(z, step).wait_recv()
-            front_sum[...] = (
-                front_sum[...].astype(full) + front_line_in[z + (step + 1) // 2].astype(full)
-            ).astype(low)
-    for ahead in range(1, n_ctx):
-        front_across(ahead).start()
-    front_in[c] = front_sum[c]
-    hidden_sum[...] = result_ref[...] + mix_own(z)
-    for step in (-1, 1):
-        @pl.when(in_line(-step))
-        def _():
-            mix_line(z, step).wait_recv()
-            hidden_sum[...] += mix_in[z + (step + 1) // 2].astype(full)
-    output_ref[...] = hidden_sum[...].astype(low)
-    small_out[...] = small_all[here]
-
-    @pl.loop(1, devices)
-    def _(ahead):
-        small_copy(ahead).wait_recv()
-        small_out[...] += small_in[ahead]
-
-    for ahead in range(1, n_ctx):
-        front_across(ahead).wait_recv()
-    front_out[...] = front_in[...].astype(full)
-
-    @pl.loop(1, devices)
-    def _(ahead):
-        small_copy(ahead).wait_send()
-
-    hidden.close()
-    for ahead in range(1, n_exp):
-        front_pair(ahead).wait_send()
-    for ahead in range(1, n_ctx):
-        front_across(ahead).wait_send()
-    for distance in range(1, n):
-        for step in (-1, 1):
-            target = z + step * distance
-
-            @pl.when((target >= 0) & (target < n))
-            def _():
-                front_line(target, step).wait_send()
-                mix_line(target, step).wait_send()
-
-
-def scatter(hidden, front, middle, tokens, gain, small, sent, pick, result, sizes, collective, part=512):
+    @pl.when(step == first_chunk + chunks)
+    def _():
+        for ahead in range(1, n_exp):
+            front_pair(ahead).start()
+        hidden = SquareScatter(
+            sizes, shared, far_in, turn_out, turn_in, hidden_send, hidden_recv, tokens
+        )
+        hidden.start(1)
+        hidden.start(0)
+        total[0:b_rows, :] = arrived[z].astype(full)
+
+        def add_last(slot):
+            total[0:b_rows, :] += back_arrived(slot)
+
+        end_line(back_line, add_last)
+        back_store = pltpu.make_async_copy(total.at[pl.ds(0, b_rows)], back_out, stage_sem.at[0])
+        back_store.start()
+        back_store.wait()
+        if n > 2:
+            mix_line(0, n - 2)
+        for ahead in range(1, n_exp):
+            front_pair(ahead).wait_recv()
+        for target in range(n):
+            summed = fronts[target, :, :, k].astype(full)
+            for ahead in range(1, n_exp):
+                summed = summed + front_pairs[ahead - 1, target].astype(full)
+            fronts[target, :, :, k] = summed.astype(low)
+        along_line(front_line, add_front, n - 1)
+        for distance in range(n - 3, 0, -1):
+            mix_line(0, distance)
+        start_total(0)
+        mix_end(0)
+        front_own = pltpu.make_async_copy(
+            fronts.at[z, c // (n_ctx // 2), lax.rem(c, n_ctx // 2), k], front_out.at[c],
+            stage_sem.at[0],
+        )
+        for piece in range(1, pieces):
+            mix_in(piece)
+            mix_line(piece, n - 1)
+            start_total(piece)
+            for distance in range(n - 2, 0, -1):
+                if piece == 1:
+                    along_line(front_line, add_front, distance)
+                mix_line(piece, distance)
+                if piece == pieces - 1 and distance == max(1, n - 2):
+                    hidden.turn()
+            if piece == 1:
+                end_line(front_line, lambda slot: add_front(z, slot))
+                for ahead in range(1, n_ctx):
+                    front_across(ahead).start()
+                front_own.start()
+            mix_end(piece)
+        front_own.wait()
+        staged[...] = total[...].astype(low)
+        output_store = pltpu.make_async_copy(staged, output_ref, stage_sem.at[0])
+        output_store.start()
+
+        load_part(middle_ref, 0).start()
+        hidden.finish(total)
+        x = token_ref[...].astype(full)
+        inverse = lax.rsqrt(jnp.mean(x * x, axis=-1, keepdims=True) + eps_norm)
+        normed = x * inverse
+        grad = total[...]
+        gain_grad = jnp.sum(grad * normed, axis=0, keepdims=True)
+        owned, gain_owned = width // devices, head // devices
+        for index in range(devices):
+            small_all[index, 0:1, 0:owned] = gain_grad[:, index * owned : (index + 1) * owned]
+            for which in (0, 1):
+                small_all[index, 1 + which : 2 + which, 0:gain_owned] = head_gains[
+                    which : which + 1, index * gain_owned : (index + 1) * gain_owned
+                ]
+
+        @pl.loop(1, devices)
+        def _(ahead):
+            small_copy(ahead).start()
+
+        scaled = grad * gain_ref[...]
+        total[...] = inverse * (scaled - normed * jnp.mean(scaled * normed, axis=-1, keepdims=True))
+        output_store.wait()
+        for piece in range(pieces):
+            if piece + 1 < pieces:
+                load_part(middle_ref, piece + 1).start()
+            load_part(middle_ref, piece).wait()
+            columns = pl.ds(piece * part, part)
+            staged[:, columns] = (total[:, columns] + loaded[piece % 2]).astype(low)
+        tokens_store = pltpu.make_async_copy(staged, tokens_grad_ref, stage_sem.at[0])
+        tokens_store.start()
+        small_out[...] = small_all[here]
+
+        @pl.loop(1, devices)
+        def _(ahead):
+            small_copy(ahead).wait_recv()
+            small_out[...] += small_in[ahead]
+
+        for ahead in range(1, n_ctx):
+            front_across(ahead).wait()
+        tokens_store.wait()
+
+        @pl.loop(1, devices)
+        def _(ahead):
+            small_copy(ahead).wait_send()
+
+        hidden.close()
+        for ahead in range(1, n_exp):
+            front_pair(ahead).wait_send()
+        for piece in range(pieces):
+            for ahead in range(1, number):
+                plane_copy(piece, ahead).wait_send()
+            close_line(line_of(piece))
+        close_line(back_line)
+        close_line(front_line)
+
+
+def finish(
+    bounds, turned, grad, raw, scales, cosine, sine, hidden, weight, back, rows_back, pick, result,
+    middle_grad, tokens, gain, small, heads, kv_heads, head, sizes, collective, part=512,
+):
     n, n_ctx, n_exp = sizes["dp"], sizes["ctx"], sizes["exp"]
+    devices, number = n * n_ctx * n_exp, n_ctx * n_exp
     low, full = jnp.bfloat16, jnp.float32
-    _, rows, width = hidden.shape
-    f_rows, f_cols = front.shape[3:]
-    number, back_rows, _ = sent.shape
-    devices, s_rows, s_cols = small.shape
+    rows, columns = raw.shape
+    count, width = tokens.shape
+    b_rows = back.shape[2]
+    f_rows = width // devices
+    chunk = width // (2 * n)
+    group = heads // kv_heads
+    back_rows = rows_back.shape[1]
+    s_rows, s_cols = small.shape[1:]
+    pieces = width // part
+    first_chunk = heads + 2 * kv_heads
+    within = lambda h: jnp.minimum(h, heads - 1)
+    now = lambda h: jnp.clip(h - first_chunk, 0, 2 * n - 1)
+    once = pl.Buffered(buffer_count=1)
+    whole = lambda shape: pl.BlockSpec(shape, lambda h: (0,) * len(shape), pipeline_mode=once)
+    anywhere = pl.BlockSpec(memory_space=pl.ANY)
+    vmem = lambda *shape: pltpu.VMEM(shape, low)
+    wide = lambda *shape: pltpu.VMEM(shape, full)
     dma = lambda *shape: pltpu.SemaphoreType.DMA(shape)
-    vmem = pl.BlockSpec(memory_space=pltpu.VMEM)
+    half = n_ctx // 2
     return pl.pallas_call(
-        functools.partial(scatter_kernel, sizes=sizes, part=part),
-        in_specs=[vmem] * 6 + [pl.BlockSpec(memory_space=pl.ANY), vmem, vmem],
-        out_specs=[vmem] * 4,
+        functools.partial(
+            finish_kernel, block=count, heads=heads, group=group, score_scale=head ** (-0.5),
+            sizes=sizes, part=part, chunk=chunk,
+        ),
+        grid=(first_chunk + 2 * n + 1,),
+        in_specs=[
+            pl.BlockSpec(memory_space=pltpu.SMEM),
+            pl.BlockSpec((rows, head), lambda h: (0, within(h))),
+            pl.BlockSpec((rows, head), lambda h: (0, heads + within(h) // group)),
+            pl.BlockSpec((rows, head), lambda h: (0, heads + kv_heads + within(h) // group)),
+            pl.BlockSpec((rows, head), lambda h: (0, within(h))),
+            pl.BlockSpec((rows, head), lambda h: (0, jnp.minimum(h, heads + kv_heads - 1))),
+            whole(scales.shape),
+            whole(cosine.shape),
+            whole(sine.shape),
+            pl.BlockSpec((rows, chunk), lambda h: (0, now(h))),
+            pl.BlockSpec((chunk, weight.shape[1]), lambda h: (now(h), 0)),
+            anywhere,
+            anywhere,
+            whole(pick.shape),
+            anywhere,
+            anywhere,
+            whole(tokens.shape),
+            whole(gain.shape),
+            anywhere,
+        ],
+        out_specs=[anywhere] * 4
+        + [pl.BlockSpec((s_rows, s_cols), lambda h: (0, 0)), anywhere, anywhere],
         out_shape=[
-            jax.ShapeDtypeStruct((rows, width), low),
-            jax.ShapeDtypeStruct((n_ctx, f_rows, f_cols), full),
-            jax.ShapeDtypeStruct((rows, width), low),
+            jax.ShapeDtypeStruct((count, width), low),
+            jax.ShapeDtypeStruct((n_ctx, f_rows, columns), low),
+            jax.ShapeDtypeStruct((count, width), low),
+            jax.ShapeDtypeStruct((b_rows, width), full),
             jax.ShapeDtypeStruct((s_rows, s_cols), full),
+            jax.ShapeDtypeStruct(rows_back.shape, low),
+            jax.ShapeDtypeStruct((n + 1, b_rows, width), low),
         ],
         scratch_shapes=[
-            pltpu.VMEM((2, 2, rows, width // 2), low),
-            pltpu.VMEM((2, rows, width // 2), low),
-            pltpu.VMEM((2, rows, width // 2), low),
-            pltpu.VMEM((rows, width), full),
-            pltpu.VMEM((n_exp - 1, n, n_ctx, f_rows, f_cols), low),
-            pltpu.VMEM((n_ctx, f_rows, f_cols), low),
-            pltpu.VMEM((n + 1, n_ctx, f_rows, f_cols), low),
-            pltpu.VMEM((n, n_ctx, f_rows, f_cols), low),
-            pltpu.VMEM((n_ctx, f_rows, f_cols), low),
-            pltpu.VMEM((2, number, back_rows, part), low),
-            pltpu.VMEM((n, rows, width), low),
-            pltpu.VMEM((n + 1, rows, width), low),
-            pltpu.VMEM((devices, s_rows, s_cols), full),
-            pltpu.VMEM((devices, s_rows, s_cols), full),
-            dma(6), dma(6), dma(n_exp), dma(n_exp), dma(n), dma(n + 1), dma(n_ctx), dma(n_ctx),
-            dma(2), dma(n), dma(n + 1), dma(devices), dma(devices),
+            wide(kv_heads, rows, head),
+            wide(kv_heads, rows, head),
+            vmem(rows, columns),
+            wide(2, head),
+            vmem(n_ctx, max(count, n_exp * b_rows), width),
+            vmem(n_ctx, b_rows, width),
+            vmem(b_rows, width),
+            vmem(n, 2, half, n_exp, f_rows, columns),
+            vmem(n_exp - 1, n, 2, half, f_rows, columns),
+            vmem(n + 1, 2, half, f_rows, columns),
+            vmem(number, back_rows, part),
+            vmem(n, count, width),
+            vmem(n + 1, count, width),
+            *square_scratch(count, width),
+            wide(count, width),
+            wide(2, count, part),
+            vmem(count, width),
+            wide(devices, s_rows, s_cols),
+            wide(devices, s_rows, s_cols),
+            dma(2), dma(3), dma(2), dma(n_exp), dma(n_exp), dma(n_ctx), dma(n_ctx), dma(n),
+            dma(n + 1), dma(n_exp), dma(n_exp), dma(n), dma(n + 1), dma(n_ctx), dma(n_ctx),
+            dma(pieces, number), dma(pieces, number), dma(pieces), dma(pieces, n),
+            dma(pieces, n + 1), dma(devices), dma(devices),
         ],
         compiler_params=pltpu.CompilerParams(
             collective_id=collective, has_side_effects=True, vmem_limit_bytes=VMEM
         ),
-    )(hidden, front, middle, tokens, gain, small, sent, pick, result)
+    )(
+        bounds, turned, turned, turned, grad, raw, scales, cosine, sine, hidden, weight, back,
+        rows_back, pick, result, middle_grad, tokens, gain, small,
+    )
 
 
 def shards(
@@ -1479,7 +1597,6 @@
     whole_tokens = whole_tokens.reshape(seq_len, width)
     front = front.reshape(width, -1)
     output_part = output_part.reshape(q_cols, width)
-    front_weight = front[:, : q_cols + 2 * kv_cols]
     small = front[:, q_cols + 2 * kv_cols :]
     first_gain = small[:, 0].astype(full)
     second_gain = small[:, 1].astype(full)
@@ -1506,7 +1623,6 @@
     slot_at = grouped(jnp.where(hot > 0, before + block_first, -1.0))
     slots = jnp.arange(slot_rows, dtype=full)
     pick = (slot_at.transpose(0, 2, 1)[:, :, None, :] == slots[:, None]).astype(low)
-    pick_back = (slot_at[:, :, :, None] == slots).astype(low).reshape(groups, -1, plane * slot_rows)
 
     positions = jnp.arange(seq_len, dtype=jnp.int32)
     cosine, sine = rope_tables(positions, head_dim)
@@ -1533,66 +1649,39 @@
     active, gate_grad, up_grad, row_grads, scaled_out, dot_rows = expert(
         here[None], expert_in, part_rows, grad_rows, gate_weight, up_weight, down_weight, experts
     )
-    scaled_out, branch_low, middle_grad, second_gain_grad, router_grad = combine(
-        row_grads, dot_rows, pick_back, scaled_out, middle, cotangent[0], second_gain[None],
-        own_gates, router_wide, experts, sizes, 2,
-    )
+    branch_low, middle_grad, second_gain_grad, router_grad, gate_w_grad, up_w_grad, down_grad = combine(
+        row_grads, dot_rows, pick, middle, cotangent[0], second_gain[None], own_gates, router_wide,
+        expert_in, grad_rows, active, gate_grad, up_grad, experts, sizes, 2,
+    )
+    gate_w_grad, up_w_grad, down_grad = gate_w_grad[None], up_w_grad[None], down_grad[None]
     router_grad = router_grad[:experts].T
     branch_low = branch_low.reshape(seq_len, width)
-    weight_sum = lambda left, right: jnp.einsum(
-        "scd,scf->df", left, right, preferred_element_type=full
-    )[None]
-    down_grad = weight_sum(active, grad_rows)
-    gate_w_grad = weight_sum(expert_in, gate_grad)
-    up_w_grad = weight_sum(expert_in, up_grad)
-    scaled_out = swap(scaled_out, PLANE)
-
     output_w_grad = jnp.einsum("ti,td->id", attended_low, branch_low, preferred_element_type=full)
     attended_grad = jnp.einsum("td,id->ti", branch_low, output_part, preferred_element_type=full)
-    raw_grad, head_gain_grads, output_share = attend_back(
-        bounds, turned, attended_grad.astype(low), raw, scales, cosine, sine,
-        output_w_grad.astype(low).reshape(n_ctx, n_exp, -1, width), heads_here, kv_here,
-        head_dim, tok_count, sizes, 5,
-    )
-    query_gain_grad, key_gain_grad = head_gain_grads[0], head_gain_grads[1]
-    hidden_grad = jnp.einsum("ti,di->td", raw_grad, front_weight, preferred_element_type=full)
-    front_grad = jnp.einsum("td,ti->di", hidden, raw_grad, preferred_element_type=full).astype(low)
-    packed = jnp.concatenate(
-        [
-            jnp.zeros((devices, rows), full),
-            second_gain_grad.reshape(devices, -1),
-            query_gain_grad.reshape(devices, -1),
-            key_gain_grad.reshape(devices, -1),
-            router_grad.reshape(devices, -1),
-        ],
-        axis=1,
-    )
-    packed = jnp.pad(packed, ((0, 0), (0, -packed.shape[1] % 1024))).reshape(devices, 8, -1)
-    tokens_grad, front_grad, output, packed = scatter(
-        hidden_grad.astype(low).reshape(n_ctx, tok_count, width),
-        front_grad.reshape(n_dp, n_ctx, n_exp, rows, -1),
-        middle_grad,
-        tokens[0],
-        first_gain[None],
-        packed,
-        scaled_out,
-        pick_back,
-        middle,
-        sizes,
-        4,
-    )
+    rest = jnp.concatenate(
+        [second_gain_grad.reshape(devices, -1), router_grad.reshape(devices, -1)], axis=1
+    )
+    columns = -(-rest.shape[1] // (5 * 128)) * 128
+    rest = jnp.pad(rest, ((0, 0), (0, 5 * columns - rest.shape[1]))).reshape(devices, 5, columns)
+    small = jnp.pad(rest, ((0, 0), (3, 0), (0, 0)))
+    tokens_grad, front_grad, output, output_share, small, _, _ = finish(
+        bounds, turned, attended_grad.astype(low), raw, scales, cosine, sine, hidden, front,
+        output_w_grad.astype(low).reshape(n_ctx, n_exp, -1, width), scaled_out, pick, middle,
+        middle_grad, tokens[0], first_gain[None], small, heads_here, kv_here, head_dim, sizes, 4,
+        part=512 if n_ctx * n_exp <= 8 else 256,
+    )
+    tokens_grad = tokens_grad[None]
     output = output[None]
-    tokens_grad = tokens_grad[None]
+    front_grad = front_grad.astype(full)
     query_share = front_grad[:, :, :q_cols].transpose(1, 0, 2).reshape(rows, -1)
     key_share = front_grad[:, :, q_cols : q_cols + kv_cols].transpose(1, 0, 2).reshape(rows, -1)
     value_share = front_grad[:, :, q_cols + kv_cols :].transpose(1, 0, 2).reshape(rows, -1)
-    packed = packed.reshape(-1)
-    ends = [rows, 2 * rows, 2 * rows + gain_len, 2 * rows + 2 * gain_len]
-    first_share = packed[: ends[0]]
-    second_share = packed[ends[0] : ends[1]]
-    query_gain_share = packed[ends[1] : ends[2]]
-    key_gain_share = packed[ends[2] : ends[3]]
-    router_share = packed[ends[3] : ends[3] + rows * experts].reshape(rows, experts)
+    first_share = small[0, :rows]
+    query_gain_share = small[1, :gain_len]
+    key_gain_share = small[2, :gain_len]
+    rest = small[3:].reshape(-1)
+    second_share = rest[:rows]
+    router_share = rest[rows : rows + rows * experts].reshape(rows, experts)
     return (
         output,
         tokens_grad,

time: 1050 us -> 905 us (0.86)
  Pallas kernels: 919 us -> 831 us
  matrix products: 62.2 us -> 14.4 us
    pallas_call x2 -> x1, Pallas kernels: 286 us -> 213 us  [finish(): pl.pallas_call(functools.partial(finish_kernel, block=count, heads=heads,...]
    dot_general x5 -> x0, matrix products: 47.8 us -> none  [the longest x3 29.9 us: shards(): jnp.einsum('scd,scf->df', left, right, preferred_element_type=full)[None]]
    pallas_call x1, Pallas kernels: 283 us -> 260 us  [dispatch(): pl.pallas_call(functools.partial(dispatch_kernel, sizes=sizes, pieces=pie...]
  transfers between devices with their start and end apart: 1 -> 0, of which waited for: 0 -> 0; matrix products, arithmetic and copies ran while one was open for 6% -> 0% of each run, Pallas kernels for 15% -> 0%
where the time goes in v4:
time: 905 us; the launch traced here: 895 us
  Pallas kernels  831 us (92%)
  local copies, waits for them, and re-layouts  28.4 us (3%)
  other arithmetic  20.1 us (2%)
  matrix products  14.4 us (2%)
    pallas_call x1, Pallas kernels, dispatch(): pl.pallas_call(functools.partial(dispatch_kernel, sizes=sizes, pieces=pie...  260 us
    pallas_call x1, Pallas kernels, finish(): pl.pallas_call(functools.partial(finish_kernel, block=count, heads=heads,...  213 us
    pallas_call x1, Pallas kernels, combine(): pl.pallas_call(functools.partial(combine_kernel, sizes=sizes, pieces=piec...  173 us
    pallas_call x1, Pallas kernels, gather(): pl.pallas_call(functools.partial(gather_kernel, sizes=sizes), in_specs=[p...  95.2 us
    pallas_call x1, Pallas kernels, expert(): pl.pallas_call(functools.partial(expert_kernel, experts=experts), grid=(s...  56.4 us
    pallas_call x1, Pallas kernels, attend(): pl.pallas_call(functools.partial(attend_kernel, block=block, score_scale=...  20.8 us

profile of v4, /device:TPU:14, one launch (start us, length us, event | category | flops | bytes accessed | tf_op | source)
XLA Modules:
  0.0 895.0 jit_solution(1805915047071867948)
XLA Ops:
  3.7 1.0 bitcast_bitcast_fusion.1
  4.7 1.3 convert_element_type.99
  8.6 95.2 %shard_map.263 = (bf16[4,256,2048]{2,1,0:T(8,128)(2,1)}, bf16[4,4,2,64,1408]{4,3,2,1,0:T(8,128)(2,1)}, bf16[4,2,128,2048]{3,2,1,0:T(8,128)(2,1)}, s32[4,256,8]{2,1,0:T(8,128)}) custom-call(bf16[256,2048]{1,0:T(8,128)(2,1)} %bitcast.91, bf16[4,64,1408]{2,1,0:T(8,128)(2,1)} %pad_maximum_fusion.front_ref, bf16[128,2048]{1,0:T(8,128)(2,1)} %convert_element_type.102.back_ref, ...), custom_call_target="tpu_custom_call" | custom-call | tf_op jit(solution)/shard_map/pallas_call | solution.py:945
  103.8 1.4 slice_reduce_fusion
  106.3 2.4 convert_reduce_fusion
  108.9 2.7 fusion.5
  111.8 1.0 pad_maximum_fusion.2.sin_ref
  112.8 12.4 %shard_map.264 = (bf16[1024,2048]{1,0:T(8,128)(2,1)}, f32[1024,1280]{1,0:T(8,128)}, bf16[1024,1280]{1,0:T(8,128)(2,1)}) custom-call(bf16[1024,2048]{1,0:T(8,128)(2,1)} %bitcast.125, f32[1,2048]{1,0:T(1,128)} %bitcast.123, bf16[2048,1408]{1,0:T(8,128)(2,1)} %bitcast.88, f32[2,128]{1,0:T(2,128)} %maximum_convert_fusion.scale_ref, ...), custom_call_target="tpu_custom_call" | custom-call | flops 5368709120 | bytes 31457280 | tf_op jit(solution)/shard_map/pallas_call | solution.py:53
  125.3 20.8 %shard_map.265.attended_ref = bf16[1024,1024]{1,0:T(8,128)(2,1)} custom-call(s32[1,2]{1,0:T(1,128)} %bounds_ref.3, bf16[1024,1280]{1,0:T(8,128)(2,1)} %get-tuple-element.46.query_ref.key_ref.value_ref, bf16[1024,1280]{1,0:T(8,128)(2,1)} %get-tuple-element.46.query_ref.key_ref.value_ref, bf16[1024,1280]{1,0:T(8,128)(2,1)} %get-tuple-element.46.query_ref.key_ref.value_ref), custom_call_target="tpu_custom_call" | custom-call | flops 2147483648 | bytes 6291456 | tf_op jit(solution)/shard_map/pallas_call | solution.py:112
  146.7 2.0 fusion.pick_ref
  148.6 1.2 slice.88
  151.9 260.2 %shard_map.266 = (bf16[8,288,2048]{2,1,0:T(8,128)(2,1)}, bf16[8,288,2048]{2,1,0:T(8,128)(2,1)}, bf16[8,288,128]{2,1,0:T(8,128)(2,1)}, f32[256,2048]{1,0:T(8,128)}, f32[256,128]{1,0:T(8,128)}) custom-call(bf16[1024,1024]{1,0:T(8,128)(2,1)} %shard_map.265.attended_ref, bf16[1024,2048]{1,0:T(8,128)(2,1)} %bitcast.106, bf16[256,2048]{1,0:T(8,128)(2,1)} %bitcast.92, ...), custom_call_target="tpu_custom_call" | custom-call | tf_op jit(solution)/shard_map/pallas_call | solution.py:451
  412.1 56.4 %shard_map.267 = (bf16[8,288,768]{2,1,0:T(8,128)(2,1)}, bf16[8,288,768]{2,1,0:T(8,128)(2,1)}, bf16[8,288,768]{2,1,0:T(8,128)(2,1)}, bf16[8,288,2048]{2,1,0:T(8,1...) custom-call(s32[1]{0:T(128)} %bitcast.10.here_ref, ...), custom_call_target="tpu_custom_call" | custom-call | flops 43486543872 | bytes 62914560 | tf_op jit(solution)/shard_map/pallas_call | solution.py:744
  468.5 173.0 %shard_map.268 = (bf16[4,256,2048]{2,1,0:T(8,128)(2,1)}, f32[256,2048]{1,0:T(8,128)}, f32[1,2048]{1,0:T(1,128)}, f32[128,2048]{1,0:T(8,128)}, f32[2048,768]{1,0:...) custom-call(bf16[8,288,2048]{2,1,0:T(8,128)(2,1)} %get-tuple-element.52.rows_ref, ...), custom_call_target="tpu_custom_call" | custom-call | tf_op jit(solution)/shard_map/pallas_call | solution.py:666
  641.6 1.1 slice_bitcast_fusion.1
  644.0 1.4 reduce.9
  646.7 8.5 convolution_convert_fusion
  655.1 5.8 convolution_convert_fusion.1.grad_ref
  660.9 212.7 %shard_map.269 = (bf16[256,2048]{1,0:T(8,128)(2,1)}, bf16[4,64,1280]{2,1,0:T(8,128)(2,1)}, bf16[256,2048]{1,0:T(8,128)(2,1)}, f32[128,2048]{1,0:T(8,128)}, f32[8...) custom-call(s32[1,2]{1,0:T(1,128)} %bounds_ref.3, ...), custom_call_target="tpu_custom_call" | custom-call | tf_op jit(solution)/shard_map/pallas_call | solution.py:1457
  873.6 1.3 convert_element_type.115
  875.1 1.1 copy.58
  882.7 6.1 copy.78
  888.8 2.8 copy.79
  891.9 2.7 copy.80
  (85 shorter events, 19.3 us)
Async XLA Ops:
  0.6 6.3 copy-start.9
  0.7 7.1 copy-start.3
  125.3 20.8 %copy-start.7 = (s32[4,256,8]{2,1,0:T(8,128)S(1)}, s32[4,256,8]{2,1,0:T(8,128)}, u32[]{:S(2)}) copy-start(s32[4,256,8]{2,1,0:T(8,128)} %get-tuple-element.48) | copy-start | bytes 98308
  146.0 4.8 copy-start.2
  641.6 5.1 copy-start
  646.7 8.5 copy-start.1
  646.7 8.5 copy-start.10
  873.6 3.9 copy-start.8
  873.6 6.2 copy-start.6
  874.9 5.9 copy-start.5
  875.0 6.7 copy-start.4
  880.8 8.0 slice-start.2
  882.7 6.1 slice-start.3
  882.7 8.9 slice-start
  888.8 3.1 slice-start.1

commit v5 on v4

--- a/solution.py
+++ b/solution.py
@@ -21,61 +21,6 @@
     angles = positions.astype(jnp.float32)[:, None] * frequency[None, :]
     angles = jnp.concatenate([angles, angles], axis=-1)
     return (jnp.cos(angles), jnp.sin(angles))
-
-
-def project_kernel(x_ref, gain_ref, weight_ref, scale_ref, cos_ref, sin_ref, hidden_ref, raw_ref, out_ref, *, q_heads, kv_heads):
-    x = x_ref[...].astype(jnp.float32)
-    inverse = lax.rsqrt(jnp.mean(x * x, axis=-1, keepdims=True) + eps_norm)
-    hidden = ((x * inverse) * gain_ref[...]).astype(jnp.bfloat16)
-    hidden_ref[...] = hidden
-    raw = jnp.dot(
-        hidden, weight_ref[:, : raw_ref.shape[1]], preferred_element_type=jnp.float32
-    )
-    raw_ref[...] = raw
-    width = cos_ref.shape[1]
-    cosine, sine = cos_ref[...], sin_ref[...]
-    for h in range(q_heads + kv_heads):
-        here = slice(h * width, (h + 1) * width)
-        part = raw[:, here]
-        scale = scale_ref[0:1, :] if h < q_heads else scale_ref[1:2, :]
-        factor = lax.rsqrt(jnp.mean(part * part, axis=-1, keepdims=True) + eps_norm)
-        scaled = part * factor * scale
-        turned = pltpu.roll(scaled, width // 2, 1)
-        out_ref[:, here] = (scaled * cosine + turned * sine).astype(jnp.bfloat16)
-    rest = slice((q_heads + kv_heads) * width, raw.shape[1])
-    out_ref[:, rest] = raw[:, rest].astype(jnp.bfloat16)
-
-
-def project(x, gain, weight, columns, scales, cosine, sine, q_heads, kv_heads, block):
-    rows, width = x.shape
-    head = cosine.shape[1]
-    whole = lambda shape: pl.BlockSpec(shape, lambda i: (0, 0))
-    return pl.pallas_call(
-        functools.partial(project_kernel, q_heads=q_heads, kv_heads=kv_heads),
-        grid=(rows // block,),
-        in_specs=[
-            pl.BlockSpec((block, width), lambda i: (i, 0)),
-            whole((1, width)),
-            whole(weight.shape),
-            whole((2, head)),
-            pl.BlockSpec((block, head), lambda i: (i, 0)),
-            pl.BlockSpec((block, head), lambda i: (i, 0)),
-        ],
-        out_specs=[
-            pl.BlockSpec((block, width), lambda i: (i, 0)),
-            pl.BlockSpec((block, columns), lambda i: (i, 0)),
-            pl.BlockSpec((block, columns), lambda i: (i, 0)),
-        ],
-        out_shape=[
-            jax.ShapeDtypeStruct((rows, width), jnp.bfloat16),
-            jax.ShapeDtypeStruct((rows, columns), jnp.float32),
-            jax.ShapeDtypeStruct((rows, columns), jnp.bfloat16),
-        ],
-        compiler_params=pltpu.CompilerParams(vmem_limit_bytes=VMEM),
-        cost_estimate=pl.CostEstimate(
-            flops=2 * rows * width * columns, bytes_accessed=30 << 20, transcendentals=0
-        ),
-    )(x, gain, weight, scales, cosine, sine)
 
 
 def seen(bounds_ref, first, rows, keys):
@@ -93,40 +38,6 @@
     scores = jnp.where(allowed, scores * score_scale, masked_score)
     weights = jnp.exp(scores - jnp.max(scores, axis=-1, keepdims=True))
     return weights / jnp.sum(weights, axis=-1, keepdims=True)
-
-
-def attend_kernel(bounds_ref, query_ref, key_ref, value_ref, out_ref, *, block, score_scale):
-    rows = query_ref.shape[0]
-    for first in range(0, rows, block):
-        last = first + block
-        allowed = seen(bounds_ref, first, block, last)
-        shares = shares_of(query_ref[first:last, :], key_ref[:last, :], allowed, score_scale)
-        out_ref[first:last, :] = jnp.dot(
-            shares.astype(jnp.bfloat16), value_ref[:last, :], preferred_element_type=jnp.float32
-        ).astype(jnp.bfloat16)
-
-
-def attend(bounds, turned, heads, kv_heads, head, block):
-    rows = turned.shape[0]
-    group = heads // kv_heads
-    return pl.pallas_call(
-        functools.partial(attend_kernel, block=block, score_scale=head ** (-0.5)),
-        grid=(heads,),
-        in_specs=[
-            pl.BlockSpec(memory_space=pltpu.SMEM),
-            pl.BlockSpec((rows, head), lambda h: (0, h)),
-            pl.BlockSpec((rows, head), lambda h: (0, heads + h // group)),
-            pl.BlockSpec((rows, head), lambda h: (0, heads + kv_heads + h // group)),
-        ],
-        out_specs=pl.BlockSpec((rows, head), lambda h: (0, h)),
-        out_shape=jax.ShapeDtypeStruct((rows, heads * head), jnp.bfloat16),
-        compiler_params=pltpu.CompilerParams(vmem_limit_bytes=VMEM),
-        cost_estimate=pl.CostEstimate(
-            flops=2 * heads * rows * rows * head,
-            bytes_accessed=6 << 20,
-            transcendentals=heads * rows * rows // 2,
-        ),
-    )(bounds, turned, turned, turned)
 
 
 def square(sizes):
@@ -186,18 +97,23 @@
 class SquareScatter:
     def __init__(self, sizes, parts, far_in, turn_out, turn_in, send, recv, rows):
         self.parts, self.far_in, self.turn_out, self.turn_in = parts, far_in, turn_out, turn_in
-        self.send, self.recv, self.rows = send, recv, pl.ds(0, rows)
+        self.send, self.recv, self.rows = send, recv, rows
         self.me = lax.axis_index("ctx")
         self.by = square(sizes)
         self.far = sizes["ctx"] - 1 - self.me
-        half = parts.shape[2] // 2
+        half = parts.shape[-1] // 2
         self.columns = (pl.ds(0, half), pl.ds(half, half))
+
+    def at(self, place, side):
+        if len(self.parts.shape) == 2:
+            return pl.ds(place * self.rows, self.rows), self.columns[side]
+        return place, pl.ds(0, self.rows), self.columns[side]
 
     def first(self, side, number):
         place = self.by[side] if number == 0 else self.far
         index = 2 * side + number
         return remote(
-            self.parts.at[place, self.rows, self.columns[side]], self.far_in.at[side, number],
+            self.parts.at[self.at(place, side)], self.far_in.at[side, number],
             self.send.at[index], self.recv.at[index], {"ctx": self.by[side]},
         )
 
@@ -214,7 +130,7 @@
     def turn(self):
         for side in (0, 1):
             self.first(side, 1).wait_recv()
-            own = self.parts[self.by[1 - side], self.rows, self.columns[side]].astype(jnp.float32)
+            own = self.parts[self.at(self.by[1 - side], side)].astype(jnp.float32)
             self.turn_out[side] = (own + self.far_in[side, 1].astype(jnp.float32)).astype(
                 jnp.bfloat16
             )
@@ -225,7 +141,7 @@
             self.first(side, 0).wait_recv()
             self.second(side).wait_recv()
             total[:, self.columns[side]] = (
-                self.parts[self.me, self.rows, self.columns[side]].astype(jnp.float32)
+                self.parts[self.at(self.me, side)].astype(jnp.float32)
                 + self.far_in[side, 0].astype(jnp.float32)
                 + self.turn_in[side].astype(jnp.float32)
             )
@@ -280,6 +196,21 @@
     return {"ctx": index // sizes["exp"], "exp": lax.rem(index, sizes["exp"])}
 
 
+def partner(sizes, turn):
+    n_ctx, n_exp = sizes["ctx"], sizes["exp"]
+    number = n_ctx * n_exp
+    here = plane_index(sizes)
+    if (n_ctx, n_exp) != (4, 2):
+        return lax.rem(here + turn, number), lax.rem(here + number - turn, number)
+    c, k = lax.axis_index("ctx"), lax.axis_index("exp")
+    one_of = lambda *turns: sum(jnp.where(turn == t, 1, 0) for t in turns)
+    over_x = lax.rem(lax.rem(c, 2) + one_of(2, 4, 6, 7), 2)
+    over_y = lax.rem(c // 2 + one_of(3, 5, 6, 7), 2)
+    over_k = lax.rem(k + one_of(1, 4, 5, 7), 2)
+    other = (over_y * 2 + over_x) * 2 + over_k
+    return other, other
+
+
 def cut(widths, part):
     pieces = []
     for number, width in enumerate(widths):
@@ -288,18 +219,28 @@
     return pieces
 
 
+def staged_rows(slots):
+    return min(256, 1 << (slots.bit_length() - 1))
+
+
 def dispatch_kernel(
     attended_ref, back_ref, token_ref, gain_ref, router_ref, chosen_ref, cot_ref, pick_ref,
-    grads_out, mixed_out, parts_out, middle_ref, gates_ref,
-    branch, far_in, turn_out, turn_in, sq_send, sq_recv, mixed, *refs, sizes, pieces, experts,
+    gate_w_ref, up_w_ref, down_w_ref,
+    grads_out, mixed_out, parts_out, middle_ref, gates_ref, active_out, gate_out, up_out, rows_out,
+    scaled_out, dots_out,
+    branch, far_in, turn_out, turn_in, sq_send, sq_recv, cot_column, mixed_column, parts_column,
+    packed, packed_parts, parts_in, active, gate_grad, up_grad, scaled, dots,
+    line_send, line_recv, plane_send, plane_recv, own_sem, row_send, row_recv, part_send, part_recv,
+    load_sem, store_sem, *, sizes, pieces, experts,
 ):
-    outs, refs = (grads_out, mixed_out, parts_out), refs
-    columns, packed = refs[:3], refs[3:6]
-    line_send, line_recv, plane_send, plane_recv, own_sem = refs[6:]
+    outs = (grads_out, mixed_out, parts_out)
+    columns = (cot_column, mixed_column, parts_column)
+    targets = (packed, packed, packed_parts)
     n, n_ctx, number = sizes["dp"], sizes["ctx"], sizes["ctx"] * sizes["exp"]
     me, here = lax.axis_index("dp"), plane_index(sizes)
     tokens, width = token_ref.shape
     groups, dests, rows, span = pick_ref.shape
+    slots = groups * rows
     full, low = jnp.float32, jnp.bfloat16
     greet(sizes)
 
@@ -323,7 +264,7 @@
         a, first, part = pieces[f]
         target = peer(sizes, ahead)
         return remote(
-            packed[a].at[target, :, pl.ds(first, part)],
+            packed.at[target, pl.ds(0, slots), pl.ds(first, part)],
             outs[a].at[here, :, pl.ds(first, part)],
             plane_send.at[f, ahead],
             plane_recv.at[f, ahead],
@@ -333,13 +274,35 @@
     def own_copy(f):
         a, first, part = pieces[f]
         return pltpu.make_async_copy(
-            packed[a].at[here, :, pl.ds(first, part)],
+            packed.at[here, pl.ds(0, slots), pl.ds(first, part)],
             outs[a].at[here, :, pl.ds(first, part)],
             own_sem.at[f],
         )
 
+    cots = len([p for p in pieces if p[0] == 0])
+    early = cots + cots // 2
+    last_columns = pl.ds(pieces[early][1], width - pieces[early][1])
+
+    def row_copy(turn):
+        target, _ = partner(sizes, turn)
+        return remote(
+            packed.at[target, pl.ds(0, slots), last_columns], mixed_out.at[here, :, last_columns],
+            row_send.at[turn], row_recv.at[turn], place(sizes, target),
+        )
+
+    def part_copy(turn):
+        target, _ = partner(sizes, turn)
+        return remote(
+            packed_parts.at[target], parts_out.at[here], part_send.at[turn], part_recv.at[turn],
+            place(sizes, target),
+        )
+
+    def send_rows(turns):
+        for turn in turns:
+            part_copy(turn).start()
+            row_copy(turn).start()
+
     def spread(f):
-        a, first, part = pieces[f]
         for distance in range(1, n):
             for step in (-1, 1):
                 origin = me - step * distance
@@ -355,13 +318,16 @@
 
             if distance == max(1, n - 2) and f + 1 < len(pieces):
                 send_own(f + 1)
+
+    def pick_rows(f):
+        a, first, part = pieces[f]
         for g in range(groups):
             given = columns[a][pl.ds(g * span // tokens, span // tokens), :, pl.ds(first, part)]
             given = given.reshape(span, part)
 
             @pl.loop(0, dests)
             def _(j):
-                packed[a][j, pl.ds(g * rows, rows), pl.ds(first, part)] = jnp.dot(
+                targets[a][j, pl.ds(g * rows, rows), pl.ds(first, part)] = jnp.dot(
                     pick_ref[g, j], given, preferred_element_type=full
                 ).astype(low)
 
@@ -370,18 +336,34 @@
             plane_copy(f, ahead).start()
         own_copy(f).start()
 
-    columns[0][me] = cot_ref[...]
+    deep = staged_rows(slots)
+    blocks = back_ref.shape[0] // deep
+    weight_copies = [
+        pltpu.make_async_copy(
+            back_ref.at[pl.ds(i * deep, deep)], packed.at[i, pl.ds(0, deep)], load_sem.at[i]
+        )
+        for i in range(blocks)
+    ]
+    own_cot = pltpu.make_async_copy(cot_ref, cot_column.at[me], own_sem.at[0])
+    own_cot.start()
+    for copy in weight_copies:
+        copy.start()
+    own_cot.wait()
     send_own(0)
-
-    scatter = SquareScatter(
-        sizes, branch, far_in, turn_out, turn_in, sq_send, sq_recv, tokens
-    )
-
-    def project_block(place):
-        branch[place] = jnp.dot(
-            attended_ref[pl.ds(place * tokens, tokens), :], back_ref[...],
-            preferred_element_type=full,
-        ).astype(low)
+    for copy in weight_copies:
+        copy.wait()
+
+    scatter = SquareScatter(sizes, branch, far_in, turn_out, turn_in, sq_send, sq_recv, tokens)
+
+    def project_block(index):
+        at = pl.ds(index * tokens, tokens)
+        total = jnp.zeros((tokens, width), full)
+        for i in range(blocks):
+            total += jnp.dot(
+                attended_ref[at, i * deep : (i + 1) * deep], packed[i, 0:deep],
+                preferred_element_type=full,
+            )
+        branch[at] = total.astype(low)
 
     project_block(scatter.far)
     scatter.start(1)
@@ -390,15 +372,15 @@
     scatter.start(0)
     project_block(scatter.me)
     spread(0)
+    pick_rows(0)
     scatter.turn()
     push(0)
     scatter.finish(middle_ref)
     middle_ref[...] += token_ref[...].astype(full)
     middle = middle_ref[...]
     inverse = lax.rsqrt(jnp.mean(middle * middle, axis=-1, keepdims=True) + eps_norm)
-    mixed[...] = ((middle * inverse) * gain_ref[...]).astype(low)
-    columns[1][me] = mixed[...]
-    logits = jnp.dot(mixed[...], router_ref[...], preferred_element_type=full)
+    mixed_column[me] = ((middle * inverse) * gain_ref[...]).astype(low)
+    logits = jnp.dot(mixed_column[me], router_ref[...], preferred_element_type=full)
     chosen = chosen_ref[...] > 0
     logits = jnp.where(chosen, logits, masked_score)
     gates = jnp.exp(logits - jnp.max(logits, axis=-1, keepdims=True))
@@ -417,13 +399,160 @@
             + pltpu.roll(second_part, experts, 1)
             + pltpu.roll(third_part, 2 * experts, 1)
         )
-    columns[2][me] = terms.astype(low)
-
-    for f in range(1, len(pieces)):
+    parts_column[me] = terms.astype(low)
+
+    def sent(f):
+        for ahead in range(1, number):
+            plane_copy(f, ahead).wait_send()
+        own_copy(f).wait()
+
+    for f in range(1, cots):
         spread(f)
+        pick_rows(f)
         push(f)
-
     scatter.close()
+    for f in range(cots, early):
+        spread(f)
+        sent(f - cots)
+        pick_rows(f)
+        push(f)
+    for f in range(early, len(pieces)):
+        spread(f)
+    for f in range(early - cots, cots):
+        sent(f)
+
+    def pick_turns(first_turn, last_turn):
+        @pl.loop(first_turn, last_turn)
+        def _(turn):
+            j, _ = partner(sizes, turn)
+            for a, first, part in pieces[early:]:
+                for g in range(groups):
+                    given = columns[a][
+                        pl.ds(g * span // tokens, span // tokens), :, pl.ds(first, part)
+                    ]
+                    targets[a][j, pl.ds(g * rows, rows), pl.ds(first, part)] = jnp.dot(
+                        pick_ref[g, j], given.reshape(span, part), preferred_element_type=full
+                    ).astype(low)
+
+    waves = [range(2, number)]
+    pick_turns(1, waves[0][-1] + 1)
+    send_rows((*waves[0], 1))
+    pick_turns(0, 1)
+    if len(waves) > 1:
+        pick_turns(waves[1][0], number)
+    own_rows = [
+        pltpu.make_async_copy(
+            packed.at[here, pl.ds(0, slots), last_columns], mixed_out.at[here, :, last_columns],
+            own_sem.at[0],
+        ),
+        pltpu.make_async_copy(packed_parts.at[here], parts_out.at[here], own_sem.at[1]),
+    ]
+    for copy in own_rows:
+        copy.start()
+    for copy in own_rows:
+        copy.wait()
+    for f in range(cots, early):
+        own_copy(f).wait()
+
+    across = (((1,), (1,)), ((), ()))
+    expert = me * number + here
+    column = lax.broadcasted_iota(jnp.int32, (1, parts_in.shape[1]), 1)
+    mine = (lax.rem(column, experts) == expert) & (column < 3 * experts)
+    in_rows, in_grads, out_rows = (pl.ds(i * slots, slots) for i in range(3))
+    cut_rows = slots
+
+    def stores(source):
+        given = (
+            (branch.at[out_rows], rows_out), (scaled, scaled_out), (active, active_out),
+            (gate_grad, gate_out), (up_grad, up_out), (dots, dots_out),
+        )
+        return [
+            pltpu.make_async_copy(value, out.at[source], store_sem.at[i])
+            for i, (value, out) in enumerate(given)
+        ]
+
+    @pl.loop(0, number)
+    def _(i):
+        _, source = partner(sizes, i)
+        for wave, later in zip(waves, waves[1:]):
+            @pl.when(i == wave[0])
+            def _():
+                for turn in wave:
+                    row_copy(turn).wait_send()
+                send_rows(later)
+
+        @pl.when(i > 0)
+        def _():
+            row_copy(i).wait_recv()
+            part_copy(i).wait_recv()
+
+        @pl.when(i == 1)
+        def _():
+            for f in range(early):
+                for ahead in range(1, number):
+                    plane_copy(f, ahead).wait_recv()
+
+        loads = [
+            pltpu.make_async_copy(mixed_out.at[source], branch.at[in_rows], load_sem.at[0]),
+            pltpu.make_async_copy(grads_out.at[source], branch.at[in_grads], load_sem.at[1]),
+            pltpu.make_async_copy(parts_out.at[source], parts_in, load_sem.at[2]),
+        ]
+        for copy in loads:
+            copy.start()
+
+        @pl.when(i > 0)
+        def _():
+            for copy in stores(source):
+                copy.wait()
+
+        for copy in loads:
+            copy.wait()
+
+        @pl.loop(0, slots // cut_rows)
+        def _(part):
+            at = pl.ds(pl.multiple_of(part * cut_rows, cut_rows), cut_rows)
+            at_in = at
+            at_grads = pl.ds(pl.multiple_of(slots + part * cut_rows, cut_rows), cut_rows)
+            at_out = pl.ds(pl.multiple_of(2 * slots + part * cut_rows, cut_rows), cut_rows)
+            parts = parts_in[at].astype(full)
+            slot_gates = jnp.sum(jnp.where(mine, parts, 0.0), axis=-1, keepdims=True)
+            gate_pre = jnp.dot(branch[at_in], gate_w_ref[0], preferred_element_type=full)
+            up_pre = jnp.dot(branch[at_in], up_w_ref[0], preferred_element_type=full)
+            act_grad = slot_gates * lax.dot_general(
+                branch[at_grads], down_w_ref[0], across, preferred_element_type=full
+            )
+            sigma = 1.0 / (1.0 + jnp.exp(-gate_pre))
+            silu = gate_pre * sigma
+            activated = silu * up_pre
+            active_low = activated.astype(low)
+            active[at] = (slot_gates * activated).astype(low)
+            up_low = (act_grad * silu).astype(low)
+            gate_low = (act_grad * up_pre * sigma * (1.0 + gate_pre * (1.0 - sigma))).astype(low)
+            up_grad[at] = up_low
+            gate_grad[at] = gate_low
+            branch[at_out] = (
+                lax.dot_general(gate_low, gate_w_ref[0], across, preferred_element_type=full)
+                + lax.dot_general(up_low, up_w_ref[0], across, preferred_element_type=full)
+            ).astype(low)
+            given = jnp.dot(active_low, down_w_ref[0], preferred_element_type=full)
+            given = given.astype(low).astype(full)
+            scaled[at] = (slot_gates * given).astype(low)
+            dot = jnp.sum(given * branch[at_grads].astype(full), axis=-1, keepdims=True)
+            first = dot.astype(low).astype(full)
+            second = (dot - first).astype(low).astype(full)
+            third = dot - first - second
+            terms = jnp.where(
+                column < experts, first, jnp.where(column < 2 * experts, second, third)
+            )
+            dots[at] = jnp.where(mine, terms, 0.0).astype(low)
+
+        for copy in stores(source):
+            copy.start()
+
+    for copy in stores(here):
+        copy.wait()
+    for turn in waves[-1]:
+        row_copy(turn).wait_send()
     for f in range(len(pieces)):
         for distance in range(n):
             for step in (-1, 1):
@@ -434,48 +563,68 @@
                 def _():
                     line_copy(f, origin, step).wait_send()
 
+    for f in range(cots, early):
         for ahead in range(1, number):
-            plane_copy(f, ahead).wait()
-        own_copy(f).wait()
-
-
-def dispatch(attended, back, tokens, gain, router, chosen, cot, pick, experts, sizes, collective, part=512):
+            plane_copy(f, ahead).wait_send()
+    row_copy(1).wait_send()
+    for turn in range(1, number):
+        part_copy(turn).wait_send()
+
+
+def dispatch(
+    attended, back, tokens, gain, router, chosen, cot, pick, gate_weight, up_weight, down_weight,
+    experts, sizes, collective, part=512,
+):
     rows_here, width = tokens.shape
+    inner = gate_weight.shape[2]
     lanes = router.shape[1]
-    widths = [width, width, lanes if 3 * experts <= lanes else 3 * lanes]
+    extra = lanes if 3 * experts <= lanes else 3 * lanes
+    widths = [width, width, extra]
     n, n_ctx, number = sizes["dp"], sizes["ctx"], sizes["ctx"] * sizes["exp"]
     groups, dests, rows, _ = pick.shape
+    slots = groups * rows
     pieces = cut(widths, part)
     count = len(pieces)
+    low, full = jnp.bfloat16, jnp.float32
     vmem, anywhere = pl.BlockSpec(memory_space=pltpu.VMEM), pl.BlockSpec(memory_space=pl.ANY)
+    block = lambda *shape: pltpu.VMEM(shape, low)
+    dma = lambda *shape: pltpu.SemaphoreType.DMA(shape)
+    by_source = lambda columns: jax.ShapeDtypeStruct((number, slots, columns), low)
     return pl.pallas_call(
         functools.partial(dispatch_kernel, sizes=sizes, pieces=pieces, experts=experts),
-        in_specs=[vmem] * 8,
-        out_specs=[anywhere] * 3 + [vmem] * 2,
-        out_shape=[
-            jax.ShapeDtypeStruct((number, groups * rows, columns), jnp.bfloat16)
-            for columns in widths
+        in_specs=[vmem, anywhere] + [vmem] * 4 + [anywhere] + [vmem] * 4,
+        out_specs=[anywhere] * 3 + [vmem] * 2 + [anywhere] * 6,
+        out_shape=[by_source(columns) for columns in widths]
+        + [
+            jax.ShapeDtypeStruct((rows_here, width), full),
+            jax.ShapeDtypeStruct((rows_here, lanes), full),
         ]
-        + [
-            jax.ShapeDtypeStruct((rows_here, width), jnp.float32),
-            jax.ShapeDtypeStruct((rows_here, lanes), jnp.float32),
-        ],
-        scratch_shapes=[pltpu.VMEM((n_ctx, rows_here, width), jnp.bfloat16)]
-        + square_scratch(rows_here, width)
-        + [pltpu.VMEM((rows_here, width), jnp.bfloat16)]
-        + [pltpu.VMEM((n, rows_here, columns), jnp.bfloat16) for columns in widths]
-        + [pltpu.VMEM((dests, groups * rows, columns), jnp.bfloat16) for columns in widths]
-        + [
-            pltpu.SemaphoreType.DMA((count, n, 2)),
-            pltpu.SemaphoreType.DMA((count, n)),
-            pltpu.SemaphoreType.DMA((count, number)),
-            pltpu.SemaphoreType.DMA((count, number)),
-            pltpu.SemaphoreType.DMA((count,)),
+        + [by_source(columns) for columns in (inner, inner, inner, width, width, extra)],
+        scratch_shapes=[
+            block(max(n_ctx * rows_here, 3 * slots), width),
+            *square_scratch(rows_here, width),
+            block(n, rows_here, width),
+            block(n, rows_here, width),
+            block(n, rows_here, extra),
+            block(dests, slots, width),
+            block(dests, slots, extra),
+            block(slots, extra),
+            block(slots, inner),
+            block(slots, inner),
+            block(slots, inner),
+            block(slots, width),
+            block(slots, extra),
+            dma(count, n, 2), dma(count, n), dma(count, number), dma(count, number), dma(count),
+            dma(number), dma(number), dma(number), dma(number),
+            dma(max(3, back.shape[0] // staged_rows(slots))), dma(6),
         ],
         compiler_params=pltpu.CompilerParams(
             collective_id=collective, has_side_effects=True, vmem_limit_bytes=VMEM
         ),
-    )(attended, back, tokens, gain, router, chosen, cot, pick)
+    )(
+        attended, back, tokens, gain, router, chosen, cot, pick, gate_weight, up_weight,
+        down_weight,
+    )
 
 
 def combine_kernel(
@@ -695,90 +844,22 @@
     )
 
 
-def expert_kernel(
-    here_ref, in_ref, parts_ref, grad_ref, gate_w_ref, up_w_ref, down_w_ref, active_ref, gate_ref,
-    up_ref, rows_ref, scaled_ref, dots_ref, *, experts,
-):
-    full, low = jnp.float32, jnp.bfloat16
-    across = (((1,), (1,)), ((), ()))
-    grads = grad_ref[0]
-    column = lax.broadcasted_iota(jnp.int32, (1, parts_ref.shape[2]), 1)
-    mine = lax.rem(column, experts) == here_ref[0]
-    parts = parts_ref[0].astype(full)
-    gates = jnp.sum(jnp.where(mine & (column < 3 * experts), parts, 0.0), axis=-1, keepdims=True)
-    gate_pre = jnp.dot(in_ref[0], gate_w_ref[0], preferred_element_type=full)
-    up_pre = jnp.dot(in_ref[0], up_w_ref[0], preferred_element_type=full)
-    act_grad = gates * lax.dot_general(grads, down_w_ref[0], across, preferred_element_type=full)
-    sigma = 1.0 / (1.0 + jnp.exp(-gate_pre))
-    silu = gate_pre * sigma
-    activated = silu * up_pre
-    active = activated.astype(low)
-    active_ref[0] = (gates * activated).astype(low)
-    up_grad = (act_grad * silu).astype(low)
-    gate_grad = (act_grad * up_pre * sigma * (1.0 + gate_pre * (1.0 - sigma))).astype(low)
-    up_ref[0] = up_grad
-    gate_ref[0] = gate_grad
-    rows_ref[0] = (
-        lax.dot_general(gate_grad, gate_w_ref[0], across, preferred_element_type=full)
-        + lax.dot_general(up_grad, up_w_ref[0], across, preferred_element_type=full)
-    ).astype(low)
-    given = jnp.dot(active, down_w_ref[0], preferred_element_type=full).astype(low).astype(full)
-    scaled_ref[0] = (gates * given).astype(low)
-    dots = jnp.sum(given * grads.astype(full), axis=-1, keepdims=True)
-    first = dots.astype(low).astype(full)
-    second = (dots - first).astype(low).astype(full)
-    third = dots - first - second
-    spread = jnp.where(column < experts, first, jnp.where(column < 2 * experts, second, third))
-    dots_ref[0] = jnp.where(mine & (column < 3 * experts), spread, 0.0).astype(low)
-
-
-def expert(here, rows_in, parts, grads, gate_weight, up_weight, down_weight, experts):
-    sources, rows, width = rows_in.shape
-    inner = gate_weight.shape[2]
-    extra = parts.shape[2]
-    by_source = lambda columns: pl.BlockSpec((1, rows, columns), lambda i: (i, 0, 0))
-    fixed = lambda shape: pl.BlockSpec(
-        shape, lambda i: (0, 0, 0), pipeline_mode=pl.Buffered(buffer_count=1)
-    )
-    out = lambda columns: jax.ShapeDtypeStruct((sources, rows, columns), jnp.bfloat16)
-    return pl.pallas_call(
-        functools.partial(expert_kernel, experts=experts),
-        grid=(sources,),
-        in_specs=[
-            pl.BlockSpec(memory_space=pltpu.SMEM),
-            by_source(width),
-            by_source(extra),
-            by_source(width),
-            fixed((1, width, inner)),
-            fixed((1, width, inner)),
-            fixed((1, inner, width)),
-        ],
-        out_specs=[by_source(c) for c in (inner, inner, inner, width, width, extra)],
-        out_shape=[out(c) for c in (inner, inner, inner, width, width, extra)],
-        compiler_params=pltpu.CompilerParams(vmem_limit_bytes=VMEM),
-        cost_estimate=pl.CostEstimate(
-            flops=12 * sources * rows * width * inner, bytes_accessed=60 << 20, transcendentals=0
-        ),
-    )(here, rows_in, parts, grads, gate_weight, up_weight, down_weight)
-
-
 def gather_kernel(
-    token_ref, front_ref, back_ref, route_ref, tokens_ref, fronts_ref, backs_ref, routes_ref,
-    held, sq_send, sq_recv, own_sem, fa_send, fa_recv, fl_send, fl_recv, fp_send, fp_recv,
-    bl_send, bl_recv, ba_send, ba_recv, bp_send, bp_recv, rl_send, rl_recv, *, sizes,
+    token_ref, front_ref, back_ref, route_ref, cos_ref, sin_ref, bounds_ref,
+    fronts_out, backs_ref, routes_ref, hidden_out, raw_out, turned_out, attended_ref,
+    tokens_ref, fronts_ref, held, hidden, raw, turned,
+    sq_send, sq_recv, own_sem, fa_send, fa_recv, fl_send, fl_recv, fp_send, fp_recv,
+    bl_send, bl_recv, ba_send, ba_recv, bp_send, bp_recv, rl_send, rl_recv, store_sem,
+    *, sizes, gain_len, heads, kv_heads,
 ):
     n, n_ctx, n_exp = sizes["dp"], sizes["ctx"], sizes["exp"]
     z, c, k = (lax.axis_index(a) for a in ALL)
-    by_x, by_y = square(sizes)
-    far = n_ctx - 1 - c
-    half = token_ref.shape[1] // 2
+    low, full = jnp.bfloat16, jnp.float32
+    count, width = token_ref.shape
+    owned = front_ref.shape[1]
+    head = cos_ref.shape[1]
+    columns = raw.shape[1]
     greet(sizes)
-
-    def remote(source, target, send, recv, device):
-        return pltpu.make_async_remote_copy(
-            src_ref=source, dst_ref=target, send_sem=send, recv_sem=recv, device_id=device,
-            device_id_type=MESH,
-        )
 
     def front_across(ahead):
         target = lax.rem(c + ahead, n_ctx)
@@ -826,23 +907,38 @@
             here, here, rl_send.at[origin, (step + 1) // 2], rl_recv.at[origin], {"dp": z + step}
         )
 
-    def columns(part):
-        return pl.ds(part * half, half)
-
-    def token_copy(place, part, to_y, number):
-        here = tokens_ref.at[place, :, columns(part)]
-        source = token_ref.at[:, columns(part)] if number < 4 else here
-        return remote(
-            source, here, sq_send.at[number], sq_recv.at[number], {"ctx": by_y if to_y else by_x}
-        )
-
-    firsts = [(0, False, 0), (1, True, 1), (1, False, 2), (0, True, 3)]
-
     def in_line(step):
         return (z + step >= 0) & (z + step < n)
 
+    def start_line(line):
+        for step in (-1, 1):
+            @pl.when(in_line(step))
+            def _():
+                line(z, step).start()
+
+    def pass_on(line, distance, after):
+        for step in (-1, 1):
+            origin = z - step * distance
+
+            @pl.when((origin >= 0) & (origin < n))
+            def _():
+                line(origin, step).wait_recv()
+
+                @pl.when(in_line(step))
+                def _():
+                    line(origin, step).start()
+
+                after(origin)
+
+    def nothing(origin):
+        pass
+
+    def to_siblings(origin):
+        for ahead in range(1, n_exp):
+            front_pair(origin, ahead).start()
+
+    tokens = SquareGather(sizes, token_ref, tokens_ref, sq_send, sq_recv, own_sem.at[0])
     own_copies = [
-        pltpu.make_async_copy(token_ref, tokens_ref.at[c], own_sem.at[0]),
         pltpu.make_async_copy(front_ref.at[c], fronts_ref.at[z, c, k], own_sem.at[1]),
         pltpu.make_async_copy(back_ref, held.at[z], own_sem.at[2]),
         pltpu.make_async_copy(route_ref, routes_ref.at[z], own_sem.at[3]),
@@ -851,80 +947,131 @@
         copy.start()
     for ahead in range(1, n_ctx):
         front_across(ahead).start()
-    for part, to_y, number in firsts:
-        token_copy(c, part, to_y, number).start()
+    tokens.start()
     for copy in own_copies:
         copy.wait()
-
-    def start_line(line):
-        for step in (-1, 1):
-            @pl.when(in_line(step))
-            def _():
-                line(z, step).start()
-
     start_line(back_line)
     start_line(route_line)
-
-    def pass_on(line, origin, step, after):
-        @pl.when((origin >= 0) & (origin < n))
-        def _():
-            line(origin, step).wait_recv()
-
-            @pl.when(in_line(step))
-            def _():
-                line(origin, step).start()
-
-            after(origin)
-
-    def nothing(origin):
-        pass
-
-    def to_siblings(origin):
-        for ahead in range(1, n_exp):
-            front_pair(origin, ahead).start()
-
     for ahead in range(1, n_ctx):
         front_across(ahead).wait_recv()
+    start_line(front_line)
     to_siblings(z)
+    pass_on(back_line, 1, nothing)
+    tokens.pass_on()
     for distance in range(1, n):
-        for step in (-1, 1):
-            pass_on(back_line, z - step * distance, step, nothing)
-        if distance == 1:
-            token_copy(by_x, 0, False, 0).wait_recv()
-            token_copy(by_x, 0, True, 4).start()
-            token_copy(by_y, 1, True, 1).wait_recv()
-            token_copy(by_y, 1, False, 5).start()
-        if distance == max(1, n - 2):
-            start_line(front_line)
+        pass_on(front_line, distance, to_siblings)
+        pass_on(route_line, distance, nothing)
+    for origin in range(n):
+        for ahead in range(1, n_exp):
+            front_pair(origin, ahead).wait_recv()
+    tokens.finish()
+    fronts_store = pltpu.make_async_copy(fronts_ref, fronts_out, store_sem.at[0])
+    fronts_store.start()
+
+    gains = fronts_ref[..., columns : columns + 128].reshape(width, 128).astype(full).T
+    gain = gains[0:1, :]
+    row = lax.broadcasted_iota(jnp.int32, (width, head), 0)
+    lane = lax.broadcasted_iota(jnp.int32, (width, head), 1)
+    spot = lane // gain_len * owned + lax.rem(lane, gain_len)
+    packed = gains[0:8, :].astype(low)
+    scales = [
+        jnp.dot(packed, (row == spot + shift).astype(low), preferred_element_type=full)[2:3, :]
+        for shift in (0, gain_len)
+    ]
+
+    def hidden_store(i):
+        return pltpu.make_async_copy(
+            hidden, hidden_out.at[pl.ds(pl.multiple_of(i * count, count), count)], store_sem.at[1]
+        )
+
+    def raw_store(i):
+        return pltpu.make_async_copy(
+            raw, raw_out.at[pl.ds(pl.multiple_of(i * count, count), count)], store_sem.at[2]
+        )
+
+    def project(first, last):
+        @pl.loop(first, last)
+        def _(i):
+            x = tokens_ref[i].astype(full)
+            inverse = lax.rsqrt(jnp.mean(x * x, axis=-1, keepdims=True) + eps_norm)
+
+            @pl.when(i > 0)
+            def _():
+                hidden_store(i).wait()
+                raw_store(i).wait()
+
+            hidden[...] = ((x * inverse) * gain).astype(low)
+            hidden_store(i).start()
+            raw[...] = jnp.dot(
+                hidden[...], fronts_ref[..., 0:columns].reshape(width, columns),
+                preferred_element_type=full,
+            )
+            raw_store(i).start()
+            at = pl.ds(pl.multiple_of(i * count, count), count)
+            cosine, sine = cos_ref[at], sin_ref[at]
+            for h in range(heads + kv_heads):
+                here = slice(h * head, (h + 1) * head)
+                part = raw[:, here]
+                factor = lax.rsqrt(jnp.mean(part * part, axis=-1, keepdims=True) + eps_norm)
+                scaled = part * factor * scales[0 if h < heads else 1]
+                spun = pltpu.roll(scaled, head // 2, 1)
+                turned[at, here] = (scaled * cosine + spun * sine).astype(low)
+            rest = slice((heads + kv_heads) * head, columns)
+            turned[at, rest] = raw[:, rest].astype(low)
+
+    rows = n_ctx * count
+    group = heads // kv_heads
+
+    def attend(first_head, last_head):
+        @pl.loop(first_head, last_head)
+        def _(h):
+            at = lambda which: pl.ds(pl.multiple_of(which * head, head), head)
+            kv = h // group
+            for first in range(0, rows, count):
+                last = first + count
+                allowed = seen(bounds_ref, first, count, last)
+                shares = shares_of(
+                    turned[first:last, at(h)], turned[0:last, at(heads + kv)], allowed,
+                    head ** (-0.5),
+                )
+                attended_ref[first:last, at(h)] = jnp.dot(
+                    shares.astype(low), turned[0:last, at(heads + kv_heads + kv)],
+                    preferred_element_type=full,
+                ).astype(low)
+
+    project(0, n_ctx // 2)
+    if n > 2:
+        pass_on(back_line, 2, nothing)
+    project(n_ctx // 2, n_ctx)
+    turned_store = pltpu.make_async_copy(turned, turned_out, store_sem.at[3])
+    turned_store.start()
+    attend(0, heads // 4)
+    for distance in range(3, n):
+        pass_on(back_line, distance, nothing)
     for ahead in range(1, n_ctx):
         back_across(ahead).start()
     own_back = pltpu.make_async_copy(held.at[c], backs_ref.at[c, k], own_sem.at[4])
     own_back.start()
+    attend(heads // 4, heads)
     own_back.wait()
     for ahead in range(1, n_exp):
         back_pair(c, ahead).start()
-    for distance in range(1, n):
-        for step in (-1, 1):
-            pass_on(front_line, z - step * distance, step, to_siblings)
-            pass_on(route_line, z - step * distance, step, nothing)
     for behind in range(1, n_ctx):
         back_across(behind).wait_recv()
         source = lax.rem(c + n_ctx - behind, n_ctx)
         for ahead in range(1, n_exp):
             back_pair(source, ahead).start()
 
-    token_copy(by_x, 1, False, 2).wait_recv()
-    token_copy(by_y, 0, True, 3).wait_recv()
-    token_copy(far, 0, True, 4).wait_recv()
-    token_copy(far, 1, False, 5).wait_recv()
-    for part, to_y, number in firsts + [(0, True, 4), (1, False, 5)]:
-        token_copy(c, part, to_y, number).wait_send()
+    fronts_store.wait()
+    hidden_store(n_ctx - 1).wait()
+    raw_store(n_ctx - 1).wait()
+    turned_store.wait()
     for ahead in range(1, n_ctx):
         front_across(ahead).wait_send()
         back_across(ahead).wait_send()
     for origin in range(n):
         for ahead in range(1, n_exp):
-            front_pair(origin, ahead).wait()
+            front_pair(origin, ahead).wait_send()
     for source in range(n_ctx):
         for ahead in range(1, n_exp):
             back_pair(source, ahead).wait()
@@ -938,31 +1085,49 @@
                     line(origin, step).wait_send()
 
 
-def gather(tokens, front, back, routes, sizes, collective):
+def gather(
+    tokens, front, back, routes, cosine, sine, bounds, gain_len, heads, kv_heads, sizes, collective
+):
     n, n_ctx, n_exp = sizes["dp"], sizes["ctx"], sizes["exp"]
-    _, rows, columns = front.shape
+    _, rows, front_columns = front.shape
+    count, width = tokens.shape
+    head = cosine.shape[1]
+    columns = (heads + 2 * kv_heads) * head
+    seq = n_ctx * count
+    low, full = jnp.bfloat16, jnp.float32
     dma = lambda *shape: pltpu.SemaphoreType.DMA(shape)
+    vmem, anywhere = pl.BlockSpec(memory_space=pltpu.VMEM), pl.BlockSpec(memory_space=pl.ANY)
     return pl.pallas_call(
-        functools.partial(gather_kernel, sizes=sizes),
-        in_specs=[pl.BlockSpec(memory_space=pltpu.VMEM)] * 4,
-        out_specs=[pl.BlockSpec(memory_space=pl.ANY)] * 4,
+        functools.partial(
+            gather_kernel, sizes=sizes, gain_len=gain_len, heads=heads, kv_heads=kv_heads
+        ),
+        in_specs=[vmem] * 6 + [pl.BlockSpec(memory_space=pltpu.SMEM)],
+        out_specs=[anywhere] * 6 + [vmem],
         out_shape=[
-            jax.ShapeDtypeStruct((n_ctx,) + tokens.shape, tokens.dtype),
-            jax.ShapeDtypeStruct((n, n_ctx, n_exp, rows, columns), front.dtype),
-            jax.ShapeDtypeStruct((n_ctx, n_exp) + back.shape, back.dtype),
+            jax.ShapeDtypeStruct((n, n_ctx, n_exp, rows, front_columns), low),
+            jax.ShapeDtypeStruct((n_ctx, n_exp) + back.shape, low),
             jax.ShapeDtypeStruct((n,) + routes.shape, routes.dtype),
+            jax.ShapeDtypeStruct((seq, width), low),
+            jax.ShapeDtypeStruct((seq, columns), full),
+            jax.ShapeDtypeStruct((seq, columns), low),
+            jax.ShapeDtypeStruct((seq, heads * head), low),
         ],
         scratch_shapes=[
-            pltpu.VMEM((n,) + back.shape, back.dtype),
+            pltpu.VMEM((n_ctx, count, width), low),
+            pltpu.VMEM((n, n_ctx, n_exp, rows, front_columns), low),
+            pltpu.VMEM((n,) + back.shape, low),
+            pltpu.VMEM((count, width), low),
+            pltpu.VMEM((count, columns), full),
+            pltpu.VMEM((seq, columns), low),
             dma(6), dma(6), dma(5),
             dma(n_ctx), dma(n_ctx), dma(n, 2), dma(n), dma(n, n_exp), dma(n, n_exp),
             dma(n, 2), dma(n), dma(n_ctx), dma(n_ctx), dma(n_ctx, n_exp), dma(n_ctx, n_exp),
-            dma(n, 2), dma(n),
+            dma(n, 2), dma(n), dma(4),
         ],
         compiler_params=pltpu.CompilerParams(
             collective_id=collective, has_side_effects=True, vmem_limit_bytes=VMEM
         ),
-    )(tokens, front, back, routes)
+    )(tokens, front, back, routes, cosine, sine, bounds)
 
 
 def finish_kernel(
@@ -1311,14 +1476,31 @@
     def small_copy(ahead):
         target = lax.rem(here + ahead, devices)
         return remote(
-            small_all.at[target], small_in.at[ahead], s_send.at[ahead], s_recv.at[ahead],
+            small_all.at[target], small_in.at[ahead], s_send.at[0], s_recv.at[0],
             device_of(target),
+        )
+
+    def all_small():
+        others = pl.ds(1, devices - 1)
+        return remote(
+            small_all.at[others], small_in.at[others], s_send.at[0], s_recv.at[0], {"dp": z}
         )
 
     @pl.when(step == first_chunk + chunks)
     def _():
         for ahead in range(1, n_exp):
             front_pair(ahead).start()
+        gain_owned = head // devices
+        for index in range(devices):
+            for which in (0, 1):
+                small_all[index, which : which + 1, 0:gain_owned] = head_gains[
+                    which : which + 1, index * gain_owned : (index + 1) * gain_owned
+                ]
+
+        @pl.loop(1, devices)
+        def _(ahead):
+            small_copy(ahead).start()
+
         hidden = SquareScatter(
             sizes, shared, far_in, turn_out, turn_in, hidden_send, hidden_recv, tokens
         )
@@ -1352,6 +1534,9 @@
             stage_sem.at[0],
         )
         for piece in range(1, pieces):
+            if piece == pieces - 1:
+                all_small().wait_recv()
+                small_out[...] = small_all[here] + jnp.sum(small_in[1:devices], axis=0)
             mix_in(piece)
             mix_line(piece, n - 1)
             start_total(piece)
@@ -1378,19 +1563,6 @@
         inverse = lax.rsqrt(jnp.mean(x * x, axis=-1, keepdims=True) + eps_norm)
         normed = x * inverse
         grad = total[...]
-        gain_grad = jnp.sum(grad * normed, axis=0, keepdims=True)
-        owned, gain_owned = width // devices, head // devices
-        for index in range(devices):
-            small_all[index, 0:1, 0:owned] = gain_grad[:, index * owned : (index + 1) * owned]
-            for which in (0, 1):
-                small_all[index, 1 + which : 2 + which, 0:gain_owned] = head_gains[
-                    which : which + 1, index * gain_owned : (index + 1) * gain_owned
-                ]
-
-        @pl.loop(1, devices)
-        def _(ahead):
-            small_copy(ahead).start()
-
         scaled = grad * gain_ref[...]
         total[...] = inverse * (scaled - normed * jnp.mean(scaled * normed, axis=-1, keepdims=True))
         output_store.wait()
@@ -1402,21 +1574,11 @@
             staged[:, columns] = (total[:, columns] + loaded[piece % 2]).astype(low)
         tokens_store = pltpu.make_async_copy(staged, tokens_grad_ref, stage_sem.at[0])
         tokens_store.start()
-        small_out[...] = small_all[here]
-
-        @pl.loop(1, devices)
-        def _(ahead):
-            small_copy(ahead).wait_recv()
-            small_out[...] += small_in[ahead]
-
         for ahead in range(1, n_ctx):
             front_across(ahead).wait()
         tokens_store.wait()
 
-        @pl.loop(1, devices)
-        def _(ahead):
-            small_copy(ahead).wait_send()
-
+        all_small().wait_send()
         hidden.close()
         for ahead in range(1, n_exp):
             front_pair(ahead).wait_send()
@@ -1515,7 +1677,7 @@
             dma(2), dma(3), dma(2), dma(n_exp), dma(n_exp), dma(n_ctx), dma(n_ctx), dma(n),
             dma(n + 1), dma(n_exp), dma(n_exp), dma(n), dma(n + 1), dma(n_ctx), dma(n_ctx),
             dma(pieces, number), dma(pieces, number), dma(pieces), dma(pieces, n),
-            dma(pieces, n + 1), dma(devices), dma(devices),
+            dma(pieces, n + 1), dma(1), dma(1),
         ],
         compiler_params=pltpu.CompilerParams(
             collective_id=collective, has_side_effects=True, vmem_limit_bytes=VMEM
@@ -1591,10 +1753,14 @@
         axis=2,
     )
     sizes = {"dp": n_dp, "ctx": n_ctx, "exp": n_exp}
-    whole_tokens, front, output_part, column_routes = gather(
-        tokens[0], front, output_weight.astype(low), routes[0], sizes, 3
+    heads_here = heads // n_ctx
+    cosine, sine = rope_tables(jnp.arange(seq_len, dtype=jnp.int32), head_dim)
+    half = head_dim // 2
+    sine = jnp.concatenate([-sine[:, :half], sine[:, half:]], axis=1)
+    front, output_part, column_routes, hidden, raw, turned, attended_low = gather(
+        tokens[0], front, output_weight.astype(low), routes[0], cosine, sine, bounds, gain_len,
+        heads_here, kv_here, sizes, 3,
     )
-    whole_tokens = whole_tokens.reshape(seq_len, width)
     front = front.reshape(width, -1)
     output_part = output_part.reshape(q_cols, width)
     small = front[:, q_cols + 2 * kv_cols :]
@@ -1624,30 +1790,19 @@
     slots = jnp.arange(slot_rows, dtype=full)
     pick = (slot_at.transpose(0, 2, 1)[:, :, None, :] == slots[:, None]).astype(low)
 
-    positions = jnp.arange(seq_len, dtype=jnp.int32)
-    cosine, sine = rope_tables(positions, head_dim)
-    half = head_dim // 2
-    sine = jnp.concatenate([-sine[:, :half], sine[:, half:]], axis=1)
     scales = jnp.stack([query_scale, key_scale])
-    heads_here = heads // n_ctx
-    hidden, raw, turned = project(
-        whole_tokens, first_gain[None], front, q_cols + 2 * kv_cols, scales, cosine, sine,
-        heads_here, kv_here, tok_count,
-    )
-    attended_low = attend(bounds, turned, heads_here, kv_here, head_dim, tok_count)
 
     lanes = -(-experts // 128) * 128
     router_wide = jnp.pad(router_full, ((0, 0), (0, lanes - experts)))
     own_chosen = jnp.any(
         routes[0][:, :, None] == jnp.arange(lanes, dtype=jnp.int32), axis=1
     ).astype(full)
-    grad_rows, expert_in, part_rows, middle, own_gates = dispatch(
+    (
+        grad_rows, expert_in, _, middle, own_gates, active, gate_grad, up_grad, row_grads,
+        scaled_out, dot_rows,
+    ) = dispatch(
         attended_low, output_part, tokens[0], second_gain[None], router_wide, own_chosen,
-        cotangent[0], pick, experts, sizes, 1,
-    )
-    here = (dp_index * n_ctx + lax.axis_index("ctx")) * n_exp + lax.axis_index("exp")
-    active, gate_grad, up_grad, row_grads, scaled_out, dot_rows = expert(
-        here[None], expert_in, part_rows, grad_rows, gate_weight, up_weight, down_weight, experts
+        cotangent[0], pick, gate_weight, up_weight, down_weight, experts, sizes, 1,
     )
     branch_low, middle_grad, second_gain_grad, router_grad, gate_w_grad, up_w_grad, down_grad = combine(
         row_grads, dot_rows, pick, middle, cotangent[0], second_gain[None], own_gates, router_wide,
@@ -1676,9 +1831,14 @@
     query_share = front_grad[:, :, :q_cols].transpose(1, 0, 2).reshape(rows, -1)
     key_share = front_grad[:, :, q_cols : q_cols + kv_cols].transpose(1, 0, 2).reshape(rows, -1)
     value_share = front_grad[:, :, q_cols + kv_cols :].transpose(1, 0, 2).reshape(rows, -1)
-    first_share = small[0, :rows]
-    query_gain_share = small[1, :gain_len]
-    key_gain_share = small[2, :gain_len]
+    first_share = sum(
+        jnp.sum(weight.astype(low).astype(full) * grad, axis=1)
+        for weight, grad in (
+            (query_weight, query_share), (key_weight, key_share), (value_weight, value_share)
+        )
+    ) / attention_gain.astype(low).astype(full)
+    query_gain_share = small[0, :gain_len]
+    key_gain_share = small[1, :gain_len]
     rest = small[3:].reshape(-1)
     second_share = rest[:rows]
     router_share = rest[rows : rows + rows * experts].reshape(rows, experts)

time: 905 us -> 860 us (0.950)
  Pallas kernels: 831 us -> 789 us
    pallas_call x4 -> x1, Pallas kernels: 185 us -> 111 us  [gather(): pl.pallas_call(functools.partial(gather_kernel, sizes=sizes, gain_len=gai...]
    pallas_call x1, Pallas kernels: 260 us -> 288 us  [dispatch(): pl.pallas_call(functools.partial(dispatch_kernel, sizes=sizes, pieces=pie...]
    pallas_call x1, Pallas kernels: 173 us -> 183 us  [combine(): pl.pallas_call(functools.partial(combine_kernel, sizes=sizes, pieces=piec...]
    unnamed x41 -> x51, local copies, waits for them, and re-layouts: 16.5 us -> 19.4 us
where the time goes in v5:
time: 860 us; the launch traced here: 852 us
  Pallas kernels  789 us (92%)
  local copies, waits for them, and re-layouts  29.3 us (3%)
  other arithmetic  17.3 us (2%)
  matrix products  15.4 us (2%)
    pallas_call x1, Pallas kernels, dispatch(): pl.pallas_call(functools.partial(dispatch_kernel, sizes=sizes, pieces=pie...  288 us
    pallas_call x1, Pallas kernels, finish(): pl.pallas_call(functools.partial(finish_kernel, block=count, heads=heads,...  207 us
    pallas_call x1, Pallas kernels, combine(): pl.pallas_call(functools.partial(combine_kernel, sizes=sizes, pieces=piec...  183 us
    pallas_call x1, Pallas kernels, gather(): pl.pallas_call(functools.partial(gather_kernel, sizes=sizes, gain_len=gai...  111 us
    unnamed x51, local copies, waits for them, and re-layouts  19.4 us

profile of v5, /device:TPU:14, one launch (start us, length us, event | category | flops | bytes accessed | tf_op | source)
XLA Modules:
  0.0 852.0 jit_solution(1407351149637394651)
XLA Ops:
  1.0 2.7 fusion.5
  3.9 1.0 pad_maximum_fusion.2.sin_ref
  5.4 0.9 pad_maximum_fusion.front_ref
  7.9 110.6 %shard_map.263 = (bf16[4,4,2,64,1408]{4,3,2,1,0:T(8,128)(2,1)}, bf16[4,2,128,2048]{3,2,1,0:T(8,128)(2,1)}, s32[4,256,8]{2,1,0:T(8,128)}, bf16[1024,2048]{1,0:T(8...) custom-call(bf16[256,2048]{1,0:T(8,128)(2,1)} %bitcast.86, ...), custom_call_target="tpu_custom_call" | custom-call | tf_op jit(solution)/shard_map/pallas_call | solution.py:1100
  118.6 1.2 copy.48
  120.3 2.0 fusion.pick_ref
  122.2 2.4 convert_reduce_fusion
  124.6 1.2 slice.80
  125.9 0.9 pad.23.router_ref
  127.9 287.9 %shard_map.264 = (bf16[8,288,2048]{2,1,0:T(8,128)(2,1)}, bf16[8,288,2048]{2,1,0:T(8,128)(2,1)}, bf16[8,288,128]{2,1,0:T(8,128)(2,1)}, f32[256,2048]{1,0:T(8,128)...) custom-call(bf16[1024,1024]{1,0:T(8,128)(2,1)} %get-tuple-element.44, ...), custom_call_target="tpu_custom_call" | custom-call | tf_op jit(solution)/shard_map/pallas_call | solution.py:593
  415.8 183.1 %shard_map.265 = (bf16[4,256,2048]{2,1,0:T(8,128)(2,1)}, f32[256,2048]{1,0:T(8,128)}, f32[1,2048]{1,0:T(1,128)}, f32[128,2048]{1,0:T(8,128)}, f32[2048,768]{1,0:...) custom-call(bf16[8,288,2048]{2,1,0:T(8,128)(2,1)} %get-tuple-element.48.rows_ref, ...), custom_call_target="tpu_custom_call" | custom-call | tf_op jit(solution)/shard_map/pallas_call | solution.py:815
  598.9 1.0 slice_bitcast_fusion.1
  601.2 1.4 reduce.9
  603.8 9.6 %convolution_convert_fusion = bf16[1024,2048]{1,0:T(8,128)(2,1)} fusion(bf16[1024,1024]{1,0:T(8,128)(2,1)} %get-tuple-element.44.attended_ref, bf16[1024,2048]{1,0:T(8,128)(2,1)} %bitcast.118), kind=kOutput, calls=%fused_computation.2 | convolution fusion | flops 4297064448 | bytes 10485760 | tf_op jit(solution)/shard_map/ti,td->id/dot_general | solution.py:1814
  613.4 5.7 convolution_convert_fusion.1.grad_ref
  619.1 1.4 slice_reduce_fusion
  621.5 207.1 %shard_map.266 = (bf16[256,2048]{1,0:T(8,128)(2,1)}, bf16[4,64,1280]{2,1,0:T(8,128)(2,1)}, bf16[256,2048]{1,0:T(8,128)(2,1)}, f32[128,2048]{1,0:T(8,128)}, f32[8...) custom-call(s32[1,2]{1,0:T(1,128)} %bounds_ref.3, ...), custom_call_target="tpu_custom_call" | custom-call | tf_op jit(solution)/shard_map/pallas_call | solution.py:1619
  828.6 1.2 convert_element_type.132
  834.2 2.3 copy.75
  836.5 2.5 copy.76
  839.0 1.0 copy.77
  840.0 6.1 copy.78
  846.0 2.8 copy.79
  849.1 2.7 copy.80
  (93 shorter events, 12.2 us)
Async XLA Ops:
  0.6 4.3 copy-start.11
  0.7 4.2 copy-start.12
  0.7 4.2 copy-start.9
  0.7 4.3 copy-start.14
  0.7 4.3 copy-start.15
  0.7 4.5 copy-start.6
  0.7 4.5 copy-start.7
  0.7 4.5 copy-start.1
  3.7 2.6 copy-start.10
  3.7 3.4 copy-start.4
  7.9 118.8 %copy-start.3 = (s32[1,256,8]{2,1,0:T(8,128)S(1)}, s32[1,256,8]{2,1,0:T(8,128)}, u32[]{:S(2)}) copy-start(s32[1,256,8]{2,1,0:T(8,128)} %copy.47) | copy-start | bytes 24580
  603.8 9.6 %copy-start = (bf16[4,2,128,2048]{3,2,1,0:T(8,128)(2,1)S(1)}, bf16[4,2,128,2048]{3,2,1,0:T(8,128)(2,1)}, u32[]{:S(2)}) copy-start(bf16[4,2,128,2048]{3,2,1,0:T(8,128)(2,1)} %get-tuple-element.45) | copy-start | bytes 12582916
  603.8 9.6 %copy-start.13 = (bf16[4,256,2048]{2,1,0:T(8,128)(2,1)S(1)}, bf16[4,256,2048]{2,1,0:T(8,128)(2,1)}, u32[]{:S(2)}) copy-start(bf16[4,256,2048]{2,1,0:T(8,128)(2,1)} %get-tuple-element.57) | copy-start | bytes 12582916
  829.8 2.6 copy-start.8
  830.1 9.9 %copy-start.2 = (f32[4,8,8,1024]{3,2,0,1:T(8,128)}, f32[4,8,8,1024]{3,2,0,1:T(8,128)S(1)}, u32[]{:S(2)}) copy-start(f32[4,8,8,1024]{3,2,0,1:T(8,128)S(1)} %copy.58) | copy-start | bytes 3145732
  830.1 8.9 %copy-start.5 = (f32[128,2048]{1,0:T(8,128)S(1)}, f32[128,2048]{1,0:T(8,128)}, u32[]{:S(2)}) copy-start(f32[128,2048]{1,0:T(8,128)} %get-tuple-element.142) | copy-start | bytes 3145732
  836.5 9.5 %slice-start.2 = ((s8[6291456]{0:T(1024)(128)(4,1)}), s8[4194304]{0:T(1024)(128)(4,1)S(1)}, s32[]{:S(2)}) async-start(s8[6291456]{0:T(1024)(128)(4,1)} %bitcast.94), calls=%async_computation.2 | async-start | bytes 8388608
  840.0 6.1 slice-start.3
  840.0 8.9 %slice-start = ((s8[6291456]{0:T(1024)(128)(4,1)}), s8[4194304]{0:T(1024)(128)(4,1)S(1)}, s32[]{:S(2)}) async-start(s8[6291456]{0:T(1024)(128)(4,1)} %bitcast.91), calls=%async_computation | async-start | bytes 8388608
  846.0 3.1 slice-start.1

commit v6 on v5

--- a/solution.py
+++ b/solution.py
@@ -224,14 +224,14 @@
 
 
 def dispatch_kernel(
-    attended_ref, back_ref, token_ref, gain_ref, router_ref, chosen_ref, cot_ref, pick_ref,
+    attended_ref, back_ref, token_ref, gain_ref, router_ref, chosen_ref, cot_ref, routes_ref,
     gate_w_ref, up_w_ref, down_w_ref,
     grads_out, mixed_out, parts_out, middle_ref, gates_ref, active_out, gate_out, up_out, rows_out,
-    scaled_out, dots_out,
-    branch, far_in, turn_out, turn_in, sq_send, sq_recv, cot_column, mixed_column, parts_column,
+    scaled_out, dots_out, pick_out,
+    pick_ref, branch, far_in, turn_out, turn_in, sq_send, sq_recv, cot_column, mixed_column, parts_column,
     packed, packed_parts, parts_in, active, gate_grad, up_grad, scaled, dots,
     line_send, line_recv, plane_send, plane_recv, own_sem, row_send, row_recv, part_send, part_recv,
-    load_sem, store_sem, *, sizes, pieces, experts,
+    load_sem, store_sem, *, sizes, pieces, experts, capacity,
 ):
     outs = (grads_out, mixed_out, parts_out)
     columns = (cot_column, mixed_column, parts_column)
@@ -350,6 +350,27 @@
         copy.start()
     own_cot.wait()
     send_own(0)
+
+    together = span // tokens
+    low_row = lax.broadcasted_iota(jnp.int32, (tokens, tokens), 0)
+    low_lane = lax.broadcasted_iota(jnp.int32, (tokens, tokens), 1)
+    earlier = (low_row < low_lane).astype(low)
+    named = me * dests + lax.broadcasted_iota(jnp.int32, (dests, 1), 0)
+    spots = lax.broadcasted_iota(jnp.int32, (rows, 1), 0).astype(full)
+    for b in range(n):
+        listed = routes_ref[b]
+        hot = jnp.zeros((dests, tokens), full)
+        for which in range(listed.shape[0]):
+            hot += (listed[which : which + 1, :] == named).astype(full)
+        before = jnp.dot(hot.astype(low), earlier, preferred_element_type=full)
+        spot = jnp.where(hot > 0, before + b % together * capacity, -1.0)
+        at = b % together * tokens
+        for j in range(dests):
+            pick_ref[b // together, j, :, at : at + tokens] = (
+                spot[j : j + 1, :] == spots
+            ).astype(low)
+    pick_store = pltpu.make_async_copy(pick_ref, pick_out, store_sem.at[6])
+    pick_store.start()
     for copy in weight_copies:
         copy.wait()
 
@@ -551,6 +572,7 @@
 
     for copy in stores(here):
         copy.wait()
+    pick_store.wait()
     for turn in waves[-1]:
         row_copy(turn).wait_send()
     for f in range(len(pieces)):
@@ -572,8 +594,8 @@
 
 
 def dispatch(
-    attended, back, tokens, gain, router, chosen, cot, pick, gate_weight, up_weight, down_weight,
-    experts, sizes, collective, part=512,
+    attended, back, tokens, gain, router, chosen, cot, routes, gate_weight, up_weight, down_weight,
+    experts, capacity, sizes, collective, part=512,
 ):
     rows_here, width = tokens.shape
     inner = gate_weight.shape[2]
@@ -581,7 +603,9 @@
     extra = lanes if 3 * experts <= lanes else 3 * lanes
     widths = [width, width, extra]
     n, n_ctx, number = sizes["dp"], sizes["ctx"], sizes["ctx"] * sizes["exp"]
-    groups, dests, rows, _ = pick.shape
+    together = 2 if 2 * capacity % 16 == 0 and n % 2 == 0 else n
+    groups, dests, rows = n // together, number, -(-together * capacity // 16) * 16
+    pick = (groups, dests, rows, together * rows_here)
     slots = groups * rows
     pieces = cut(widths, part)
     count = len(pieces)
@@ -591,16 +615,20 @@
     dma = lambda *shape: pltpu.SemaphoreType.DMA(shape)
     by_source = lambda columns: jax.ShapeDtypeStruct((number, slots, columns), low)
     return pl.pallas_call(
-        functools.partial(dispatch_kernel, sizes=sizes, pieces=pieces, experts=experts),
+        functools.partial(
+            dispatch_kernel, sizes=sizes, pieces=pieces, experts=experts, capacity=capacity
+        ),
         in_specs=[vmem, anywhere] + [vmem] * 4 + [anywhere] + [vmem] * 4,
-        out_specs=[anywhere] * 3 + [vmem] * 2 + [anywhere] * 6,
+        out_specs=[anywhere] * 3 + [vmem] * 2 + [anywhere] * 7,
         out_shape=[by_source(columns) for columns in widths]
         + [
             jax.ShapeDtypeStruct((rows_here, width), full),
             jax.ShapeDtypeStruct((rows_here, lanes), full),
         ]
-        + [by_source(columns) for columns in (inner, inner, inner, width, width, extra)],
+        + [by_source(columns) for columns in (inner, inner, inner, width, width, extra)]
+        + [jax.ShapeDtypeStruct(pick, low)],
         scratch_shapes=[
+            block(*pick),
             block(max(n_ctx * rows_here, 3 * slots), width),
             *square_scratch(rows_here, width),
             block(n, rows_here, width),
@@ -616,13 +644,13 @@
             block(slots, extra),
             dma(count, n, 2), dma(count, n), dma(count, number), dma(count, number), dma(count),
             dma(number), dma(number), dma(number), dma(number),
-            dma(max(3, back.shape[0] // staged_rows(slots))), dma(6),
+            dma(max(3, back.shape[0] // staged_rows(slots))), dma(7),
         ],
         compiler_params=pltpu.CompilerParams(
             collective_id=collective, has_side_effects=True, vmem_limit_bytes=VMEM
         ),
     )(
-        attended, back, tokens, gain, router, chosen, cot, pick, gate_weight, up_weight,
+        attended, back, tokens, gain, router, chosen, cot, routes, gate_weight, up_weight,
         down_weight,
     )
 
@@ -846,11 +874,12 @@
 
 def gather_kernel(
     token_ref, front_ref, back_ref, route_ref, cos_ref, sin_ref, bounds_ref,
-    fronts_out, backs_ref, routes_ref, hidden_out, raw_out, turned_out, attended_ref,
+    fronts_out, backs_ref, routes_ref, hidden_out, raw_out, turned_out, attended_ref, gains_ref,
+    scales_ref,
     tokens_ref, fronts_ref, held, hidden, raw, turned,
     sq_send, sq_recv, own_sem, fa_send, fa_recv, fl_send, fl_recv, fp_send, fp_recv,
     bl_send, bl_recv, ba_send, ba_recv, bp_send, bp_recv, rl_send, rl_recv, store_sem,
-    *, sizes, gain_len, heads, kv_heads,
+    *, sizes, gain_len, heads, kv_heads, experts,
 ):
     n, n_ctx, n_exp = sizes["dp"], sizes["ctx"], sizes["exp"]
     z, c, k = (lax.axis_index(a) for a in ALL)
@@ -968,16 +997,21 @@
     fronts_store = pltpu.make_async_copy(fronts_ref, fronts_out, store_sem.at[0])
     fronts_store.start()
 
-    gains = fronts_ref[..., columns : columns + 128].reshape(width, 128).astype(full).T
-    gain = gains[0:1, :]
+    place_of = columns + experts // 128 * 128
+    spun = fronts_ref[..., place_of : place_of + 128].reshape(width, 128).astype(full).T
+    lead = experts % 128
+    gain = spun[lead : lead + 1, :]
+    gains_ref[...] = spun[lead : lead + 8, :]
     row = lax.broadcasted_iota(jnp.int32, (width, head), 0)
     lane = lax.broadcasted_iota(jnp.int32, (width, head), 1)
     spot = lane // gain_len * owned + lax.rem(lane, gain_len)
-    packed = gains[0:8, :].astype(low)
+    packed = spun[lead : lead + 8, :].astype(low)
     scales = [
         jnp.dot(packed, (row == spot + shift).astype(low), preferred_element_type=full)[2:3, :]
         for shift in (0, gain_len)
     ]
+    scales_ref[0:1, :] = scales[0]
+    scales_ref[1:2, :] = scales[1]
 
     def hidden_store(i):
         return pltpu.make_async_copy(
@@ -1086,7 +1120,8 @@
 
 
 def gather(
-    tokens, front, back, routes, cosine, sine, bounds, gain_len, heads, kv_heads, sizes, collective
+    tokens, front, back, routes, cosine, sine, bounds, gain_len, heads, kv_heads, experts, sizes,
+    collective,
 ):
     n, n_ctx, n_exp = sizes["dp"], sizes["ctx"], sizes["exp"]
     _, rows, front_columns = front.shape
@@ -1099,10 +1134,11 @@
     vmem, anywhere = pl.BlockSpec(memory_space=pltpu.VMEM), pl.BlockSpec(memory_space=pl.ANY)
     return pl.pallas_call(
         functools.partial(
-            gather_kernel, sizes=sizes, gain_len=gain_len, heads=heads, kv_heads=kv_heads
+            gather_kernel, sizes=sizes, gain_len=gain_len, heads=heads, kv_heads=kv_heads,
+            experts=experts,
         ),
         in_specs=[vmem] * 6 + [pl.BlockSpec(memory_space=pltpu.SMEM)],
-        out_specs=[anywhere] * 6 + [vmem],
+        out_specs=[anywhere] * 6 + [vmem] * 3,
         out_shape=[
             jax.ShapeDtypeStruct((n, n_ctx, n_exp, rows, front_columns), low),
             jax.ShapeDtypeStruct((n_ctx, n_exp) + back.shape, low),
@@ -1111,6 +1147,8 @@
             jax.ShapeDtypeStruct((seq, columns), full),
             jax.ShapeDtypeStruct((seq, columns), low),
             jax.ShapeDtypeStruct((seq, heads * head), low),
+            jax.ShapeDtypeStruct((8, width), full),
+            jax.ShapeDtypeStruct((2, head), full),
         ],
         scratch_shapes=[
             pltpu.VMEM((n_ctx, count, width), low),
@@ -1281,9 +1319,13 @@
         for ahead in range(1, n_ctx):
             back_across(ahead).start()
         arrived[c] = shared[c, 0:b_rows]
-        for piece in range(pieces):
+        push(0)
+        small_load().wait()
+
+    for piece in range(1, pieces):
+        @pl.when(step == min(1 + 4 * piece, first_chunk))
+        def _():
             push(piece)
-        small_load().wait()
 
     for distance in range(n - 1, 0, -1):
         @pl.when(step == min(6 + 3 * (n - 1 - distance), first_chunk + chunks - 2))
@@ -1730,10 +1772,10 @@
     gain_len = query_gain.shape[0]
     small = jnp.concatenate(
         [
+            router_weight,
             attention_gain[:, None],
             mixture_gain[:, None],
             jnp.pad(jnp.concatenate([query_gain, key_gain]), (0, rows - 2 * gain_len))[:, None],
-            router_weight,
         ],
         axis=1,
     ).astype(low)
@@ -1757,55 +1799,32 @@
     cosine, sine = rope_tables(jnp.arange(seq_len, dtype=jnp.int32), head_dim)
     half = head_dim // 2
     sine = jnp.concatenate([-sine[:, :half], sine[:, half:]], axis=1)
-    front, output_part, column_routes, hidden, raw, turned, attended_low = gather(
-        tokens[0], front, output_weight.astype(low), routes[0], cosine, sine, bounds, gain_len,
-        heads_here, kv_here, sizes, 3,
+    (
+        front, output_part, column_routes, hidden, raw, turned, attended_low, gains, scales
+    ) = gather(
+        tokens[0], front, output_weight.astype(low), routes[0].T, cosine, sine, bounds, gain_len,
+        heads_here, kv_here, experts, sizes, 3,
     )
     front = front.reshape(width, -1)
     output_part = output_part.reshape(q_cols, width)
-    small = front[:, q_cols + 2 * kv_cols :]
-    first_gain = small[:, 0].astype(full)
-    second_gain = small[:, 1].astype(full)
-    head_gains = small[:, 2].reshape(devices, rows)
-    query_scale = head_gains[:, :gain_len].reshape(-1).astype(full)
-    key_scale = head_gains[:, gain_len : 2 * gain_len].reshape(-1).astype(full)
-    router_full = small[:, 3 : 3 + experts]
-
-    chosen = jnp.any(
-        column_routes[:, :, :, None] == jnp.arange(experts, dtype=jnp.int32), axis=2
-    )
-    hot = lax.dynamic_slice_in_dim(chosen.astype(low), dp_index * plane, plane, 2)
-    row_ids = jnp.arange(tok_count, dtype=jnp.int32)
-    earlier = (row_ids[None, :] < row_ids[:, None]).astype(low)
-    before = jnp.einsum("st,btj->bsj", earlier, hot, preferred_element_type=full)
-    together = 2 if 2 * capacity % 16 == 0 and n_dp % 2 == 0 else n_dp
-    groups = n_dp // together
-    slot_rows = -(-together * capacity // 16) * 16
-
-    def grouped(v):
-        return v.reshape(groups, together * tok_count, -1)
-
-    block_first = jnp.tile(jnp.arange(together, dtype=full) * capacity, groups)[:, None, None]
-    slot_at = grouped(jnp.where(hot > 0, before + block_first, -1.0))
-    slots = jnp.arange(slot_rows, dtype=full)
-    pick = (slot_at.transpose(0, 2, 1)[:, :, None, :] == slots[:, None]).astype(low)
-
-    scales = jnp.stack([query_scale, key_scale])
+    first_gain, second_gain = gains[0:1], gains[1:2]
 
     lanes = -(-experts // 128) * 128
-    router_wide = jnp.pad(router_full, ((0, 0), (0, lanes - experts)))
+    after = q_cols + 2 * kv_cols
+    router_wide = front[:, after : after + lanes]
     own_chosen = jnp.any(
         routes[0][:, :, None] == jnp.arange(lanes, dtype=jnp.int32), axis=1
     ).astype(full)
     (
         grad_rows, expert_in, _, middle, own_gates, active, gate_grad, up_grad, row_grads,
-        scaled_out, dot_rows,
+        scaled_out, dot_rows, pick,
     ) = dispatch(
-        attended_low, output_part, tokens[0], second_gain[None], router_wide, own_chosen,
-        cotangent[0], pick, gate_weight, up_weight, down_weight, experts, sizes, 1,
+        attended_low, output_part, tokens[0], second_gain, router_wide, own_chosen,
+        cotangent[0], column_routes, gate_weight, up_weight, down_weight, experts, capacity, sizes,
+        1,
     )
     branch_low, middle_grad, second_gain_grad, router_grad, gate_w_grad, up_w_grad, down_grad = combine(
-        row_grads, dot_rows, pick, middle, cotangent[0], second_gain[None], own_gates, router_wide,
+        row_grads, dot_rows, pick, middle, cotangent[0], second_gain, own_gates, router_wide,
         expert_in, grad_rows, active, gate_grad, up_grad, experts, sizes, 2,
     )
     gate_w_grad, up_w_grad, down_grad = gate_w_grad[None], up_w_grad[None], down_grad[None]
@@ -1822,7 +1841,7 @@
     tokens_grad, front_grad, output, output_share, small, _, _ = finish(
         bounds, turned, attended_grad.astype(low), raw, scales, cosine, sine, hidden, front,
         output_w_grad.astype(low).reshape(n_ctx, n_exp, -1, width), scaled_out, pick, middle,
-        middle_grad, tokens[0], first_gain[None], small, heads_here, kv_here, head_dim, sizes, 4,
+        middle_grad, tokens[0], first_gain, small, heads_here, kv_here, head_dim, sizes, 4,
         part=512 if n_ctx * n_exp <= 8 else 256,
     )
     tokens_grad = tokens_grad[None]

time: 860 us -> 847 us (0.985)
  Pallas kernels: 789 us -> 778 us
    unnamed x51 -> x48, local copies, waits for them, and re-layouts: 19.4 us -> 18.6 us
where the time goes in v6:
time: 847 us; the launch traced here: 834 us
  Pallas kernels  778 us (92%)
  local copies, waits for them, and re-layouts  26.8 us (3%)
  matrix products  15.3 us (2%)
  other arithmetic  12.2 us (1%)
    pallas_call x1, Pallas kernels, dispatch(): pl.pallas_call(functools.partial(dispatch_kernel, sizes=sizes, pieces=pie...  287 us
    pallas_call x1, Pallas kernels, finish(): pl.pallas_call(functools.partial(finish_kernel, block=count, heads=heads,...  208 us
    pallas_call x1, Pallas kernels, combine(): pl.pallas_call(functools.partial(combine_kernel, sizes=sizes, pieces=piec...  177 us
    pallas_call x1, Pallas kernels, gather(): pl.pallas_call(functools.partial(gather_kernel, sizes=sizes, gain_len=gai...  107 us
    unnamed x48, local copies, waits for them, and re-layouts  18.6 us

profile of v6, /device:TPU:14, one launch (start us, length us, event | category | flops | bytes accessed | tf_op | source)
XLA Modules:
  0.0 833.9 jit_solution(14258691911769739780)
XLA Ops:
  1.0 2.7 fusion.1
  3.9 1.0 pad_maximum_fusion.2.sin_ref
  5.4 0.9 pad_maximum_fusion.front_ref
  6.3 0.9 convert_element_type.61.back_ref
  7.2 106.9 %shard_map.263 = (bf16[4,4,2,64,1408]{4,3,2,1,0:T(8,128)(2,1)}, bf16[4,2,128,2048]{3,2,1,0:T(8,128)(2,1)}, s32[4,8,256]{2,1,0:T(8,128)}, bf16[1024,2048]{1,0:T(8...) custom-call(bf16[256,2048]{1,0:T(8,128)(2,1)} %bitcast.72, ...), custom_call_target="tpu_custom_call" | custom-call | tf_op jit(solution)/shard_map/pallas_call | solution.py:1135
  114.1 1.9 slice.62.router_ref
  116.0 1.5 fusion.5
  118.7 287.0 %shard_map.264 = (bf16[8,288,2048]{2,1,0:T(8,128)(2,1)}, bf16[8,288,2048]{2,1,0:T(8,128)(2,1)}, bf16[8,288,128]{2,1,0:T(8,128)(2,1)}, f32[256,2048]{1,0:T(8,128)...) custom-call(bf16[1024,1024]{1,0:T(8,128)(2,1)} %get-tuple-element.47, ...), custom_call_target="tpu_custom_call" | custom-call | tf_op jit(solution)/shard_map/pallas_call | solution.py:617
  405.7 176.8 %shard_map.265 = (bf16[4,256,2048]{2,1,0:T(8,128)(2,1)}, f32[256,2048]{1,0:T(8,128)}, f32[1,2048]{1,0:T(1,128)}, f32[128,2048]{1,0:T(8,128)}, f32[2048,768]{1,0:...) custom-call(bf16[8,288,2048]{2,1,0:T(8,128)(2,1)} %get-tuple-element.52.rows_ref, ...), custom_call_target="tpu_custom_call" | custom-call | tf_op jit(solution)/shard_map/pallas_call | solution.py:843
  582.5 1.0 slice_bitcast_fusion.1
  584.8 1.4 reduce.3
  586.6 0.9 pad.20.small_ref
  587.5 9.6 %convolution_convert_fusion = bf16[1024,2048]{1,0:T(8,128)(2,1)} fusion(bf16[1024,1024]{1,0:T(8,128)(2,1)} %get-tuple-element.47.attended_ref, bf16[1024,2048]{1,0:T(8,128)(2,1)} %bitcast.102), kind=kOutput, calls=%fused_computation | convolution fusion | flops 4297064448 | bytes 10485760 | tf_op jit(solution)/shard_map/ti,td->id/dot_general | solution.py:1833
  597.0 5.7 convolution_convert_fusion.1.grad_ref
  602.7 207.7 %shard_map.266 = (bf16[256,2048]{1,0:T(8,128)(2,1)}, bf16[4,64,1280]{2,1,0:T(8,128)(2,1)}, bf16[256,2048]{1,0:T(8,128)(2,1)}, f32[128,2048]{1,0:T(8,128)}, f32[8...) custom-call(s32[1,2]{1,0:T(1,128)} %bounds_ref.3, ...), custom_call_target="tpu_custom_call" | custom-call | tf_op jit(solution)/shard_map/pallas_call | solution.py:1661
  810.5 1.2 convert_element_type.67
  812.2 0.8 multiply_reduce_fusion.2
  812.9 0.8 multiply_reduce_fusion.1
  816.1 2.3 copy.74
  818.4 2.5 copy.75
  820.8 1.0 copy.76
  821.8 6.1 copy.77
  827.9 2.8 copy.78
  831.0 2.7 copy.79
  (77 shorter events, 6.8 us)
Async XLA Ops:
  0.6 4.2 copy-start.10
  0.7 4.2 copy-start.11
  0.7 4.2 copy-start.9
  0.7 4.3 copy-start.13
  0.7 4.3 copy-start.14
  0.7 4.5 copy-start.5
  0.7 4.5 copy-start.6
  0.7 4.5 copy-start
  3.7 2.6 copy-start.3
  5.3 112.2 %copy-start.7 = (s32[1,256,8]{1,2,0:T(8,128)S(1)}, s32[1,256,8]{1,2,0:T(8,128)}, u32[]{:S(2)}) copy-start(s32[1,256,8]{1,2,0:T(8,128)} %param.29) | copy-start | bytes 24580
  587.5 9.6 %copy-start.2 = (bf16[4,2,128,2048]{3,2,1,0:T(8,128)(2,1)S(1)}, bf16[4,2,128,2048]{3,2,1,0:T(8,128)(2,1)}, u32[]{:S(2)}) copy-start(bf16[4,2,128,2048]{3,2,1,0:T(8,128)(2,1)} %get-tuple-element.48) | copy-start | bytes 12582916
  587.5 9.6 %copy-start.12 = (bf16[4,256,2048]{2,1,0:T(8,128)(2,1)S(1)}, bf16[4,256,2048]{2,1,0:T(8,128)(2,1)}, u32[]{:S(2)}) copy-start(bf16[4,256,2048]{2,1,0:T(8,128)(2,1)} %get-tuple-element.62) | copy-start | bytes 12582916
  811.7 2.6 copy-start.8
  811.9 9.9 %copy-start.1 = (f32[4,8,8,1024]{3,2,0,1:T(8,128)}, f32[4,8,8,1024]{3,2,0,1:T(8,128)S(1)}, u32[]{:S(2)}) copy-start(f32[4,8,8,1024]{3,2,0,1:T(8,128)S(1)} %copy.57) | copy-start | bytes 3145732
  811.9 8.9 %copy-start.4 = (f32[128,2048]{1,0:T(8,128)S(1)}, f32[128,2048]{1,0:T(8,128)}, u32[]{:S(2)}) copy-start(f32[128,2048]{1,0:T(8,128)} %get-tuple-element.146) | copy-start | bytes 3145732
  818.4 9.5 %slice-start.2 = ((s8[6291456]{0:T(1024)(128)(4,1)}), s8[4194304]{0:T(1024)(128)(4,1)S(1)}, s32[]{:S(2)}) async-start(s8[6291456]{0:T(1024)(128)(4,1)} %bitcast.82), calls=%async_computation.2 | async-start | bytes 8388608
  821.8 6.1 slice-start.3
  821.8 8.9 %slice-start = ((s8[6291456]{0:T(1024)(128)(4,1)}), s8[4194304]{0:T(1024)(128)(4,1)S(1)}, s32[]{:S(2)}) async-start(s8[6291456]{0:T(1024)(128)(4,1)} %bitcast.79), calls=%async_computation | async-start | bytes 8388608
  827.9 3.1 slice-start.1

commit v7 on v6

--- a/solution.py
+++ b/solution.py
@@ -989,6 +989,8 @@
     tokens.pass_on()
     for distance in range(1, n):
         pass_on(front_line, distance, to_siblings)
+        if distance == 2:
+            pass_on(back_line, 2, nothing)
         pass_on(route_line, distance, nothing)
     for origin in range(n):
         for ahead in range(1, n_exp):
@@ -1073,10 +1075,7 @@
                     preferred_element_type=full,
                 ).astype(low)
 
-    project(0, n_ctx // 2)
-    if n > 2:
-        pass_on(back_line, 2, nothing)
-    project(n_ctx // 2, n_ctx)
+    project(0, n_ctx)
     turned_store = pltpu.make_async_copy(turned, turned_out, store_sem.at[3])
     turned_store.start()
     attend(0, heads // 4)

time: 847 us -> 858 us (1.013)
  Pallas kernels: 778 us -> 791 us
where the time goes in v7:
time: 858 us; the launch traced here: 846 us
  Pallas kernels  791 us (92%)
  local copies, waits for them, and re-layouts  26.8 us (3%)
  matrix products  15.3 us (2%)
  other arithmetic  12.2 us (1%)
    pallas_call x1, Pallas kernels, dispatch(): pl.pallas_call(functools.partial(dispatch_kernel, sizes=sizes, pieces=pie...  295 us
    pallas_call x1, Pallas kernels, finish(): pl.pallas_call(functools.partial(finish_kernel, block=count, heads=heads,...  207 us
    pallas_call x1, Pallas kernels, combine(): pl.pallas_call(functools.partial(combine_kernel, sizes=sizes, pieces=piec...  182 us
    pallas_call x1, Pallas kernels, gather(): pl.pallas_call(functools.partial(gather_kernel, sizes=sizes, gain_len=gai...  106 us
    unnamed x48, local copies, waits for them, and re-layouts  18.6 us

profile of v7, /device:TPU:14, one launch (start us, length us, event | category | flops | bytes accessed | tf_op | source)
XLA Modules:
  0.0 846.4 jit_solution(6586762723936948042)
XLA Ops:
  1.0 2.7 fusion.1
  3.9 1.0 pad_maximum_fusion.2.sin_ref
  5.4 0.9 pad_maximum_fusion.front_ref
  6.3 0.9 convert_element_type.61.back_ref
  7.2 106.4 %shard_map.263 = (bf16[4,4,2,64,1408]{4,3,2,1,0:T(8,128)(2,1)}, bf16[4,2,128,2048]{3,2,1,0:T(8,128)(2,1)}, s32[4,8,256]{2,1,0:T(8,128)}, bf16[1024,2048]{1,0:T(8...) custom-call(bf16[256,2048]{1,0:T(8,128)(2,1)} %bitcast.72, ...), custom_call_target="tpu_custom_call" | custom-call | tf_op jit(solution)/shard_map/pallas_call | solution.py:1134
  113.6 1.9 slice.62.router_ref
  115.4 1.5 fusion.5
  118.2 295.1 %shard_map.264 = (bf16[8,288,2048]{2,1,0:T(8,128)(2,1)}, bf16[8,288,2048]{2,1,0:T(8,128)(2,1)}, bf16[8,288,128]{2,1,0:T(8,128)(2,1)}, f32[256,2048]{1,0:T(8,128)...) custom-call(bf16[1024,1024]{1,0:T(8,128)(2,1)} %get-tuple-element.47, ...), custom_call_target="tpu_custom_call" | custom-call | tf_op jit(solution)/shard_map/pallas_call | solution.py:617
  413.3 181.8 %shard_map.265 = (bf16[4,256,2048]{2,1,0:T(8,128)(2,1)}, f32[256,2048]{1,0:T(8,128)}, f32[1,2048]{1,0:T(1,128)}, f32[128,2048]{1,0:T(8,128)}, f32[2048,768]{1,0:...) custom-call(bf16[8,288,2048]{2,1,0:T(8,128)(2,1)} %get-tuple-element.52.rows_ref, ...), custom_call_target="tpu_custom_call" | custom-call | tf_op jit(solution)/shard_map/pallas_call | solution.py:843
  595.2 1.0 slice_bitcast_fusion.1
  597.5 1.4 reduce.3
  599.2 0.9 pad.20.small_ref
  600.1 9.6 %convolution_convert_fusion = bf16[1024,2048]{1,0:T(8,128)(2,1)} fusion(bf16[1024,1024]{1,0:T(8,128)(2,1)} %get-tuple-element.47.attended_ref, bf16[1024,2048]{1,0:T(8,128)(2,1)} %bitcast.102), kind=kOutput, calls=%fused_computation | convolution fusion | flops 4297064448 | bytes 10485760 | tf_op jit(solution)/shard_map/ti,td->id/dot_general | solution.py:1832
  609.7 5.7 convolution_convert_fusion.1.grad_ref
  615.4 207.4 %shard_map.266 = (bf16[256,2048]{1,0:T(8,128)(2,1)}, bf16[4,64,1280]{2,1,0:T(8,128)(2,1)}, bf16[256,2048]{1,0:T(8,128)(2,1)}, f32[128,2048]{1,0:T(8,128)}, f32[8...) custom-call(s32[1,2]{1,0:T(1,128)} %bounds_ref.3, ...), custom_call_target="tpu_custom_call" | custom-call | tf_op jit(solution)/shard_map/pallas_call | solution.py:1660
  822.8 1.2 convert_element_type.67
  824.5 0.8 multiply_reduce_fusion.2
  825.2 0.8 multiply_reduce_fusion.1
  828.4 2.3 copy.74
  830.7 2.5 copy.75
  833.1 1.0 copy.76
  834.1 6.1 copy.77
  840.2 2.8 copy.78
  843.3 2.7 copy.79
  (77 shorter events, 6.8 us)
Async XLA Ops:
  0.6 4.2 copy-start.10
  0.7 4.2 copy-start.11
  0.7 4.2 copy-start.9
  0.7 4.3 copy-start.13
  0.7 4.3 copy-start.14
  0.7 4.5 copy-start.5
  0.7 4.5 copy-start.6
  0.7 4.5 copy-start
  3.7 2.6 copy-start.3
  5.3 111.6 %copy-start.7 = (s32[1,256,8]{1,2,0:T(8,128)S(1)}, s32[1,256,8]{1,2,0:T(8,128)}, u32[]{:S(2)}) copy-start(s32[1,256,8]{1,2,0:T(8,128)} %param.29) | copy-start | bytes 24580
  600.1 9.6 %copy-start.2 = (bf16[4,2,128,2048]{3,2,1,0:T(8,128)(2,1)S(1)}, bf16[4,2,128,2048]{3,2,1,0:T(8,128)(2,1)}, u32[]{:S(2)}) copy-start(bf16[4,2,128,2048]{3,2,1,0:T(8,128)(2,1)} %get-tuple-element.48) | copy-start | bytes 12582916
  600.1 9.6 %copy-start.12 = (bf16[4,256,2048]{2,1,0:T(8,128)(2,1)S(1)}, bf16[4,256,2048]{2,1,0:T(8,128)(2,1)}, u32[]{:S(2)}) copy-start(bf16[4,256,2048]{2,1,0:T(8,128)(2,1)} %get-tuple-element.62) | copy-start | bytes 12582916
  824.0 2.6 copy-start.8
  824.2 9.9 %copy-start.1 = (f32[4,8,8,1024]{3,2,0,1:T(8,128)}, f32[4,8,8,1024]{3,2,0,1:T(8,128)S(1)}, u32[]{:S(2)}) copy-start(f32[4,8,8,1024]{3,2,0,1:T(8,128)S(1)} %copy.57) | copy-start | bytes 3145732
  824.2 8.9 %copy-start.4 = (f32[128,2048]{1,0:T(8,128)S(1)}, f32[128,2048]{1,0:T(8,128)}, u32[]{:S(2)}) copy-start(f32[128,2048]{1,0:T(8,128)} %get-tuple-element.146) | copy-start | bytes 3145732
  830.7 9.5 %slice-start.2 = ((s8[6291456]{0:T(1024)(128)(4,1)}), s8[4194304]{0:T(1024)(128)(4,1)S(1)}, s32[]{:S(2)}) async-start(s8[6291456]{0:T(1024)(128)(4,1)} %bitcast.82), calls=%async_computation.2 | async-start | bytes 8388608
  834.1 6.1 slice-start.3
  834.1 8.9 %slice-start = ((s8[6291456]{0:T(1024)(128)(4,1)}), s8[4194304]{0:T(1024)(128)(4,1)S(1)}, s32[]{:S(2)}) async-start(s8[6291456]{0:T(1024)(128)(4,1)} %bitcast.79), calls=%async_computation | async-start | bytes 8388608
  840.2 3.1 slice-start.1
